TPU v7x, 32 devices: a whole 2x2x4 slice. The times are simulated.
32 devices in a mesh: grp: 2 (over y), op: 16 (over z, x, core).
Axes of the slice: x: 2, y: 2, z: 4, core: 2. Of those that a mesh axis runs over, the one named last changes fastest.
Arguments:
- state: bfloat16 [32, 128, 128], P(('grp', 'op')), parts along dimension 0, may hold values from -6 to 6
- sector_sizes: int32 [32], P('grp'), parts along dimension 0, may hold values from 16 to 128, as said below
- left_ops: bfloat16 [384, 12, 128, 128], P(('grp', 'op')), parts along dimension 0
- right_ops: bfloat16 [384, 12, 128, 128], P(('grp', 'op')), parts along dimension 0
- block_source: int32 [384, 12], P(('grp', 'op')), parts along dimension 0, may hold values from 0 to 15
- block_target: int32 [384, 12], P(('grp', 'op')), parts along dimension 0, may hold values from 0 to 15, as said below
- preconditioner: float32 [32, 128, 128], P(('grp', 'op')), parts along dimension 0, may hold values from 0.3 to 3
Outputs:
- sigma_first: float32 [32, 128, 128], P(('grp', 'op')), parts along dimension 0
- direction: bfloat16 [32, 128, 128], P(('grp', 'op')), parts along dimension 0
- sigma_second: float32 [32, 128, 128], P(('grp', 'op')), parts along dimension 0
- subspace: float32 [8], P('grp'), parts along dimension 0
There are 2 independent parts, one for each index of `grp`. A program takes and returns all parts, laid end to end along the dimension named above; each array names one. Nothing has to cross between parts.
Inputs may be any that keep to these rules, and one draw needn't show every extreme that they name: `sector_sizes`: each sector holds between 16 and 128 states; some sector holds exactly 128. `block_target`: in every operator term, a block whose index n is a multiple of 3 writes the sector that it reads; the targets of all other blocks are drawn apart from their sources.
All inputs are finite; a program needn't handle non-finite values.
Results may differ from a plain program's by a relative error of at most 0.0039.
Values may be sent and summed in bfloat16 or wider, within the bound.
No kernel may reach another device: no remote copies, remote signals or barrier semaphores. Data moves between devices by JAX's collectives and lax.ppermute only.
A program may use at most 128 MiB of HBM per device.

v0:
```python
import jax
import jax.numpy as jnp
from jax import lax
from jax.sharding import PartitionSpec as P

CAP = 128


def local_mask(sector_sizes, sec_count):
    first_sector = lax.axis_index("op") * sec_count
    own_sizes = lax.dynamic_slice(sector_sizes, (first_sector,), (sec_count,))
    width = sector_sizes.shape[0] * 0 + CAP
    rows = jnp.arange(width, dtype=jnp.int32)
    inside = rows[None, :] < own_sizes[:, None]
    return (inside[:, :, None] & inside[:, None, :]).astype(jnp.float32)


def apply_hamiltonian(vector_shard, left_ops, right_ops, block_source, block_target, mask):
    gathered = lax.all_gather(vector_shard, "op", axis=0, tiled=True)
    sector_total = gathered.shape[0]
    width = gathered.shape[1]
    source_flat = block_source.reshape(-1)
    target_flat = block_target.reshape(-1)
    left_flat = left_ops.reshape(-1, width, width)
    right_flat = right_ops.reshape(-1, width, width)
    blocks = gathered[source_flat]
    left_prod = jnp.einsum(
        "pij,pjk->pik", left_flat, blocks, preferred_element_type=jnp.float32
    ).astype(jnp.bfloat16)
    product = jnp.einsum("pik,plk->pil", left_prod, right_flat, preferred_element_type=jnp.float32)
    partial_sum = jnp.zeros((sector_total, width, width), jnp.float32).at[target_flat].add(product)
    owned = lax.psum_scatter(partial_sum, "op", scatter_dimension=0, tiled=True)
    return owned * mask


def shards(state, sector_sizes, left_ops, right_ops, block_source, block_target, preconditioner):
    mask = local_mask(sector_sizes, state.shape[0])
    wave = (state.astype(jnp.float32) * mask).astype(jnp.bfloat16)
    wave_f = wave.astype(jnp.float32)
    sigma_first = apply_hamiltonian(wave, left_ops, right_ops, block_source, block_target, mask)
    norm_wave, rayleigh = lax.psum((jnp.sum(wave_f * wave_f), jnp.sum(wave_f * sigma_first)), "op")
    energy = rayleigh / norm_wave
    scaled = preconditioner * (sigma_first - energy * wave_f)
    intersection = lax.psum(jnp.sum(wave_f * scaled), "op")
    direction = (scaled - intersection / norm_wave * wave_f).astype(jnp.bfloat16)
    sigma_second = apply_hamiltonian(
        direction, left_ops, right_ops, block_source, block_target, mask
    )
    dir_f = direction.astype(jnp.float32)
    cross_first, cross_second, dir_norm = lax.psum(
        (jnp.sum(wave_f * sigma_second), jnp.sum(dir_f * sigma_second), jnp.sum(dir_f * dir_f)),
        "op",
    )
    subspace = jnp.stack([rayleigh, cross_first, cross_second, dir_norm]) / norm_wave
    return (sigma_first, direction, sigma_second, subspace)


def solution(mesh):
    in_specs = (
        P(("grp", "op"), None, None),
        P("grp"),
        P(("grp", "op"), None, None, None),
        P(("grp", "op"), None, None, None),
        P(("grp", "op"), None),
        P(("grp", "op"), None),
        P(("grp", "op"), None, None),
    )
    out_specs = (
        P(("grp", "op"), None, None),
        P(("grp", "op"), None, None),
        P(("grp", "op"), None, None),
        P("grp"),
    )
    return jax.shard_map(shards, mesh=mesh, in_specs=in_specs, out_specs=out_specs, check_vma=False)
```

profile of v0, /device:TPU:0, one launch (start us, length us, event | category | flops | bytes accessed | tf_op | source)
XLA Modules:
  0.0 353.7 jit_solution(634355512421090099)
XLA Ops:
  7.2 0.0 reduce-scatter.3.cloned.1.call-start
  7.2 1.2 dynamic_slice.3
  8.5 0.6 iota_compare_fusion
  9.1 0.8 fusion.10
  10.0 24.6 %all_gather.6 = bf16[16,128,128]{2,1,0:T(8,128)(2,1)S(1)} all-gather(bf16[1,128,128]{2,1,0:T(8,128)(2,1)S(1)} %fusion.10), channel_id=1, replica_groups=mesh['grp'=2,'op'=16] {'op'}, dimensions={0}, use_global_device_ids=true | all-gather | bytes 557056 | tf_op jit(solution)/shard_map/all_gather | solution.py:19
  34.5 0.8 reshape.142
  35.4 0.8 reshape.141
  36.1 7.6 %gather_fusion = bf16[144,128,128]{2,1,0:T(8,128)(2,1)} fusion(bf16[16,128,128]{2,1,0:T(8,128)(2,1)S(1)} %all_gather.6, s32[1024]{0:T(1024)S(1)} %pad_clamp_fusion), kind=kCustom, calls=%fused_computation | custom fusion | bytes 9437760 | tf_op jit(solution)/shard_map/gather | solution.py:26
  43.8 11.8 %fusion.2 = f32[144,128,128]{2,1,0:T(8,128)} fusion(bf16[144,128,128]{2,1,0:T(8,128)(2,1)} %bitcast.15, bf16[144,128,128]{2,1,0:T(8,128)(2,1)} %gather_fusion, bf16[144,128,128]{2,1,0:T(8,128)(2,1)} %bitcast.17), kind=kOutput, calls=%fused_computation.6 | convolution fusion | flops 1210318848 | bytes 23592960 | tf_op jit(solution)/shard_map/pik,plk->pil/dot_general | solution.py:30
  55.6 0.1 broadcast.94.clone
  55.7 0.0 copy-start.2
  55.7 0.0 copy-start.5
  55.7 19.1 %scatter_fusion = f32[16,128,128]{2,1,0:T(8,128)S(1)} fusion(f32[16,128,128]{2,1,0:T(8,128)S(1)} %broadcast.94.clone, s32[144]{0:T(256)S(1)} %bitcast.19, f32[144,128,128]{2,1,0:T(8,128)} %fusion.2), kind=kCustom, calls=%fused_computation.2 | custom fusion | flops 2359296 | bytes 28312128 | tf_op jit(solution)/shard_map/scatter-add | solution.py:31
  74.8 0.0 copy-start.1
  74.9 1.0 copy-done.1
  75.8 0.0 reduce-scatter.3.cloned.1.call-update
  75.9 0.0 reduce-scatter.5.cloned.1.call-start
  75.9 54.8 %reduce-scatter.3.cloned.1.call-done = f32[1,128,128]{2,1,0:T(8,128)} async-done(((f32[16,128,128]{2,1,0:T(8,128)}), f32[1,128,128]{2,1,0:T(8,128)}) %reduce-scatter.3.cloned.1.call-update) | async-done | bytes 65552 | tf_op jit(solution)/shard_map/reduce_scatter | solution.py:32
  130.7 0.0 copy-done.2
  130.7 1.5 fusion.12
  132.3 0.0 copy-start.3
  132.3 30.2 %all-reduce.1 = (f32[]{:T(128)}, f32[]{:T(128)}) all-reduce(f32[]{:T(128)} %get-tuple-element.8, f32[]{:T(128)} %get-tuple-element.7), channel_id=1, replica_groups=mesh['grp'=2,'op'=16] {'op'}, use_global_device_ids=true, to_apply=%region_3.0 | all-reduce | flops 2 | bytes 16 | tf_op jit(solution)/shard_map/psum | solution.py:41
  163.8 0.0 copy-done.5
  163.8 0.7 fusion.15
  164.5 30.1 %psum.44 = f32[]{:T(128)} all-reduce(f32[]{:T(128)} %fusion.15), channel_id=1, replica_groups=mesh['grp'=2,'op'=16] {'op'}, use_global_device_ids=true, to_apply=%region_7.0 | all-reduce | flops 1 | bytes 8 | tf_op jit(solution)/shard_map/psum | solution.py:44
  195.9 0.1 fusion.17
  196.0 0.0 copy-start.4
  196.0 18.9 %all_gather.7 = bf16[16,128,128]{2,1,0:T(8,128)(2,1)S(1)} all-gather(bf16[1,128,128]{2,1,0:T(8,128)(2,1)S(1)} %fusion.17), channel_id=1, replica_groups=mesh['grp'=2,'op'=16] {'op'}, dimensions={0}, use_global_device_ids=true | all-gather | bytes 557056 | tf_op jit(solution)/shard_map/all_gather | solution.py:19
  214.9 7.6 %gather_fusion.1 = bf16[144,128,128]{2,1,0:T(8,128)(2,1)} fusion(bf16[16,128,128]{2,1,0:T(8,128)(2,1)S(1)} %all_gather.7, s32[1024]{0:T(1024)S(1)} %pad_clamp_fusion), kind=kCustom, calls=%fused_computation.1 | custom fusion | bytes 9437760 | tf_op jit(solution)/shard_map/gather | solution.py:26
  222.5 0.0 copy-done.3
  222.5 11.9 %fusion = f32[144,128,128]{2,1,0:T(8,128)} fusion(bf16[144,128,128]{2,1,0:T(8,128)(2,1)} %bitcast.16, bf16[144,128,128]{2,1,0:T(8,128)(2,1)} %gather_fusion.1, bf16[144,128,128]{2,1,0:T(8,128)(2,1)} %bitcast.18), kind=kOutput, calls=%fused_computation.4 | convolution fusion | flops 1210318848 | bytes 23592960 | tf_op jit(solution)/shard_map/pik,plk->pil/dot_general | solution.py:30
  234.4 0.1 broadcast.94
  234.5 19.1 %scatter_fusion.1 = f32[16,128,128]{2,1,0:T(8,128)S(1)} fusion(f32[16,128,128]{2,1,0:T(8,128)S(1)} %broadcast.94, s32[144]{0:T(256)S(1)} %bitcast.20, f32[144,128,128]{2,1,0:T(8,128)} %fusion), kind=kCustom, calls=%fused_computation.3 | custom fusion | flops 2359296 | bytes 28312128 | tf_op jit(solution)/shard_map/scatter-add | solution.py:31
  253.6 0.0 copy-start
  253.6 1.0 copy-done
  254.6 0.0 reduce-scatter.5.cloned.1.call-update
  254.6 56.1 %reduce-scatter.5.cloned.1.call-done = f32[1,128,128]{2,1,0:T(8,128)} async-done(((f32[16,128,128]{2,1,0:T(8,128)}), f32[1,128,128]{2,1,0:T(8,128)}) %reduce-scatter.5.cloned.1.call-update) | async-done | bytes 65552 | tf_op jit(solution)/shard_map/reduce_scatter | solution.py:32
  310.7 0.0 copy-done.4
  310.7 2.2 fusion.18
  312.9 30.2 %all-reduce = (f32[1]{0:T(128)}, f32[1]{0:T(128)}, f32[1]{0:T(128)}) all-reduce(f32[1]{0:T(128)} %bitcast.8, f32[1]{0:T(128)} %bitcast.7, f32[1]{0:T(128)} %bitcast.6), channel_id=1, replica_groups=mesh['grp'=2,'op'=16] {'op'}, use_global_device_ids=true, to_apply=%region_15.0 | all-reduce | flops 3 | bytes 24 | tf_op jit(solution)/shard_map/psum | solution.py:50
  343.2 3.7 %maximum_divide_fusion = f32[4]{0:T(128)} fusion(f32[1]{0:T(128)} %get-tuple-element.9, f32[1]{0:T(128)} %get-tuple-element.10, f32[1]{0:T(128)} %get-tuple-element.11, f32[1]{0:T(128)} %bitcast.5, f32[]{:T(128)} %get-tuple-element.13), kind=kLoop, calls=%fused_computation.35 | loop fusion | flops 16 | bytes 36 | tf_op jit(solution)/shard_map/div | solution.py:54
  (3 shorter events, 0.0 us)
Async XLA Ops:
  7.2 123.6 %reduce-scatter.3.cloned.1.call-start = ((), (), s32[]{:S(2)}) async-start(), calls=%async_computation.2 | async-start | bytes 1114112 | tf_op jit(solution)/shard_map/reduce_scatter | solution.py:32
  55.7 75.0 %copy-start.2 = (bf16[1,128,128]{2,1,0:T(8,128)(2,1)S(1)}, bf16[1,128,128]{2,1,0:T(8,128)(2,1)}, u32[]{:S(2)}) copy-start(bf16[1,128,128]{2,1,0:T(8,128)(2,1)} %param.7) | copy-start | bytes 98308
  55.7 108.1 %copy-start.5 = (f32[1,128,128]{2,1,0:T(8,128)S(1)}, f32[1,128,128]{2,1,0:T(8,128)}, u32[]{:S(2)}) copy-start(f32[1,128,128]{2,1,0:T(8,128)} %param.13) | copy-start | bytes 196612
  74.8 1.0 copy-start.1
  75.9 234.9 %reduce-scatter.5.cloned.1.call-start = ((), (), s32[]{:S(2)}) async-start(), calls=%async_computation.3 | async-start | bytes 1114112 | tf_op jit(solution)/shard_map/reduce_scatter | solution.py:32
  132.3 90.3 %copy-start.3 = (f32[1,128,128]{2,1,0:T(8,128)}, f32[1,128,128]{2,1,0:T(8,128)S(1)}, u32[]{:S(2)}) copy-start(f32[1,128,128]{2,1,0:T(8,128)S(1)} %get-tuple-element.15) | copy-start | bytes 196612
  196.0 114.7 %copy-start.4 = (bf16[1,128,128]{2,1,0:T(8,128)(2,1)}, bf16[1,128,128]{2,1,0:T(8,128)(2,1)S(1)}, u32[]{:S(2)}) copy-start(bf16[1,128,128]{2,1,0:T(8,128)(2,1)S(1)} %fusion.17) | copy-start | bytes 98308
  253.6 1.0 copy-start
Sparse Core Ops, SparseCore 0:
  76.0 54.7 reduce-scatter.2
  254.7 55.9 reduce-scatter.4
where the time goes:
time: 355 us; the launch traced here: 354 us
  blocking collectives  134 us (38%)
  waiting for transfers between devices  111 us (31%)
  other arithmetic  48 us (14%)
  matrix products  23.7 us (7%)
  local copies, waits for them, and re-layouts  20.2 us (6%)
  between operations  16.8 us (5%)
    reduce_scatter x2, waiting for transfers between devices, apply_hamiltonian(): owned = lax.psum_scatter(partial_sum, 'op', scatter_dimension=0, tiled=True)  111 us
    all_gather x2, blocking collectives, apply_hamiltonian(): gathered = lax.all_gather(vector_shard, 'op', axis=0, tiled=True)  43.5 us
    scatter-add x2, other arithmetic, apply_hamiltonian(): jnp.zeros((sector_total, width, width), jnp.float32).at[target_flat]  38.2 us
    psum x1, blocking collectives, shards(): lax.psum((jnp.sum(wave_f * sigma_second), jnp.sum(dir_f * sigma_second),...  30.2 us
    psum x1, blocking collectives, shards(): lax.psum((jnp.sum(wave_f * wave_f), jnp.sum(wave_f * sigma_first)), 'op')  30.2 us
    psum x1, blocking collectives, shards(): intersection = lax.psum(jnp.sum(wave_f * scaled), 'op')  30.1 us
    dot_general x2, matrix products, apply_hamiltonian(): jnp.einsum('pik,plk->pil', left_prod, right_flat, preferred_element_type=...  23.7 us
    gather x2, local copies, waits for them, and re-layouts, apply_hamiltonian(): blocks = gathered[source_flat]  15.2 us
  transfers between devices with their start and end apart: 2, of which 2 were waited for; matrix products, arithmetic and copies ran while one was open for 0% of the time, Pallas kernels for 0%

commit v1 on v0

v1 whole, which is shorter than its diff:
```python
import jax
import jax.numpy as jnp
from jax import lax
from jax.experimental import pallas as pl
from jax.experimental.pallas import tpu as pltpu
from jax.sharding import Mesh
from jax.sharding import PartitionSpec as P

BF16 = jnp.bfloat16
F32 = jnp.float32
TAIL = 16
LIMIT = 36 << 20


def each(count, body, carry):
    if count <= 8:
        for j in range(count):
            carry = body(j, carry)
        return carry
    return lax.fori_loop(0, count, body, carry)


def mask_of(size, width):
    rows = lax.broadcasted_iota(jnp.int32, (width, width), 0)
    cols = lax.broadcasted_iota(jnp.int32, (width, width), 1)
    return (rows < size) & (cols < size)


def fold(x):
    return jnp.sum(x, axis=0, keepdims=True)


def tail_of(rows):
    pieces = []
    for row in rows:
        rest = row
        for _ in range(3):
            piece = rest.astype(BF16).astype(F32)
            pieces.append(piece)
            rest = rest - piece
    lanes = rows[0].shape[1]
    place = lax.broadcasted_iota(jnp.int32, (TAIL, lanes), 0)
    tail = jnp.zeros((TAIL, lanes), F32)
    for at, piece in enumerate(pieces):
        tail = jnp.where(place == at, piece, tail)
    return tail.astype(BF16)


def rows_of(tail, count):
    wide = tail.astype(F32)
    return [
        (wide[3 * i : 3 * i + 1] + wide[3 * i + 1 : 3 * i + 2]) + wide[3 * i + 2 : 3 * i + 3]
        for i in range(count)
    ]


def total(row):
    return jnp.broadcast_to(jnp.sum(row, axis=1, keepdims=True), row.shape)


def apply_blocks(src, tgt, vec, left, right, acc, chips, core):
    terms, nnz = left.shape[0], left.shape[1]
    per = 3 if terms % 3 == 0 else 1

    def place(s):
        return (s >> 1) + chips * ((s ^ core) & 1)

    acc[...] = jnp.zeros_like(acc)

    def step(i, carry):
        items = [(i * per + k, n) for k in range(per) for n in range(nnz)]
        prods = [
            jnp.dot(left[k, n], vec[place(src[k, n])], preferred_element_type=F32).astype(BF16)
            for k, n in items
        ]
        for (k, n), prod in zip(items, prods):
            at = place(tgt[k, n])
            acc[at] += lax.dot_general(
                prod, right[k, n], (((1,), (1,)), ((), ())), preferred_element_type=F32
            )
        return carry

    lax.fori_loop(0, terms // per, step, 0)


def first_kernel(src, tgt, sizes, own, other, left, right, theirs, mine, wave, sums, acc):
    chips, width = own.shape[0], own.shape[2]
    core = lax.axis_index("core")

    def load(j, carry):
        here, there = carry
        a = jnp.where(mask_of(sizes[2 * j + core], width), own[j].astype(F32), 0.0)
        b = jnp.where(mask_of(sizes[2 * j + 1 - core], width), other[j].astype(F32), 0.0)
        wave[j] = a.astype(BF16)
        wave[chips + j] = b.astype(BF16)
        return here + fold(a * a), there + fold(b * b)

    zero = jnp.zeros((1, width), F32)
    here, there = each(chips, load, (zero, zero))
    apply_blocks(src, tgt, wave, left, right, acc, chips, core)

    def store(j, ray):
        a, b = acc[j], acc[chips + j]
        mine[j] = a
        theirs[j, 0:width] = b.astype(BF16)
        ray = ray + fold(wave[j].astype(F32) * a)
        return ray + fold(wave[chips + j].astype(F32) * b)

    ray = each(chips, store, zero)
    tail = tail_of([ray])
    theirs[0, width : width + TAIL] = tail
    sums[0:1] = here + there
    sums[1:2] = ray


def second_kernel(src, tgt, own, other, wave, left, right, theirs, mine, sums, vec, acc):
    chips, width = own.shape[0], own.shape[2]
    core = lax.axis_index("core")

    def load(j, carry):
        vec[j] = own[j, 0:width]
        vec[chips + j] = other[j, 0:width]
        a = rows_of(own[j, width : width + TAIL], 3)
        b = rows_of(other[j, width : width + TAIL], 3)
        return tuple(x + y for x, y in zip(carry, a + b))

    zero = jnp.zeros((1, width), F32)
    got = each(chips, load, (zero,) * 6)
    apply_blocks(src, tgt, vec, left, right, acc, chips, core)

    def store(j, carry):
        first, second = carry
        a, b = acc[j], acc[chips + j]
        mine[j] = a
        theirs[j, 0:width] = b.astype(BF16)
        first = first + fold(wave[j].astype(F32) * a) + fold(wave[chips + j].astype(F32) * b)
        second = second + fold(vec[j].astype(F32) * a) + fold(vec[chips + j].astype(F32) * b)
        return first, second

    first, second = each(chips, store, (zero, zero))
    theirs[0, width : width + TAIL] = tail_of([first, second])
    for i in range(3):
        sums[i : i + 1] = got[i] + got[3 + i]
    sums[3:4] = first
    sums[4:5] = second


def chip_kernel(at, count, mine, got, sums, out):
    chips, width = mine.shape[0], mine.shape[2]
    rows = rows_of(got[0, width : width + TAIL], count)
    tail = tail_of([sums[at + i : at + i + 1] + rows[i] for i in range(count)])

    def store(j, carry):
        out[j, 0:width] = (mine[j] + got[j, 0:width].astype(F32)).astype(BF16)
        out[j, width : width + TAIL] = tail
        return carry

    each(chips, store, 0)


def gather_sums(got, count):
    chips, width = got.shape[0], got.shape[2]

    def add(j, carry):
        block = carry[0] + got[j, 0:width].astype(F32)
        rows = rows_of(got[j, width : width + TAIL], count)
        return (block,) + tuple(x + y for x, y in zip(carry[1:], rows))

    zero = jnp.zeros((1, width), F32)
    return each(chips, add, (jnp.zeros((width, width), F32),) + (zero,) * count)


def residual_kernel(sizes, got, state, precond, sums, sigma, resid, send, keep):
    chips, width = got.shape[0], got.shape[2]
    inside = mask_of(sizes[2 * lax.axis_index("chip") + lax.axis_index("core")], width)
    block, ray = gather_sums(got, 1)
    first = jnp.where(inside, block, 0.0)
    wave = jnp.where(inside, state[0].astype(F32), 0.0)
    norm, ray = total(sums[0:1]), total(ray)
    q = precond[0] * (first - ray / norm * wave)
    low = q.astype(BF16)
    tail = tail_of([fold(wave * q), fold(low.astype(F32) * first), fold(q * q)])
    sigma[0] = first
    resid[0] = q
    keep[0:1] = norm
    keep[1:2] = ray

    def store(j, carry):
        send[j, 0:width] = low
        send[j, width : width + TAIL] = tail
        return carry

    each(chips, store, 0)


def final_kernel(sizes, got, state, first, resid, keep, sums, direction, sigma, subspace):
    width = got.shape[2]
    inside = mask_of(sizes[2 * lax.axis_index("chip") + lax.axis_index("core")], width)
    block, cross, square = gather_sums(got, 2)
    wave = jnp.where(inside, state[0].astype(F32), 0.0)
    norm, ray = keep[0:1], keep[1:2]
    inter, mixed, length = (total(sums[i : i + 1]) for i in range(3))
    cross, square = total(cross), total(square)
    c = inter / norm
    direction[0] = (resid[0] - c * wave).astype(BF16)
    sigma[0] = jnp.where(inside, block, 0.0) - c * first[0]
    values = (
        ray,
        cross - c * ray,
        square - c * mixed - c * (cross - c * ray),
        length - 2.0 * c * inter + c * c * norm,
    )
    for i, value in enumerate(values):
        subspace[i] = jnp.max(value / norm)


VMEM = pl.BlockSpec(memory_space=pltpu.VMEM)
SMEM = pl.BlockSpec(memory_space=pltpu.SMEM)


def call(kernel, name, ins, outs, scratch, args, flops, out_specs=None):
    moved = sum(a.size * a.dtype.itemsize for a in args)
    return pl.pallas_call(
        kernel,
        name=name,
        in_specs=ins,
        out_specs=out_specs or [VMEM] * len(outs),
        out_shape=[jax.ShapeDtypeStruct(s, d) for s, d in outs],
        scratch_shapes=scratch,
        compiler_params=pltpu.CompilerParams(vmem_limit_bytes=LIMIT),
        cost_estimate=pl.CostEstimate(flops=flops, bytes_accessed=moved, transcendentals=0),
    )(*args)


def shards(state, sector_sizes, left, right, source, target, precond):
    chips = lax.axis_size("chip")
    width = state.shape[1]
    high = width + TAIL
    swap = [(0, 1), (1, 0)]
    every = 2 * chips
    flops = 4 * left.size * width

    with jax.named_scope("gather_state"):
        copies = jnp.broadcast_to(state, (chips, width, width))
        own = lax.all_to_all(copies, "chip", 0, 0, tiled=True)
        other = lax.ppermute(own, "core", swap)
    with jax.named_scope("first_sigma"):
        theirs, mine, wave, sums = call(
            first_kernel, "first_sigma", [SMEM] * 3 + [VMEM] * 4,
            [((chips, high, width), BF16), ((chips, width, width), F32),
             ((every, width, width), BF16), ((8, width), F32)],
            [pltpu.VMEM((every, width, width), F32)],
            (source, target, sector_sizes, own, other, left, right), flops,
        )
    with jax.named_scope("sum_first"):
        got = lax.ppermute(theirs, "core", swap)
        (part,) = call(
            lambda *refs: chip_kernel(1, 1, *refs), "chip_sum", [VMEM] * 3,
            [((chips, high, width), BF16)], [], (mine, got, sums), mine.size,
        )
        got = lax.all_to_all(part, "chip", 0, 0, tiled=True)
    with jax.named_scope("residual"):
        first, resid, send, keep = call(
            residual_kernel, "residual", [SMEM] + [VMEM] * 4,
            [((1, width, width), F32), ((1, width, width), F32),
             ((chips, high, width), BF16), ((8, width), F32)],
            [], (sector_sizes, got, state, precond, sums), mine.size,
        )
    with jax.named_scope("gather_residual"):
        own = lax.all_to_all(send, "chip", 0, 0, tiled=True)
        other = lax.ppermute(own, "core", swap)
    with jax.named_scope("second_sigma"):
        theirs, mine, sums = call(
            second_kernel, "second_sigma", [SMEM] * 2 + [VMEM] * 5,
            [((chips, high, width), BF16), ((chips, width, width), F32), ((8, width), F32)],
            [pltpu.VMEM((every, width, width), BF16), pltpu.VMEM((every, width, width), F32)],
            (source, target, own, other, wave, left, right), flops,
        )
    with jax.named_scope("sum_second"):
        got = lax.ppermute(theirs, "core", swap)
        (part,) = call(
            lambda *refs: chip_kernel(3, 2, *refs), "chip_sum", [VMEM] * 3,
            [((chips, high, width), BF16)], [], (mine, got, sums), mine.size,
        )
        got = lax.all_to_all(part, "chip", 0, 0, tiled=True)
    with jax.named_scope("outputs"):
        direction, second, subspace = call(
            final_kernel, "outputs", [SMEM] + [VMEM] * 6,
            [((1, width, width), BF16), ((1, width, width), F32), ((4,), F32)],
            [], (sector_sizes, got, state, first, resid, keep, sums), mine.size,
            [VMEM, VMEM, SMEM],
        )
    return first, direction, second, subspace


def solution(mesh):
    groups, members = mesh.shape["grp"], mesh.shape["op"]
    split = Mesh(mesh.devices.reshape(groups, members // 2, 2), ("grp", "chip", "core"))
    rows = P(("grp", "chip", "core"))
    return jax.shard_map(
        shards,
        mesh=split,
        in_specs=(rows, P("grp"), rows, rows, rows, rows, rows),
        out_specs=(rows, rows, rows, P("grp")),
        check_vma=False,
    )
```

time: 355 us -> 87.1 us (0.25)
  waiting for transfers between devices: 111 us -> 5.97 us
  blocking collectives: 134 us -> 56.4 us
  other arithmetic: 48 us -> 0 us
  matrix products: 23.7 us -> 0 us
  between operations: 16.8 us -> 0.72 us
  Pallas kernels: 0 us -> 15.5 us
  local copies, waits for them, and re-layouts: 20.2 us -> 7.56 us
    reduce_scatter x2 -> x0, waiting for transfers between devices: 111 us -> none  [apply_hamiltonian(): owned = lax.psum_scatter(partial_sum, 'op', scatter_dimension=0, tiled=True)]
    psum x3 -> x0, blocking collectives: 90.5 us -> none  [the longest x1 30.2 us: shards(): lax.psum((jnp.sum(wave_f * sigma_second), jnp.sum(dir_f * sigma_second),...]
    all_to_all x0 -> x4, blocking collectives: none -> 56.4 us  [the longest x2 27.4 us: shards(): got = lax.all_to_all(part, 'chip', 0, 0, tiled=True)]
    all_gather x2 -> x0, blocking collectives: 43.5 us -> none  [apply_hamiltonian(): gathered = lax.all_gather(vector_shard, 'op', axis=0, tiled=True)]
    scatter-add x2 -> x0, other arithmetic: 38.2 us -> none  [apply_hamiltonian(): jnp.zeros((sector_total, width, width), jnp.float32).at[target_flat]]
    dot_general x2 -> x0, matrix products: 23.7 us -> none  [apply_hamiltonian(): jnp.einsum('pik,plk->pil', left_prod, right_flat, preferred_element_type=...]
    pallas_call x0 -> x6, Pallas kernels: none -> 15.5 us  [call(): pl.pallas_call(kernel, name=name, in_specs=ins, out_specs=out_specs or [V...]
    gather x2 -> x0, local copies, waits for them, and re-layouts: 15.2 us -> none  [apply_hamiltonian(): blocks = gathered[source_flat]]
  transfers between devices with their start and end apart: 2 -> 4, of which waited for: 2 -> 4; matrix products, arithmetic and copies ran while one was open for 0% -> 0% of each run, Pallas kernels for 0% -> 0%
where the time goes in v1:
time: 87.1 us; the launch traced here: 86.6 us
  blocking collectives  56.4 us (65%)
  Pallas kernels  15.5 us (18%)
  local copies, waits for them, and re-layouts  7.56 us (9%)
  waiting for transfers between devices  5.97 us (7%)
    all_to_all x2, blocking collectives, shards(): got = lax.all_to_all(part, 'chip', 0, 0, tiled=True)  27.4 us
    all_to_all x1, blocking collectives, shards(): own = lax.all_to_all(copies, 'chip', 0, 0, tiled=True)  16.1 us
    pallas_call x6, Pallas kernels, call(): pl.pallas_call(kernel, name=name, in_specs=ins, out_specs=out_specs or [V...  15.5 us
    all_to_all x1, blocking collectives, shards(): own = lax.all_to_all(send, 'chip', 0, 0, tiled=True)  12.9 us
    unnamed x26, local copies, waits for them, and re-layouts  6.77 us
    ppermute x2, waiting for transfers between devices, shards(): other = lax.ppermute(own, 'core', swap)  3.11 us
    ppermute x2, waiting for transfers between devices, shards(): got = lax.ppermute(theirs, 'core', swap)  2.85 us
  transfers between devices with their start and end apart: 4, of which 4 were waited for; matrix products, arithmetic and copies ran while one was open for 0% of the time, Pallas kernels for 0%

profile of v1, /device:TPU:0, one launch (start us, length us, event | category | flops | bytes accessed | tf_op | source)
XLA Modules:
  0.0 86.6 jit_solution(10588737898035978470)
XLA Ops:
  0.6 0.8 broadcast_in_dim.8
  1.4 0.0 copy-start.4
  1.4 0.0 copy-start.5
  1.5 0.0 copy-start.12
  1.5 0.0 copy-start.8
  1.5 0.0 copy-start.10
  1.5 16.1 %all_to_all.20.own = bf16[8,128,128]{2,1,0:T(8,128)(2,1)S(1)} all-to-all(bf16[8,128,128]{2,1,0:T(8,128)(2,1)S(1)} %broadcast_in_dim.8), channel_id=1, replica_groups=mesh['grp'=2,'chip'=8,'core'=2] {'chip'}, dimensions={0} | all-to-all | bytes 524288 | tf_op jit(solution)/shard_map/gather_state/all_to_all | solution.py:245
  17.6 0.0 collective-permute-start
  17.6 1.5 %collective-permute-done.other = bf16[8,128,128]{2,1,0:T(8,128)(2,1)S(1)} collective-permute-done((bf16[8,128,128]{2,1,0:T(8,128)(2,1)S(1)}, bf16[8,128,128]{2,1,0:T(8,128)(2,1)S(1)}, u32[]{:S(2)}, u32[]{:S(2)}) %collective-permute-start) | collective-permute-done | bytes 262176 | tf_op jit(solution)/shard_map/gather_state/ppermute | solution.py:246
  19.1 0.0 copy-start
  19.1 2.3 %copy-done = bf16[12,12,128,128]{3,2,1,0:T(8,128)(2,1)S(1)} copy-done((bf16[12,12,128,128]{3,2,1,0:T(8,128)(2,1)S(1)}, bf16[12,12,128,128]{3,2,1,0:T(8,128)(2,1)}, u32[]{:S(2)}) %copy-start) | copy-done | bytes 4718616
  21.5 0.0 copy-start.2
  21.5 2.3 %copy-done.2 = bf16[12,12,128,128]{3,2,1,0:T(8,128)(2,1)S(1)} copy-done((bf16[12,12,128,128]{3,2,1,0:T(8,128)(2,1)S(1)}, bf16[12,12,128,128]{3,2,1,0:T(8,128)(2,1)}, u32[]{:S(2)}) %copy-start.2) | copy-done | bytes 4718616
  23.8 0.0 copy-start.7
  23.8 0.7 copy-done.7
  24.5 0.0 copy-start.9
  24.5 0.7 copy-done.9
  25.2 0.0 copy-start.11
  25.2 0.7 copy-done.11
  25.9 0.0 copy-start.1
  25.9 0.0 copy-start.3
  25.9 6.5 %first_sigma.1 = (bf16[8,144,128]{2,1,0:T(8,128)(2,1)S(1)}, f32[8,128,128]{2,1,0:T(8,128)S(1)}, bf16[16,128,128]{2,1,0:T(8,128)(2,1)S(1)}, f32[8,128]{1,0:T(8,128)S(1)}) custom-call(s32[12,12]{1,0:T(8,128)S(1)} %copy-done.7, s32[12,12]{1,0:T(8,128)S(1)} %copy-done.9, s32[16]{0:T(128)S(1)} %copy-done.11, bf16[8,128,128]{2,1,0:T(8,128)(2,1)S(1)} %all_to_all.20.own, ...), custom_call_target="tpu_custom_call" | custom-call | flops 1207959552 | bytes 9962688 | tf_op jit(solution)/shard_map/first_sigma/first_sigma/pallas_call | solution.py:223
  32.4 0.2 collective-permute-start.1
  32.6 1.4 %collective-permute-done.1.refs_1_ = bf16[8,144,128]{2,1,0:T(8,128)(2,1)S(1)} collective-permute-done((bf16[8,144,128]{2,1,0:T(8,128)(2,1)S(1)}, bf16[8,144,128]{2,1,0:T(8,128)(2,1)S(1)}, u32[]{:S(2)}, u32[]{:S(2)}) %collective-permute-start.1) | collective-permute-done | bytes 294944 | tf_op jit(solution)/shard_map/sum_first/ppermute | solution.py:256
  34.0 0.1 chip_sum.2
  34.1 14.0 %all_to_all.21.got = bf16[8,144,128]{2,1,0:T(8,128)(2,1)S(1)} all-to-all(bf16[8,144,128]{2,1,0:T(8,128)(2,1)S(1)} %chip_sum.2), channel_id=1, replica_groups=mesh['grp'=2,'chip'=8,'core'=2] {'chip'}, dimensions={0} | all-to-all | bytes 589824 | tf_op jit(solution)/shard_map/sum_first/all_to_all | solution.py:261
  48.1 0.0 copy-done.4
  48.1 0.0 copy-done.5
  48.1 0.0 copy-done.12
  48.1 1.2 %residual.1 = (f32[1,128,128]{2,1,0:T(8,128)}, f32[1,128,128]{2,1,0:T(8,128)S(1)}, bf16[8,144,128]{2,1,0:T(8,128)(2,1)S(1)}, f32[8,128]{1,0:T(8,128)S(1)}) custom-call(s32[16]{0:T(128)S(1)} %copy-done.12, bf16[8,144,128]{2,1,0:T(8,128)(2,1)S(1)} %all_to_all.21.got, bf16[1,128,128]{2,1,0:T(8,128)(2,1)S(1)} %copy-done.4, f32[1,128,128]{2,1,0:T(8,128)S(1)} %copy-done.5, ...), custom_call_target="tpu_custom_call" | custom-call | flops 131072 | bytes 397376 | tf_op jit(solution)/shard_map/residual/residual/pallas_call | solution.py:223
  49.3 12.9 %all_to_all.22.own = bf16[8,144,128]{2,1,0:T(8,128)(2,1)S(1)} all-to-all(bf16[8,144,128]{2,1,0:T(8,128)(2,1)S(1)} %get-tuple-element.22), channel_id=1, replica_groups=mesh['grp'=2,'chip'=8,'core'=2] {'chip'}, dimensions={0} | all-to-all | bytes 589824 | tf_op jit(solution)/shard_map/gather_residual/all_to_all | solution.py:270
  62.2 0.0 collective-permute-start.2
  62.2 1.6 %collective-permute-done.2.other = bf16[8,144,128]{2,1,0:T(8,128)(2,1)S(1)} collective-permute-done((bf16[8,144,128]{2,1,0:T(8,128)(2,1)S(1)}, bf16[8,144,128]{2,1,0:T(8,128)(2,1)S(1)}, u32[]{:S(2)}, u32[]{:S(2)}) %collective-permute-start.2) | collective-permute-done | bytes 294944 | tf_op jit(solution)/shard_map/gather_residual/ppermute | solution.py:271
  63.8 0.0 copy-done.8
  63.8 0.0 copy-done.10
  63.8 0.0 copy-done.1
  63.8 0.0 copy-done.3
  63.8 0.0 copy-start.6
  63.9 6.4 %second_sigma.1 = (bf16[8,144,128]{2,1,0:T(8,128)(2,1)S(1)}, f32[8,128,128]{2,1,0:T(8,128)S(1)}, f32[8,128]{1,0:T(8,128)S(1)}) custom-call(s32[12,12]{1,0:T(8,128)S(1)} %copy-done.8, s32[12,12]{1,0:T(8,128)S(1)} %copy-done.10, bf16[8,144,128]{2,1,0:T(8,128)(2,1)S(1)} %all_to_all.22.own, bf16[8,144,128]{2,1,0:T(8,128)(2,1)S(1)} %collective-permute-done.2.other, ...), custom_call_target="tpu_custom_call" | custom-call | flops 1207959552 | bytes 10552448 | tf_op jit(solution)/shard_map/second_sigma/second_sigma/pallas_call | solution.py:223
  70.2 0.2 collective-permute-start.3
  70.5 1.4 %collective-permute-done.3.refs_1_ = bf16[8,144,128]{2,1,0:T(8,128)(2,1)S(1)} collective-permute-done((bf16[8,144,128]{2,1,0:T(8,128)(2,1)S(1)}, bf16[8,144,128]{2,1,0:T(8,128)(2,1)S(1)}, u32[]{:S(2)}, u32[]{:S(2)}) %collective-permute-start.3) | collective-permute-done | bytes 294944 | tf_op jit(solution)/shard_map/sum_second/ppermute | solution.py:280
  71.9 0.1 chip_sum.3
  71.9 13.4 %all_to_all.23.got = bf16[8,144,128]{2,1,0:T(8,128)(2,1)S(1)} all-to-all(bf16[8,144,128]{2,1,0:T(8,128)(2,1)S(1)} %chip_sum.3), channel_id=1, replica_groups=mesh['grp'=2,'chip'=8,'core'=2] {'chip'}, dimensions={0} | all-to-all | bytes 589824 | tf_op jit(solution)/shard_map/sum_second/all_to_all | solution.py:285
  85.3 0.0 copy-done.6
  85.3 1.3 %outputs.1 = (bf16[1,128,128]{2,1,0:T(8,128)(2,1)}, f32[1,128,128]{2,1,0:T(8,128)}, f32[4]{0:T(128)}) custom-call(s32[16]{0:T(128)S(1)} %copy-done.12, bf16[8,144,128]{2,1,0:T(8,128)(2,1)S(1)} %all_to_all.23.got, bf16[1,128,128]{2,1,0:T(8,128)(2,1)S(1)} %copy-done.4, f32[1,128,128]{2,1,0:T(8,128)S(1)} %copy-done.6, ...), custom_call_target="tpu_custom_call" | custom-call | flops 131072 | bytes 467008 | tf_op jit(solution)/shard_map/outputs/outputs/pallas_call | solution.py:223
Async XLA Ops:
  1.4 46.7 %copy-start.4 = (bf16[1,128,128]{2,1,0:T(8,128)(2,1)S(1)}, bf16[1,128,128]{2,1,0:T(8,128)(2,1)}, u32[]{:S(2)}) copy-start(bf16[1,128,128]{2,1,0:T(8,128)(2,1)} %state.3) | copy-start | bytes 98308
  1.4 46.7 %copy-start.5 = (f32[1,128,128]{2,1,0:T(8,128)S(1)}, f32[1,128,128]{2,1,0:T(8,128)}, u32[]{:S(2)}) copy-start(f32[1,128,128]{2,1,0:T(8,128)} %precond.1) | copy-start | bytes 196612
  1.5 46.6 %copy-start.12 = (s32[16]{0:T(128)S(1)}, s32[16]{0:T(128)}, u32[]{:S(2)}) copy-start(s32[16]{0:T(128)} %sizes.5) | copy-start | bytes 196
  1.5 62.4 %copy-start.8 = (s32[12,12]{1,0:T(8,128)S(1)}, s32[12,12]{1,0:T(8,128)}, u32[]{:S(2)}) copy-start(s32[12,12]{1,0:T(8,128)} %src.3) | copy-start | bytes 1732
  1.5 62.3 %copy-start.10 = (s32[12,12]{1,0:T(8,128)S(1)}, s32[12,12]{1,0:T(8,128)}, u32[]{:S(2)}) copy-start(s32[12,12]{1,0:T(8,128)} %tgt.3) | copy-start | bytes 1732
  17.6 1.5 %collective-permute-start = (bf16[8,128,128]{2,1,0:T(8,128)(2,1)S(1)}, bf16[8,128,128]{2,1,0:T(8,128)(2,1)S(1)}, u32[]{:S(2)}, u32[]{:S(2)}) collective-permute-start(bf16[8,128,128]{2,1,0:T(8,128)(2,1)S(1)} %all_to_all.20.own), channel_id=1, source_target_pairs={{0,1},{1,0},{2,3},{3,2},{4,5},{5,4},{6,7},{7,6},{8,9},{9,8},{10,11... | collective-permute-start | bytes 786440 | tf_op jit(solution)/shard_map/gather_state/ppermute | solution.py:246
  19.1 2.3 %copy-start = (bf16[12,12,128,128]{3,2,1,0:T(8,128)(2,1)S(1)}, bf16[12,12,128,128]{3,2,1,0:T(8,128)(2,1)}, u32[]{:S(2)}) copy-start(bf16[12,12,128,128]{3,2,1,0:T(8,128)(2,1)} %left.3) | copy-start | bytes 14155780
  21.5 2.3 %copy-start.2 = (bf16[12,12,128,128]{3,2,1,0:T(8,128)(2,1)S(1)}, bf16[12,12,128,128]{3,2,1,0:T(8,128)(2,1)}, u32[]{:S(2)}) copy-start(bf16[12,12,128,128]{3,2,1,0:T(8,128)(2,1)} %right.3) | copy-start | bytes 14155780
  23.8 0.7 copy-start.7
  24.5 0.7 copy-start.9
  25.2 0.7 copy-start.11
  25.9 38.0 %copy-start.1 = (bf16[12,12,128,128]{3,2,1,0:T(8,128)(2,1)S(1)}, bf16[12,12,128,128]{3,2,1,0:T(8,128)(2,1)}, u32[]{:S(2)}) copy-start(bf16[12,12,128,128]{3,2,1,0:T(8,128)(2,1)} %left.3) | copy-start | bytes 14155780
  25.9 38.0 %copy-start.3 = (bf16[12,12,128,128]{3,2,1,0:T(8,128)(2,1)S(1)}, bf16[12,12,128,128]{3,2,1,0:T(8,128)(2,1)}, u32[]{:S(2)}) copy-start(bf16[12,12,128,128]{3,2,1,0:T(8,128)(2,1)} %right.3) | copy-start | bytes 14155780
  32.4 1.6 %collective-permute-start.1 = (bf16[8,144,128]{2,1,0:T(8,128)(2,1)S(1)}, bf16[8,144,128]{2,1,0:T(8,128)(2,1)S(1)}, u32[]{:S(2)}, u32[]{:S(2)}) collective-permute-start(bf16[8,144,128]{2,1,0:T(8,128)(2,1)S(1)} %get-tuple-element.19), channel_id=1, source_target_pairs={{0,1},{1,0},{2,3},{3,2},{4,5},{5,4},{6,7},{7,6},{8,9},{9,8},{10,11... | collective-permute-start | bytes 884744 | tf_op jit(solution)/shard_map/sum_first/ppermute | solution.py:256
  62.2 1.6 %collective-permute-start.2 = (bf16[8,144,128]{2,1,0:T(8,128)(2,1)S(1)}, bf16[8,144,128]{2,1,0:T(8,128)(2,1)S(1)}, u32[]{:S(2)}, u32[]{:S(2)}) collective-permute-start(bf16[8,144,128]{2,1,0:T(8,128)(2,1)S(1)} %all_to_all.22.own), channel_id=1, source_target_pairs={{0,1},{1,0},{2,3},{3,2},{4,5},{5,4},{6,7},{7,6},{8,9},{9,8},{10,11... | collective-permute-start | bytes 884744 | tf_op jit(solution)/shard_map/gather_residual/ppermute | solution.py:271
  63.8 21.5 %copy-start.6 = (f32[1,128,128]{2,1,0:T(8,128)S(1)}, f32[1,128,128]{2,1,0:T(8,128)}, u32[]{:S(2)}) copy-start(f32[1,128,128]{2,1,0:T(8,128)} %get-tuple-element.14.first) | copy-start | bytes 196612
  70.2 1.6 %collective-permute-start.3 = (bf16[8,144,128]{2,1,0:T(8,128)(2,1)S(1)}, bf16[8,144,128]{2,1,0:T(8,128)(2,1)S(1)}, u32[]{:S(2)}, u32[]{:S(2)}) collective-permute-start(bf16[8,144,128]{2,1,0:T(8,128)(2,1)S(1)} %get-tuple-element.25), channel_id=1, source_target_pairs={{0,1},{1,0},{2,3},{3,2},{4,5},{5,4},{6,7},{7,6},{8,9},{9,8},{10,11... | collective-permute-start | bytes 884744 | tf_op jit(solution)/shard_map/sum_second/ppermute | solution.py:280

commit v2 on v1

--- a/solution.py
+++ b/solution.py
@@ -10,6 +10,7 @@
 F32 = jnp.float32
 TAIL = 16
 LIMIT = 36 << 20
+LONG = 10**11
 
 
 def each(count, body, carry):
@@ -81,6 +82,11 @@
         return carry
 
     lax.fori_loop(0, terms // per, step, 0)
+
+
+def copy_kernel(block, out):
+    for j in range(out.shape[0]):
+        out[j] = block[0]
 
 
 def first_kernel(src, tgt, sizes, own, other, left, right, theirs, mine, wave, sums, acc):
@@ -241,7 +247,10 @@
     flops = 4 * left.size * width
 
     with jax.named_scope("gather_state"):
-        copies = jnp.broadcast_to(state, (chips, width, width))
+        (copies,) = call(
+            copy_kernel, "copies", [VMEM], [((chips, width, width), BF16)], [], (state,),
+            LONG,
+        )
         own = lax.all_to_all(copies, "chip", 0, 0, tiled=True)
         other = lax.ppermute(own, "core", swap)
     with jax.named_scope("first_sigma"):

time: 87.1 us -> 80.4 us (0.923)
  local copies, waits for them, and re-layouts: 7.56 us -> 0.93 us
    unnamed x26 -> x18, local copies, waits for them, and re-layouts: 6.77 us -> 0.93 us
    pallas_call x6 -> x7, Pallas kernels: 15.5 us -> 15.6 us  [call(): pl.pallas_call(kernel, name=name, in_specs=ins, out_specs=out_specs or [V...]
where the time goes in v2:
time: 80.4 us; the launch traced here: 80.1 us
  blocking collectives  56.5 us (70%)
  Pallas kernels  15.6 us (19%)
  waiting for transfers between devices  6.06 us (8%)
  local copies, waits for them, and re-layouts  0.93 us (1%)
    all_to_all x2, blocking collectives, shards(): got = lax.all_to_all(part, 'chip', 0, 0, tiled=True)  27.3 us
    all_to_all x1, blocking collectives, shards(): own = lax.all_to_all(copies, 'chip', 0, 0, tiled=True)  16.2 us
    pallas_call x7, Pallas kernels, call(): pl.pallas_call(kernel, name=name, in_specs=ins, out_specs=out_specs or [V...  15.6 us
    all_to_all x1, blocking collectives, shards(): own = lax.all_to_all(send, 'chip', 0, 0, tiled=True)  12.9 us
    ppermute x2, waiting for transfers between devices, shards(): other = lax.ppermute(own, 'core', swap)  3.11 us
    ppermute x2, waiting for transfers between devices, shards(): got = lax.ppermute(theirs, 'core', swap)  2.95 us
  transfers between devices with their start and end apart: 4, of which 4 were waited for; matrix products, arithmetic and copies ran while one was open for 0% of the time, Pallas kernels for 0%

profile of v2, /device:TPU:0, one launch (start us, length us, event | category | flops | bytes accessed | tf_op | source)
XLA Modules:
  0.0 80.1 jit_solution(4444138835870384691)
XLA Ops:
  0.6 0.0 copy-start.1
  0.6 0.0 copy-start
  0.7 0.0 copy-start.2
  0.7 0.9 %copy-done.2 = bf16[1,128,128]{2,1,0:T(8,128)(2,1)S(1)} copy-done((bf16[1,128,128]{2,1,0:T(8,128)(2,1)S(1)}, bf16[1,128,128]{2,1,0:T(8,128)(2,1)}, u32[]{:S(2)}) %copy-start.2) | copy-done | bytes 32792
  1.6 0.0 copy-start.6
  1.6 0.0 copy-start.7
  1.6 0.0 copy-start.8
  1.6 16.2 %all_to_all.20.own = bf16[8,128,128]{2,1,0:T(8,128)(2,1)S(1)} all-to-all(bf16[8,128,128]{2,1,0:T(8,128)(2,1)S(1)} %copies.1), channel_id=1, replica_groups=mesh['grp'=2,'chip'=8,'core'=2] {'chip'}, dimensions={0} | all-to-all | bytes 524288 | tf_op jit(solution)/shard_map/gather_state/all_to_all | solution.py:254
  17.8 0.0 copy-start.3
  17.8 0.0 copy-start.4
  17.8 0.0 collective-permute-start
  17.8 1.5 %collective-permute-done.other = bf16[8,128,128]{2,1,0:T(8,128)(2,1)S(1)} collective-permute-done((bf16[8,128,128]{2,1,0:T(8,128)(2,1)S(1)}, bf16[8,128,128]{2,1,0:T(8,128)(2,1)S(1)}, u32[]{:S(2)}, u32[]{:S(2)}) %collective-permute-start) | collective-permute-done | bytes 262176 | tf_op jit(solution)/shard_map/gather_state/ppermute | solution.py:255
  19.4 0.0 copy-done.1
  19.4 0.0 copy-done
  19.4 0.0 copy-done.6
  19.4 0.0 copy-done.7
  19.4 0.0 copy-done.8
  19.4 6.5 %first_sigma.1 = (bf16[8,144,128]{2,1,0:T(8,128)(2,1)S(1)}, f32[8,128,128]{2,1,0:T(8,128)S(1)}, bf16[16,128,128]{2,1,0:T(8,128)(2,1)S(1)}, f32[8,128]{1,0:T(8,128)S(1)}) custom-call(s32[12,12]{1,0:T(8,128)S(1)} %copy-done.6, s32[12,12]{1,0:T(8,128)S(1)} %copy-done.7, s32[16]{0:T(128)S(1)} %copy-done.8, bf16[8,128,128]{2,1,0:T(8,128)(2,1)S(1)} %all_to_all.20.own, ...), custom_call_target="tpu_custom_call" | custom-call | flops 1207959552 | bytes 9962688 | tf_op jit(solution)/shard_map/first_sigma/first_sigma/pallas_call | solution.py:229
  25.9 0.2 collective-permute-start.1
  26.1 1.4 %collective-permute-done.1.refs_1_ = bf16[8,144,128]{2,1,0:T(8,128)(2,1)S(1)} collective-permute-done((bf16[8,144,128]{2,1,0:T(8,128)(2,1)S(1)}, bf16[8,144,128]{2,1,0:T(8,128)(2,1)S(1)}, u32[]{:S(2)}, u32[]{:S(2)}) %collective-permute-start.1) | collective-permute-done | bytes 294944 | tf_op jit(solution)/shard_map/sum_first/ppermute | solution.py:265
  27.6 0.1 chip_sum.2
  27.6 14.0 %all_to_all.21.got = bf16[8,144,128]{2,1,0:T(8,128)(2,1)S(1)} all-to-all(bf16[8,144,128]{2,1,0:T(8,128)(2,1)S(1)} %chip_sum.2), channel_id=1, replica_groups=mesh['grp'=2,'chip'=8,'core'=2] {'chip'}, dimensions={0} | all-to-all | bytes 589824 | tf_op jit(solution)/shard_map/sum_first/all_to_all | solution.py:270
  41.7 0.0 copy-done.3
  41.7 0.0 copy-done.4
  41.7 1.2 %residual.1 = (f32[1,128,128]{2,1,0:T(8,128)}, f32[1,128,128]{2,1,0:T(8,128)S(1)}, bf16[8,144,128]{2,1,0:T(8,128)(2,1)S(1)}, f32[8,128]{1,0:T(8,128)S(1)}) custom-call(s32[16]{0:T(128)S(1)} %copy-done.8, bf16[8,144,128]{2,1,0:T(8,128)(2,1)S(1)} %all_to_all.21.got, bf16[1,128,128]{2,1,0:T(8,128)(2,1)S(1)} %copy-done.3, f32[1,128,128]{2,1,0:T(8,128)S(1)} %copy-done.4, ...), custom_call_target="tpu_custom_call" | custom-call | flops 131072 | bytes 397376 | tf_op jit(solution)/shard_map/residual/residual/pallas_call | solution.py:229
  42.9 12.9 %all_to_all.22.own = bf16[8,144,128]{2,1,0:T(8,128)(2,1)S(1)} all-to-all(bf16[8,144,128]{2,1,0:T(8,128)(2,1)S(1)} %get-tuple-element.22), channel_id=1, replica_groups=mesh['grp'=2,'chip'=8,'core'=2] {'chip'}, dimensions={0} | all-to-all | bytes 589824 | tf_op jit(solution)/shard_map/gather_residual/all_to_all | solution.py:279
  55.8 0.0 collective-permute-start.2
  55.8 1.6 %collective-permute-done.2.other = bf16[8,144,128]{2,1,0:T(8,128)(2,1)S(1)} collective-permute-done((bf16[8,144,128]{2,1,0:T(8,128)(2,1)S(1)}, bf16[8,144,128]{2,1,0:T(8,128)(2,1)S(1)}, u32[]{:S(2)}, u32[]{:S(2)}) %collective-permute-start.2) | collective-permute-done | bytes 294944 | tf_op jit(solution)/shard_map/gather_residual/ppermute | solution.py:280
  57.4 0.0 copy-start.5
  57.4 6.4 %second_sigma.1 = (bf16[8,144,128]{2,1,0:T(8,128)(2,1)S(1)}, f32[8,128,128]{2,1,0:T(8,128)S(1)}, f32[8,128]{1,0:T(8,128)S(1)}) custom-call(s32[12,12]{1,0:T(8,128)S(1)} %copy-done.6, s32[12,12]{1,0:T(8,128)S(1)} %copy-done.7, bf16[8,144,128]{2,1,0:T(8,128)(2,1)S(1)} %all_to_all.22.own, bf16[8,144,128]{2,1,0:T(8,128)(2,1)S(1)} %collective-permute-done.2.other, ...), custom_call_target="tpu_custom_call" | custom-call | flops 1207959552 | bytes 10552448 | tf_op jit(solution)/shard_map/second_sigma/second_sigma/pallas_call | solution.py:229
  63.8 0.1 collective-permute-start.3
  63.9 1.5 %collective-permute-done.3.refs_1_ = bf16[8,144,128]{2,1,0:T(8,128)(2,1)S(1)} collective-permute-done((bf16[8,144,128]{2,1,0:T(8,128)(2,1)S(1)}, bf16[8,144,128]{2,1,0:T(8,128)(2,1)S(1)}, u32[]{:S(2)}, u32[]{:S(2)}) %collective-permute-start.3) | collective-permute-done | bytes 294944 | tf_op jit(solution)/shard_map/sum_second/ppermute | solution.py:289
  65.5 0.1 chip_sum.3
  65.5 13.3 %all_to_all.23.got = bf16[8,144,128]{2,1,0:T(8,128)(2,1)S(1)} all-to-all(bf16[8,144,128]{2,1,0:T(8,128)(2,1)S(1)} %chip_sum.3), channel_id=1, replica_groups=mesh['grp'=2,'chip'=8,'core'=2] {'chip'}, dimensions={0} | all-to-all | bytes 589824 | tf_op jit(solution)/shard_map/sum_second/all_to_all | solution.py:294
  78.8 0.0 copy-done.5
  78.8 1.3 %outputs.1 = (bf16[1,128,128]{2,1,0:T(8,128)(2,1)}, f32[1,128,128]{2,1,0:T(8,128)}, f32[4]{0:T(128)}) custom-call(s32[16]{0:T(128)S(1)} %copy-done.8, bf16[8,144,128]{2,1,0:T(8,128)(2,1)S(1)} %all_to_all.23.got, bf16[1,128,128]{2,1,0:T(8,128)(2,1)S(1)} %copy-done.3, f32[1,128,128]{2,1,0:T(8,128)S(1)} %copy-done.5, ...), custom_call_target="tpu_custom_call" | custom-call | flops 131072 | bytes 467008 | tf_op jit(solution)/shard_map/outputs/outputs/pallas_call | solution.py:229
  (1 shorter events, 0.0 us)
Async XLA Ops:
  0.6 18.8 %copy-start.1 = (bf16[12,12,128,128]{3,2,1,0:T(8,128)(2,1)S(1)}, bf16[12,12,128,128]{3,2,1,0:T(8,128)(2,1)}, u32[]{:S(2)}) copy-start(bf16[12,12,128,128]{3,2,1,0:T(8,128)(2,1)} %right.3) | copy-start | bytes 14155780
  0.6 18.7 %copy-start = (bf16[12,12,128,128]{3,2,1,0:T(8,128)(2,1)S(1)}, bf16[12,12,128,128]{3,2,1,0:T(8,128)(2,1)}, u32[]{:S(2)}) copy-start(bf16[12,12,128,128]{3,2,1,0:T(8,128)(2,1)} %left.3) | copy-start | bytes 14155780
  0.7 0.9 %copy-start.2 = (bf16[1,128,128]{2,1,0:T(8,128)(2,1)S(1)}, bf16[1,128,128]{2,1,0:T(8,128)(2,1)}, u32[]{:S(2)}) copy-start(bf16[1,128,128]{2,1,0:T(8,128)(2,1)} %state.3) | copy-start | bytes 98308
  1.6 17.8 %copy-start.6 = (s32[12,12]{1,0:T(8,128)S(1)}, s32[12,12]{1,0:T(8,128)}, u32[]{:S(2)}) copy-start(s32[12,12]{1,0:T(8,128)} %src.3) | copy-start | bytes 1732
  1.6 17.8 %copy-start.7 = (s32[12,12]{1,0:T(8,128)S(1)}, s32[12,12]{1,0:T(8,128)}, u32[]{:S(2)}) copy-start(s32[12,12]{1,0:T(8,128)} %tgt.3) | copy-start | bytes 1732
  1.6 17.8 %copy-start.8 = (s32[16]{0:T(128)S(1)}, s32[16]{0:T(128)}, u32[]{:S(2)}) copy-start(s32[16]{0:T(128)} %sizes.5) | copy-start | bytes 196
  17.8 23.8 %copy-start.3 = (bf16[1,128,128]{2,1,0:T(8,128)(2,1)S(1)}, bf16[1,128,128]{2,1,0:T(8,128)(2,1)}, u32[]{:S(2)}) copy-start(bf16[1,128,128]{2,1,0:T(8,128)(2,1)} %state.3) | copy-start | bytes 98308
  17.8 23.8 %copy-start.4 = (f32[1,128,128]{2,1,0:T(8,128)S(1)}, f32[1,128,128]{2,1,0:T(8,128)}, u32[]{:S(2)}) copy-start(f32[1,128,128]{2,1,0:T(8,128)} %precond.1) | copy-start | bytes 196612
  17.8 1.5 %collective-permute-start = (bf16[8,128,128]{2,1,0:T(8,128)(2,1)S(1)}, bf16[8,128,128]{2,1,0:T(8,128)(2,1)S(1)}, u32[]{:S(2)}, u32[]{:S(2)}) collective-permute-start(bf16[8,128,128]{2,1,0:T(8,128)(2,1)S(1)} %all_to_all.20.own), channel_id=1, source_target_pairs={{0,1},{1,0},{2,3},{3,2},{4,5},{5,4},{6,7},{7,6},{8,9},{9,8},{10,11... | collective-permute-start | bytes 786440 | tf_op jit(solution)/shard_map/gather_state/ppermute | solution.py:255
  25.9 1.6 %collective-permute-start.1 = (bf16[8,144,128]{2,1,0:T(8,128)(2,1)S(1)}, bf16[8,144,128]{2,1,0:T(8,128)(2,1)S(1)}, u32[]{:S(2)}, u32[]{:S(2)}) collective-permute-start(bf16[8,144,128]{2,1,0:T(8,128)(2,1)S(1)} %get-tuple-element.19), channel_id=1, source_target_pairs={{0,1},{1,0},{2,3},{3,2},{4,5},{5,4},{6,7},{7,6},{8,9},{9,8},{10,11... | collective-permute-start | bytes 884744 | tf_op jit(solution)/shard_map/sum_first/ppermute | solution.py:265
  55.8 1.6 %collective-permute-start.2 = (bf16[8,144,128]{2,1,0:T(8,128)(2,1)S(1)}, bf16[8,144,128]{2,1,0:T(8,128)(2,1)S(1)}, u32[]{:S(2)}, u32[]{:S(2)}) collective-permute-start(bf16[8,144,128]{2,1,0:T(8,128)(2,1)S(1)} %all_to_all.22.own), channel_id=1, source_target_pairs={{0,1},{1,0},{2,3},{3,2},{4,5},{5,4},{6,7},{7,6},{8,9},{9,8},{10,11... | collective-permute-start | bytes 884744 | tf_op jit(solution)/shard_map/gather_residual/ppermute | solution.py:280
  57.4 21.4 %copy-start.5 = (f32[1,128,128]{2,1,0:T(8,128)S(1)}, f32[1,128,128]{2,1,0:T(8,128)}, u32[]{:S(2)}) copy-start(f32[1,128,128]{2,1,0:T(8,128)} %get-tuple-element.14.first) | copy-start | bytes 196612
  63.8 1.6 %collective-permute-start.3 = (bf16[8,144,128]{2,1,0:T(8,128)(2,1)S(1)}, bf16[8,144,128]{2,1,0:T(8,128)(2,1)S(1)}, u32[]{:S(2)}, u32[]{:S(2)}) collective-permute-start(bf16[8,144,128]{2,1,0:T(8,128)(2,1)S(1)} %get-tuple-element.25), channel_id=1, source_target_pairs={{0,1},{1,0},{2,3},{3,2},{4,5},{5,4},{6,7},{7,6},{8,9},{9,8},{10,11... | collective-permute-start | bytes 884744 | tf_op jit(solution)/shard_map/sum_second/ppermute | solution.py:289

commit v3 on v2

--- a/solution.py
+++ b/solution.py
@@ -59,9 +59,9 @@
     return jnp.broadcast_to(jnp.sum(row, axis=1, keepdims=True), row.shape)
 
 
-def apply_blocks(src, tgt, vec, left, right, acc, chips, core):
+def apply_blocks(src, tgt, vec, left, right, acc, chips, core, keep=None):
     terms, nnz = left.shape[0], left.shape[1]
-    per = 3 if terms % 3 == 0 else 1
+    per = 6 if terms % 6 == 0 else 1
 
     def place(s):
         return (s >> 1) + chips * ((s ^ core) & 1)
@@ -76,9 +76,11 @@
         ]
         for (k, n), prod in zip(items, prods):
             at = place(tgt[k, n])
-            acc[at] += lax.dot_general(
-                prod, right[k, n], (((1,), (1,)), ((), ())), preferred_element_type=F32
-            )
+            turned = right[k, n]
+            if keep is not None:
+                turned = turned.T
+                keep[k, n] = turned
+            acc[at] += jnp.dot(prod, turned, preferred_element_type=F32)
         return carry
 
     lax.fori_loop(0, terms // per, step, 0)
@@ -89,7 +91,7 @@
         out[j] = block[0]
 
 
-def first_kernel(src, tgt, sizes, own, other, left, right, theirs, mine, wave, sums, acc):
+def first_kernel(src, tgt, sizes, own, other, left, right, theirs, mine, wave, flip, sums, acc):
     chips, width = own.shape[0], own.shape[2]
     core = lax.axis_index("core")
 
@@ -103,7 +105,7 @@
 
     zero = jnp.zeros((1, width), F32)
     here, there = each(chips, load, (zero, zero))
-    apply_blocks(src, tgt, wave, left, right, acc, chips, core)
+    apply_blocks(src, tgt, wave, left, right, acc, chips, core, flip)
 
     def store(j, ray):
         a, b = acc[j], acc[chips + j]
@@ -254,10 +256,10 @@
         own = lax.all_to_all(copies, "chip", 0, 0, tiled=True)
         other = lax.ppermute(own, "core", swap)
     with jax.named_scope("first_sigma"):
-        theirs, mine, wave, sums = call(
+        theirs, mine, wave, flip, sums = call(
             first_kernel, "first_sigma", [SMEM] * 3 + [VMEM] * 4,
             [((chips, high, width), BF16), ((chips, width, width), F32),
-             ((every, width, width), BF16), ((8, width), F32)],
+             ((every, width, width), BF16), (right.shape, BF16), ((8, width), F32)],
             [pltpu.VMEM((every, width, width), F32)],
             (source, target, sector_sizes, own, other, left, right), flops,
         )
@@ -283,7 +285,7 @@
             second_kernel, "second_sigma", [SMEM] * 2 + [VMEM] * 5,
             [((chips, high, width), BF16), ((chips, width, width), F32), ((8, width), F32)],
             [pltpu.VMEM((every, width, width), BF16), pltpu.VMEM((every, width, width), F32)],
-            (source, target, own, other, wave, left, right), flops,
+            (source, target, own, other, wave, left, flip), flops,
         )
     with jax.named_scope("sum_second"):
         got = lax.ppermute(theirs, "core", swap)

time: 80.4 us -> 76.3 us (0.949)
  Pallas kernels: 15.6 us -> 11.5 us
    pallas_call x7, Pallas kernels: 15.6 us -> 11.5 us  [call(): pl.pallas_call(kernel, name=name, in_specs=ins, out_specs=out_specs or [V...]
where the time goes in v3:
time: 76.3 us; the launch traced here: 76 us
  blocking collectives  56.5 us (74%)
  Pallas kernels  11.5 us (15%)
  waiting for transfers between devices  6.01 us (8%)
  local copies, waits for them, and re-layouts  0.93 us (1%)
    all_to_all x2, blocking collectives, shards(): got = lax.all_to_all(part, 'chip', 0, 0, tiled=True)  27.3 us
    all_to_all x1, blocking collectives, shards(): own = lax.all_to_all(copies, 'chip', 0, 0, tiled=True)  16.2 us
    all_to_all x1, blocking collectives, shards(): own = lax.all_to_all(send, 'chip', 0, 0, tiled=True)  12.9 us
    pallas_call x7, Pallas kernels, call(): pl.pallas_call(kernel, name=name, in_specs=ins, out_specs=out_specs or [V...  11.5 us
    ppermute x2, waiting for transfers between devices, shards(): other = lax.ppermute(own, 'core', swap)  3.11 us
    ppermute x2, waiting for transfers between devices, shards(): got = lax.ppermute(theirs, 'core', swap)  2.9 us
  transfers between devices with their start and end apart: 4, of which 4 were waited for; matrix products, arithmetic and copies ran while one was open for 0% of the time, Pallas kernels for 0%

profile of v3, /device:TPU:0, one launch (start us, length us, event | category | flops | bytes accessed | tf_op | source)
XLA Modules:
  0.0 76.0 jit_solution(4232899742458465227)
XLA Ops:
  0.6 0.0 copy-start
  0.6 0.0 copy-start.1
  0.7 0.0 copy-start.2
  0.7 0.9 %copy-done.2 = bf16[1,128,128]{2,1,0:T(8,128)(2,1)S(1)} copy-done((bf16[1,128,128]{2,1,0:T(8,128)(2,1)S(1)}, bf16[1,128,128]{2,1,0:T(8,128)(2,1)}, u32[]{:S(2)}) %copy-start.2) | copy-done | bytes 32792
  1.6 0.0 copy-start.6
  1.6 0.0 copy-start.7
  1.6 0.0 copy-start.8
  1.6 16.2 %all_to_all.20.own = bf16[8,128,128]{2,1,0:T(8,128)(2,1)S(1)} all-to-all(bf16[8,128,128]{2,1,0:T(8,128)(2,1)S(1)} %copies.1), channel_id=1, replica_groups=mesh['grp'=2,'chip'=8,'core'=2] {'chip'}, dimensions={0} | all-to-all | bytes 524288 | tf_op jit(solution)/shard_map/gather_state/all_to_all | solution.py:256
  17.8 0.0 copy-start.3
  17.8 0.0 copy-start.4
  17.8 0.0 collective-permute-start
  17.8 1.5 %collective-permute-done.other = bf16[8,128,128]{2,1,0:T(8,128)(2,1)S(1)} collective-permute-done((bf16[8,128,128]{2,1,0:T(8,128)(2,1)S(1)}, bf16[8,128,128]{2,1,0:T(8,128)(2,1)S(1)}, u32[]{:S(2)}, u32[]{:S(2)}) %collective-permute-start) | collective-permute-done | bytes 262176 | tf_op jit(solution)/shard_map/gather_state/ppermute | solution.py:257
  19.4 0.0 copy-done
  19.4 0.0 copy-done.1
  19.4 0.0 copy-done.6
  19.4 0.0 copy-done.7
  19.4 0.0 copy-done.8
  19.4 4.5 %first_sigma.1 = (bf16[8,144,128]{2,1,0:T(8,128)(2,1)S(1)}, f32[8,128,128]{2,1,0:T(8,128)S(1)}, bf16[16,128,128]{2,1,0:T(8,128)(2,1)S(1)}, bf16[12,12,128,128]{3,2,1,0:T(8,128)(2,1)S(1)}, f32[8,128]{1,0:T(8,128)S(1)}) custom-call(s32[12,12]{1,0:T(8,128)S(1)} %copy-done.6, s32[12,12]{1,0:T(8,128)S(1)} %copy-done.7, s32[16]{0:T(128)S(1)} %copy-done.8, ...), custom_call_target="tpu_custom_call" | custom-call | flops 1207959552 | bytes 9962688 | tf_op jit(solution)/shard_map/first_sigma/first_sigma/pallas_call | solution.py:231
  23.9 0.2 collective-permute-start.1
  24.1 1.5 %collective-permute-done.1.refs_1_ = bf16[8,144,128]{2,1,0:T(8,128)(2,1)S(1)} collective-permute-done((bf16[8,144,128]{2,1,0:T(8,128)(2,1)S(1)}, bf16[8,144,128]{2,1,0:T(8,128)(2,1)S(1)}, u32[]{:S(2)}, u32[]{:S(2)}) %collective-permute-start.1) | collective-permute-done | bytes 294944 | tf_op jit(solution)/shard_map/sum_first/ppermute | solution.py:267
  25.6 0.1 chip_sum.2
  25.6 14.0 %all_to_all.21.got = bf16[8,144,128]{2,1,0:T(8,128)(2,1)S(1)} all-to-all(bf16[8,144,128]{2,1,0:T(8,128)(2,1)S(1)} %chip_sum.2), channel_id=1, replica_groups=mesh['grp'=2,'chip'=8,'core'=2] {'chip'}, dimensions={0} | all-to-all | bytes 589824 | tf_op jit(solution)/shard_map/sum_first/all_to_all | solution.py:272
  39.7 0.0 copy-done.3
  39.7 0.0 copy-done.4
  39.7 1.2 %residual.1 = (f32[1,128,128]{2,1,0:T(8,128)}, f32[1,128,128]{2,1,0:T(8,128)S(1)}, bf16[8,144,128]{2,1,0:T(8,128)(2,1)S(1)}, f32[8,128]{1,0:T(8,128)S(1)}) custom-call(s32[16]{0:T(128)S(1)} %copy-done.8, bf16[8,144,128]{2,1,0:T(8,128)(2,1)S(1)} %all_to_all.21.got, bf16[1,128,128]{2,1,0:T(8,128)(2,1)S(1)} %copy-done.3, f32[1,128,128]{2,1,0:T(8,128)S(1)} %copy-done.4, ...), custom_call_target="tpu_custom_call" | custom-call | flops 131072 | bytes 397376 | tf_op jit(solution)/shard_map/residual/residual/pallas_call | solution.py:231
  40.9 12.9 %all_to_all.22.own = bf16[8,144,128]{2,1,0:T(8,128)(2,1)S(1)} all-to-all(bf16[8,144,128]{2,1,0:T(8,128)(2,1)S(1)} %get-tuple-element.23), channel_id=1, replica_groups=mesh['grp'=2,'chip'=8,'core'=2] {'chip'}, dimensions={0} | all-to-all | bytes 589824 | tf_op jit(solution)/shard_map/gather_residual/all_to_all | solution.py:281
  53.8 0.0 collective-permute-start.2
  53.8 1.6 %collective-permute-done.2.other = bf16[8,144,128]{2,1,0:T(8,128)(2,1)S(1)} collective-permute-done((bf16[8,144,128]{2,1,0:T(8,128)(2,1)S(1)}, bf16[8,144,128]{2,1,0:T(8,128)(2,1)S(1)}, u32[]{:S(2)}, u32[]{:S(2)}) %collective-permute-start.2) | collective-permute-done | bytes 294944 | tf_op jit(solution)/shard_map/gather_residual/ppermute | solution.py:282
  55.4 0.0 copy-start.5
  55.4 4.3 %second_sigma.1 = (bf16[8,144,128]{2,1,0:T(8,128)(2,1)S(1)}, f32[8,128,128]{2,1,0:T(8,128)S(1)}, f32[8,128]{1,0:T(8,128)S(1)}) custom-call(s32[12,12]{1,0:T(8,128)S(1)} %copy-done.6, s32[12,12]{1,0:T(8,128)S(1)} %copy-done.7, bf16[8,144,128]{2,1,0:T(8,128)(2,1)S(1)} %all_to_all.22.own, bf16[8,144,128]{2,1,0:T(8,128)(2,1)S(1)} %collective-permute-done.2.other, ...), custom_call_target="tpu_custom_call" | custom-call | flops 1207959552 | bytes 10552448 | tf_op jit(solution)/shard_map/second_sigma/second_sigma/pallas_call | solution.py:231
  59.7 0.2 collective-permute-start.3
  59.9 1.5 %collective-permute-done.3.refs_1_ = bf16[8,144,128]{2,1,0:T(8,128)(2,1)S(1)} collective-permute-done((bf16[8,144,128]{2,1,0:T(8,128)(2,1)S(1)}, bf16[8,144,128]{2,1,0:T(8,128)(2,1)S(1)}, u32[]{:S(2)}, u32[]{:S(2)}) %collective-permute-start.3) | collective-permute-done | bytes 294944 | tf_op jit(solution)/shard_map/sum_second/ppermute | solution.py:291
  61.3 0.1 chip_sum.3
  61.4 13.3 %all_to_all.23.got = bf16[8,144,128]{2,1,0:T(8,128)(2,1)S(1)} all-to-all(bf16[8,144,128]{2,1,0:T(8,128)(2,1)S(1)} %chip_sum.3), channel_id=1, replica_groups=mesh['grp'=2,'chip'=8,'core'=2] {'chip'}, dimensions={0} | all-to-all | bytes 589824 | tf_op jit(solution)/shard_map/sum_second/all_to_all | solution.py:296
  74.7 0.0 copy-done.5
  74.7 1.3 %outputs.1 = (bf16[1,128,128]{2,1,0:T(8,128)(2,1)}, f32[1,128,128]{2,1,0:T(8,128)}, f32[4]{0:T(128)}) custom-call(s32[16]{0:T(128)S(1)} %copy-done.8, bf16[8,144,128]{2,1,0:T(8,128)(2,1)S(1)} %all_to_all.23.got, bf16[1,128,128]{2,1,0:T(8,128)(2,1)S(1)} %copy-done.3, f32[1,128,128]{2,1,0:T(8,128)S(1)} %copy-done.5, ...), custom_call_target="tpu_custom_call" | custom-call | flops 131072 | bytes 467008 | tf_op jit(solution)/shard_map/outputs/outputs/pallas_call | solution.py:231
  (1 shorter events, 0.0 us)
Async XLA Ops:
  0.6 18.8 %copy-start = (bf16[12,12,128,128]{3,2,1,0:T(8,128)(2,1)S(1)}, bf16[12,12,128,128]{3,2,1,0:T(8,128)(2,1)}, u32[]{:S(2)}) copy-start(bf16[12,12,128,128]{3,2,1,0:T(8,128)(2,1)} %left.3) | copy-start | bytes 14155780
  0.6 18.7 %copy-start.1 = (bf16[12,12,128,128]{3,2,1,0:T(8,128)(2,1)S(1)}, bf16[12,12,128,128]{3,2,1,0:T(8,128)(2,1)}, u32[]{:S(2)}) copy-start(bf16[12,12,128,128]{3,2,1,0:T(8,128)(2,1)} %right.1) | copy-start | bytes 14155780
  0.7 0.9 %copy-start.2 = (bf16[1,128,128]{2,1,0:T(8,128)(2,1)S(1)}, bf16[1,128,128]{2,1,0:T(8,128)(2,1)}, u32[]{:S(2)}) copy-start(bf16[1,128,128]{2,1,0:T(8,128)(2,1)} %state.3) | copy-start | bytes 98308
  1.6 17.8 %copy-start.6 = (s32[12,12]{1,0:T(8,128)S(1)}, s32[12,12]{1,0:T(8,128)}, u32[]{:S(2)}) copy-start(s32[12,12]{1,0:T(8,128)} %src.3) | copy-start | bytes 1732
  1.6 17.8 %copy-start.7 = (s32[12,12]{1,0:T(8,128)S(1)}, s32[12,12]{1,0:T(8,128)}, u32[]{:S(2)}) copy-start(s32[12,12]{1,0:T(8,128)} %tgt.3) | copy-start | bytes 1732
  1.6 17.8 %copy-start.8 = (s32[16]{0:T(128)S(1)}, s32[16]{0:T(128)}, u32[]{:S(2)}) copy-start(s32[16]{0:T(128)} %sizes.5) | copy-start | bytes 196
  17.8 21.8 %copy-start.3 = (bf16[1,128,128]{2,1,0:T(8,128)(2,1)S(1)}, bf16[1,128,128]{2,1,0:T(8,128)(2,1)}, u32[]{:S(2)}) copy-start(bf16[1,128,128]{2,1,0:T(8,128)(2,1)} %state.3) | copy-start | bytes 98308
  17.8 21.8 %copy-start.4 = (f32[1,128,128]{2,1,0:T(8,128)S(1)}, f32[1,128,128]{2,1,0:T(8,128)}, u32[]{:S(2)}) copy-start(f32[1,128,128]{2,1,0:T(8,128)} %precond.1) | copy-start | bytes 196612
  17.8 1.5 %collective-permute-start = (bf16[8,128,128]{2,1,0:T(8,128)(2,1)S(1)}, bf16[8,128,128]{2,1,0:T(8,128)(2,1)S(1)}, u32[]{:S(2)}, u32[]{:S(2)}) collective-permute-start(bf16[8,128,128]{2,1,0:T(8,128)(2,1)S(1)} %all_to_all.20.own), channel_id=1, source_target_pairs={{0,1},{1,0},{2,3},{3,2},{4,5},{5,4},{6,7},{7,6},{8,9},{9,8},{10,11... | collective-permute-start | bytes 786440 | tf_op jit(solution)/shard_map/gather_state/ppermute | solution.py:257
  23.9 1.6 %collective-permute-start.1 = (bf16[8,144,128]{2,1,0:T(8,128)(2,1)S(1)}, bf16[8,144,128]{2,1,0:T(8,128)(2,1)S(1)}, u32[]{:S(2)}, u32[]{:S(2)}) collective-permute-start(bf16[8,144,128]{2,1,0:T(8,128)(2,1)S(1)} %get-tuple-element.20), channel_id=1, source_target_pairs={{0,1},{1,0},{2,3},{3,2},{4,5},{5,4},{6,7},{7,6},{8,9},{9,8},{10,11... | collective-permute-start | bytes 884744 | tf_op jit(solution)/shard_map/sum_first/ppermute | solution.py:267
  53.8 1.6 %collective-permute-start.2 = (bf16[8,144,128]{2,1,0:T(8,128)(2,1)S(1)}, bf16[8,144,128]{2,1,0:T(8,128)(2,1)S(1)}, u32[]{:S(2)}, u32[]{:S(2)}) collective-permute-start(bf16[8,144,128]{2,1,0:T(8,128)(2,1)S(1)} %all_to_all.22.own), channel_id=1, source_target_pairs={{0,1},{1,0},{2,3},{3,2},{4,5},{5,4},{6,7},{7,6},{8,9},{9,8},{10,11... | collective-permute-start | bytes 884744 | tf_op jit(solution)/shard_map/gather_residual/ppermute | solution.py:282
  55.4 19.3 %copy-start.5 = (f32[1,128,128]{2,1,0:T(8,128)S(1)}, f32[1,128,128]{2,1,0:T(8,128)}, u32[]{:S(2)}) copy-start(f32[1,128,128]{2,1,0:T(8,128)} %get-tuple-element.15.first) | copy-start | bytes 196612
  59.7 1.6 %collective-permute-start.3 = (bf16[8,144,128]{2,1,0:T(8,128)(2,1)S(1)}, bf16[8,144,128]{2,1,0:T(8,128)(2,1)S(1)}, u32[]{:S(2)}, u32[]{:S(2)}) collective-permute-start(bf16[8,144,128]{2,1,0:T(8,128)(2,1)S(1)} %get-tuple-element.27), channel_id=1, source_target_pairs={{0,1},{1,0},{2,3},{3,2},{4,5},{5,4},{6,7},{7,6},{8,9},{9,8},{10,11... | collective-permute-start | bytes 884744 | tf_op jit(solution)/shard_map/sum_second/ppermute | solution.py:291

commit v4 on v3

v4 whole, which is shorter than its diff:
```python
import jax
import jax.numpy as jnp
from jax import lax
from jax.experimental import pallas as pl
from jax.experimental.pallas import tpu as pltpu
from jax.sharding import Mesh
from jax.sharding import PartitionSpec as P

BF16 = jnp.bfloat16
F32 = jnp.float32
TAIL = 16
LIMIT = 36 << 20
LONG = 10**11
NEAR = 4


def each(count, body, carry):
    if count <= 8:
        for j in range(count):
            carry = body(j, carry)
        return carry
    return lax.fori_loop(0, count, body, carry)


def mask_of(size, width):
    rows = lax.broadcasted_iota(jnp.int32, (width, width), 0)
    cols = lax.broadcasted_iota(jnp.int32, (width, width), 1)
    return (rows < size) & (cols < size)


def fold(x):
    return jnp.sum(x, axis=0, keepdims=True)


def tail_of(rows):
    pieces = []
    for row in rows:
        rest = row
        for _ in range(3):
            piece = rest.astype(BF16).astype(F32)
            pieces.append(piece)
            rest = rest - piece
    lanes = rows[0].shape[1]
    place = lax.broadcasted_iota(jnp.int32, (TAIL, lanes), 0)
    tail = jnp.zeros((TAIL, lanes), F32)
    for at, piece in enumerate(pieces):
        tail = jnp.where(place == at, piece, tail)
    return tail.astype(BF16)


def rows_of(tail, count):
    wide = tail.astype(F32)
    return [
        (wide[3 * i : 3 * i + 1] + wide[3 * i + 1 : 3 * i + 2]) + wide[3 * i + 2 : 3 * i + 3]
        for i in range(count)
    ]


def total(row):
    return jnp.broadcast_to(jnp.sum(row, axis=1, keepdims=True), row.shape)


def halve(rows):
    while rows.shape[0] > 1:
        half = rows.shape[0] // 2
        rows = rows[:half] + rows[half:]
    return rows


def place_of(core, chip, chips):
    return lambda s: ((s >> 1) ^ chip) + chips * ((s ^ core) & 1)


def apply_blocks(src, tgt, vec, left, right, acc, place, keep=None):
    terms, nnz = left.shape[0], left.shape[1]
    per = 6 if terms % 6 == 0 else 1
    acc[...] = jnp.zeros_like(acc)

    def step(i, carry):
        items = [(i * per + k, n) for k in range(per) for n in range(nnz)]
        prods = [
            jnp.dot(left[k, n], vec[place(src[k, n])], preferred_element_type=F32).astype(BF16)
            for k, n in items
        ]
        for (k, n), prod in zip(items, prods):
            at = place(tgt[k, n])
            turned = right[k, n]
            if keep is not None:
                turned = turned.T
                keep[k, n] = turned
            acc[at] += jnp.dot(prod, turned, preferred_element_type=F32)
        return carry

    lax.fori_loop(0, terms // per, step, 0)


def mask_kernel(sizes, inside):
    own = 2 * lax.axis_index("chip") + lax.axis_index("core")
    inside[0] = mask_of(sizes[own], inside.shape[2]).astype(F32)


def first_kernel(src, tgt, sizes, *refs):
    pieces, ins, outs = refs[: 2 * NEAR], refs[2 * NEAR : 2 * NEAR + 3], refs[2 * NEAR + 3 :]
    left, right, inside = ins
    theirs, mine, wave, flip, sums, acc, rows = outs
    span, width = pieces[0].shape[0], pieces[0].shape[2]
    chips = NEAR * span
    core, chip = lax.axis_index("core"), lax.axis_index("chip")

    for other in range(2):
        for k in range(NEAR):
            piece = pieces[other * NEAR + k]

            def load(i, carry, other=other, k=k, piece=piece):
                rel = NEAR * i + k
                size = sizes[2 * (chip ^ rel) + (core ^ other)]
                block = piece[i].astype(F32)
                if other == 0 and k == 0 and span <= 8 and i == 0:
                    block = jnp.where(inside[0] > 0.0, block, 0.0)
                else:
                    block = jnp.where(mask_of(size, width), block, 0.0)
                wave[other * chips + rel] = block.astype(BF16)
                rows[pl.ds(other * chips + rel, 1)] = fold(block * block)
                return carry

            each(span, load, 0)
    apply_blocks(src, tgt, wave, left, right, acc, place_of(core, chip, chips), flip)

    def store(j, ray):
        a, b = acc[j], acc[chips + j]
        mine[j] = a
        theirs[j, 0:width] = b.astype(BF16)
        ray = ray + fold(wave[j].astype(F32) * a)
        return ray + fold(wave[chips + j].astype(F32) * b)

    ray = each(chips, store, jnp.zeros((1, width), F32))
    theirs[0, width : width + TAIL] = tail_of([ray])
    sums[0:1] = halve(rows[...])
    sums[1:2] = ray


def second_kernel(src, tgt, *refs):
    pieces, ins, outs = refs[: 2 * NEAR], refs[2 * NEAR : 2 * NEAR + 6], refs[2 * NEAR + 6 :]
    wave, left, right, resid, first, keep = ins
    theirs, mine, sums, sigma, direction, vec, acc, rows, low, sems = outs
    span, width = pieces[0].shape[0], pieces[0].shape[2]
    chips = NEAR * span
    core, chip = lax.axis_index("core"), lax.axis_index("chip")
    copies = [
        pltpu.make_async_copy(first, sigma, sems.at[0]),
        pltpu.make_async_copy(low, direction, sems.at[1]),
    ]
    copies[0].start()

    for other in range(2):
        for k in range(NEAR):
            piece = pieces[other * NEAR + k]

            def load(i, carry, other=other, k=k, piece=piece):
                at = other * chips + NEAR * i + k
                vec[at] = piece[i, 0:width]
                for n, row in enumerate(rows_of(piece[i, width : width + TAIL], 3)):
                    rows[n, pl.ds(at, 1)] = row
                return carry

            each(span, load, 0)
    inter, mixed, length = (total(halve(rows[n])) for n in range(3))
    low[0] = (resid[0] - inter / keep[0:1] * wave[0].astype(F32)).astype(BF16)
    copies[1].start()
    apply_blocks(src, tgt, vec, left, right, acc, place_of(core, chip, chips))

    def store(j, carry):
        cross, square = carry
        a, b = acc[j], acc[chips + j]
        mine[j] = a
        theirs[j, 0:width] = b.astype(BF16)
        cross = cross + fold(wave[j].astype(F32) * a) + fold(wave[chips + j].astype(F32) * b)
        square = square + fold(vec[j].astype(F32) * a) + fold(vec[chips + j].astype(F32) * b)
        return cross, square

    zero = jnp.zeros((1, width), F32)
    cross, square = each(chips, store, (zero, zero))
    theirs[0, width : width + TAIL] = tail_of([cross, square])
    for i, row in enumerate((inter, mixed, length, cross, square)):
        sums[i : i + 1] = row
    for copy in copies:
        copy.wait()


def chip_kernel(at, count, mine, got, sums, base, *sends):
    width = mine.shape[2]
    rows = rows_of(got[0, width : width + TAIL], count)
    rows = [sums[at + i : at + i + 1] + rows[i] for i in range(count)]
    tail = tail_of(rows)

    def store(i, carry):
        base[i, 0:width] = mine[NEAR * i] + got[NEAR * i, 0:width].astype(F32)
        for k, send in enumerate(sends, 1):
            rel = NEAR * i + k
            send[i, 0:width] = (mine[rel] + got[rel, 0:width].astype(F32)).astype(BF16)
        return carry

    each(base.shape[0], store, 0)
    for send in sends:
        send[0, width : width + TAIL] = tail
    for i, row in enumerate(rows):
        base[0, width + i : width + i + 1] = row


def near_kernel(count, base, *refs):
    gots, (low, high) = refs[:-2], refs[-2:]
    span, width = base.shape[0], base.shape[2]
    half = span // 2
    parts = [[base[0, width + i : width + i + 1] for i in range(count)]]
    parts += [rows_of(got[0, width : width + TAIL], count) for got in gots]
    rows = [halve(jnp.concatenate([part[i] for part in parts], axis=0)) for i in range(count)]

    def add(i):
        block = base[i, 0:width]
        for got in gots:
            block = block + got[i, 0:width].astype(F32)
        return block

    def store(i, carry):
        low[i, 0:width] = add(i)
        high[i, 0:width] = add(half + i).astype(high.dtype)
        for n, row in enumerate(rows):
            low[i, width + n : width + n + 1] = row
        if high.dtype == BF16:
            high[i, width : width + TAIL] = tail_of(rows)
        else:
            for n, row in enumerate(rows):
                high[i, width + n : width + n + 1] = row
        return carry

    each(half, store, 0)


def last_sums(low, got, count):
    width = got.shape[2]
    block = low[0, 0:width] + got[0, 0:width].astype(F32)
    if got.dtype == BF16:
        rows = rows_of(got[0, width : width + TAIL], count)
    else:
        rows = [got[0, width + i : width + i + 1] for i in range(count)]
    return [block] + [low[0, width + i : width + i + 1] + rows[i] for i in range(count)]


def residual_kernel(half, got, wave, inside, precond, sums, sigma, resid, send, keep):
    width = got.shape[2]
    block, ray = last_sums(half, got, 1)
    first = block * inside[0]
    own = wave[0].astype(F32)
    norm, ray = total(sums[0:1]), total(ray)
    q = precond[0] * (first - ray / norm * own)
    low = q.astype(BF16)
    sigma[0] = first
    resid[0] = q
    send[0, 0:width] = low
    send[0, width : width + TAIL] = tail_of(
        [fold(own * q), fold(low.astype(F32) * first), fold(q * q)]
    )
    keep[0:1] = norm
    keep[1:2] = ray


def final_kernel(half, got, inside, first, keep, sums, sigma, subspace):
    block, cross, square = last_sums(half, got, 2)
    norm, ray = keep[0:1], keep[1:2]
    inter, mixed, length = (sums[i : i + 1] for i in range(3))
    cross, square = total(cross), total(square)
    c = inter / norm
    sigma[0] = block * inside[0] - c * first[0]
    values = (
        ray,
        cross - c * ray,
        square - c * mixed - c * (cross - c * ray),
        length - 2.0 * c * inter + c * c * norm,
    )
    for i, value in enumerate(values):
        subspace[i] = jnp.max(value / norm)


VMEM = pl.BlockSpec(memory_space=pltpu.VMEM)
SMEM = pl.BlockSpec(memory_space=pltpu.SMEM)
HBM = pl.BlockSpec(memory_space=pl.ANY)


def call(kernel, name, ins, outs, scratch, args, flops, out_specs=None):
    moved = sum(a.size * a.dtype.itemsize for a in args)
    return pl.pallas_call(
        kernel,
        name=name,
        in_specs=ins,
        out_specs=out_specs or [VMEM] * len(outs),
        out_shape=outs,
        scratch_shapes=scratch,
        compiler_params=pltpu.CompilerParams(vmem_limit_bytes=LIMIT),
        cost_estimate=pl.CostEstimate(flops=flops, bytes_accessed=moved, transcendentals=0),
    )(*args)


def shape(*dims, dtype=F32):
    return jax.ShapeDtypeStruct(dims, dtype)


def swap(x):
    return lax.ppermute(x, "core", [(0, 1), (1, 0)])


def flip_chip(x, bits):
    chips = lax.axis_size("chip")
    return lax.ppermute(x, "chip", [(i, i ^ bits) for i in range(chips)])


def gather(block):
    step = NEAR
    while step < lax.axis_size("chip"):
        block = jnp.concatenate([block, flip_chip(block, step)], axis=0)
        step *= 2
    pieces = [block] + [flip_chip(block, k) for k in range(1, NEAR)]
    return pieces + [swap(piece) for piece in pieces]


def scatter(theirs, mine, sums, at, count, narrow):
    chips, width = mine.shape[0], mine.shape[2]
    span, high, wide = chips // NEAR, width + TAIL, width + 8
    sent = [shape(span, high, width, dtype=BF16)] * (NEAR - 1)
    base, *sends = call(
        lambda *refs: chip_kernel(at, count, *refs), "chip_sum", [VMEM] * 3,
        [shape(span, wide, width)] + sent, [], (mine, swap(theirs), sums), mine.size,
    )
    gots = [flip_chip(send, k) for k, send in enumerate(sends, 1)]
    half = span // 2
    last = shape(half, high, width, dtype=BF16) if narrow and half == 1 else shape(half, wide, width)
    low, far = call(
        lambda *refs: near_kernel(count, *refs), "near_sum", [VMEM] * NEAR,
        [shape(half, wide, width), last], [], (base, *gots), mine.size,
    )
    got = flip_chip(far, NEAR * half)
    while half > 1:
        half //= 2
        low = low + got
        low, got = low[:half], flip_chip(low[half:], NEAR * half)
    return low, got


def shards(state, sector_sizes, left, right, source, target, precond):
    chips = lax.axis_size("chip")
    width = state.shape[1]
    high = width + TAIL
    every = 2 * chips
    flops = 4 * left.size * width
    near = [VMEM] * (2 * NEAR)
    block = shape(1, width, width)
    sums_of = shape(8, width)

    with jax.named_scope("own_mask"):
        (inside,) = call(mask_kernel, "own_mask", [SMEM], [block], [], (sector_sizes,), LONG)
    with jax.named_scope("gather_state"):
        pieces = gather(state)
    with jax.named_scope("first_sigma"):
        theirs, mine, wave, flip, sums = call(
            first_kernel, "first_sigma", [SMEM] * 3 + near + [VMEM] * 3,
            [shape(chips, high, width, dtype=BF16), shape(chips, width, width),
             shape(every, width, width, dtype=BF16), shape(*right.shape, dtype=BF16), sums_of],
            [pltpu.VMEM((every, width, width), F32), pltpu.VMEM((every, width), F32)],
            (source, target, sector_sizes, *pieces, left, right, inside), flops,
        )
    with jax.named_scope("sum_first"):
        low, got = scatter(theirs, mine, sums, 1, 1, False)
    with jax.named_scope("residual"):
        first, resid, send, keep = call(
            residual_kernel, "residual", [VMEM] * 6,
            [block, block, shape(1, high, width, dtype=BF16), sums_of],
            [], (low, got, wave, inside, precond, sums), mine.size,
        )
    with jax.named_scope("gather_residual"):
        pieces = gather(send)
    with jax.named_scope("second_sigma"):
        theirs, mine, sums, sigma, direction = call(
            second_kernel, "second_sigma", [SMEM] * 2 + near + [VMEM] * 6,
            [shape(chips, high, width, dtype=BF16), shape(chips, width, width), sums_of,
             block, shape(1, width, width, dtype=BF16)],
            [pltpu.VMEM((every, width, width), BF16), pltpu.VMEM((every, width, width), F32),
             pltpu.VMEM((3, every, width), F32), pltpu.VMEM((1, width, width), BF16),
             pltpu.SemaphoreType.DMA((2,))],
            (source, target, *pieces, wave, left, flip, resid, first, keep), flops,
            [VMEM] * 3 + [HBM] * 2,
        )
    with jax.named_scope("sum_second"):
        low, got = scatter(theirs, mine, sums, 3, 2, True)
    with jax.named_scope("outputs"):
        second, subspace = call(
            final_kernel, "outputs", [VMEM] * 6, [block, shape(4)],
            [], (low, got, inside, first, keep, sums), mine.size, [VMEM, SMEM],
        )
    return sigma, direction, second, subspace


def solution(mesh):
    groups, members = mesh.shape["grp"], mesh.shape["op"]
    split = Mesh(mesh.devices.reshape(groups, members // 2, 2), ("grp", "chip", "core"))
    rows = P(("grp", "chip", "core"))
    return jax.shard_map(
        shards,
        mesh=split,
        in_specs=(rows, P("grp"), rows, rows, rows, rows, rows),
        out_specs=(rows, rows, rows, P("grp")),
        check_vma=False,
    )
```

time: 76.3 us -> 68.9 us (0.903)
  blocking collectives: 56.5 us -> 0 us
  starting transfers between devices: 0.4 us -> 27.2 us
  waiting for transfers between devices: 6.01 us -> 28.6 us
  Pallas kernels: 11.5 us -> 10.6 us
    all_to_all x4 -> x0, blocking collectives: 56.5 us -> none  [the longest x2 27.3 us: shards(): got = lax.all_to_all(part, 'chip', 0, 0, tiled=True)]
    ppermute x4 -> x26, starting transfers between devices: 0.4 us -> 27.2 us  [the longest x16 26.4 us: flip_chip(): return lax.ppermute(x, 'chip', [(i, i ^ bits) for i in range(chips)])]
    ppermute x4 -> x26, waiting for transfers between devices: 6.01 us -> 28.6 us  [the longest x16 24.7 us: flip_chip(): return lax.ppermute(x, 'chip', [(i, i ^ bits) for i in range(chips)])]
    pallas_call x7 -> x9, Pallas kernels: 11.5 us -> 10.6 us  [call(): pl.pallas_call(kernel, name=name, in_specs=ins, out_specs=out_specs or [V...]
  transfers between devices with their start and end apart: 4 -> 26, of which waited for: 4 -> 19; matrix products, arithmetic and copies ran while one was open for 0% -> 1% of each run, Pallas kernels for 0% -> 1%
where the time goes in v4:
time: 68.9 us; the launch traced here: 68.7 us
  waiting for transfers between devices  28.6 us (42%)
  starting transfers between devices  27.2 us (39%)
  Pallas kernels  10.6 us (15%)
  local copies, waits for them, and re-layouts  1.51 us (2%)
  between operations  0.82 us (1%)
    ppermute x16, starting transfers between devices, flip_chip(): return lax.ppermute(x, 'chip', [(i, i ^ bits) for i in range(chips)])  26.4 us
    ppermute x16, waiting for transfers between devices, flip_chip(): return lax.ppermute(x, 'chip', [(i, i ^ bits) for i in range(chips)])  24.7 us
    pallas_call x9, Pallas kernels, call(): pl.pallas_call(kernel, name=name, in_specs=ins, out_specs=out_specs or [V...  10.6 us
    ppermute x10, waiting for transfers between devices, swap(): return lax.ppermute(x, 'core', [(0, 1), (1, 0)])  3.9 us
    unnamed x18, local copies, waits for them, and re-layouts  1.5 us
  transfers between devices with their start and end apart: 26, of which 19 were waited for; matrix products, arithmetic and copies ran while one was open for 1% of the time, Pallas kernels for 1%

profile of v4, /device:TPU:0, one launch (start us, length us, event | category | flops | bytes accessed | tf_op | source)
XLA Modules:
  0.0 68.7 jit_solution(6557703879879040647)
XLA Ops:
  0.6 4.1 %collective-permute-start = (bf16[1,128,128]{2,1,0:T(8,128)(2,1)}, bf16[1,128,128]{2,1,0:T(8,128)(2,1)S(1)}, u32[]{:S(2)}, u32[]{:S(2)}) collective-permute-start(bf16[1,128,128]{2,1,0:T(8,128)(2,1)} %param.7), channel_id=1, source_target_pairs={{0,8},{2,10},{4,12},{6,14},{8,0},{10,2},{12,4},{14,6},{1,9},{3,11}... | collective-permute-start | bytes 98312 | tf_op jit(solution)/shard_map/gather_state/ppermute | solution.py:313
  4.7 0.8 %constant_dynamic-update-slice_fusion.1 = bf16[2,128,128]{2,1,0:T(8,128)(2,1)S(1)} fusion(bf16[1,128,128]{2,1,0:T(8,128)(2,1)} %param.7), kind=kLoop, calls=%fused_computation.1 | loop fusion | bytes 65536
  5.5 1.7 %collective-permute-done = bf16[1,128,128]{2,1,0:T(8,128)(2,1)S(1)} collective-permute-done((bf16[1,128,128]{2,1,0:T(8,128)(2,1)}, bf16[1,128,128]{2,1,0:T(8,128)(2,1)S(1)}, u32[]{:S(2)}, u32[]{:S(2)}) %collective-permute-start) | collective-permute-done | bytes 32800 | tf_op jit(solution)/shard_map/gather_state/ppermute | solution.py:313
  7.2 0.0 slice-start.1
  7.2 0.0 slice-start.3
  7.2 0.0 copy-start.1
  7.2 0.0 copy-start.2
  7.3 2.5 %collective-permute-start.3 = (bf16[2,128,128]{2,1,0:T(8,128)(2,1)S(1)}, bf16[2,128,128]{2,1,0:T(8,128)(2,1)S(1)}, u32[]{:S(2)}, u32[]{:S(2)}) collective-permute-start(bf16[2,128,128]{2,1,0:T(8,128)(2,1)S(1)} %constant_dynamic-update-slice_fusion.refs_0_), channel_id=1, source_target_pairs={{0,6},{2,4},{4,2},{6,0},{8,14},{10,12},{12,10},{14,8},{1,7},{3,5},... | collective-permute-start | bytes 196616 | tf_op jit(solution)/shard_map/gather_state/ppermute | solution.py:313
  9.8 0.7 collective-permute-start.2
  10.5 0.3 collective-permute-start.1
  10.8 0.0 collective-permute-start.4
  10.8 1.7 %collective-permute-done.3.refs_3_ = bf16[2,128,128]{2,1,0:T(8,128)(2,1)S(1)} collective-permute-done((bf16[2,128,128]{2,1,0:T(8,128)(2,1)S(1)}, bf16[2,128,128]{2,1,0:T(8,128)(2,1)S(1)}, u32[]{:S(2)}, u32[]{:S(2)}) %collective-permute-start.3) | collective-permute-done | bytes 65568 | tf_op jit(solution)/shard_map/gather_state/ppermute | solution.py:313
  12.5 0.0 collective-permute-start.7
  12.5 1.6 %collective-permute-done.2.refs_2_ = bf16[2,128,128]{2,1,0:T(8,128)(2,1)S(1)} collective-permute-done((bf16[2,128,128]{2,1,0:T(8,128)(2,1)S(1)}, bf16[2,128,128]{2,1,0:T(8,128)(2,1)S(1)}, u32[]{:S(2)}, u32[]{:S(2)}) %collective-permute-start.2) | collective-permute-done | bytes 65568 | tf_op jit(solution)/shard_map/gather_state/ppermute | solution.py:313
  14.1 0.0 collective-permute-start.6
  14.1 0.7 collective-permute-done.1.refs_1_
  14.7 0.0 collective-permute-start.5
  14.8 0.7 copy-done.3
  15.4 0.6 own_mask.1.refs_10_.inside
  16.0 0.0 copy-start
  16.0 0.0 collective-permute-done.4.refs_4_
  16.0 0.0 collective-permute-done.7.refs_7_
  16.0 0.0 collective-permute-done.6.refs_6_
  16.1 4.5 %first_sigma.1 = (bf16[8,144,128]{2,1,0:T(8,128)(2,1)S(1)}, f32[8,128,128]{2,1,0:T(8,128)S(1)}, bf16[16,128,128]{2,1,0:T(8,128)(2,1)S(1)}, bf16[12,12,128,128]{3,2,1,0:T(8,128)(2,1)S(1)}, f32[8,128]{1,0:T(8,128)S(1)}) custom-call(s32[12,12]{1,0:T(8,128)S(1)} %copy-done.1, s32[12,12]{1,0:T(8,128)S(1)} %copy-done.2, s32[16]{0:T(128)S(1)} %copy-done.3, ...), custom_call_target="tpu_custom_call" | custom-call | flops 1207959552 | bytes 10028224 | tf_op jit(solution)/shard_map/first_sigma/first_sigma/pallas_call | solution.py:291
  20.6 0.6 collective-permute-start.8
  21.2 1.2 %collective-permute-done.8.refs_1_ = bf16[8,144,128]{2,1,0:T(8,128)(2,1)S(1)} collective-permute-done((bf16[8,144,128]{2,1,0:T(8,128)(2,1)S(1)}, bf16[8,144,128]{2,1,0:T(8,128)(2,1)S(1)}, u32[]{:S(2)}, u32[]{:S(2)}) %collective-permute-start.8) | collective-permute-done | bytes 294944 | tf_op jit(solution)/shard_map/sum_first/ppermute | solution.py:308
  22.4 0.1 chip_sum.2
  22.5 0.4 collective-permute-start.9
  22.9 1.6 %collective-permute-start.10 = (bf16[2,144,128]{2,1,0:T(8,128)(2,1)S(1)}, bf16[2,144,128]{2,1,0:T(8,128)(2,1)S(1)}, u32[]{:S(2)}, u32[]{:S(2)}) collective-permute-start(bf16[2,144,128]{2,1,0:T(8,128)(2,1)S(1)} %get-tuple-element.37), channel_id=1, source_target_pairs={{0,4},{2,6},{4,0},{6,2},{8,12},{10,14},{12,8},{14,10},{1,5},{3,7},... | collective-permute-start | bytes 221192 | tf_op jit(solution)/shard_map/sum_first/ppermute | solution.py:313
  24.4 1.6 %collective-permute-start.11 = (bf16[2,144,128]{2,1,0:T(8,128)(2,1)S(1)}, bf16[2,144,128]{2,1,0:T(8,128)(2,1)S(1)}, u32[]{:S(2)}, u32[]{:S(2)}) collective-permute-start(bf16[2,144,128]{2,1,0:T(8,128)(2,1)S(1)} %get-tuple-element.38), channel_id=1, source_target_pairs={{0,6},{2,4},{4,2},{6,0},{8,14},{10,12},{12,10},{14,8},{1,7},{3,5},... | collective-permute-start | bytes 221192 | tf_op jit(solution)/shard_map/sum_first/ppermute | solution.py:313
  26.0 1.0 %collective-permute-done.9.refs_1_ = bf16[2,144,128]{2,1,0:T(8,128)(2,1)S(1)} collective-permute-done((bf16[2,144,128]{2,1,0:T(8,128)(2,1)S(1)}, bf16[2,144,128]{2,1,0:T(8,128)(2,1)S(1)}, u32[]{:S(2)}, u32[]{:S(2)}) %collective-permute-start.9) | collective-permute-done | bytes 73760 | tf_op jit(solution)/shard_map/sum_first/ppermute | solution.py:313
  27.1 0.1 collective-permute-done.10.refs_2_
  27.2 2.7 %collective-permute-done.11.refs_3_ = bf16[2,144,128]{2,1,0:T(8,128)(2,1)S(1)} collective-permute-done((bf16[2,144,128]{2,1,0:T(8,128)(2,1)S(1)}, bf16[2,144,128]{2,1,0:T(8,128)(2,1)S(1)}, u32[]{:S(2)}, u32[]{:S(2)}) %collective-permute-start.11) | collective-permute-done | bytes 73760 | tf_op jit(solution)/shard_map/sum_first/ppermute | solution.py:313
  30.0 2.6 %collective-permute-start.12 = (f32[1,136,128]{2,1,0:T(8,128)S(1)}, f32[1,136,128]{2,1,0:T(8,128)S(1)}, u32[]{:S(2)}, u32[]{:S(2)}) collective-permute-start(f32[1,136,128]{2,1,0:T(8,128)S(1)} %get-tuple-element.40), channel_id=1, source_target_pairs={{0,8},{2,10},{4,12},{6,14},{8,0},{10,2},{12,4},{14,6},{1,9},{3,11}... | collective-permute-start | bytes 208904 | tf_op jit(solution)/shard_map/sum_first/ppermute | solution.py:313
  32.6 2.7 %collective-permute-done.12.got = f32[1,136,128]{2,1,0:T(8,128)S(1)} collective-permute-done((f32[1,136,128]{2,1,0:T(8,128)S(1)}, f32[1,136,128]{2,1,0:T(8,128)S(1)}, u32[]{:S(2)}, u32[]{:S(2)}) %collective-permute-start.12) | collective-permute-done | bytes 69664 | tf_op jit(solution)/shard_map/sum_first/ppermute | solution.py:313
  35.3 0.1 residual.1
  35.4 2.7 %collective-permute-start.13 = (bf16[1,144,128]{2,1,0:T(8,128)(2,1)S(1)}, bf16[1,144,128]{2,1,0:T(8,128)(2,1)S(1)}, u32[]{:S(2)}, u32[]{:S(2)}) collective-permute-start(bf16[1,144,128]{2,1,0:T(8,128)(2,1)S(1)} %get-tuple-element.42), channel_id=1, source_target_pairs={{0,8},{2,10},{4,12},{6,14},{8,0},{10,2},{12,4},{14,6},{1,9},{3,11}... | collective-permute-start | bytes 110600 | tf_op jit(solution)/shard_map/gather_residual/ppermute | solution.py:313
  38.1 2.2 %collective-permute-done.13 = bf16[1,144,128]{2,1,0:T(8,128)(2,1)S(1)} collective-permute-done((bf16[1,144,128]{2,1,0:T(8,128)(2,1)S(1)}, bf16[1,144,128]{2,1,0:T(8,128)(2,1)S(1)}, u32[]{:S(2)}, u32[]{:S(2)}) %collective-permute-start.13) | collective-permute-done | bytes 36896 | tf_op jit(solution)/shard_map/gather_residual/ppermute | solution.py:313
  40.3 1.5 %collective-permute-start.16 = (bf16[2,144,128]{2,1,0:T(8,128)(2,1)S(1)}, bf16[2,144,128]{2,1,0:T(8,128)(2,1)S(1)}, u32[]{:S(2)}, u32[]{:S(2)}) collective-permute-start(bf16[2,144,128]{2,1,0:T(8,128)(2,1)S(1)} %constant_dynamic-update-slice_fusion.2.refs_0_), channel_id=1, source_target_pairs={{0,6},{2,4},{4,2},{6,0},{8,14},{10,12},{12,10},{14,8},{1,7},{3,5},... | collective-permute-start | bytes 221192 | tf_op jit(solution)/shard_map/gather_residual/ppermute | solution.py:313
  41.8 2.0 %collective-permute-start.15 = (bf16[2,144,128]{2,1,0:T(8,128)(2,1)S(1)}, bf16[2,144,128]{2,1,0:T(8,128)(2,1)S(1)}, u32[]{:S(2)}, u32[]{:S(2)}) collective-permute-start(bf16[2,144,128]{2,1,0:T(8,128)(2,1)S(1)} %constant_dynamic-update-slice_fusion.2.refs_0_), channel_id=1, source_target_pairs={{0,4},{2,6},{4,0},{6,2},{8,12},{10,14},{12,8},{14,10},{1,5},{3,7},... | collective-permute-start | bytes 221192 | tf_op jit(solution)/shard_map/gather_residual/ppermute | solution.py:313
  43.8 0.1 collective-permute-start.14
  43.9 0.0 collective-permute-start.17
  43.9 1.8 %collective-permute-done.16.refs_3_ = bf16[2,144,128]{2,1,0:T(8,128)(2,1)S(1)} collective-permute-done((bf16[2,144,128]{2,1,0:T(8,128)(2,1)S(1)}, bf16[2,144,128]{2,1,0:T(8,128)(2,1)S(1)}, u32[]{:S(2)}, u32[]{:S(2)}) %collective-permute-start.16) | collective-permute-done | bytes 73760 | tf_op jit(solution)/shard_map/gather_residual/ppermute | solution.py:313
  45.6 1.3 %collective-permute-done.15.refs_2_ = bf16[2,144,128]{2,1,0:T(8,128)(2,1)S(1)} collective-permute-done((bf16[2,144,128]{2,1,0:T(8,128)(2,1)S(1)}, bf16[2,144,128]{2,1,0:T(8,128)(2,1)S(1)}, u32[]{:S(2)}, u32[]{:S(2)}) %collective-permute-start.15) | collective-permute-done | bytes 73760 | tf_op jit(solution)/shard_map/gather_residual/ppermute | solution.py:313
  46.9 0.0 collective-permute-start.19
  46.9 1.2 %collective-permute-done.14.refs_1_ = bf16[2,144,128]{2,1,0:T(8,128)(2,1)S(1)} collective-permute-done((bf16[2,144,128]{2,1,0:T(8,128)(2,1)S(1)}, bf16[2,144,128]{2,1,0:T(8,128)(2,1)S(1)}, u32[]{:S(2)}, u32[]{:S(2)}) %collective-permute-start.14) | collective-permute-done | bytes 73760 | tf_op jit(solution)/shard_map/gather_residual/ppermute | solution.py:313
  48.2 0.0 collective-permute-start.18
  48.2 0.0 collective-permute-done.17.refs_4_
  48.2 0.0 collective-permute-done.19.refs_6_
  48.2 1.2 %collective-permute-done.18.refs_5_ = bf16[2,144,128]{2,1,0:T(8,128)(2,1)S(1)} collective-permute-done((bf16[2,144,128]{2,1,0:T(8,128)(2,1)S(1)}, bf16[2,144,128]{2,1,0:T(8,128)(2,1)S(1)}, u32[]{:S(2)}, u32[]{:S(2)}) %collective-permute-start.18) | collective-permute-done | bytes 73760 | tf_op jit(solution)/shard_map/gather_residual/ppermute | solution.py:308
  49.4 4.4 %second_sigma.1 = (bf16[8,144,128]{2,1,0:T(8,128)(2,1)S(1)}, f32[8,128,128]{2,1,0:T(8,128)S(1)}, f32[8,128]{1,0:T(8,128)S(1)}, f32[1,128,128]{2,1,0:T(8,128)}, bf16[1,128,128]{2,1,0:T(8,128)(2,1)}) custom-call(s32[12,12]{1,0:T(8,128)S(1)} %copy-done.1, s32[12,12]{1,0:T(8,128)S(1)} %copy-done.2, ...), custom_call_target="tpu_custom_call" | custom-call | flops 1207959552 | bytes 10687616 | tf_op jit(solution)/shard_map/second_sigma/second_sigma/pallas_call | solution.py:291
  53.9 0.2 collective-permute-start.21
  54.1 1.4 %collective-permute-done.21.refs_1_ = bf16[8,144,128]{2,1,0:T(8,128)(2,1)S(1)} collective-permute-done((bf16[8,144,128]{2,1,0:T(8,128)(2,1)S(1)}, bf16[8,144,128]{2,1,0:T(8,128)(2,1)S(1)}, u32[]{:S(2)}, u32[]{:S(2)}) %collective-permute-start.21) | collective-permute-done | bytes 294944 | tf_op jit(solution)/shard_map/sum_second/ppermute | solution.py:308
  55.5 0.1 chip_sum.3
  55.6 0.3 collective-permute-start.22
  55.9 1.7 %collective-permute-start.23 = (bf16[2,144,128]{2,1,0:T(8,128)(2,1)S(1)}, bf16[2,144,128]{2,1,0:T(8,128)(2,1)S(1)}, u32[]{:S(2)}, u32[]{:S(2)}) collective-permute-start(bf16[2,144,128]{2,1,0:T(8,128)(2,1)S(1)} %get-tuple-element.54), channel_id=1, source_target_pairs={{0,4},{2,6},{4,0},{6,2},{8,12},{10,14},{12,8},{14,10},{1,5},{3,7},... | collective-permute-start | bytes 221192 | tf_op jit(solution)/shard_map/sum_second/ppermute | solution.py:313
  57.5 1.6 %collective-permute-start.24 = (bf16[2,144,128]{2,1,0:T(8,128)(2,1)S(1)}, bf16[2,144,128]{2,1,0:T(8,128)(2,1)S(1)}, u32[]{:S(2)}, u32[]{:S(2)}) collective-permute-start(bf16[2,144,128]{2,1,0:T(8,128)(2,1)S(1)} %get-tuple-element.55), channel_id=1, source_target_pairs={{0,6},{2,4},{4,2},{6,0},{8,14},{10,12},{12,10},{14,8},{1,7},{3,5},... | collective-permute-start | bytes 221192 | tf_op jit(solution)/shard_map/sum_second/ppermute | solution.py:313
  59.1 0.9 %collective-permute-done.22.refs_1_ = bf16[2,144,128]{2,1,0:T(8,128)(2,1)S(1)} collective-permute-done((bf16[2,144,128]{2,1,0:T(8,128)(2,1)S(1)}, bf16[2,144,128]{2,1,0:T(8,128)(2,1)S(1)}, u32[]{:S(2)}, u32[]{:S(2)}) %collective-permute-start.22) | collective-permute-done | bytes 73760 | tf_op jit(solution)/shard_map/sum_second/ppermute | solution.py:313
  60.0 0.8 %collective-permute-done.23.refs_2_ = bf16[2,144,128]{2,1,0:T(8,128)(2,1)S(1)} collective-permute-done((bf16[2,144,128]{2,1,0:T(8,128)(2,1)S(1)}, bf16[2,144,128]{2,1,0:T(8,128)(2,1)S(1)}, u32[]{:S(2)}, u32[]{:S(2)}) %collective-permute-start.23) | collective-permute-done | bytes 73760 | tf_op jit(solution)/shard_map/sum_second/ppermute | solution.py:313
  60.8 2.2 %collective-permute-done.24.refs_3_ = bf16[2,144,128]{2,1,0:T(8,128)(2,1)S(1)} collective-permute-done((bf16[2,144,128]{2,1,0:T(8,128)(2,1)S(1)}, bf16[2,144,128]{2,1,0:T(8,128)(2,1)S(1)}, u32[]{:S(2)}, u32[]{:S(2)}) %collective-permute-start.24) | collective-permute-done | bytes 73760 | tf_op jit(solution)/shard_map/sum_second/ppermute | solution.py:313
  63.0 0.1 near_sum.3
  63.1 2.8 %collective-permute-start.25 = (bf16[1,144,128]{2,1,0:T(8,128)(2,1)S(1)}, bf16[1,144,128]{2,1,0:T(8,128)(2,1)S(1)}, u32[]{:S(2)}, u32[]{:S(2)}) collective-permute-start(bf16[1,144,128]{2,1,0:T(8,128)(2,1)S(1)} %get-tuple-element.57), channel_id=1, source_target_pairs={{0,8},{2,10},{4,12},{6,14},{8,0},{10,2},{12,4},{14,6},{1,9},{3,11}... | collective-permute-start | bytes 110600 | tf_op jit(solution)/shard_map/sum_second/ppermute | solution.py:313
  65.9 2.2 %collective-permute-done.25.got = bf16[1,144,128]{2,1,0:T(8,128)(2,1)S(1)} collective-permute-done((bf16[1,144,128]{2,1,0:T(8,128)(2,1)S(1)}, bf16[1,144,128]{2,1,0:T(8,128)(2,1)S(1)}, u32[]{:S(2)}, u32[]{:S(2)}) %collective-permute-start.25) | collective-permute-done | bytes 36896 | tf_op jit(solution)/shard_map/sum_second/ppermute | solution.py:313
  68.0 0.7 %outputs.1 = (f32[1,128,128]{2,1,0:T(8,128)}, f32[4]{0:T(128)}) custom-call(f32[1,136,128]{2,1,0:T(8,128)S(1)} %get-tuple-element.56.half, bf16[1,144,128]{2,1,0:T(8,128)(2,1)S(1)} %collective-permute-done.25.got, f32[1,128,128]{2,1,0:T(8,128)S(1)} %own_mask.1.refs_10_.inside, f32[1,128,128]{2,1,0:T(8,128)S(1)} %get-tuple-element.45.refs_12_.first, ...), custom_call_target="tpu_custom_call" | custom-call | flops 131072 | bytes 245760 | tf_op jit(solution)/shard_map/outputs/outputs/pallas_call | solution.py:291
  (19 shorter events, 0.1 us)
Async XLA Ops:
  0.6 6.6 %collective-permute-start = (bf16[1,128,128]{2,1,0:T(8,128)(2,1)}, bf16[1,128,128]{2,1,0:T(8,128)(2,1)S(1)}, u32[]{:S(2)}, u32[]{:S(2)}) collective-permute-start(bf16[1,128,128]{2,1,0:T(8,128)(2,1)} %param.7), channel_id=1, source_target_pairs={{0,8},{2,10},{4,12},{6,14},{8,0},{10,2},{12,4},{14,6},{1,9},{3,11}... | collective-permute-start | bytes 98312 | tf_op jit(solution)/shard_map/gather_state/ppermute | solution.py:313
  7.2 8.8 %slice-start = ((s8[4718592]{0:T(1024)(128)(4,1)}), s8[4194304]{0:T(1024)(128)(4,1)S(1)}, s32[]{:S(2)}) async-start(s8[4718592]{0:T(1024)(128)(4,1)} %bitcast), calls=%async_computation | async-start | bytes 8388608
  7.2 8.8 %slice-start.2 = ((s8[4718592]{0:T(1024)(128)(4,1)}), s8[4194304]{0:T(1024)(128)(4,1)S(1)}, s32[]{:S(2)}) async-start(s8[4718592]{0:T(1024)(128)(4,1)} %bitcast.2), calls=%async_computation.2 | async-start | bytes 8388608
  7.2 8.8 %slice-start.1 = ((s8[4718592]{0:T(1024)(128)(4,1)}), s8[524288]{0:T(1024)(128)(4,1)S(1)}, s32[]{:S(2)}) async-start(s8[4718592]{0:T(1024)(128)(4,1)} %bitcast), calls=%async_computation.1 | async-start | bytes 1048576
  7.2 8.8 %slice-start.3 = ((s8[4718592]{0:T(1024)(128)(4,1)}), s8[524288]{0:T(1024)(128)(4,1)S(1)}, s32[]{:S(2)}) async-start(s8[4718592]{0:T(1024)(128)(4,1)} %bitcast.2), calls=%async_computation.3 | async-start | bytes 1048576
  7.2 8.8 %copy-start.1 = (s32[12,12]{1,0:T(8,128)S(1)}, s32[12,12]{1,0:T(8,128)}, u32[]{:S(2)}) copy-start(s32[12,12]{1,0:T(8,128)} %src.3) | copy-start | bytes 1732
  7.2 8.8 %copy-start.2 = (s32[12,12]{1,0:T(8,128)S(1)}, s32[12,12]{1,0:T(8,128)}, u32[]{:S(2)}) copy-start(s32[12,12]{1,0:T(8,128)} %tgt.3) | copy-start | bytes 1732
  7.3 5.2 %collective-permute-start.3 = (bf16[2,128,128]{2,1,0:T(8,128)(2,1)S(1)}, bf16[2,128,128]{2,1,0:T(8,128)(2,1)S(1)}, u32[]{:S(2)}, u32[]{:S(2)}) collective-permute-start(bf16[2,128,128]{2,1,0:T(8,128)(2,1)S(1)} %constant_dynamic-update-slice_fusion.refs_0_), channel_id=1, source_target_pairs={{0,6},{2,4},{4,2},{6,0},{8,14},{10,12},{12,10},{14,8},{1,7},{3,5},... | collective-permute-start | bytes 196616 | tf_op jit(solution)/shard_map/gather_state/ppermute | solution.py:313
  9.8 4.3 %collective-permute-start.2 = (bf16[2,128,128]{2,1,0:T(8,128)(2,1)S(1)}, bf16[2,128,128]{2,1,0:T(8,128)(2,1)S(1)}, u32[]{:S(2)}, u32[]{:S(2)}) collective-permute-start(bf16[2,128,128]{2,1,0:T(8,128)(2,1)S(1)} %constant_dynamic-update-slice_fusion.refs_0_), channel_id=1, source_target_pairs={{0,4},{2,6},{4,0},{6,2},{8,12},{10,14},{12,8},{14,10},{1,5},{3,7},... | collective-permute-start | bytes 196616 | tf_op jit(solution)/shard_map/gather_state/ppermute | solution.py:313
  10.5 4.3 %collective-permute-start.1 = (bf16[2,128,128]{2,1,0:T(8,128)(2,1)S(1)}, bf16[2,128,128]{2,1,0:T(8,128)(2,1)S(1)}, u32[]{:S(2)}, u32[]{:S(2)}) collective-permute-start(bf16[2,128,128]{2,1,0:T(8,128)(2,1)S(1)} %constant_dynamic-update-slice_fusion.refs_0_), channel_id=1, source_target_pairs={{0,2},{2,0},{4,6},{6,4},{8,10},{10,8},{12,14},{14,12},{1,3},{3,1},... | collective-permute-start | bytes 196616 | tf_op jit(solution)/shard_map/gather_state/ppermute | solution.py:313
  10.8 5.2 %collective-permute-start.4 = (bf16[2,128,128]{2,1,0:T(8,128)(2,1)S(1)}, bf16[2,128,128]{2,1,0:T(8,128)(2,1)S(1)}, u32[]{:S(2)}, u32[]{:S(2)}) collective-permute-start(bf16[2,128,128]{2,1,0:T(8,128)(2,1)S(1)} %constant_dynamic-update-slice_fusion.refs_0_), channel_id=1, source_target_pairs={{0,1},{1,0},{2,3},{3,2},{4,5},{5,4},{6,7},{7,6},{8,9},{9,8},{10,11... | collective-permute-start | bytes 196616 | tf_op jit(solution)/shard_map/gather_state/ppermute | solution.py:308
  12.5 3.5 %collective-permute-start.7 = (bf16[2,128,128]{2,1,0:T(8,128)(2,1)S(1)}, bf16[2,128,128]{2,1,0:T(8,128)(2,1)S(1)}, u32[]{:S(2)}, u32[]{:S(2)}) collective-permute-start(bf16[2,128,128]{2,1,0:T(8,128)(2,1)S(1)} %collective-permute-done.3.refs_3_), channel_id=1, source_target_pairs={{0,1},{1,0},{2,3},{3,2},{4,5},{5,4},{6,7},{7,6},{8,9},{9,8},{10,11... | collective-permute-start | bytes 196616 | tf_op jit(solution)/shard_map/gather_state/ppermute | solution.py:308
  14.1 1.9 %collective-permute-start.6 = (bf16[2,128,128]{2,1,0:T(8,128)(2,1)S(1)}, bf16[2,128,128]{2,1,0:T(8,128)(2,1)S(1)}, u32[]{:S(2)}, u32[]{:S(2)}) collective-permute-start(bf16[2,128,128]{2,1,0:T(8,128)(2,1)S(1)} %collective-permute-done.2.refs_2_), channel_id=1, source_target_pairs={{0,1},{1,0},{2,3},{3,2},{4,5},{5,4},{6,7},{7,6},{8,9},{9,8},{10,11... | collective-permute-start | bytes 196616 | tf_op jit(solution)/shard_map/gather_state/ppermute | solution.py:308
  14.7 1.3 %collective-permute-start.5 = (bf16[2,128,128]{2,1,0:T(8,128)(2,1)S(1)}, bf16[2,128,128]{2,1,0:T(8,128)(2,1)S(1)}, u32[]{:S(2)}, u32[]{:S(2)}) collective-permute-start(bf16[2,128,128]{2,1,0:T(8,128)(2,1)S(1)} %collective-permute-done.1.refs_1_), channel_id=1, source_target_pairs={{0,1},{1,0},{2,3},{3,2},{4,5},{5,4},{6,7},{7,6},{8,9},{9,8},{10,11... | collective-permute-start | bytes 196616 | tf_op jit(solution)/shard_map/gather_state/ppermute | solution.py:308
  14.7 0.7 copy-start.3
  16.0 19.3 %copy-start = (f32[1,128,128]{2,1,0:T(8,128)S(1)}, f32[1,128,128]{2,1,0:T(8,128)}, u32[]{:S(2)}) copy-start(f32[1,128,128]{2,1,0:T(8,128)} %precond.1) | copy-start | bytes 196612
  20.6 1.8 %collective-permute-start.8 = (bf16[8,144,128]{2,1,0:T(8,128)(2,1)S(1)}, bf16[8,144,128]{2,1,0:T(8,128)(2,1)S(1)}, u32[]{:S(2)}, u32[]{:S(2)}) collective-permute-start(bf16[8,144,128]{2,1,0:T(8,128)(2,1)S(1)} %get-tuple-element.33), channel_id=1, source_target_pairs={{0,1},{1,0},{2,3},{3,2},{4,5},{5,4},{6,7},{7,6},{8,9},{9,8},{10,11... | collective-permute-start | bytes 884744 | tf_op jit(solution)/shard_map/sum_first/ppermute | solution.py:308
  22.5 4.6 %collective-permute-start.9 = (bf16[2,144,128]{2,1,0:T(8,128)(2,1)S(1)}, bf16[2,144,128]{2,1,0:T(8,128)(2,1)S(1)}, u32[]{:S(2)}, u32[]{:S(2)}) collective-permute-start(bf16[2,144,128]{2,1,0:T(8,128)(2,1)S(1)} %get-tuple-element.36), channel_id=1, source_target_pairs={{0,2},{2,0},{4,6},{6,4},{8,10},{10,8},{12,14},{14,12},{1,3},{3,1},... | collective-permute-start | bytes 221192 | tf_op jit(solution)/shard_map/sum_first/ppermute | solution.py:313
  22.9 4.4 %collective-permute-start.10 = (bf16[2,144,128]{2,1,0:T(8,128)(2,1)S(1)}, bf16[2,144,128]{2,1,0:T(8,128)(2,1)S(1)}, u32[]{:S(2)}, u32[]{:S(2)}) collective-permute-start(bf16[2,144,128]{2,1,0:T(8,128)(2,1)S(1)} %get-tuple-element.37), channel_id=1, source_target_pairs={{0,4},{2,6},{4,0},{6,2},{8,12},{10,14},{12,8},{14,10},{1,5},{3,7},... | collective-permute-start | bytes 221192 | tf_op jit(solution)/shard_map/sum_first/ppermute | solution.py:313
  24.4 5.5 %collective-permute-start.11 = (bf16[2,144,128]{2,1,0:T(8,128)(2,1)S(1)}, bf16[2,144,128]{2,1,0:T(8,128)(2,1)S(1)}, u32[]{:S(2)}, u32[]{:S(2)}) collective-permute-start(bf16[2,144,128]{2,1,0:T(8,128)(2,1)S(1)} %get-tuple-element.38), channel_id=1, source_target_pairs={{0,6},{2,4},{4,2},{6,0},{8,14},{10,12},{12,10},{14,8},{1,7},{3,5},... | collective-permute-start | bytes 221192 | tf_op jit(solution)/shard_map/sum_first/ppermute | solution.py:313
  30.0 5.3 %collective-permute-start.12 = (f32[1,136,128]{2,1,0:T(8,128)S(1)}, f32[1,136,128]{2,1,0:T(8,128)S(1)}, u32[]{:S(2)}, u32[]{:S(2)}) collective-permute-start(f32[1,136,128]{2,1,0:T(8,128)S(1)} %get-tuple-element.40), channel_id=1, source_target_pairs={{0,8},{2,10},{4,12},{6,14},{8,0},{10,2},{12,4},{14,6},{1,9},{3,11}... | collective-permute-start | bytes 208904 | tf_op jit(solution)/shard_map/sum_first/ppermute | solution.py:313
  35.4 4.9 %collective-permute-start.13 = (bf16[1,144,128]{2,1,0:T(8,128)(2,1)S(1)}, bf16[1,144,128]{2,1,0:T(8,128)(2,1)S(1)}, u32[]{:S(2)}, u32[]{:S(2)}) collective-permute-start(bf16[1,144,128]{2,1,0:T(8,128)(2,1)S(1)} %get-tuple-element.42), channel_id=1, source_target_pairs={{0,8},{2,10},{4,12},{6,14},{8,0},{10,2},{12,4},{14,6},{1,9},{3,11}... | collective-permute-start | bytes 110600 | tf_op jit(solution)/shard_map/gather_residual/ppermute | solution.py:313
  40.3 5.3 %collective-permute-start.16 = (bf16[2,144,128]{2,1,0:T(8,128)(2,1)S(1)}, bf16[2,144,128]{2,1,0:T(8,128)(2,1)S(1)}, u32[]{:S(2)}, u32[]{:S(2)}) collective-permute-start(bf16[2,144,128]{2,1,0:T(8,128)(2,1)S(1)} %constant_dynamic-update-slice_fusion.2.refs_0_), channel_id=1, source_target_pairs={{0,6},{2,4},{4,2},{6,0},{8,14},{10,12},{12,10},{14,8},{1,7},{3,5},... | collective-permute-start | bytes 221192 | tf_op jit(solution)/shard_map/gather_residual/ppermute | solution.py:313
  41.8 5.1 %collective-permute-start.15 = (bf16[2,144,128]{2,1,0:T(8,128)(2,1)S(1)}, bf16[2,144,128]{2,1,0:T(8,128)(2,1)S(1)}, u32[]{:S(2)}, u32[]{:S(2)}) collective-permute-start(bf16[2,144,128]{2,1,0:T(8,128)(2,1)S(1)} %constant_dynamic-update-slice_fusion.2.refs_0_), channel_id=1, source_target_pairs={{0,4},{2,6},{4,0},{6,2},{8,12},{10,14},{12,8},{14,10},{1,5},{3,7},... | collective-permute-start | bytes 221192 | tf_op jit(solution)/shard_map/gather_residual/ppermute | solution.py:313
  43.8 4.4 %collective-permute-start.14 = (bf16[2,144,128]{2,1,0:T(8,128)(2,1)S(1)}, bf16[2,144,128]{2,1,0:T(8,128)(2,1)S(1)}, u32[]{:S(2)}, u32[]{:S(2)}) collective-permute-start(bf16[2,144,128]{2,1,0:T(8,128)(2,1)S(1)} %constant_dynamic-update-slice_fusion.2.refs_0_), channel_id=1, source_target_pairs={{0,2},{2,0},{4,6},{6,4},{8,10},{10,8},{12,14},{14,12},{1,3},{3,1},... | collective-permute-start | bytes 221192 | tf_op jit(solution)/shard_map/gather_residual/ppermute | solution.py:313
  43.9 4.3 %collective-permute-start.17 = (bf16[2,144,128]{2,1,0:T(8,128)(2,1)S(1)}, bf16[2,144,128]{2,1,0:T(8,128)(2,1)S(1)}, u32[]{:S(2)}, u32[]{:S(2)}) collective-permute-start(bf16[2,144,128]{2,1,0:T(8,128)(2,1)S(1)} %constant_dynamic-update-slice_fusion.2.refs_0_), channel_id=1, source_target_pairs={{0,1},{1,0},{2,3},{3,2},{4,5},{5,4},{6,7},{7,6},{8,9},{9,8},{10,11... | collective-permute-start | bytes 221192 | tf_op jit(solution)/shard_map/gather_residual/ppermute | solution.py:308
  45.6 2.5 %collective-permute-start.20 = (bf16[2,144,128]{2,1,0:T(8,128)(2,1)S(1)}, bf16[2,144,128]{2,1,0:T(8,128)(2,1)S(1)}, u32[]{:S(2)}, u32[]{:S(2)}) collective-permute-start(bf16[2,144,128]{2,1,0:T(8,128)(2,1)S(1)} %collective-permute-done.16.refs_3_), channel_id=1, source_target_pairs={{0,1},{1,0},{2,3},{3,2},{4,5},{5,4},{6,7},{7,6},{8,9},{9,8},{10,11... | collective-permute-start | bytes 221192 | tf_op jit(solution)/shard_map/gather_residual/ppermute | solution.py:308
  46.9 1.3 %collective-permute-start.19 = (bf16[2,144,128]{2,1,0:T(8,128)(2,1)S(1)}, bf16[2,144,128]{2,1,0:T(8,128)(2,1)S(1)}, u32[]{:S(2)}, u32[]{:S(2)}) collective-permute-start(bf16[2,144,128]{2,1,0:T(8,128)(2,1)S(1)} %collective-permute-done.15.refs_2_), channel_id=1, source_target_pairs={{0,1},{1,0},{2,3},{3,2},{4,5},{5,4},{6,7},{7,6},{8,9},{9,8},{10,11... | collective-permute-start | bytes 221192 | tf_op jit(solution)/shard_map/gather_residual/ppermute | solution.py:308
  48.2 1.3 %collective-permute-start.18 = (bf16[2,144,128]{2,1,0:T(8,128)(2,1)S(1)}, bf16[2,144,128]{2,1,0:T(8,128)(2,1)S(1)}, u32[]{:S(2)}, u32[]{:S(2)}) collective-permute-start(bf16[2,144,128]{2,1,0:T(8,128)(2,1)S(1)} %collective-permute-done.14.refs_1_), channel_id=1, source_target_pairs={{0,1},{1,0},{2,3},{3,2},{4,5},{5,4},{6,7},{7,6},{8,9},{9,8},{10,11... | collective-permute-start | bytes 221192 | tf_op jit(solution)/shard_map/gather_residual/ppermute | solution.py:308
  53.9 1.6 %collective-permute-start.21 = (bf16[8,144,128]{2,1,0:T(8,128)(2,1)S(1)}, bf16[8,144,128]{2,1,0:T(8,128)(2,1)S(1)}, u32[]{:S(2)}, u32[]{:S(2)}) collective-permute-start(bf16[8,144,128]{2,1,0:T(8,128)(2,1)S(1)} %get-tuple-element.50), channel_id=1, source_target_pairs={{0,1},{1,0},{2,3},{3,2},{4,5},{5,4},{6,7},{7,6},{8,9},{9,8},{10,11... | collective-permute-start | bytes 884744 | tf_op jit(solution)/shard_map/sum_second/ppermute | solution.py:308
  55.6 4.4 %collective-permute-start.22 = (bf16[2,144,128]{2,1,0:T(8,128)(2,1)S(1)}, bf16[2,144,128]{2,1,0:T(8,128)(2,1)S(1)}, u32[]{:S(2)}, u32[]{:S(2)}) collective-permute-start(bf16[2,144,128]{2,1,0:T(8,128)(2,1)S(1)} %get-tuple-element.53), channel_id=1, source_target_pairs={{0,2},{2,0},{4,6},{6,4},{8,10},{10,8},{12,14},{14,12},{1,3},{3,1},... | collective-permute-start | bytes 221192 | tf_op jit(solution)/shard_map/sum_second/ppermute | solution.py:313
  55.9 4.9 %collective-permute-start.23 = (bf16[2,144,128]{2,1,0:T(8,128)(2,1)S(1)}, bf16[2,144,128]{2,1,0:T(8,128)(2,1)S(1)}, u32[]{:S(2)}, u32[]{:S(2)}) collective-permute-start(bf16[2,144,128]{2,1,0:T(8,128)(2,1)S(1)} %get-tuple-element.54), channel_id=1, source_target_pairs={{0,4},{2,6},{4,0},{6,2},{8,12},{10,14},{12,8},{14,10},{1,5},{3,7},... | collective-permute-start | bytes 221192 | tf_op jit(solution)/shard_map/sum_second/ppermute | solution.py:313
  57.5 5.5 %collective-permute-start.24 = (bf16[2,144,128]{2,1,0:T(8,128)(2,1)S(1)}, bf16[2,144,128]{2,1,0:T(8,128)(2,1)S(1)}, u32[]{:S(2)}, u32[]{:S(2)}) collective-permute-start(bf16[2,144,128]{2,1,0:T(8,128)(2,1)S(1)} %get-tuple-element.55), channel_id=1, source_target_pairs={{0,6},{2,4},{4,2},{6,0},{8,14},{10,12},{12,10},{14,8},{1,7},{3,5},... | collective-permute-start | bytes 221192 | tf_op jit(solution)/shard_map/sum_second/ppermute | solution.py:313
  63.1 4.9 %collective-permute-start.25 = (bf16[1,144,128]{2,1,0:T(8,128)(2,1)S(1)}, bf16[1,144,128]{2,1,0:T(8,128)(2,1)S(1)}, u32[]{:S(2)}, u32[]{:S(2)}) collective-permute-start(bf16[1,144,128]{2,1,0:T(8,128)(2,1)S(1)} %get-tuple-element.57), channel_id=1, source_target_pairs={{0,8},{2,10},{4,12},{6,14},{8,0},{10,2},{12,4},{14,6},{1,9},{3,11}... | collective-permute-start | bytes 110600 | tf_op jit(solution)/shard_map/sum_second/ppermute | solution.py:313

commit v5 on v4

--- a/solution.py
+++ b/solution.py
@@ -95,13 +95,14 @@
 
 
 def mask_kernel(sizes, inside):
-    own = 2 * lax.axis_index("chip") + lax.axis_index("core")
-    inside[0] = mask_of(sizes[own], inside.shape[2]).astype(F32)
+    for i in range(2):
+        sector = 2 * (lax.axis_index("chip") ^ (NEAR * i)) + lax.axis_index("core")
+        inside[i] = mask_of(sizes[sector], inside.shape[2]).astype(F32)
 
 
 def first_kernel(src, tgt, sizes, *refs):
-    pieces, ins, outs = refs[: 2 * NEAR], refs[2 * NEAR : 2 * NEAR + 3], refs[2 * NEAR + 3 :]
-    left, right, inside = ins
+    pieces, ins, outs = refs[: 2 * NEAR], refs[2 * NEAR : 2 * NEAR + 4], refs[2 * NEAR + 4 :]
+    left, right, inside, _ = ins
     theirs, mine, wave, flip, sums, acc, rows = outs
     span, width = pieces[0].shape[0], pieces[0].shape[2]
     chips = NEAR * span
@@ -116,7 +117,7 @@
                 size = sizes[2 * (chip ^ rel) + (core ^ other)]
                 block = piece[i].astype(F32)
                 if other == 0 and k == 0 and span <= 8 and i == 0:
-                    block = jnp.where(inside[0] > 0.0, block, 0.0)
+                    block = block * inside[0]
                 else:
                     block = jnp.where(mask_of(size, width), block, 0.0)
                 wave[other * chips + rel] = block.astype(BF16)
@@ -140,33 +141,24 @@
 
 
 def second_kernel(src, tgt, *refs):
-    pieces, ins, outs = refs[: 2 * NEAR], refs[2 * NEAR : 2 * NEAR + 6], refs[2 * NEAR + 6 :]
-    wave, left, right, resid, first, keep = ins
-    theirs, mine, sums, sigma, direction, vec, acc, rows, low, sems = outs
+    pieces, ins, outs = refs[: 2 * NEAR], refs[2 * NEAR : 2 * NEAR + 5], refs[2 * NEAR + 5 :]
+    wave, left, right, first, keep = ins
+    theirs, mine, sums, sigma, vec, acc, sem = outs
     span, width = pieces[0].shape[0], pieces[0].shape[2]
     chips = NEAR * span
     core, chip = lax.axis_index("core"), lax.axis_index("chip")
-    copies = [
-        pltpu.make_async_copy(first, sigma, sems.at[0]),
-        pltpu.make_async_copy(low, direction, sems.at[1]),
-    ]
-    copies[0].start()
+    copy = pltpu.make_async_copy(first, sigma, sem)
+    copy.start()
 
     for other in range(2):
         for k in range(NEAR):
             piece = pieces[other * NEAR + k]
 
             def load(i, carry, other=other, k=k, piece=piece):
-                at = other * chips + NEAR * i + k
-                vec[at] = piece[i, 0:width]
-                for n, row in enumerate(rows_of(piece[i, width : width + TAIL], 3)):
-                    rows[n, pl.ds(at, 1)] = row
+                vec[other * chips + NEAR * i + k] = piece[i]
                 return carry
 
             each(span, load, 0)
-    inter, mixed, length = (total(halve(rows[n])) for n in range(3))
-    low[0] = (resid[0] - inter / keep[0:1] * wave[0].astype(F32)).astype(BF16)
-    copies[1].start()
     apply_blocks(src, tgt, vec, left, right, acc, place_of(core, chip, chips))
 
     def store(j, carry):
@@ -179,12 +171,11 @@
         return cross, square
 
     zero = jnp.zeros((1, width), F32)
-    cross, square = each(chips, store, (zero, zero))
-    theirs[0, width : width + TAIL] = tail_of([cross, square])
-    for i, row in enumerate((inter, mixed, length, cross, square)):
+    rows = list(each(chips, store, (zero, zero))) + [keep[2 + i : 3 + i] for i in range(3)]
+    theirs[0, width : width + TAIL] = tail_of(rows)
+    for i, row in enumerate(rows):
         sums[i : i + 1] = row
-    for copy in copies:
-        copy.wait()
+    copy.wait()
 
 
 def chip_kernel(at, count, mine, got, sums, base, *sends):
@@ -208,68 +199,77 @@
 
 
 def near_kernel(count, base, *refs):
-    gots, (low, high) = refs[:-2], refs[-2:]
-    span, width = base.shape[0], base.shape[2]
-    half = span // 2
+    gots, out = refs[:-1], refs[-1]
+    width = base.shape[2]
     parts = [[base[0, width + i : width + i + 1] for i in range(count)]]
     parts += [rows_of(got[0, width : width + TAIL], count) for got in gots]
     rows = [halve(jnp.concatenate([part[i] for part in parts], axis=0)) for i in range(count)]
 
-    def add(i):
+    def store(i, carry):
         block = base[i, 0:width]
         for got in gots:
             block = block + got[i, 0:width].astype(F32)
-        return block
-
-    def store(i, carry):
-        low[i, 0:width] = add(i)
-        high[i, 0:width] = add(half + i).astype(high.dtype)
+        out[i, 0:width] = block
         for n, row in enumerate(rows):
-            low[i, width + n : width + n + 1] = row
-        if high.dtype == BF16:
-            high[i, width : width + TAIL] = tail_of(rows)
-        else:
-            for n, row in enumerate(rows):
-                high[i, width + n : width + n + 1] = row
+            out[i, width + n : width + n + 1] = row
         return carry
 
-    each(half, store, 0)
-
-
-def last_sums(low, got, count):
-    width = got.shape[2]
-    block = low[0, 0:width] + got[0, 0:width].astype(F32)
-    if got.dtype == BF16:
-        rows = rows_of(got[0, width : width + TAIL], count)
-    else:
-        rows = [got[0, width + i : width + i + 1] for i in range(count)]
-    return [block] + [low[0, width + i : width + i + 1] + rows[i] for i in range(count)]
-
-
-def residual_kernel(half, got, wave, inside, precond, sums, sigma, resid, send, keep):
-    width = got.shape[2]
-    block, ray = last_sums(half, got, 1)
-    first = block * inside[0]
+    each(base.shape[0], store, 0)
+
+
+def both_kernel(count, part, out):
+    width = part.shape[2]
+    block = part[1, 0:width]
+    high = block.astype(BF16)
+    out[0, 0:width] = high
+    out[0, width : 2 * width] = (block - high.astype(F32)).astype(BF16)
+    out[0, 2 * width : 3 * width] = part[0, 0:width].astype(BF16)
+    out[0, 3 * width : 3 * width + TAIL] = tail_of(
+        [part[0, width + i : width + i + 1] for i in range(count)]
+    )
+
+
+def far_kernel(count, part, out):
+    width = part.shape[2]
+    out[0, 0:width] = part[1, 0:width].astype(BF16)
+    out[0, width : width + TAIL] = tail_of(
+        [part[0, width + i : width + i + 1] for i in range(count)]
+    )
+
+
+def residual_kernel(part, got, wave, inside, precond, far, sums, sigma, resid, send, keep):
+    width = part.shape[2]
+    (ray,) = rows_of(got[0, 3 * width : 3 * width + TAIL], 1)
+    norm, ray = total(sums[0:1]), total(part[0, width : width + 1] + ray)
+    energy = ray / norm
+
+    def piece(i):
+        return got[0, i * width : (i + 1) * width].astype(F32)
+
     own = wave[0].astype(F32)
-    norm, ray = total(sums[0:1]), total(ray)
-    q = precond[0] * (first - ray / norm * own)
+    first = (part[0, 0:width] + (piece(0) + piece(1))) * inside[0]
+    q = precond[0] * (first - energy * own)
     low = q.astype(BF16)
     sigma[0] = first
     resid[0] = q
-    send[0, 0:width] = low
-    send[0, width : width + TAIL] = tail_of(
-        [fold(own * q), fold(low.astype(F32) * first), fold(q * q)]
-    )
-    keep[0:1] = norm
-    keep[1:2] = ray
-
-
-def final_kernel(half, got, inside, first, keep, sums, sigma, subspace):
-    block, cross, square = last_sums(half, got, 2)
+    send[0] = low
+    there = (part[1, 0:width] + piece(2)) * inside[1]
+    send[1] = (far[0] * (there - energy * wave[NEAR].astype(F32))).astype(BF16)
+    rows = (norm, ray, fold(own * q), fold(low.astype(F32) * first), fold(q * q))
+    for i, row in enumerate(rows):
+        keep[i : i + 1] = row
+
+
+def final_kernel(part, got, wave, inside, first, resid, keep, direction, sigma, subspace):
+    width = part.shape[2]
+    rows = rows_of(got[0, width : width + TAIL], 5)
+    cross, square, inter, mixed, length = (
+        total(part[0, width + i : width + i + 1] + rows[i]) for i in range(5)
+    )
     norm, ray = keep[0:1], keep[1:2]
-    inter, mixed, length = (sums[i : i + 1] for i in range(3))
-    cross, square = total(cross), total(square)
     c = inter / norm
+    direction[0] = (resid[0] - c * wave[0].astype(F32)).astype(BF16)
+    block = part[0, 0:width] + got[0, 0:width].astype(F32)
     sigma[0] = block * inside[0] - c * first[0]
     values = (
         ray,
@@ -314,7 +314,7 @@
 
 
 def gather(block):
-    step = NEAR
+    step = NEAR * block.shape[0]
     while step < lax.axis_size("chip"):
         block = jnp.concatenate([block, flip_chip(block, step)], axis=0)
         step *= 2
@@ -322,7 +322,7 @@
     return pieces + [swap(piece) for piece in pieces]
 
 
-def scatter(theirs, mine, sums, at, count, narrow):
+def scatter(theirs, mine, sums, at, count):
     chips, width = mine.shape[0], mine.shape[2]
     span, high, wide = chips // NEAR, width + TAIL, width + 8
     sent = [shape(span, high, width, dtype=BF16)] * (NEAR - 1)
@@ -331,18 +331,14 @@
         [shape(span, wide, width)] + sent, [], (mine, swap(theirs), sums), mine.size,
     )
     gots = [flip_chip(send, k) for k, send in enumerate(sends, 1)]
-    half = span // 2
-    last = shape(half, high, width, dtype=BF16) if narrow and half == 1 else shape(half, wide, width)
-    low, far = call(
+    (part,) = call(
         lambda *refs: near_kernel(count, *refs), "near_sum", [VMEM] * NEAR,
-        [shape(half, wide, width), last], [], (base, *gots), mine.size,
-    )
-    got = flip_chip(far, NEAR * half)
-    while half > 1:
-        half //= 2
-        low = low + got
-        low, got = low[:half], flip_chip(low[half:], NEAR * half)
-    return low, got
+        [shape(span, wide, width)], [], (base, *gots), mine.size,
+    )
+    while span > 2:
+        span //= 2
+        part = part[:span] + flip_chip(part[span:], NEAR * span)
+    return part
 
 
 def shards(state, sector_sizes, left, right, source, target, precond):
@@ -354,46 +350,58 @@
     near = [VMEM] * (2 * NEAR)
     block = shape(1, width, width)
     sums_of = shape(8, width)
+    after_h = [shape(chips, high, width, dtype=BF16), shape(chips, width, width)]
 
     with jax.named_scope("own_mask"):
-        (inside,) = call(mask_kernel, "own_mask", [SMEM], [block], [], (sector_sizes,), LONG)
+        (inside,) = call(
+            mask_kernel, "own_mask", [SMEM], [shape(2, width, width)], [], (sector_sizes,), LONG
+        )
     with jax.named_scope("gather_state"):
         pieces = gather(state)
+        far = flip_chip(precond, NEAR)
     with jax.named_scope("first_sigma"):
         theirs, mine, wave, flip, sums = call(
-            first_kernel, "first_sigma", [SMEM] * 3 + near + [VMEM] * 3,
-            [shape(chips, high, width, dtype=BF16), shape(chips, width, width),
-             shape(every, width, width, dtype=BF16), shape(*right.shape, dtype=BF16), sums_of],
+            first_kernel, "first_sigma", [SMEM] * 3 + near + [VMEM] * 4,
+            after_h + [shape(every, width, width, dtype=BF16), shape(*right.shape, dtype=BF16), sums_of],
             [pltpu.VMEM((every, width, width), F32), pltpu.VMEM((every, width), F32)],
-            (source, target, sector_sizes, *pieces, left, right, inside), flops,
+            (source, target, sector_sizes, *pieces, left, right, inside, far), flops,
         )
     with jax.named_scope("sum_first"):
-        low, got = scatter(theirs, mine, sums, 1, 1, False)
+        part = scatter(theirs, mine, sums, 1, 1)
+        (both,) = call(
+            lambda *refs: both_kernel(1, *refs), "for_far", [VMEM],
+            [shape(1, 3 * width + TAIL, width, dtype=BF16)], [], (part,), part.size,
+        )
+        got = flip_chip(both, NEAR)
     with jax.named_scope("residual"):
         first, resid, send, keep = call(
-            residual_kernel, "residual", [VMEM] * 6,
-            [block, block, shape(1, high, width, dtype=BF16), sums_of],
-            [], (low, got, wave, inside, precond, sums), mine.size,
+            residual_kernel, "residual", [VMEM] * 7,
+            [block, block, shape(2, width, width, dtype=BF16), sums_of],
+            [], (part, got, wave, inside, precond, far, sums), mine.size,
         )
     with jax.named_scope("gather_residual"):
         pieces = gather(send)
     with jax.named_scope("second_sigma"):
-        theirs, mine, sums, sigma, direction = call(
-            second_kernel, "second_sigma", [SMEM] * 2 + near + [VMEM] * 6,
-            [shape(chips, high, width, dtype=BF16), shape(chips, width, width), sums_of,
-             block, shape(1, width, width, dtype=BF16)],
+        theirs, mine, sums, sigma = call(
+            second_kernel, "second_sigma", [SMEM] * 2 + near + [VMEM] * 5,
+            after_h + [sums_of, block],
             [pltpu.VMEM((every, width, width), BF16), pltpu.VMEM((every, width, width), F32),
-             pltpu.VMEM((3, every, width), F32), pltpu.VMEM((1, width, width), BF16),
-             pltpu.SemaphoreType.DMA((2,))],
-            (source, target, *pieces, wave, left, flip, resid, first, keep), flops,
-            [VMEM] * 3 + [HBM] * 2,
+             pltpu.SemaphoreType.DMA],
+            (source, target, *pieces, wave, left, flip, first, keep), flops,
+            [VMEM] * 3 + [HBM],
         )
     with jax.named_scope("sum_second"):
-        low, got = scatter(theirs, mine, sums, 3, 2, True)
+        part = scatter(theirs, mine, sums, 0, 5)
+        (both,) = call(
+            lambda *refs: far_kernel(5, *refs), "for_far", [VMEM],
+            [shape(1, high, width, dtype=BF16)], [], (part,), part.size,
+        )
+        got = flip_chip(both, NEAR)
     with jax.named_scope("outputs"):
-        second, subspace = call(
-            final_kernel, "outputs", [VMEM] * 6, [block, shape(4)],
-            [], (low, got, inside, first, keep, sums), mine.size, [VMEM, SMEM],
+        direction, second, subspace = call(
+            final_kernel, "outputs", [VMEM] * 7,
+            [shape(1, width, width, dtype=BF16), block, shape(4)],
+            [], (part, got, wave, inside, first, resid, keep), mine.size, [VMEM, VMEM, SMEM],
         )
     return sigma, direction, second, subspace
 

time: 68.9 us -> 65 us (0.943)
  waiting for transfers between devices: 28.6 us -> 23.1 us
  starting transfers between devices: 27.2 us -> 28.9 us
    ppermute x16, waiting for transfers between devices: 24.7 us -> 19.2 us  [flip_chip(): return lax.ppermute(x, 'chip', [(i, i ^ bits) for i in range(chips)])]
    ppermute x10, starting transfers between devices: 0.82 us -> 1.66 us  [swap(): return lax.ppermute(x, 'core', [(0, 1), (1, 0)])]
    ppermute x16, starting transfers between devices: 26.4 us -> 27.2 us  [flip_chip(): return lax.ppermute(x, 'chip', [(i, i ^ bits) for i in range(chips)])]
    pallas_call x9 -> x11, Pallas kernels: 10.6 us -> 10.5 us  [call(): pl.pallas_call(kernel, name=name, in_specs=ins, out_specs=out_specs or [V...]
    unnamed x18 -> x17, local copies, waits for them, and re-layouts: 1.5 us -> 1.49 us
  transfers between devices with their start and end apart: 26 -> 26, of which waited for: 19 -> 18; matrix products, arithmetic and copies ran while one was open for 1% -> 1% of each run, Pallas kernels for 1% -> 1%
where the time goes in v5:
time: 65 us; the launch traced here: 64.8 us
  starting transfers between devices  28.9 us (44%)
  waiting for transfers between devices  23.1 us (36%)
  Pallas kernels  10.5 us (16%)
  local copies, waits for them, and re-layouts  1.5 us (2%)
  between operations  0.82 us (1%)
    ppermute x16, starting transfers between devices, flip_chip(): return lax.ppermute(x, 'chip', [(i, i ^ bits) for i in range(chips)])  27.2 us
    ppermute x16, waiting for transfers between devices, flip_chip(): return lax.ppermute(x, 'chip', [(i, i ^ bits) for i in range(chips)])  19.2 us
    pallas_call x11, Pallas kernels, call(): pl.pallas_call(kernel, name=name, in_specs=ins, out_specs=out_specs or [V...  10.5 us
    ppermute x10, waiting for transfers between devices, swap(): return lax.ppermute(x, 'core', [(0, 1), (1, 0)])  3.92 us
    ppermute x10, starting transfers between devices, swap(): return lax.ppermute(x, 'core', [(0, 1), (1, 0)])  1.66 us
    unnamed x17, local copies, waits for them, and re-layouts  1.49 us
  transfers between devices with their start and end apart: 26, of which 18 were waited for; matrix products, arithmetic and copies ran while one was open for 1% of the time, Pallas kernels for 1%

profile of v5, /device:TPU:0, one launch (start us, length us, event | category | flops | bytes accessed | tf_op | source)
XLA Modules:
  0.0 64.8 jit_solution(15432055206229050123)
XLA Ops:
  0.6 4.1 %collective-permute-start = (bf16[1,128,128]{2,1,0:T(8,128)(2,1)}, bf16[1,128,128]{2,1,0:T(8,128)(2,1)S(1)}, u32[]{:S(2)}, u32[]{:S(2)}) collective-permute-start(bf16[1,128,128]{2,1,0:T(8,128)(2,1)} %param.7), channel_id=1, source_target_pairs={{0,8},{2,10},{4,12},{6,14},{8,0},{10,2},{12,4},{14,6},{1,9},{3,11}... | collective-permute-start | bytes 98312 | tf_op jit(solution)/shard_map/gather_state/ppermute | solution.py:313
  4.7 0.8 %constant_dynamic-update-slice_fusion.1 = bf16[2,128,128]{2,1,0:T(8,128)(2,1)S(1)} fusion(bf16[1,128,128]{2,1,0:T(8,128)(2,1)} %param.7), kind=kLoop, calls=%fused_computation.1 | loop fusion | bytes 65536
  5.5 1.7 %collective-permute-done = bf16[1,128,128]{2,1,0:T(8,128)(2,1)S(1)} collective-permute-done((bf16[1,128,128]{2,1,0:T(8,128)(2,1)}, bf16[1,128,128]{2,1,0:T(8,128)(2,1)S(1)}, u32[]{:S(2)}, u32[]{:S(2)}) %collective-permute-start) | collective-permute-done | bytes 32800 | tf_op jit(solution)/shard_map/gather_state/ppermute | solution.py:313
  7.2 0.0 slice-start.1
  7.2 0.0 slice-start.3
  7.2 0.0 copy-start.1
  7.2 0.0 copy-start.2
  7.3 2.5 %collective-permute-start.3 = (bf16[2,128,128]{2,1,0:T(8,128)(2,1)S(1)}, bf16[2,128,128]{2,1,0:T(8,128)(2,1)S(1)}, u32[]{:S(2)}, u32[]{:S(2)}) collective-permute-start(bf16[2,128,128]{2,1,0:T(8,128)(2,1)S(1)} %constant_dynamic-update-slice_fusion.refs_0_), channel_id=1, source_target_pairs={{0,6},{2,4},{4,2},{6,0},{8,14},{10,12},{12,10},{14,8},{1,7},{3,5},... | collective-permute-start | bytes 196616 | tf_op jit(solution)/shard_map/gather_state/ppermute | solution.py:313
  9.8 0.7 %collective-permute-start.2 = (bf16[2,128,128]{2,1,0:T(8,128)(2,1)S(1)}, bf16[2,128,128]{2,1,0:T(8,128)(2,1)S(1)}, u32[]{:S(2)}, u32[]{:S(2)}) collective-permute-start(bf16[2,128,128]{2,1,0:T(8,128)(2,1)S(1)} %constant_dynamic-update-slice_fusion.refs_0_), channel_id=1, source_target_pairs={{0,4},{2,6},{4,0},{6,2},{8,12},{10,14},{12,8},{14,10},{1,5},{3,7},... | collective-permute-start | bytes 196616 | tf_op jit(solution)/shard_map/gather_state/ppermute | solution.py:313
  10.5 0.3 collective-permute-start.1
  10.8 2.6 %collective-permute-start.8 = (f32[1,128,128]{2,1,0:T(8,128)}, f32[1,128,128]{2,1,0:T(8,128)S(1)}, u32[]{:S(2)}, u32[]{:S(2)}) collective-permute-start(f32[1,128,128]{2,1,0:T(8,128)} %precond.1), channel_id=1, source_target_pairs={{0,8},{2,10},{4,12},{6,14},{8,0},{10,2},{12,4},{14,6},{1,9},{3,11}... | collective-permute-start | bytes 196616 | tf_op jit(solution)/shard_map/gather_state/ppermute | solution.py:313
  13.4 0.0 collective-permute-start.4
  13.4 0.0 collective-permute-done.3.refs_3_
  13.4 0.5 collective-permute-start.7
  13.9 0.2 collective-permute-done.2.refs_2_
  14.1 0.0 collective-permute-start.6
  14.1 0.6 collective-permute-done.1.refs_1_
  14.7 0.0 collective-permute-start.5
  14.8 0.7 %copy-done.3 = s32[16]{0:T(128)S(1)} copy-done((s32[16]{0:T(128)S(1)}, s32[16]{0:T(128)}, u32[]{:S(2)}) %copy-start.3) | copy-done | bytes 88
  15.4 0.6 own_mask.1.refs_10_.inside
  16.0 0.0 copy-start
  16.0 0.2 collective-permute-done.8.refs_11_.far
  16.2 0.0 collective-permute-done.4.refs_4_
  16.2 0.0 collective-permute-done.6.refs_6_
  16.2 0.0 collective-permute-done.5.refs_5_
  16.3 4.5 %first_sigma.1 = (bf16[8,144,128]{2,1,0:T(8,128)(2,1)S(1)}, f32[8,128,128]{2,1,0:T(8,128)S(1)}, bf16[16,128,128]{2,1,0:T(8,128)(2,1)S(1)}, bf16[12,12,128,128]{3,2,1,0:T(8,128)(2,1)S(1)}, f32[8,128]{1,0:T(8,128)S(1)}) custom-call(s32[12,12]{1,0:T(8,128)S(1)} %copy-done.1, s32[12,12]{1,0:T(8,128)S(1)} %copy-done.2, s32[16]{0:T(128)S(1)} %copy-done.3, ...), custom_call_target="tpu_custom_call" | custom-call | flops 1207959552 | bytes 10159296 | tf_op jit(solution)/shard_map/first_sigma/first_sigma/pallas_call | solution.py:291
  20.8 0.4 collective-permute-start.9
  21.2 1.2 %collective-permute-done.9.refs_1_ = bf16[8,144,128]{2,1,0:T(8,128)(2,1)S(1)} collective-permute-done((bf16[8,144,128]{2,1,0:T(8,128)(2,1)S(1)}, bf16[8,144,128]{2,1,0:T(8,128)(2,1)S(1)}, u32[]{:S(2)}, u32[]{:S(2)}) %collective-permute-start.9) | collective-permute-done | bytes 294944 | tf_op jit(solution)/shard_map/sum_first/ppermute | solution.py:308
  22.4 0.1 chip_sum.2
  22.5 1.8 %collective-permute-start.10 = (bf16[2,144,128]{2,1,0:T(8,128)(2,1)S(1)}, bf16[2,144,128]{2,1,0:T(8,128)(2,1)S(1)}, u32[]{:S(2)}, u32[]{:S(2)}) collective-permute-start(bf16[2,144,128]{2,1,0:T(8,128)(2,1)S(1)} %get-tuple-element.32), channel_id=1, source_target_pairs={{0,2},{2,0},{4,6},{6,4},{8,10},{10,8},{12,14},{14,12},{1,3},{3,1},... | collective-permute-start | bytes 221192 | tf_op jit(solution)/shard_map/sum_first/ppermute | solution.py:313
  24.3 1.3 %collective-permute-start.11 = (bf16[2,144,128]{2,1,0:T(8,128)(2,1)S(1)}, bf16[2,144,128]{2,1,0:T(8,128)(2,1)S(1)}, u32[]{:S(2)}, u32[]{:S(2)}) collective-permute-start(bf16[2,144,128]{2,1,0:T(8,128)(2,1)S(1)} %get-tuple-element.33), channel_id=1, source_target_pairs={{0,4},{2,6},{4,0},{6,2},{8,12},{10,14},{12,8},{14,10},{1,5},{3,7},... | collective-permute-start | bytes 221192 | tf_op jit(solution)/shard_map/sum_first/ppermute | solution.py:313
  25.6 0.4 collective-permute-start.12
  26.1 1.0 %collective-permute-done.10.refs_1_ = bf16[2,144,128]{2,1,0:T(8,128)(2,1)S(1)} collective-permute-done((bf16[2,144,128]{2,1,0:T(8,128)(2,1)S(1)}, bf16[2,144,128]{2,1,0:T(8,128)(2,1)S(1)}, u32[]{:S(2)}, u32[]{:S(2)}) %collective-permute-start.10) | collective-permute-done | bytes 73760 | tf_op jit(solution)/shard_map/sum_first/ppermute | solution.py:313
  27.1 2.3 %collective-permute-done.11.refs_2_ = bf16[2,144,128]{2,1,0:T(8,128)(2,1)S(1)} collective-permute-done((bf16[2,144,128]{2,1,0:T(8,128)(2,1)S(1)}, bf16[2,144,128]{2,1,0:T(8,128)(2,1)S(1)}, u32[]{:S(2)}, u32[]{:S(2)}) %collective-permute-start.11) | collective-permute-done | bytes 73760 | tf_op jit(solution)/shard_map/sum_first/ppermute | solution.py:313
  29.3 1.5 %collective-permute-done.12.refs_3_ = bf16[2,144,128]{2,1,0:T(8,128)(2,1)S(1)} collective-permute-done((bf16[2,144,128]{2,1,0:T(8,128)(2,1)S(1)}, bf16[2,144,128]{2,1,0:T(8,128)(2,1)S(1)}, u32[]{:S(2)}, u32[]{:S(2)}) %collective-permute-start.12) | collective-permute-done | bytes 73760 | tf_op jit(solution)/shard_map/sum_first/ppermute | solution.py:313
  30.9 3.3 %collective-permute-start.13 = (bf16[1,400,128]{2,1,0:T(8,128)(2,1)S(1)}, bf16[1,400,128]{2,1,0:T(8,128)(2,1)S(1)}, u32[]{:S(2)}, u32[]{:S(2)}) collective-permute-start(bf16[1,400,128]{2,1,0:T(8,128)(2,1)S(1)} %for_far.2), channel_id=1, source_target_pairs={{0,8},{2,10},{4,12},{6,14},{8,0},{10,2},{12,4},{14,6},{1,9},{3,11}... | collective-permute-start | bytes 307208 | tf_op jit(solution)/shard_map/sum_first/ppermute | solution.py:313
  34.2 3.7 %collective-permute-done.13.got = bf16[1,400,128]{2,1,0:T(8,128)(2,1)S(1)} collective-permute-done((bf16[1,400,128]{2,1,0:T(8,128)(2,1)S(1)}, bf16[1,400,128]{2,1,0:T(8,128)(2,1)S(1)}, u32[]{:S(2)}, u32[]{:S(2)}) %collective-permute-start.13) | collective-permute-done | bytes 102432 | tf_op jit(solution)/shard_map/sum_first/ppermute | solution.py:313
  37.9 0.1 residual.1
  38.0 0.9 %collective-permute-start.16 = (bf16[2,128,128]{2,1,0:T(8,128)(2,1)S(1)}, bf16[2,128,128]{2,1,0:T(8,128)(2,1)S(1)}, u32[]{:S(2)}, u32[]{:S(2)}) collective-permute-start(bf16[2,128,128]{2,1,0:T(8,128)(2,1)S(1)} %get-tuple-element.36.refs_0_), channel_id=1, source_target_pairs={{0,6},{2,4},{4,2},{6,0},{8,14},{10,12},{12,10},{14,8},{1,7},{3,5},... | collective-permute-start | bytes 196616 | tf_op jit(solution)/shard_map/gather_residual/ppermute | solution.py:313
  38.9 1.3 %collective-permute-start.15 = (bf16[2,128,128]{2,1,0:T(8,128)(2,1)S(1)}, bf16[2,128,128]{2,1,0:T(8,128)(2,1)S(1)}, u32[]{:S(2)}, u32[]{:S(2)}) collective-permute-start(bf16[2,128,128]{2,1,0:T(8,128)(2,1)S(1)} %get-tuple-element.36.refs_0_), channel_id=1, source_target_pairs={{0,4},{2,6},{4,0},{6,2},{8,12},{10,14},{12,8},{14,10},{1,5},{3,7},... | collective-permute-start | bytes 196616 | tf_op jit(solution)/shard_map/gather_residual/ppermute | solution.py:313
  40.3 1.3 %collective-permute-start.14 = (bf16[2,128,128]{2,1,0:T(8,128)(2,1)S(1)}, bf16[2,128,128]{2,1,0:T(8,128)(2,1)S(1)}, u32[]{:S(2)}, u32[]{:S(2)}) collective-permute-start(bf16[2,128,128]{2,1,0:T(8,128)(2,1)S(1)} %get-tuple-element.36.refs_0_), channel_id=1, source_target_pairs={{0,2},{2,0},{4,6},{6,4},{8,10},{10,8},{12,14},{14,12},{1,3},{3,1},... | collective-permute-start | bytes 196616 | tf_op jit(solution)/shard_map/gather_residual/ppermute | solution.py:313
  41.6 0.0 collective-permute-start.17
  41.6 1.7 %collective-permute-done.16.refs_3_ = bf16[2,128,128]{2,1,0:T(8,128)(2,1)S(1)} collective-permute-done((bf16[2,128,128]{2,1,0:T(8,128)(2,1)S(1)}, bf16[2,128,128]{2,1,0:T(8,128)(2,1)S(1)}, u32[]{:S(2)}, u32[]{:S(2)}) %collective-permute-start.16) | collective-permute-done | bytes 65568 | tf_op jit(solution)/shard_map/gather_residual/ppermute | solution.py:313
  43.2 0.0 collective-permute-start.20
  43.2 0.0 collective-permute-done.15.refs_2_
  43.2 0.5 collective-permute-start.19
  43.7 0.8 %collective-permute-done.14.refs_1_ = bf16[2,128,128]{2,1,0:T(8,128)(2,1)S(1)} collective-permute-done((bf16[2,128,128]{2,1,0:T(8,128)(2,1)S(1)}, bf16[2,128,128]{2,1,0:T(8,128)(2,1)S(1)}, u32[]{:S(2)}, u32[]{:S(2)}) %collective-permute-start.14) | collective-permute-done | bytes 65568 | tf_op jit(solution)/shard_map/gather_residual/ppermute | solution.py:313
  44.5 0.0 collective-permute-start.18
  44.5 0.0 collective-permute-done.17.refs_4_
  44.5 0.1 collective-permute-done.19.refs_6_
  44.7 1.1 %collective-permute-done.18.refs_5_ = bf16[2,128,128]{2,1,0:T(8,128)(2,1)S(1)} collective-permute-done((bf16[2,128,128]{2,1,0:T(8,128)(2,1)S(1)}, bf16[2,128,128]{2,1,0:T(8,128)(2,1)S(1)}, u32[]{:S(2)}, u32[]{:S(2)}) %collective-permute-start.18) | collective-permute-done | bytes 65568 | tf_op jit(solution)/shard_map/gather_residual/ppermute | solution.py:308
  45.8 4.3 %second_sigma.1 = (bf16[8,144,128]{2,1,0:T(8,128)(2,1)S(1)}, f32[8,128,128]{2,1,0:T(8,128)S(1)}, f32[8,128]{1,0:T(8,128)S(1)}, f32[1,128,128]{2,1,0:T(8,128)}) custom-call(s32[12,12]{1,0:T(8,128)S(1)} %copy-done.1, s32[12,12]{1,0:T(8,128)S(1)} %copy-done.2, bf16[2,128,128]{2,1,0:T(8,128)(2,1)S(1)} %get-tuple-element.36.refs_0_, ...), custom_call_target="tpu_custom_call" | custom-call | flops 1207959552 | bytes 10556544 | tf_op jit(solution)/shard_map/second_sigma/second_sigma/pallas_call | solution.py:291
  50.1 0.2 collective-permute-start.21
  50.4 1.4 %collective-permute-done.21.refs_1_ = bf16[8,144,128]{2,1,0:T(8,128)(2,1)S(1)} collective-permute-done((bf16[8,144,128]{2,1,0:T(8,128)(2,1)S(1)}, bf16[8,144,128]{2,1,0:T(8,128)(2,1)S(1)}, u32[]{:S(2)}, u32[]{:S(2)}) %collective-permute-start.21) | collective-permute-done | bytes 294944 | tf_op jit(solution)/shard_map/sum_second/ppermute | solution.py:308
  51.8 0.1 chip_sum.3
  51.9 1.4 %collective-permute-start.22 = (bf16[2,144,128]{2,1,0:T(8,128)(2,1)S(1)}, bf16[2,144,128]{2,1,0:T(8,128)(2,1)S(1)}, u32[]{:S(2)}, u32[]{:S(2)}) collective-permute-start(bf16[2,144,128]{2,1,0:T(8,128)(2,1)S(1)} %get-tuple-element.45), channel_id=1, source_target_pairs={{0,2},{2,0},{4,6},{6,4},{8,10},{10,8},{12,14},{14,12},{1,3},{3,1},... | collective-permute-start | bytes 221192 | tf_op jit(solution)/shard_map/sum_second/ppermute | solution.py:313
  53.2 0.2 collective-permute-start.23
  53.4 2.0 %collective-permute-start.24 = (bf16[2,144,128]{2,1,0:T(8,128)(2,1)S(1)}, bf16[2,144,128]{2,1,0:T(8,128)(2,1)S(1)}, u32[]{:S(2)}, u32[]{:S(2)}) collective-permute-start(bf16[2,144,128]{2,1,0:T(8,128)(2,1)S(1)} %get-tuple-element.47), channel_id=1, source_target_pairs={{0,6},{2,4},{4,2},{6,0},{8,14},{10,12},{12,10},{14,8},{1,7},{3,5},... | collective-permute-start | bytes 221192 | tf_op jit(solution)/shard_map/sum_second/ppermute | solution.py:313
  55.4 0.9 %collective-permute-done.22.refs_1_ = bf16[2,144,128]{2,1,0:T(8,128)(2,1)S(1)} collective-permute-done((bf16[2,144,128]{2,1,0:T(8,128)(2,1)S(1)}, bf16[2,144,128]{2,1,0:T(8,128)(2,1)S(1)}, u32[]{:S(2)}, u32[]{:S(2)}) %collective-permute-start.22) | collective-permute-done | bytes 73760 | tf_op jit(solution)/shard_map/sum_second/ppermute | solution.py:313
  56.3 1.8 %collective-permute-done.23.refs_2_ = bf16[2,144,128]{2,1,0:T(8,128)(2,1)S(1)} collective-permute-done((bf16[2,144,128]{2,1,0:T(8,128)(2,1)S(1)}, bf16[2,144,128]{2,1,0:T(8,128)(2,1)S(1)}, u32[]{:S(2)}, u32[]{:S(2)}) %collective-permute-start.23) | collective-permute-done | bytes 73760 | tf_op jit(solution)/shard_map/sum_second/ppermute | solution.py:313
  58.1 1.0 %collective-permute-done.24.refs_3_ = bf16[2,144,128]{2,1,0:T(8,128)(2,1)S(1)} collective-permute-done((bf16[2,144,128]{2,1,0:T(8,128)(2,1)S(1)}, bf16[2,144,128]{2,1,0:T(8,128)(2,1)S(1)}, u32[]{:S(2)}, u32[]{:S(2)}) %collective-permute-start.24) | collective-permute-done | bytes 73760 | tf_op jit(solution)/shard_map/sum_second/ppermute | solution.py:313
  59.1 3.0 %collective-permute-start.25 = (bf16[1,144,128]{2,1,0:T(8,128)(2,1)S(1)}, bf16[1,144,128]{2,1,0:T(8,128)(2,1)S(1)}, u32[]{:S(2)}, u32[]{:S(2)}) collective-permute-start(bf16[1,144,128]{2,1,0:T(8,128)(2,1)S(1)} %for_far.3), channel_id=1, source_target_pairs={{0,8},{2,10},{4,12},{6,14},{8,0},{10,2},{12,4},{14,6},{1,9},{3,11}... | collective-permute-start | bytes 110600 | tf_op jit(solution)/shard_map/sum_second/ppermute | solution.py:313
  62.1 1.9 %collective-permute-done.25.got = bf16[1,144,128]{2,1,0:T(8,128)(2,1)S(1)} collective-permute-done((bf16[1,144,128]{2,1,0:T(8,128)(2,1)S(1)}, bf16[1,144,128]{2,1,0:T(8,128)(2,1)S(1)}, u32[]{:S(2)}, u32[]{:S(2)}) %collective-permute-start.25) | collective-permute-done | bytes 36896 | tf_op jit(solution)/shard_map/sum_second/ppermute | solution.py:313
  64.1 0.7 %outputs.1 = (bf16[1,128,128]{2,1,0:T(8,128)(2,1)}, f32[1,128,128]{2,1,0:T(8,128)}, f32[4]{0:T(128)}) custom-call(f32[2,136,128]{2,1,0:T(8,128)S(1)} %near_sum.3.refs_0_.part, bf16[1,144,128]{2,1,0:T(8,128)(2,1)S(1)} %collective-permute-done.25.got, bf16[16,128,128]{2,1,0:T(8,128)(2,1)S(1)} %get-tuple-element.35.wave.refs_8_, ...), custom_call_target="tpu_custom_call" | custom-call | flops 131072 | bytes 966656 | tf_op jit(solution)/shard_map/outputs/outputs/pallas_call | solution.py:291
  (19 shorter events, 0.2 us)
Async XLA Ops:
  0.6 6.6 %collective-permute-start = (bf16[1,128,128]{2,1,0:T(8,128)(2,1)}, bf16[1,128,128]{2,1,0:T(8,128)(2,1)S(1)}, u32[]{:S(2)}, u32[]{:S(2)}) collective-permute-start(bf16[1,128,128]{2,1,0:T(8,128)(2,1)} %param.7), channel_id=1, source_target_pairs={{0,8},{2,10},{4,12},{6,14},{8,0},{10,2},{12,4},{14,6},{1,9},{3,11}... | collective-permute-start | bytes 98312 | tf_op jit(solution)/shard_map/gather_state/ppermute | solution.py:313
  7.2 9.0 %slice-start = ((s8[4718592]{0:T(1024)(128)(4,1)}), s8[4194304]{0:T(1024)(128)(4,1)S(1)}, s32[]{:S(2)}) async-start(s8[4718592]{0:T(1024)(128)(4,1)} %bitcast), calls=%async_computation | async-start | bytes 8388608
  7.2 9.0 %slice-start.2 = ((s8[4718592]{0:T(1024)(128)(4,1)}), s8[4194304]{0:T(1024)(128)(4,1)S(1)}, s32[]{:S(2)}) async-start(s8[4718592]{0:T(1024)(128)(4,1)} %bitcast.2), calls=%async_computation.2 | async-start | bytes 8388608
  7.2 9.0 %slice-start.1 = ((s8[4718592]{0:T(1024)(128)(4,1)}), s8[524288]{0:T(1024)(128)(4,1)S(1)}, s32[]{:S(2)}) async-start(s8[4718592]{0:T(1024)(128)(4,1)} %bitcast), calls=%async_computation.1 | async-start | bytes 1048576
  7.2 9.0 %slice-start.3 = ((s8[4718592]{0:T(1024)(128)(4,1)}), s8[524288]{0:T(1024)(128)(4,1)S(1)}, s32[]{:S(2)}) async-start(s8[4718592]{0:T(1024)(128)(4,1)} %bitcast.2), calls=%async_computation.3 | async-start | bytes 1048576
  7.2 9.0 %copy-start.1 = (s32[12,12]{1,0:T(8,128)S(1)}, s32[12,12]{1,0:T(8,128)}, u32[]{:S(2)}) copy-start(s32[12,12]{1,0:T(8,128)} %src.3) | copy-start | bytes 1732
  7.2 9.0 %copy-start.2 = (s32[12,12]{1,0:T(8,128)S(1)}, s32[12,12]{1,0:T(8,128)}, u32[]{:S(2)}) copy-start(s32[12,12]{1,0:T(8,128)} %tgt.3) | copy-start | bytes 1732
  7.3 6.2 %collective-permute-start.3 = (bf16[2,128,128]{2,1,0:T(8,128)(2,1)S(1)}, bf16[2,128,128]{2,1,0:T(8,128)(2,1)S(1)}, u32[]{:S(2)}, u32[]{:S(2)}) collective-permute-start(bf16[2,128,128]{2,1,0:T(8,128)(2,1)S(1)} %constant_dynamic-update-slice_fusion.refs_0_), channel_id=1, source_target_pairs={{0,6},{2,4},{4,2},{6,0},{8,14},{10,12},{12,10},{14,8},{1,7},{3,5},... | collective-permute-start | bytes 196616 | tf_op jit(solution)/shard_map/gather_state/ppermute | solution.py:313
  9.8 4.3 %collective-permute-start.2 = (bf16[2,128,128]{2,1,0:T(8,128)(2,1)S(1)}, bf16[2,128,128]{2,1,0:T(8,128)(2,1)S(1)}, u32[]{:S(2)}, u32[]{:S(2)}) collective-permute-start(bf16[2,128,128]{2,1,0:T(8,128)(2,1)S(1)} %constant_dynamic-update-slice_fusion.refs_0_), channel_id=1, source_target_pairs={{0,4},{2,6},{4,0},{6,2},{8,12},{10,14},{12,8},{14,10},{1,5},{3,7},... | collective-permute-start | bytes 196616 | tf_op jit(solution)/shard_map/gather_state/ppermute | solution.py:313
  10.5 4.3 %collective-permute-start.1 = (bf16[2,128,128]{2,1,0:T(8,128)(2,1)S(1)}, bf16[2,128,128]{2,1,0:T(8,128)(2,1)S(1)}, u32[]{:S(2)}, u32[]{:S(2)}) collective-permute-start(bf16[2,128,128]{2,1,0:T(8,128)(2,1)S(1)} %constant_dynamic-update-slice_fusion.refs_0_), channel_id=1, source_target_pairs={{0,2},{2,0},{4,6},{6,4},{8,10},{10,8},{12,14},{14,12},{1,3},{3,1},... | collective-permute-start | bytes 196616 | tf_op jit(solution)/shard_map/gather_state/ppermute | solution.py:313
  10.8 5.4 %collective-permute-start.8 = (f32[1,128,128]{2,1,0:T(8,128)}, f32[1,128,128]{2,1,0:T(8,128)S(1)}, u32[]{:S(2)}, u32[]{:S(2)}) collective-permute-start(f32[1,128,128]{2,1,0:T(8,128)} %precond.1), channel_id=1, source_target_pairs={{0,8},{2,10},{4,12},{6,14},{8,0},{10,2},{12,4},{14,6},{1,9},{3,11}... | collective-permute-start | bytes 196616 | tf_op jit(solution)/shard_map/gather_state/ppermute | solution.py:313
  13.4 2.8 %collective-permute-start.4 = (bf16[2,128,128]{2,1,0:T(8,128)(2,1)S(1)}, bf16[2,128,128]{2,1,0:T(8,128)(2,1)S(1)}, u32[]{:S(2)}, u32[]{:S(2)}) collective-permute-start(bf16[2,128,128]{2,1,0:T(8,128)(2,1)S(1)} %constant_dynamic-update-slice_fusion.refs_0_), channel_id=1, source_target_pairs={{0,1},{1,0},{2,3},{3,2},{4,5},{5,4},{6,7},{7,6},{8,9},{9,8},{10,11... | collective-permute-start | bytes 196616 | tf_op jit(solution)/shard_map/gather_state/ppermute | solution.py:308
  13.4 2.8 %collective-permute-start.7 = (bf16[2,128,128]{2,1,0:T(8,128)(2,1)S(1)}, bf16[2,128,128]{2,1,0:T(8,128)(2,1)S(1)}, u32[]{:S(2)}, u32[]{:S(2)}) collective-permute-start(bf16[2,128,128]{2,1,0:T(8,128)(2,1)S(1)} %collective-permute-done.3.refs_3_), channel_id=1, source_target_pairs={{0,1},{1,0},{2,3},{3,2},{4,5},{5,4},{6,7},{7,6},{8,9},{9,8},{10,11... | collective-permute-start | bytes 196616 | tf_op jit(solution)/shard_map/gather_state/ppermute | solution.py:308
  14.1 2.1 %collective-permute-start.6 = (bf16[2,128,128]{2,1,0:T(8,128)(2,1)S(1)}, bf16[2,128,128]{2,1,0:T(8,128)(2,1)S(1)}, u32[]{:S(2)}, u32[]{:S(2)}) collective-permute-start(bf16[2,128,128]{2,1,0:T(8,128)(2,1)S(1)} %collective-permute-done.2.refs_2_), channel_id=1, source_target_pairs={{0,1},{1,0},{2,3},{3,2},{4,5},{5,4},{6,7},{7,6},{8,9},{9,8},{10,11... | collective-permute-start | bytes 196616 | tf_op jit(solution)/shard_map/gather_state/ppermute | solution.py:308
  14.7 1.5 %collective-permute-start.5 = (bf16[2,128,128]{2,1,0:T(8,128)(2,1)S(1)}, bf16[2,128,128]{2,1,0:T(8,128)(2,1)S(1)}, u32[]{:S(2)}, u32[]{:S(2)}) collective-permute-start(bf16[2,128,128]{2,1,0:T(8,128)(2,1)S(1)} %collective-permute-done.1.refs_1_), channel_id=1, source_target_pairs={{0,1},{1,0},{2,3},{3,2},{4,5},{5,4},{6,7},{7,6},{8,9},{9,8},{10,11... | collective-permute-start | bytes 196616 | tf_op jit(solution)/shard_map/gather_state/ppermute | solution.py:308
  14.7 0.7 %copy-start.3 = (s32[16]{0:T(128)S(1)}, s32[16]{0:T(128)}, u32[]{:S(2)}) copy-start(s32[16]{0:T(128)} %sizes.3) | copy-start | bytes 196
  16.0 21.9 %copy-start = (f32[1,128,128]{2,1,0:T(8,128)S(1)}, f32[1,128,128]{2,1,0:T(8,128)}, u32[]{:S(2)}) copy-start(f32[1,128,128]{2,1,0:T(8,128)} %precond.1) | copy-start | bytes 196612
  20.8 1.6 %collective-permute-start.9 = (bf16[8,144,128]{2,1,0:T(8,128)(2,1)S(1)}, bf16[8,144,128]{2,1,0:T(8,128)(2,1)S(1)}, u32[]{:S(2)}, u32[]{:S(2)}) collective-permute-start(bf16[8,144,128]{2,1,0:T(8,128)(2,1)S(1)} %get-tuple-element.29), channel_id=1, source_target_pairs={{0,1},{1,0},{2,3},{3,2},{4,5},{5,4},{6,7},{7,6},{8,9},{9,8},{10,11... | collective-permute-start | bytes 884744 | tf_op jit(solution)/shard_map/sum_first/ppermute | solution.py:308
  22.5 4.6 %collective-permute-start.10 = (bf16[2,144,128]{2,1,0:T(8,128)(2,1)S(1)}, bf16[2,144,128]{2,1,0:T(8,128)(2,1)S(1)}, u32[]{:S(2)}, u32[]{:S(2)}) collective-permute-start(bf16[2,144,128]{2,1,0:T(8,128)(2,1)S(1)} %get-tuple-element.32), channel_id=1, source_target_pairs={{0,2},{2,0},{4,6},{6,4},{8,10},{10,8},{12,14},{14,12},{1,3},{3,1},... | collective-permute-start | bytes 221192 | tf_op jit(solution)/shard_map/sum_first/ppermute | solution.py:313
  24.3 5.1 %collective-permute-start.11 = (bf16[2,144,128]{2,1,0:T(8,128)(2,1)S(1)}, bf16[2,144,128]{2,1,0:T(8,128)(2,1)S(1)}, u32[]{:S(2)}, u32[]{:S(2)}) collective-permute-start(bf16[2,144,128]{2,1,0:T(8,128)(2,1)S(1)} %get-tuple-element.33), channel_id=1, source_target_pairs={{0,4},{2,6},{4,0},{6,2},{8,12},{10,14},{12,8},{14,10},{1,5},{3,7},... | collective-permute-start | bytes 221192 | tf_op jit(solution)/shard_map/sum_first/ppermute | solution.py:313
  25.6 5.3 %collective-permute-start.12 = (bf16[2,144,128]{2,1,0:T(8,128)(2,1)S(1)}, bf16[2,144,128]{2,1,0:T(8,128)(2,1)S(1)}, u32[]{:S(2)}, u32[]{:S(2)}) collective-permute-start(bf16[2,144,128]{2,1,0:T(8,128)(2,1)S(1)} %get-tuple-element.34), channel_id=1, source_target_pairs={{0,6},{2,4},{4,2},{6,0},{8,14},{10,12},{12,10},{14,8},{1,7},{3,5},... | collective-permute-start | bytes 221192 | tf_op jit(solution)/shard_map/sum_first/ppermute | solution.py:313
  30.9 6.9 %collective-permute-start.13 = (bf16[1,400,128]{2,1,0:T(8,128)(2,1)S(1)}, bf16[1,400,128]{2,1,0:T(8,128)(2,1)S(1)}, u32[]{:S(2)}, u32[]{:S(2)}) collective-permute-start(bf16[1,400,128]{2,1,0:T(8,128)(2,1)S(1)} %for_far.2), channel_id=1, source_target_pairs={{0,8},{2,10},{4,12},{6,14},{8,0},{10,2},{12,4},{14,6},{1,9},{3,11}... | collective-permute-start | bytes 307208 | tf_op jit(solution)/shard_map/sum_first/ppermute | solution.py:313
  38.0 5.2 %collective-permute-start.16 = (bf16[2,128,128]{2,1,0:T(8,128)(2,1)S(1)}, bf16[2,128,128]{2,1,0:T(8,128)(2,1)S(1)}, u32[]{:S(2)}, u32[]{:S(2)}) collective-permute-start(bf16[2,128,128]{2,1,0:T(8,128)(2,1)S(1)} %get-tuple-element.36.refs_0_), channel_id=1, source_target_pairs={{0,6},{2,4},{4,2},{6,0},{8,14},{10,12},{12,10},{14,8},{1,7},{3,5},... | collective-permute-start | bytes 196616 | tf_op jit(solution)/shard_map/gather_residual/ppermute | solution.py:313
  38.9 4.3 %collective-permute-start.15 = (bf16[2,128,128]{2,1,0:T(8,128)(2,1)S(1)}, bf16[2,128,128]{2,1,0:T(8,128)(2,1)S(1)}, u32[]{:S(2)}, u32[]{:S(2)}) collective-permute-start(bf16[2,128,128]{2,1,0:T(8,128)(2,1)S(1)} %get-tuple-element.36.refs_0_), channel_id=1, source_target_pairs={{0,4},{2,6},{4,0},{6,2},{8,12},{10,14},{12,8},{14,10},{1,5},{3,7},... | collective-permute-start | bytes 196616 | tf_op jit(solution)/shard_map/gather_residual/ppermute | solution.py:313
  40.3 4.3 %collective-permute-start.14 = (bf16[2,128,128]{2,1,0:T(8,128)(2,1)S(1)}, bf16[2,128,128]{2,1,0:T(8,128)(2,1)S(1)}, u32[]{:S(2)}, u32[]{:S(2)}) collective-permute-start(bf16[2,128,128]{2,1,0:T(8,128)(2,1)S(1)} %get-tuple-element.36.refs_0_), channel_id=1, source_target_pairs={{0,2},{2,0},{4,6},{6,4},{8,10},{10,8},{12,14},{14,12},{1,3},{3,1},... | collective-permute-start | bytes 196616 | tf_op jit(solution)/shard_map/gather_residual/ppermute | solution.py:313
  41.6 3.0 %collective-permute-start.17 = (bf16[2,128,128]{2,1,0:T(8,128)(2,1)S(1)}, bf16[2,128,128]{2,1,0:T(8,128)(2,1)S(1)}, u32[]{:S(2)}, u32[]{:S(2)}) collective-permute-start(bf16[2,128,128]{2,1,0:T(8,128)(2,1)S(1)} %get-tuple-element.36.refs_0_), channel_id=1, source_target_pairs={{0,1},{1,0},{2,3},{3,2},{4,5},{5,4},{6,7},{7,6},{8,9},{9,8},{10,11... | collective-permute-start | bytes 196616 | tf_op jit(solution)/shard_map/gather_residual/ppermute | solution.py:308
  43.2 1.3 %collective-permute-start.20 = (bf16[2,128,128]{2,1,0:T(8,128)(2,1)S(1)}, bf16[2,128,128]{2,1,0:T(8,128)(2,1)S(1)}, u32[]{:S(2)}, u32[]{:S(2)}) collective-permute-start(bf16[2,128,128]{2,1,0:T(8,128)(2,1)S(1)} %collective-permute-done.16.refs_3_), channel_id=1, source_target_pairs={{0,1},{1,0},{2,3},{3,2},{4,5},{5,4},{6,7},{7,6},{8,9},{9,8},{10,11... | collective-permute-start | bytes 196616 | tf_op jit(solution)/shard_map/gather_residual/ppermute | solution.py:308
  43.2 1.4 %collective-permute-start.19 = (bf16[2,128,128]{2,1,0:T(8,128)(2,1)S(1)}, bf16[2,128,128]{2,1,0:T(8,128)(2,1)S(1)}, u32[]{:S(2)}, u32[]{:S(2)}) collective-permute-start(bf16[2,128,128]{2,1,0:T(8,128)(2,1)S(1)} %collective-permute-done.15.refs_2_), channel_id=1, source_target_pairs={{0,1},{1,0},{2,3},{3,2},{4,5},{5,4},{6,7},{7,6},{8,9},{9,8},{10,11... | collective-permute-start | bytes 196616 | tf_op jit(solution)/shard_map/gather_residual/ppermute | solution.py:308
  44.5 1.3 %collective-permute-start.18 = (bf16[2,128,128]{2,1,0:T(8,128)(2,1)S(1)}, bf16[2,128,128]{2,1,0:T(8,128)(2,1)S(1)}, u32[]{:S(2)}, u32[]{:S(2)}) collective-permute-start(bf16[2,128,128]{2,1,0:T(8,128)(2,1)S(1)} %collective-permute-done.14.refs_1_), channel_id=1, source_target_pairs={{0,1},{1,0},{2,3},{3,2},{4,5},{5,4},{6,7},{7,6},{8,9},{9,8},{10,11... | collective-permute-start | bytes 196616 | tf_op jit(solution)/shard_map/gather_residual/ppermute | solution.py:308
  50.1 1.6 %collective-permute-start.21 = (bf16[8,144,128]{2,1,0:T(8,128)(2,1)S(1)}, bf16[8,144,128]{2,1,0:T(8,128)(2,1)S(1)}, u32[]{:S(2)}, u32[]{:S(2)}) collective-permute-start(bf16[8,144,128]{2,1,0:T(8,128)(2,1)S(1)} %get-tuple-element.42), channel_id=1, source_target_pairs={{0,1},{1,0},{2,3},{3,2},{4,5},{5,4},{6,7},{7,6},{8,9},{9,8},{10,11... | collective-permute-start | bytes 884744 | tf_op jit(solution)/shard_map/sum_second/ppermute | solution.py:308
  51.9 4.4 %collective-permute-start.22 = (bf16[2,144,128]{2,1,0:T(8,128)(2,1)S(1)}, bf16[2,144,128]{2,1,0:T(8,128)(2,1)S(1)}, u32[]{:S(2)}, u32[]{:S(2)}) collective-permute-start(bf16[2,144,128]{2,1,0:T(8,128)(2,1)S(1)} %get-tuple-element.45), channel_id=1, source_target_pairs={{0,2},{2,0},{4,6},{6,4},{8,10},{10,8},{12,14},{14,12},{1,3},{3,1},... | collective-permute-start | bytes 221192 | tf_op jit(solution)/shard_map/sum_second/ppermute | solution.py:313
  53.2 4.8 %collective-permute-start.23 = (bf16[2,144,128]{2,1,0:T(8,128)(2,1)S(1)}, bf16[2,144,128]{2,1,0:T(8,128)(2,1)S(1)}, u32[]{:S(2)}, u32[]{:S(2)}) collective-permute-start(bf16[2,144,128]{2,1,0:T(8,128)(2,1)S(1)} %get-tuple-element.46), channel_id=1, source_target_pairs={{0,4},{2,6},{4,0},{6,2},{8,12},{10,14},{12,8},{14,10},{1,5},{3,7},... | collective-permute-start | bytes 221192 | tf_op jit(solution)/shard_map/sum_second/ppermute | solution.py:313
  53.4 5.7 %collective-permute-start.24 = (bf16[2,144,128]{2,1,0:T(8,128)(2,1)S(1)}, bf16[2,144,128]{2,1,0:T(8,128)(2,1)S(1)}, u32[]{:S(2)}, u32[]{:S(2)}) collective-permute-start(bf16[2,144,128]{2,1,0:T(8,128)(2,1)S(1)} %get-tuple-element.47), channel_id=1, source_target_pairs={{0,6},{2,4},{4,2},{6,0},{8,14},{10,12},{12,10},{14,8},{1,7},{3,5},... | collective-permute-start | bytes 221192 | tf_op jit(solution)/shard_map/sum_second/ppermute | solution.py:313
  59.1 5.0 %collective-permute-start.25 = (bf16[1,144,128]{2,1,0:T(8,128)(2,1)S(1)}, bf16[1,144,128]{2,1,0:T(8,128)(2,1)S(1)}, u32[]{:S(2)}, u32[]{:S(2)}) collective-permute-start(bf16[1,144,128]{2,1,0:T(8,128)(2,1)S(1)} %for_far.3), channel_id=1, source_target_pairs={{0,8},{2,10},{4,12},{6,14},{8,0},{10,2},{12,4},{14,6},{1,9},{3,11}... | collective-permute-start | bytes 110600 | tf_op jit(solution)/shard_map/sum_second/ppermute | solution.py:313

commit v6 on v5

v6 whole, which is shorter than its diff:
```python
import jax
import jax.numpy as jnp
from jax import lax
from jax.experimental import pallas as pl
from jax.experimental.pallas import tpu as pltpu
from jax.sharding import Mesh
from jax.sharding import PartitionSpec as P

BF16 = jnp.bfloat16
F32 = jnp.float32
TAIL = 16
LIMIT = 36 << 20
LONG = 10**11
NEAR = 4


def each(count, body, carry):
    if count <= 8:
        for j in range(count):
            carry = body(j, carry)
        return carry
    return lax.fori_loop(0, count, body, carry)


def mask_of(size, width):
    rows = lax.broadcasted_iota(jnp.int32, (width, width), 0)
    cols = lax.broadcasted_iota(jnp.int32, (width, width), 1)
    return (rows < size) & (cols < size)


def fold(x):
    return jnp.sum(x, axis=0, keepdims=True)


def eight(x):
    return jnp.sum(x.reshape(-1, 8, x.shape[1]), axis=0)


def at(i, width):
    if isinstance(i, int):
        return slice(i * width, (i + 1) * width)
    return pl.ds(pl.multiple_of(i * width, width), width)


def tail_of(rows):
    pieces = []
    for row in rows:
        rest = row
        for _ in range(3):
            piece = rest.astype(BF16).astype(F32)
            pieces.append(piece)
            rest = rest - piece
    lanes = rows[0].shape[1]
    place = lax.broadcasted_iota(jnp.int32, (TAIL, lanes), 0)
    tail = jnp.zeros((TAIL, lanes), F32)
    for at, piece in enumerate(pieces):
        tail = jnp.where(place == at, piece, tail)
    return tail.astype(BF16)


def rows_of(tail, count):
    wide = tail.astype(F32)
    return [
        (wide[3 * i : 3 * i + 1] + wide[3 * i + 1 : 3 * i + 2]) + wide[3 * i + 2 : 3 * i + 3]
        for i in range(count)
    ]


def total(row):
    return jnp.broadcast_to(jnp.sum(row, axis=1, keepdims=True), row.shape)


def halve(rows):
    while rows.shape[0] > 1:
        half = rows.shape[0] // 2
        rows = rows[:half] + rows[half:]
    return rows


def apply_blocks(plan, vec, left, right, acc, keep=None):
    terms, nnz = left.shape[0], left.shape[1]
    per = 6 if terms % 6 == 0 else 1

    def step(i, carry):
        items = [(i * per + k, n) for k in range(per) for n in range(nnz)]
        plans = [plan[k, n] for k, n in items]
        prods = [
            jnp.dot(left[k, n], vec[p & 1023], preferred_element_type=F32).astype(BF16)
            for (k, n), p in zip(items, plans)
        ]
        for (k, n), p, prod in zip(items, plans, prods):
            turned = right[k, n]
            if keep is not None:
                turned = turned.T
                keep[k, n] = turned
            acc[p >> 10] += jnp.dot(prod, turned, preferred_element_type=F32)
        return carry

    lax.fori_loop(0, terms // per, step, 0)


def mask_kernel(sizes, block, inside, limits, own):
    own[...] = block[...]
    chips, width = limits.shape[0] // 2, inside.shape[2]
    core, chip = lax.axis_index("core"), lax.axis_index("chip")
    for i in range(2):
        inside[i] = mask_of(sizes[2 * (chip ^ (NEAR * i)) + core], width).astype(F32)

    def size(j, carry):
        for other in range(2):
            row = jnp.full((1, width), sizes[2 * (chip ^ j) + (core ^ other)], jnp.int32)
            limits[pl.ds(other * chips + j, 1)] = row
        return carry

    each(chips, size, 0)


def plan_kernel(src, tgt, plan):
    chips = lax.axis_size("chip")
    chip, core = lax.axis_index("chip"), lax.axis_index("core")

    def place(s):
        return ((s >> 1) ^ chip) + chips * ((s ^ core) & 1)

    plan[...] = place(src[...]) | (place(tgt[...]) << 10)


def pair_kernel(own, far, out):
    out[0:1] = own[...]
    out[1:2] = far[...]


def first_kernel(*refs):
    pieces, ins, outs = refs[: 2 * NEAR], refs[2 * NEAR : 2 * NEAR + 5], refs[2 * NEAR + 5 :]
    plan, limits, left, right, _ = ins
    theirs, acc, wave, flip, sums, rows, places, sem = outs
    span, width = pieces[0].shape[0], pieces[0].shape[2]
    chips = NEAR * span
    copy = pltpu.make_async_copy(plan, places, sem)
    copy.start()
    across = lax.broadcasted_iota(jnp.int32, (width, width), 0)
    along = lax.broadcasted_iota(jnp.int32, (width, width), 1)
    acc[...] = jnp.zeros_like(acc)

    for other in range(2):
        for k in range(NEAR):
            piece = pieces[other * NEAR + k]

            def load(i, carry, other=other, k=k, piece=piece):
                rel = other * chips + NEAR * i + k
                limit = limits[pl.ds(rel, 1)]
                block = jnp.where((across < limit) & (along < limit), piece[i].astype(F32), 0.0)
                wave[rel] = block.astype(BF16)
                rows[rel] = eight(block * block)
                return carry

            each(span, load, 0)
    copy.wait()
    apply_blocks(places, wave, left, right, acc, flip)

    def store(j, ray):
        a, b = acc[j], acc[chips + j]
        theirs[at(j, width)] = b.astype(BF16)
        return ray + eight(wave[j].astype(F32) * a + wave[chips + j].astype(F32) * b)

    ray = fold(each(chips, store, jnp.zeros((8, width), F32)))
    theirs[chips * width :] = tail_of([ray])
    sums[0:1] = fold(halve(rows[...])[0])
    sums[1:2] = ray


def second_kernel(*refs):
    pieces, ins, outs = refs[: 2 * NEAR], refs[2 * NEAR : 2 * NEAR + 6], refs[2 * NEAR + 6 :]
    plan, wave, left, right, first, keep = ins
    theirs, acc, sums, sigma, vec, places, sems = outs
    span, width = pieces[0].shape[0], pieces[0].shape[2]
    chips = NEAR * span
    copy = pltpu.make_async_copy(plan, places, sems.at[0])
    result = pltpu.make_async_copy(first, sigma, sems.at[1])
    copy.start()
    result.start()
    acc[...] = jnp.zeros_like(acc)

    for other in range(2):
        for k in range(NEAR):
            piece = pieces[other * NEAR + k]

            def load(i, carry, other=other, k=k, piece=piece):
                vec[other * chips + NEAR * i + k] = piece[i]
                return carry

            each(span, load, 0)
    copy.wait()
    apply_blocks(places, vec, left, right, acc)

    def store(j, carry):
        cross, square = carry
        a, b = acc[j], acc[chips + j]
        theirs[at(j, width)] = b.astype(BF16)
        cross = cross + eight(wave[j].astype(F32) * a + wave[chips + j].astype(F32) * b)
        square = square + eight(vec[j].astype(F32) * a + vec[chips + j].astype(F32) * b)
        return cross, square

    zero = jnp.zeros((8, width), F32)
    rows = [fold(x) for x in each(chips, store, (zero, zero))]
    rows += [keep[2 + i : 3 + i] for i in range(3)]
    theirs[chips * width :] = tail_of(rows)
    for i, row in enumerate(rows):
        sums[i : i + 1] = row
    result.wait()


def chip_kernel(start, count, mine, got, sums, base, *sends):
    width = mine.shape[2]
    chips, span = mine.shape[0] // 2, base.shape[0]
    rows = rows_of(got[chips * width :], count)
    rows = [sums[start + i : start + i + 1] + rows[i] for i in range(count)]
    tail = tail_of(rows)

    def store(i, carry):
        base[i, 0:width] = mine[NEAR * i] + got[at(NEAR * i, width)].astype(F32)
        for k, send in enumerate(sends, 1):
            rel = NEAR * i + k
            send[at(i, width)] = (mine[rel] + got[at(rel, width)].astype(F32)).astype(BF16)
        return carry

    each(span, store, 0)
    for send in sends:
        send[span * width :] = tail
    for i, row in enumerate(rows):
        base[0, width + i : width + i + 1] = row


def near_kernel(count, base, *refs):
    gots, out = refs[:-1], refs[-1]
    span, width = base.shape[0], base.shape[2]
    parts = [[base[0, width + i : width + i + 1] for i in range(count)]]
    parts += [rows_of(got[span * width :], count) for got in gots]
    rows = [halve(jnp.concatenate([part[i] for part in parts], axis=0)) for i in range(count)]

    def store(i, carry):
        block = base[i, 0:width]
        for got in gots:
            block = block + got[at(i, width)].astype(F32)
        out[i, 0:width] = block
        for n, row in enumerate(rows):
            out[i, width + n : width + n + 1] = row
        return carry

    each(span, store, 0)


def both_kernel(count, part, out):
    width = part.shape[2]
    block = part[1, 0:width]
    high = block.astype(BF16)
    out[at(0, width)] = high
    out[at(1, width)] = (block - high.astype(F32)).astype(BF16)
    out[at(2, width)] = part[0, 0:width].astype(BF16)
    out[3 * width :] = tail_of([part[0, width + i : width + i + 1] for i in range(count)])


def far_kernel(count, part, out):
    width = part.shape[2]
    out[at(0, width)] = part[1, 0:width].astype(BF16)
    out[width:] = tail_of([part[0, width + i : width + i + 1] for i in range(count)])


def residual_kernel(part, got, wave, inside, precond, far, sums, sigma, resid, send, keep):
    width = part.shape[2]
    (ray,) = rows_of(got[3 * width :], 1)
    norm, ray = total(sums[0:1]), total(part[0, width : width + 1] + ray)
    energy = ray / norm

    def piece(i):
        return got[at(i, width)].astype(F32)

    own = wave[0].astype(F32)
    first = (part[0, 0:width] + (piece(0) + piece(1))) * inside[0]
    q = precond[0] * (first - energy * own)
    low = q.astype(BF16)
    sigma[0] = first
    resid[0] = q
    send[0] = low
    there = (part[1, 0:width] + piece(2)) * inside[1]
    send[1] = (far[0] * (there - energy * wave[NEAR].astype(F32))).astype(BF16)
    rows = (norm, ray, fold(own * q), fold(low.astype(F32) * first), fold(q * q))
    for i, row in enumerate(rows):
        keep[i : i + 1] = row


def final_kernel(part, got, wave, inside, first, resid, keep, direction, sigma, subspace):
    width = part.shape[2]
    rows = rows_of(got[width:], 5)
    cross, square, inter, mixed, length = (
        total(part[0, width + i : width + i + 1] + rows[i]) for i in range(5)
    )
    norm, ray = keep[0:1], keep[1:2]
    c = inter / norm
    direction[0] = (resid[0] - c * wave[0].astype(F32)).astype(BF16)
    block = part[0, 0:width] + got[at(0, width)].astype(F32)
    sigma[0] = block * inside[0] - c * first[0]
    values = (
        ray,
        cross - c * ray,
        square - c * mixed - c * (cross - c * ray),
        length - 2.0 * c * inter + c * c * norm,
    )
    for i, value in enumerate(values):
        subspace[i] = jnp.max(value / norm)


VMEM = pl.BlockSpec(memory_space=pltpu.VMEM)
SMEM = pl.BlockSpec(memory_space=pltpu.SMEM)
HBM = pl.BlockSpec(memory_space=pl.ANY)


def call(kernel, name, ins, outs, scratch, args, flops, out_specs=None):
    moved = sum(a.size * a.dtype.itemsize for a in args)
    return pl.pallas_call(
        kernel,
        name=name,
        in_specs=ins,
        out_specs=out_specs or [VMEM] * len(outs),
        out_shape=outs,
        scratch_shapes=scratch,
        compiler_params=pltpu.CompilerParams(vmem_limit_bytes=LIMIT),
        cost_estimate=pl.CostEstimate(flops=flops, bytes_accessed=moved, transcendentals=0),
    )(*args)


def shape(*dims, dtype=F32):
    return jax.ShapeDtypeStruct(dims, dtype)


def swap(x):
    return lax.ppermute(x, "core", [(0, 1), (1, 0)])


def flip_chip(x, bits):
    chips = lax.axis_size("chip")
    return lax.ppermute(x, "chip", [(i, i ^ bits) for i in range(chips)])


def gather(block):
    step = NEAR * block.shape[0]
    while step < lax.axis_size("chip"):
        block = jnp.concatenate([block, flip_chip(block, step)], axis=0)
        step *= 2
    pieces = [block] + [flip_chip(block, k) for k in range(1, NEAR)]
    return pieces + [swap(piece) for piece in pieces]


def scatter(theirs, mine, sums, start, count):
    chips, width = mine.shape[0] // 2, mine.shape[2]
    span, wide = chips // NEAR, width + 8
    sent = [shape(span * width + TAIL, width, dtype=BF16)] * (NEAR - 1)
    base, *sends = call(
        lambda *refs: chip_kernel(start, count, *refs), "chip_sum", [VMEM] * 3,
        [shape(span, wide, width)] + sent, [], (mine, swap(theirs), sums), mine.size,
    )
    gots = [flip_chip(send, k) for k, send in enumerate(sends, 1)]
    (part,) = call(
        lambda *refs: near_kernel(count, *refs), "near_sum", [VMEM] * NEAR,
        [shape(span, wide, width)], [], (base, *gots), mine.size,
    )
    while span > 2:
        span //= 2
        part = part[:span] + flip_chip(part[span:], NEAR * span)
    return part


def shards(state, sector_sizes, left, right, source, target, precond):
    chips = lax.axis_size("chip")
    width = state.shape[1]
    every = 2 * chips
    flops = 4 * left.size * width
    near = [VMEM] * (2 * NEAR)
    block = shape(1, width, width)
    sums_of = shape(8, width)
    after_h = [shape(chips * width + TAIL, width, dtype=BF16), shape(every, width, width)]
    vectors = shape(every, width, width, dtype=BF16)
    places = pltpu.SMEM(source.shape, jnp.int32)

    with jax.named_scope("plan"):
        (plan,) = call(
            plan_kernel, "plan", [VMEM] * 2, [shape(*source.shape, dtype=jnp.int32)], [],
            (source, target), source.size,
        )
        inside, limits, own = call(
            mask_kernel, "masks", [SMEM, VMEM],
            [shape(2, width, width), shape(every, width, dtype=jnp.int32),
             shape(1, width, width, dtype=BF16)],
            [], (sector_sizes, state), LONG,
        )
    with jax.named_scope("gather_state"):
        (pair,) = call(
            pair_kernel, "pair", [VMEM] * 2, [shape(2, width, width, dtype=BF16)], [],
            (own, flip_chip(state, NEAR)), state.size,
        )
        pieces = gather(pair)
        far = flip_chip(precond, NEAR)
    with jax.named_scope("first_sigma"):
        theirs, mine, wave, flip, sums = call(
            first_kernel, "first_sigma", near + [HBM] + [VMEM] * 4,
            after_h + [vectors, shape(*right.shape, dtype=BF16), sums_of],
            [pltpu.VMEM((every, 8, width), F32), places, pltpu.SemaphoreType.DMA],
            (*pieces, plan, limits, left, right, far), flops,
        )
    with jax.named_scope("sum_first"):
        part = scatter(theirs, mine, sums, 1, 1)
        (both,) = call(
            lambda *refs: both_kernel(1, *refs), "for_far", [VMEM],
            [shape(3 * width + TAIL, width, dtype=BF16)], [], (part,), part.size,
        )
        got = flip_chip(both, NEAR)
    with jax.named_scope("residual"):
        first, resid, send, keep = call(
            residual_kernel, "residual", [VMEM] * 7,
            [block, block, shape(2, width, width, dtype=BF16), sums_of],
            [], (part, got, wave, inside, precond, far, sums), mine.size,
        )
    with jax.named_scope("gather_residual"):
        pieces = gather(send)
    with jax.named_scope("second_sigma"):
        theirs, mine, sums, sigma = call(
            second_kernel, "second_sigma", near + [HBM] + [VMEM] * 5, after_h + [sums_of, block],
            [pltpu.VMEM((every, width, width), BF16), places, pltpu.SemaphoreType.DMA((2,))],
            (*pieces, plan, wave, left, flip, first, keep), flops, [VMEM] * 3 + [HBM],
        )
    with jax.named_scope("sum_second"):
        part = scatter(theirs, mine, sums, 0, 5)
        (both,) = call(
            lambda *refs: far_kernel(5, *refs), "for_far", [VMEM],
            [shape(width + TAIL, width, dtype=BF16)], [], (part,), part.size,
        )
        got = flip_chip(both, NEAR)
    with jax.named_scope("outputs"):
        direction, second, subspace = call(
            final_kernel, "outputs", [VMEM] * 7,
            [shape(1, width, width, dtype=BF16), block, shape(4)],
            [], (part, got, wave, inside, first, resid, keep), mine.size, [VMEM, VMEM, SMEM],
        )
    return sigma, direction, second, subspace


def solution(mesh):
    groups, members = mesh.shape["grp"], mesh.shape["op"]
    split = Mesh(mesh.devices.reshape(groups, members // 2, 2), ("grp", "chip", "core"))
    rows = P(("grp", "chip", "core"))
    return jax.shard_map(
        shards,
        mesh=split,
        in_specs=(rows, P("grp"), rows, rows, rows, rows, rows),
        out_specs=(rows, rows, rows, P("grp")),
        check_vma=False,
    )
```

time: 65 us -> 63.6 us (0.978)
  Pallas kernels: 10.5 us -> 9.69 us
  waiting for transfers between devices: 23.1 us -> 22.4 us
    pallas_call x11 -> x13, Pallas kernels: 10.5 us -> 9.69 us  [call(): pl.pallas_call(kernel, name=name, in_specs=ins, out_specs=out_specs or [V...]
    ppermute x16, waiting for transfers between devices: 19.2 us -> 18.5 us  [flip_chip(): return lax.ppermute(x, 'chip', [(i, i ^ bits) for i in range(chips)])]
    unnamed x17 -> x14, local copies, waits for them, and re-layouts: 1.49 us -> 1.47 us
  transfers between devices with their start and end apart: 26 -> 26, of which waited for: 18 -> 18; matrix products, arithmetic and copies ran while one was open for 1% -> 0% of each run, Pallas kernels for 1% -> 1%
where the time goes in v6:
time: 63.6 us; the launch traced here: 63.4 us
  starting transfers between devices  29 us (46%)
  waiting for transfers between devices  22.4 us (35%)
  Pallas kernels  9.69 us (15%)
  local copies, waits for them, and re-layouts  1.47 us (2%)
  between operations  0.78 us (1%)
    ppermute x16, starting transfers between devices, flip_chip(): return lax.ppermute(x, 'chip', [(i, i ^ bits) for i in range(chips)])  27.2 us
    ppermute x16, waiting for transfers between devices, flip_chip(): return lax.ppermute(x, 'chip', [(i, i ^ bits) for i in range(chips)])  18.5 us
    pallas_call x13, Pallas kernels, call(): pl.pallas_call(kernel, name=name, in_specs=ins, out_specs=out_specs or [V...  9.69 us
    ppermute x10, waiting for transfers between devices, swap(): return lax.ppermute(x, 'core', [(0, 1), (1, 0)])  3.92 us
    ppermute x10, starting transfers between devices, swap(): return lax.ppermute(x, 'core', [(0, 1), (1, 0)])  1.85 us
    unnamed x14, local copies, waits for them, and re-layouts  1.47 us
  transfers between devices with their start and end apart: 26, of which 18 were waited for; matrix products, arithmetic and copies ran while one was open for 0% of the time, Pallas kernels for 1%

profile of v6, /device:TPU:0, one launch (start us, length us, event | category | flops | bytes accessed | tf_op | source)
XLA Modules:
  0.0 63.4 jit_solution(15681485766593625462)
XLA Ops:
  0.6 0.0 copy-start.2
  0.6 0.0 copy-start.4
  0.7 0.0 copy-start.3
  0.7 4.1 %collective-permute-start = (bf16[1,128,128]{2,1,0:T(8,128)(2,1)}, bf16[1,128,128]{2,1,0:T(8,128)(2,1)S(1)}, u32[]{:S(2)}, u32[]{:S(2)}) collective-permute-start(bf16[1,128,128]{2,1,0:T(8,128)(2,1)} %block.1), channel_id=1, source_target_pairs={{0,8},{2,10},{4,12},{6,14},{8,0},{10,2},{12,4},{14,6},{1,9},{3,11}... | collective-permute-start | bytes 98312 | tf_op jit(solution)/shard_map/gather_state/ppermute | solution.py:342
  4.8 0.8 %copy-done.5 = bf16[1,128,128]{2,1,0:T(8,128)(2,1)S(1)} copy-done((bf16[1,128,128]{2,1,0:T(8,128)(2,1)S(1)}, bf16[1,128,128]{2,1,0:T(8,128)(2,1)}, u32[]{:S(2)}) %copy-start.5) | copy-done | bytes 32792
  5.6 0.7 %copy-done.6 = s32[16]{0:T(128)S(1)} copy-done((s32[16]{0:T(128)S(1)}, s32[16]{0:T(128)}, u32[]{:S(2)}) %copy-start.6) | copy-done | bytes 88
  6.2 0.6 masks.1
  6.8 0.4 collective-permute-done.far
  7.2 2.5 %collective-permute-start.3 = (bf16[2,128,128]{2,1,0:T(8,128)(2,1)S(1)}, bf16[2,128,128]{2,1,0:T(8,128)(2,1)S(1)}, u32[]{:S(2)}, u32[]{:S(2)}) collective-permute-start(bf16[2,128,128]{2,1,0:T(8,128)(2,1)S(1)} %pair.1.refs_0_), channel_id=1, source_target_pairs={{0,6},{2,4},{4,2},{6,0},{8,14},{10,12},{12,10},{14,8},{1,7},{3,5},... | collective-permute-start | bytes 196616 | tf_op jit(solution)/shard_map/gather_state/ppermute | solution.py:342
  9.7 0.7 %collective-permute-start.2 = (bf16[2,128,128]{2,1,0:T(8,128)(2,1)S(1)}, bf16[2,128,128]{2,1,0:T(8,128)(2,1)S(1)}, u32[]{:S(2)}, u32[]{:S(2)}) collective-permute-start(bf16[2,128,128]{2,1,0:T(8,128)(2,1)S(1)} %pair.1.refs_0_), channel_id=1, source_target_pairs={{0,4},{2,6},{4,0},{6,2},{8,12},{10,14},{12,8},{14,10},{1,5},{3,7},... | collective-permute-start | bytes 196616 | tf_op jit(solution)/shard_map/gather_state/ppermute | solution.py:342
  10.4 0.3 collective-permute-start.1
  10.7 2.6 %collective-permute-start.8 = (f32[1,128,128]{2,1,0:T(8,128)S(1)}, f32[1,128,128]{2,1,0:T(8,128)S(1)}, u32[]{:S(2)}, u32[]{:S(2)}) collective-permute-start(f32[1,128,128]{2,1,0:T(8,128)S(1)} %copy-done.2), channel_id=1, source_target_pairs={{0,8},{2,10},{4,12},{6,14},{8,0},{10,2},{12,4},{14,6},{1,9},{3,11}... | collective-permute-start | bytes 196616 | tf_op jit(solution)/shard_map/gather_state/ppermute | solution.py:342
  13.3 0.0 collective-permute-start.4
  13.3 0.0 collective-permute-done.3.refs_3_
  13.3 0.5 collective-permute-start.7
  13.8 0.6 collective-permute-done.2.refs_2_
  14.4 0.0 collective-permute-start.6
  14.4 0.2 collective-permute-done.1.refs_1_
  14.7 0.3 collective-permute-start.5
  15.0 0.9 %collective-permute-done.8.refs_12_.far = f32[1,128,128]{2,1,0:T(8,128)S(1)} collective-permute-done((f32[1,128,128]{2,1,0:T(8,128)S(1)}, f32[1,128,128]{2,1,0:T(8,128)S(1)}, u32[]{:S(2)}, u32[]{:S(2)}) %collective-permute-start.8) | collective-permute-done | bytes 65568 | tf_op jit(solution)/shard_map/gather_state/ppermute | solution.py:342
  15.9 0.0 collective-permute-done.4.refs_4_
  15.9 0.0 collective-permute-done.7.refs_7_
  15.9 0.0 collective-permute-done.6.refs_6_
  15.9 0.0 collective-permute-done.5.refs_5_
  15.9 3.9 %first_sigma.1 = (bf16[1040,128]{1,0:T(8,128)(2,1)S(1)}, f32[16,128,128]{2,1,0:T(8,128)S(1)}, bf16[16,128,128]{2,1,0:T(8,128)(2,1)S(1)}, bf16[12,12,128,128]{3,2,1,0:T(8,128)(2,1)S(1)}, f32[8,128]{1,0:T(8,128)S(1)}) custom-call(bf16[2,128,128]{2,1,0:T(8,128)(2,1)S(1)} %pair.1.refs_0_, bf16[2,128,128]{2,1,0:T(8,128)(2,1)S(1)} %collective-permute-done.1.refs_1_, ...), custom_call_target="tpu_custom_call" | custom-call | flops 1207959552 | bytes 10035776 | tf_op jit(solution)/shard_map/first_sigma/first_sigma/pallas_call | solution.py:320
  19.9 0.3 collective-permute-start.9
  20.2 1.3 %collective-permute-done.9.refs_1_ = bf16[1040,128]{1,0:T(8,128)(2,1)S(1)} collective-permute-done((bf16[1040,128]{1,0:T(8,128)(2,1)S(1)}, bf16[1040,128]{1,0:T(8,128)(2,1)S(1)}, u32[]{:S(2)}, u32[]{:S(2)}) %collective-permute-start.9) | collective-permute-done | bytes 266272 | tf_op jit(solution)/shard_map/sum_first/ppermute | solution.py:337
  21.5 0.1 chip_sum.2
  21.6 1.8 %collective-permute-start.10 = (bf16[272,128]{1,0:T(8,128)(2,1)S(1)}, bf16[272,128]{1,0:T(8,128)(2,1)S(1)}, u32[]{:S(2)}, u32[]{:S(2)}) collective-permute-start(bf16[272,128]{1,0:T(8,128)(2,1)S(1)} %get-tuple-element.37), channel_id=1, source_target_pairs={{0,2},{2,0},{4,6},{6,4},{8,10},{10,8},{12,14},{14,12},{1,3},{3,1},... | collective-permute-start | bytes 208904 | tf_op jit(solution)/shard_map/sum_first/ppermute | solution.py:342
  23.3 1.4 %collective-permute-start.11 = (bf16[272,128]{1,0:T(8,128)(2,1)S(1)}, bf16[272,128]{1,0:T(8,128)(2,1)S(1)}, u32[]{:S(2)}, u32[]{:S(2)}) collective-permute-start(bf16[272,128]{1,0:T(8,128)(2,1)S(1)} %get-tuple-element.38), channel_id=1, source_target_pairs={{0,4},{2,6},{4,0},{6,2},{8,12},{10,14},{12,8},{14,10},{1,5},{3,7},... | collective-permute-start | bytes 208904 | tf_op jit(solution)/shard_map/sum_first/ppermute | solution.py:342
  24.7 0.4 collective-permute-start.12
  25.1 0.9 %collective-permute-done.10.refs_1_ = bf16[272,128]{1,0:T(8,128)(2,1)S(1)} collective-permute-done((bf16[272,128]{1,0:T(8,128)(2,1)S(1)}, bf16[272,128]{1,0:T(8,128)(2,1)S(1)}, u32[]{:S(2)}, u32[]{:S(2)}) %collective-permute-start.10) | collective-permute-done | bytes 69664 | tf_op jit(solution)/shard_map/sum_first/ppermute | solution.py:342
  26.0 2.4 %collective-permute-done.11.refs_2_ = bf16[272,128]{1,0:T(8,128)(2,1)S(1)} collective-permute-done((bf16[272,128]{1,0:T(8,128)(2,1)S(1)}, bf16[272,128]{1,0:T(8,128)(2,1)S(1)}, u32[]{:S(2)}, u32[]{:S(2)}) %collective-permute-start.11) | collective-permute-done | bytes 69664 | tf_op jit(solution)/shard_map/sum_first/ppermute | solution.py:342
  28.4 1.5 %collective-permute-done.12.refs_3_ = bf16[272,128]{1,0:T(8,128)(2,1)S(1)} collective-permute-done((bf16[272,128]{1,0:T(8,128)(2,1)S(1)}, bf16[272,128]{1,0:T(8,128)(2,1)S(1)}, u32[]{:S(2)}, u32[]{:S(2)}) %collective-permute-start.12) | collective-permute-done | bytes 69664 | tf_op jit(solution)/shard_map/sum_first/ppermute | solution.py:342
  30.0 3.3 %collective-permute-start.13 = (bf16[400,128]{1,0:T(8,128)(2,1)S(1)}, bf16[400,128]{1,0:T(8,128)(2,1)S(1)}, u32[]{:S(2)}, u32[]{:S(2)}) collective-permute-start(bf16[400,128]{1,0:T(8,128)(2,1)S(1)} %for_far.2), channel_id=1, source_target_pairs={{0,8},{2,10},{4,12},{6,14},{8,0},{10,2},{12,4},{14,6},{1,9},{3,11}... | collective-permute-start | bytes 307208 | tf_op jit(solution)/shard_map/sum_first/ppermute | solution.py:342
  33.2 3.7 %collective-permute-done.13.got = bf16[400,128]{1,0:T(8,128)(2,1)S(1)} collective-permute-done((bf16[400,128]{1,0:T(8,128)(2,1)S(1)}, bf16[400,128]{1,0:T(8,128)(2,1)S(1)}, u32[]{:S(2)}, u32[]{:S(2)}) %collective-permute-start.13) | collective-permute-done | bytes 102432 | tf_op jit(solution)/shard_map/sum_first/ppermute | solution.py:342
  36.9 0.1 residual.1
  37.0 0.8 %collective-permute-start.16 = (bf16[2,128,128]{2,1,0:T(8,128)(2,1)S(1)}, bf16[2,128,128]{2,1,0:T(8,128)(2,1)S(1)}, u32[]{:S(2)}, u32[]{:S(2)}) collective-permute-start(bf16[2,128,128]{2,1,0:T(8,128)(2,1)S(1)} %get-tuple-element.42.refs_0_), channel_id=1, source_target_pairs={{0,6},{2,4},{4,2},{6,0},{8,14},{10,12},{12,10},{14,8},{1,7},{3,5},... | collective-permute-start | bytes 196616 | tf_op jit(solution)/shard_map/gather_residual/ppermute | solution.py:342
  37.8 1.5 %collective-permute-start.15 = (bf16[2,128,128]{2,1,0:T(8,128)(2,1)S(1)}, bf16[2,128,128]{2,1,0:T(8,128)(2,1)S(1)}, u32[]{:S(2)}, u32[]{:S(2)}) collective-permute-start(bf16[2,128,128]{2,1,0:T(8,128)(2,1)S(1)} %get-tuple-element.42.refs_0_), channel_id=1, source_target_pairs={{0,4},{2,6},{4,0},{6,2},{8,12},{10,14},{12,8},{14,10},{1,5},{3,7},... | collective-permute-start | bytes 196616 | tf_op jit(solution)/shard_map/gather_residual/ppermute | solution.py:342
  39.3 1.2 %collective-permute-start.14 = (bf16[2,128,128]{2,1,0:T(8,128)(2,1)S(1)}, bf16[2,128,128]{2,1,0:T(8,128)(2,1)S(1)}, u32[]{:S(2)}, u32[]{:S(2)}) collective-permute-start(bf16[2,128,128]{2,1,0:T(8,128)(2,1)S(1)} %get-tuple-element.42.refs_0_), channel_id=1, source_target_pairs={{0,2},{2,0},{4,6},{6,4},{8,10},{10,8},{12,14},{14,12},{1,3},{3,1},... | collective-permute-start | bytes 196616 | tf_op jit(solution)/shard_map/gather_residual/ppermute | solution.py:342
  40.6 0.0 collective-permute-start.17
  40.6 1.7 %collective-permute-done.16.refs_3_ = bf16[2,128,128]{2,1,0:T(8,128)(2,1)S(1)} collective-permute-done((bf16[2,128,128]{2,1,0:T(8,128)(2,1)S(1)}, bf16[2,128,128]{2,1,0:T(8,128)(2,1)S(1)}, u32[]{:S(2)}, u32[]{:S(2)}) %collective-permute-start.16) | collective-permute-done | bytes 65568 | tf_op jit(solution)/shard_map/gather_residual/ppermute | solution.py:342
  42.3 0.0 collective-permute-start.20
  42.3 0.0 collective-permute-done.15.refs_2_
  42.3 0.5 collective-permute-start.19
  42.8 0.8 %collective-permute-done.14.refs_1_ = bf16[2,128,128]{2,1,0:T(8,128)(2,1)S(1)} collective-permute-done((bf16[2,128,128]{2,1,0:T(8,128)(2,1)S(1)}, bf16[2,128,128]{2,1,0:T(8,128)(2,1)S(1)}, u32[]{:S(2)}, u32[]{:S(2)}) %collective-permute-start.14) | collective-permute-done | bytes 65568 | tf_op jit(solution)/shard_map/gather_residual/ppermute | solution.py:342
  43.6 0.0 collective-permute-start.18
  43.6 0.0 collective-permute-done.17.refs_4_
  43.6 0.0 collective-permute-done.20.refs_7_
  43.6 0.1 collective-permute-done.19.refs_6_
  43.7 1.2 %collective-permute-done.18.refs_5_ = bf16[2,128,128]{2,1,0:T(8,128)(2,1)S(1)} collective-permute-done((bf16[2,128,128]{2,1,0:T(8,128)(2,1)S(1)}, bf16[2,128,128]{2,1,0:T(8,128)(2,1)S(1)}, u32[]{:S(2)}, u32[]{:S(2)}) %collective-permute-start.18) | collective-permute-done | bytes 65568 | tf_op jit(solution)/shard_map/gather_residual/ppermute | solution.py:337
  44.9 4.0 %second_sigma.1 = (bf16[1040,128]{1,0:T(8,128)(2,1)S(1)}, f32[16,128,128]{2,1,0:T(8,128)S(1)}, f32[8,128]{1,0:T(8,128)S(1)}, f32[1,128,128]{2,1,0:T(8,128)}) custom-call(bf16[2,128,128]{2,1,0:T(8,128)(2,1)S(1)} %get-tuple-element.42.refs_0_, bf16[2,128,128]{2,1,0:T(8,128)(2,1)S(1)} %collective-permute-done.14.refs_1_, ...), custom_call_target="tpu_custom_call" | custom-call | flops 1207959552 | bytes 10555968 | tf_op jit(solution)/shard_map/second_sigma/second_sigma/pallas_call | solution.py:320
  48.9 0.2 collective-permute-start.21
  49.1 1.4 %collective-permute-done.21.refs_1_ = bf16[1040,128]{1,0:T(8,128)(2,1)S(1)} collective-permute-done((bf16[1040,128]{1,0:T(8,128)(2,1)S(1)}, bf16[1040,128]{1,0:T(8,128)(2,1)S(1)}, u32[]{:S(2)}, u32[]{:S(2)}) %collective-permute-start.21) | collective-permute-done | bytes 266272 | tf_op jit(solution)/shard_map/sum_second/ppermute | solution.py:337
  50.5 0.1 chip_sum.3
  50.6 1.3 %collective-permute-start.22 = (bf16[272,128]{1,0:T(8,128)(2,1)S(1)}, bf16[272,128]{1,0:T(8,128)(2,1)S(1)}, u32[]{:S(2)}, u32[]{:S(2)}) collective-permute-start(bf16[272,128]{1,0:T(8,128)(2,1)S(1)} %get-tuple-element.51), channel_id=1, source_target_pairs={{0,2},{2,0},{4,6},{6,4},{8,10},{10,8},{12,14},{14,12},{1,3},{3,1},... | collective-permute-start | bytes 208904 | tf_op jit(solution)/shard_map/sum_second/ppermute | solution.py:342
  51.9 0.2 collective-permute-start.23
  52.0 2.1 %collective-permute-start.24 = (bf16[272,128]{1,0:T(8,128)(2,1)S(1)}, bf16[272,128]{1,0:T(8,128)(2,1)S(1)}, u32[]{:S(2)}, u32[]{:S(2)}) collective-permute-start(bf16[272,128]{1,0:T(8,128)(2,1)S(1)} %get-tuple-element.53), channel_id=1, source_target_pairs={{0,6},{2,4},{4,2},{6,0},{8,14},{10,12},{12,10},{14,8},{1,7},{3,5},... | collective-permute-start | bytes 208904 | tf_op jit(solution)/shard_map/sum_second/ppermute | solution.py:342
  54.1 0.8 %collective-permute-done.22.refs_1_ = bf16[272,128]{1,0:T(8,128)(2,1)S(1)} collective-permute-done((bf16[272,128]{1,0:T(8,128)(2,1)S(1)}, bf16[272,128]{1,0:T(8,128)(2,1)S(1)}, u32[]{:S(2)}, u32[]{:S(2)}) %collective-permute-start.22) | collective-permute-done | bytes 69664 | tf_op jit(solution)/shard_map/sum_second/ppermute | solution.py:342
  55.0 1.6 %collective-permute-done.23.refs_2_ = bf16[272,128]{1,0:T(8,128)(2,1)S(1)} collective-permute-done((bf16[272,128]{1,0:T(8,128)(2,1)S(1)}, bf16[272,128]{1,0:T(8,128)(2,1)S(1)}, u32[]{:S(2)}, u32[]{:S(2)}) %collective-permute-start.23) | collective-permute-done | bytes 69664 | tf_op jit(solution)/shard_map/sum_second/ppermute | solution.py:342
  56.6 1.0 %collective-permute-done.24.refs_3_ = bf16[272,128]{1,0:T(8,128)(2,1)S(1)} collective-permute-done((bf16[272,128]{1,0:T(8,128)(2,1)S(1)}, bf16[272,128]{1,0:T(8,128)(2,1)S(1)}, u32[]{:S(2)}, u32[]{:S(2)}) %collective-permute-start.24) | collective-permute-done | bytes 69664 | tf_op jit(solution)/shard_map/sum_second/ppermute | solution.py:342
  57.6 3.1 %collective-permute-start.25 = (bf16[144,128]{1,0:T(8,128)(2,1)S(1)}, bf16[144,128]{1,0:T(8,128)(2,1)S(1)}, u32[]{:S(2)}, u32[]{:S(2)}) collective-permute-start(bf16[144,128]{1,0:T(8,128)(2,1)S(1)} %for_far.3), channel_id=1, source_target_pairs={{0,8},{2,10},{4,12},{6,14},{8,0},{10,2},{12,4},{14,6},{1,9},{3,11}... | collective-permute-start | bytes 110600 | tf_op jit(solution)/shard_map/sum_second/ppermute | solution.py:342
  60.7 1.9 %collective-permute-done.25.got = bf16[144,128]{1,0:T(8,128)(2,1)S(1)} collective-permute-done((bf16[144,128]{1,0:T(8,128)(2,1)S(1)}, bf16[144,128]{1,0:T(8,128)(2,1)S(1)}, u32[]{:S(2)}, u32[]{:S(2)}) %collective-permute-start.25) | collective-permute-done | bytes 36896 | tf_op jit(solution)/shard_map/sum_second/ppermute | solution.py:342
  62.7 0.7 %outputs.1 = (bf16[1,128,128]{2,1,0:T(8,128)(2,1)}, f32[1,128,128]{2,1,0:T(8,128)}, f32[4]{0:T(128)}) custom-call(f32[2,136,128]{2,1,0:T(8,128)S(1)} %near_sum.3.refs_0_.part, bf16[144,128]{1,0:T(8,128)(2,1)S(1)} %collective-permute-done.25.got, bf16[16,128,128]{2,1,0:T(8,128)(2,1)S(1)} %get-tuple-element.40.wave.refs_9_, ...), custom_call_target="tpu_custom_call" | custom-call | flops 262144 | bytes 966656 | tf_op jit(solution)/shard_map/outputs/outputs/pallas_call | solution.py:320
  (15 shorter events, 0.2 us)
Async XLA Ops:
  0.6 10.1 %copy-start.2 = (f32[1,128,128]{2,1,0:T(8,128)S(1)}, f32[1,128,128]{2,1,0:T(8,128)}, u32[]{:S(2)}) copy-start(f32[1,128,128]{2,1,0:T(8,128)} %precond.1) | copy-start | bytes 196612
  0.6 14.3 %copy-start.4 = (s32[12,12]{1,0:T(8,128)S(1)}, s32[12,12]{1,0:T(8,128)}, u32[]{:S(2)}) copy-start(s32[12,12]{1,0:T(8,128)} %tgt.1) | copy-start | bytes 1732
  0.7 14.3 %copy-start.3 = (s32[12,12]{1,0:T(8,128)S(1)}, s32[12,12]{1,0:T(8,128)}, u32[]{:S(2)}) copy-start(s32[12,12]{1,0:T(8,128)} %src.1) | copy-start | bytes 1732
  0.7 15.3 %copy-start = (bf16[12,12,128,128]{3,2,1,0:T(8,128)(2,1)S(1)}, bf16[12,12,128,128]{3,2,1,0:T(8,128)(2,1)}, u32[]{:S(2)}) copy-start(bf16[12,12,128,128]{3,2,1,0:T(8,128)(2,1)} %refs_10_.3) | copy-start | bytes 14155780
  0.7 15.3 %copy-start.1 = (bf16[12,12,128,128]{3,2,1,0:T(8,128)(2,1)S(1)}, bf16[12,12,128,128]{3,2,1,0:T(8,128)(2,1)}, u32[]{:S(2)}) copy-start(bf16[12,12,128,128]{3,2,1,0:T(8,128)(2,1)} %refs_11_.1) | copy-start | bytes 14155780
  0.7 6.6 %collective-permute-start = (bf16[1,128,128]{2,1,0:T(8,128)(2,1)}, bf16[1,128,128]{2,1,0:T(8,128)(2,1)S(1)}, u32[]{:S(2)}, u32[]{:S(2)}) collective-permute-start(bf16[1,128,128]{2,1,0:T(8,128)(2,1)} %block.1), channel_id=1, source_target_pairs={{0,8},{2,10},{4,12},{6,14},{8,0},{10,2},{12,4},{14,6},{1,9},{3,11}... | collective-permute-start | bytes 98312 | tf_op jit(solution)/shard_map/gather_state/ppermute | solution.py:342
  4.8 0.8 %copy-start.5 = (bf16[1,128,128]{2,1,0:T(8,128)(2,1)S(1)}, bf16[1,128,128]{2,1,0:T(8,128)(2,1)}, u32[]{:S(2)}) copy-start(bf16[1,128,128]{2,1,0:T(8,128)(2,1)} %block.1) | copy-start | bytes 98308
  5.6 0.7 %copy-start.6 = (s32[16]{0:T(128)S(1)}, s32[16]{0:T(128)}, u32[]{:S(2)}) copy-start(s32[16]{0:T(128)} %sizes.1) | copy-start | bytes 196
  7.2 6.1 %collective-permute-start.3 = (bf16[2,128,128]{2,1,0:T(8,128)(2,1)S(1)}, bf16[2,128,128]{2,1,0:T(8,128)(2,1)S(1)}, u32[]{:S(2)}, u32[]{:S(2)}) collective-permute-start(bf16[2,128,128]{2,1,0:T(8,128)(2,1)S(1)} %pair.1.refs_0_), channel_id=1, source_target_pairs={{0,6},{2,4},{4,2},{6,0},{8,14},{10,12},{12,10},{14,8},{1,7},{3,5},... | collective-permute-start | bytes 196616 | tf_op jit(solution)/shard_map/gather_state/ppermute | solution.py:342
  9.7 4.7 %collective-permute-start.2 = (bf16[2,128,128]{2,1,0:T(8,128)(2,1)S(1)}, bf16[2,128,128]{2,1,0:T(8,128)(2,1)S(1)}, u32[]{:S(2)}, u32[]{:S(2)}) collective-permute-start(bf16[2,128,128]{2,1,0:T(8,128)(2,1)S(1)} %pair.1.refs_0_), channel_id=1, source_target_pairs={{0,4},{2,6},{4,0},{6,2},{8,12},{10,14},{12,8},{14,10},{1,5},{3,7},... | collective-permute-start | bytes 196616 | tf_op jit(solution)/shard_map/gather_state/ppermute | solution.py:342
  10.4 4.3 %collective-permute-start.1 = (bf16[2,128,128]{2,1,0:T(8,128)(2,1)S(1)}, bf16[2,128,128]{2,1,0:T(8,128)(2,1)S(1)}, u32[]{:S(2)}, u32[]{:S(2)}) collective-permute-start(bf16[2,128,128]{2,1,0:T(8,128)(2,1)S(1)} %pair.1.refs_0_), channel_id=1, source_target_pairs={{0,2},{2,0},{4,6},{6,4},{8,10},{10,8},{12,14},{14,12},{1,3},{3,1},... | collective-permute-start | bytes 196616 | tf_op jit(solution)/shard_map/gather_state/ppermute | solution.py:342
  10.7 5.2 %collective-permute-start.8 = (f32[1,128,128]{2,1,0:T(8,128)S(1)}, f32[1,128,128]{2,1,0:T(8,128)S(1)}, u32[]{:S(2)}, u32[]{:S(2)}) collective-permute-start(f32[1,128,128]{2,1,0:T(8,128)S(1)} %copy-done.2), channel_id=1, source_target_pairs={{0,8},{2,10},{4,12},{6,14},{8,0},{10,2},{12,4},{14,6},{1,9},{3,11}... | collective-permute-start | bytes 196616 | tf_op jit(solution)/shard_map/gather_state/ppermute | solution.py:342
  13.3 2.6 %collective-permute-start.4 = (bf16[2,128,128]{2,1,0:T(8,128)(2,1)S(1)}, bf16[2,128,128]{2,1,0:T(8,128)(2,1)S(1)}, u32[]{:S(2)}, u32[]{:S(2)}) collective-permute-start(bf16[2,128,128]{2,1,0:T(8,128)(2,1)S(1)} %pair.1.refs_0_), channel_id=1, source_target_pairs={{0,1},{1,0},{2,3},{3,2},{4,5},{5,4},{6,7},{7,6},{8,9},{9,8},{10,11... | collective-permute-start | bytes 196616 | tf_op jit(solution)/shard_map/gather_state/ppermute | solution.py:337
  13.3 2.6 %collective-permute-start.7 = (bf16[2,128,128]{2,1,0:T(8,128)(2,1)S(1)}, bf16[2,128,128]{2,1,0:T(8,128)(2,1)S(1)}, u32[]{:S(2)}, u32[]{:S(2)}) collective-permute-start(bf16[2,128,128]{2,1,0:T(8,128)(2,1)S(1)} %collective-permute-done.3.refs_3_), channel_id=1, source_target_pairs={{0,1},{1,0},{2,3},{3,2},{4,5},{5,4},{6,7},{7,6},{8,9},{9,8},{10,11... | collective-permute-start | bytes 196616 | tf_op jit(solution)/shard_map/gather_state/ppermute | solution.py:337
  14.4 1.5 %collective-permute-start.6 = (bf16[2,128,128]{2,1,0:T(8,128)(2,1)S(1)}, bf16[2,128,128]{2,1,0:T(8,128)(2,1)S(1)}, u32[]{:S(2)}, u32[]{:S(2)}) collective-permute-start(bf16[2,128,128]{2,1,0:T(8,128)(2,1)S(1)} %collective-permute-done.2.refs_2_), channel_id=1, source_target_pairs={{0,1},{1,0},{2,3},{3,2},{4,5},{5,4},{6,7},{7,6},{8,9},{9,8},{10,11... | collective-permute-start | bytes 196616 | tf_op jit(solution)/shard_map/gather_state/ppermute | solution.py:337
  14.7 1.3 %collective-permute-start.5 = (bf16[2,128,128]{2,1,0:T(8,128)(2,1)S(1)}, bf16[2,128,128]{2,1,0:T(8,128)(2,1)S(1)}, u32[]{:S(2)}, u32[]{:S(2)}) collective-permute-start(bf16[2,128,128]{2,1,0:T(8,128)(2,1)S(1)} %collective-permute-done.1.refs_1_), channel_id=1, source_target_pairs={{0,1},{1,0},{2,3},{3,2},{4,5},{5,4},{6,7},{7,6},{8,9},{9,8},{10,11... | collective-permute-start | bytes 196616 | tf_op jit(solution)/shard_map/gather_state/ppermute | solution.py:337
  19.9 1.6 %collective-permute-start.9 = (bf16[1040,128]{1,0:T(8,128)(2,1)S(1)}, bf16[1040,128]{1,0:T(8,128)(2,1)S(1)}, u32[]{:S(2)}, u32[]{:S(2)}) collective-permute-start(bf16[1040,128]{1,0:T(8,128)(2,1)S(1)} %get-tuple-element.34), channel_id=1, source_target_pairs={{0,1},{1,0},{2,3},{3,2},{4,5},{5,4},{6,7},{7,6},{8,9},{9,8},{10,11... | collective-permute-start | bytes 798728 | tf_op jit(solution)/shard_map/sum_first/ppermute | solution.py:337
  21.6 4.4 %collective-permute-start.10 = (bf16[272,128]{1,0:T(8,128)(2,1)S(1)}, bf16[272,128]{1,0:T(8,128)(2,1)S(1)}, u32[]{:S(2)}, u32[]{:S(2)}) collective-permute-start(bf16[272,128]{1,0:T(8,128)(2,1)S(1)} %get-tuple-element.37), channel_id=1, source_target_pairs={{0,2},{2,0},{4,6},{6,4},{8,10},{10,8},{12,14},{14,12},{1,3},{3,1},... | collective-permute-start | bytes 208904 | tf_op jit(solution)/shard_map/sum_first/ppermute | solution.py:342
  23.3 5.1 %collective-permute-start.11 = (bf16[272,128]{1,0:T(8,128)(2,1)S(1)}, bf16[272,128]{1,0:T(8,128)(2,1)S(1)}, u32[]{:S(2)}, u32[]{:S(2)}) collective-permute-start(bf16[272,128]{1,0:T(8,128)(2,1)S(1)} %get-tuple-element.38), channel_id=1, source_target_pairs={{0,4},{2,6},{4,0},{6,2},{8,12},{10,14},{12,8},{14,10},{1,5},{3,7},... | collective-permute-start | bytes 208904 | tf_op jit(solution)/shard_map/sum_first/ppermute | solution.py:342
  24.7 5.2 %collective-permute-start.12 = (bf16[272,128]{1,0:T(8,128)(2,1)S(1)}, bf16[272,128]{1,0:T(8,128)(2,1)S(1)}, u32[]{:S(2)}, u32[]{:S(2)}) collective-permute-start(bf16[272,128]{1,0:T(8,128)(2,1)S(1)} %get-tuple-element.39), channel_id=1, source_target_pairs={{0,6},{2,4},{4,2},{6,0},{8,14},{10,12},{12,10},{14,8},{1,7},{3,5},... | collective-permute-start | bytes 208904 | tf_op jit(solution)/shard_map/sum_first/ppermute | solution.py:342
  30.0 6.9 %collective-permute-start.13 = (bf16[400,128]{1,0:T(8,128)(2,1)S(1)}, bf16[400,128]{1,0:T(8,128)(2,1)S(1)}, u32[]{:S(2)}, u32[]{:S(2)}) collective-permute-start(bf16[400,128]{1,0:T(8,128)(2,1)S(1)} %for_far.2), channel_id=1, source_target_pairs={{0,8},{2,10},{4,12},{6,14},{8,0},{10,2},{12,4},{14,6},{1,9},{3,11}... | collective-permute-start | bytes 307208 | tf_op jit(solution)/shard_map/sum_first/ppermute | solution.py:342
  37.0 5.2 %collective-permute-start.16 = (bf16[2,128,128]{2,1,0:T(8,128)(2,1)S(1)}, bf16[2,128,128]{2,1,0:T(8,128)(2,1)S(1)}, u32[]{:S(2)}, u32[]{:S(2)}) collective-permute-start(bf16[2,128,128]{2,1,0:T(8,128)(2,1)S(1)} %get-tuple-element.42.refs_0_), channel_id=1, source_target_pairs={{0,6},{2,4},{4,2},{6,0},{8,14},{10,12},{12,10},{14,8},{1,7},{3,5},... | collective-permute-start | bytes 196616 | tf_op jit(solution)/shard_map/gather_residual/ppermute | solution.py:342
  37.8 4.5 %collective-permute-start.15 = (bf16[2,128,128]{2,1,0:T(8,128)(2,1)S(1)}, bf16[2,128,128]{2,1,0:T(8,128)(2,1)S(1)}, u32[]{:S(2)}, u32[]{:S(2)}) collective-permute-start(bf16[2,128,128]{2,1,0:T(8,128)(2,1)S(1)} %get-tuple-element.42.refs_0_), channel_id=1, source_target_pairs={{0,4},{2,6},{4,0},{6,2},{8,12},{10,14},{12,8},{14,10},{1,5},{3,7},... | collective-permute-start | bytes 196616 | tf_op jit(solution)/shard_map/gather_residual/ppermute | solution.py:342
  39.3 4.3 %collective-permute-start.14 = (bf16[2,128,128]{2,1,0:T(8,128)(2,1)S(1)}, bf16[2,128,128]{2,1,0:T(8,128)(2,1)S(1)}, u32[]{:S(2)}, u32[]{:S(2)}) collective-permute-start(bf16[2,128,128]{2,1,0:T(8,128)(2,1)S(1)} %get-tuple-element.42.refs_0_), channel_id=1, source_target_pairs={{0,2},{2,0},{4,6},{6,4},{8,10},{10,8},{12,14},{14,12},{1,3},{3,1},... | collective-permute-start | bytes 196616 | tf_op jit(solution)/shard_map/gather_residual/ppermute | solution.py:342
  40.6 3.0 %collective-permute-start.17 = (bf16[2,128,128]{2,1,0:T(8,128)(2,1)S(1)}, bf16[2,128,128]{2,1,0:T(8,128)(2,1)S(1)}, u32[]{:S(2)}, u32[]{:S(2)}) collective-permute-start(bf16[2,128,128]{2,1,0:T(8,128)(2,1)S(1)} %get-tuple-element.42.refs_0_), channel_id=1, source_target_pairs={{0,1},{1,0},{2,3},{3,2},{4,5},{5,4},{6,7},{7,6},{8,9},{9,8},{10,11... | collective-permute-start | bytes 196616 | tf_op jit(solution)/shard_map/gather_residual/ppermute | solution.py:337
  42.3 1.4 %collective-permute-start.20 = (bf16[2,128,128]{2,1,0:T(8,128)(2,1)S(1)}, bf16[2,128,128]{2,1,0:T(8,128)(2,1)S(1)}, u32[]{:S(2)}, u32[]{:S(2)}) collective-permute-start(bf16[2,128,128]{2,1,0:T(8,128)(2,1)S(1)} %collective-permute-done.16.refs_3_), channel_id=1, source_target_pairs={{0,1},{1,0},{2,3},{3,2},{4,5},{5,4},{6,7},{7,6},{8,9},{9,8},{10,11... | collective-permute-start | bytes 196616 | tf_op jit(solution)/shard_map/gather_residual/ppermute | solution.py:337
  42.3 1.4 %collective-permute-start.19 = (bf16[2,128,128]{2,1,0:T(8,128)(2,1)S(1)}, bf16[2,128,128]{2,1,0:T(8,128)(2,1)S(1)}, u32[]{:S(2)}, u32[]{:S(2)}) collective-permute-start(bf16[2,128,128]{2,1,0:T(8,128)(2,1)S(1)} %collective-permute-done.15.refs_2_), channel_id=1, source_target_pairs={{0,1},{1,0},{2,3},{3,2},{4,5},{5,4},{6,7},{7,6},{8,9},{9,8},{10,11... | collective-permute-start | bytes 196616 | tf_op jit(solution)/shard_map/gather_residual/ppermute | solution.py:337
  43.6 1.3 %collective-permute-start.18 = (bf16[2,128,128]{2,1,0:T(8,128)(2,1)S(1)}, bf16[2,128,128]{2,1,0:T(8,128)(2,1)S(1)}, u32[]{:S(2)}, u32[]{:S(2)}) collective-permute-start(bf16[2,128,128]{2,1,0:T(8,128)(2,1)S(1)} %collective-permute-done.14.refs_1_), channel_id=1, source_target_pairs={{0,1},{1,0},{2,3},{3,2},{4,5},{5,4},{6,7},{7,6},{8,9},{9,8},{10,11... | collective-permute-start | bytes 196616 | tf_op jit(solution)/shard_map/gather_residual/ppermute | solution.py:337
  48.9 1.6 %collective-permute-start.21 = (bf16[1040,128]{1,0:T(8,128)(2,1)S(1)}, bf16[1040,128]{1,0:T(8,128)(2,1)S(1)}, u32[]{:S(2)}, u32[]{:S(2)}) collective-permute-start(bf16[1040,128]{1,0:T(8,128)(2,1)S(1)} %get-tuple-element.48), channel_id=1, source_target_pairs={{0,1},{1,0},{2,3},{3,2},{4,5},{5,4},{6,7},{7,6},{8,9},{9,8},{10,11... | collective-permute-start | bytes 798728 | tf_op jit(solution)/shard_map/sum_second/ppermute | solution.py:337
  50.6 4.4 %collective-permute-start.22 = (bf16[272,128]{1,0:T(8,128)(2,1)S(1)}, bf16[272,128]{1,0:T(8,128)(2,1)S(1)}, u32[]{:S(2)}, u32[]{:S(2)}) collective-permute-start(bf16[272,128]{1,0:T(8,128)(2,1)S(1)} %get-tuple-element.51), channel_id=1, source_target_pairs={{0,2},{2,0},{4,6},{6,4},{8,10},{10,8},{12,14},{14,12},{1,3},{3,1},... | collective-permute-start | bytes 208904 | tf_op jit(solution)/shard_map/sum_second/ppermute | solution.py:342
  51.9 4.7 %collective-permute-start.23 = (bf16[272,128]{1,0:T(8,128)(2,1)S(1)}, bf16[272,128]{1,0:T(8,128)(2,1)S(1)}, u32[]{:S(2)}, u32[]{:S(2)}) collective-permute-start(bf16[272,128]{1,0:T(8,128)(2,1)S(1)} %get-tuple-element.52), channel_id=1, source_target_pairs={{0,4},{2,6},{4,0},{6,2},{8,12},{10,14},{12,8},{14,10},{1,5},{3,7},... | collective-permute-start | bytes 208904 | tf_op jit(solution)/shard_map/sum_second/ppermute | solution.py:342
  52.0 5.5 %collective-permute-start.24 = (bf16[272,128]{1,0:T(8,128)(2,1)S(1)}, bf16[272,128]{1,0:T(8,128)(2,1)S(1)}, u32[]{:S(2)}, u32[]{:S(2)}) collective-permute-start(bf16[272,128]{1,0:T(8,128)(2,1)S(1)} %get-tuple-element.53), channel_id=1, source_target_pairs={{0,6},{2,4},{4,2},{6,0},{8,14},{10,12},{12,10},{14,8},{1,7},{3,5},... | collective-permute-start | bytes 208904 | tf_op jit(solution)/shard_map/sum_second/ppermute | solution.py:342
  57.6 5.0 %collective-permute-start.25 = (bf16[144,128]{1,0:T(8,128)(2,1)S(1)}, bf16[144,128]{1,0:T(8,128)(2,1)S(1)}, u32[]{:S(2)}, u32[]{:S(2)}) collective-permute-start(bf16[144,128]{1,0:T(8,128)(2,1)S(1)} %for_far.3), channel_id=1, source_target_pairs={{0,8},{2,10},{4,12},{6,14},{8,0},{10,2},{12,4},{14,6},{1,9},{3,11}... | collective-permute-start | bytes 110600 | tf_op jit(solution)/shard_map/sum_second/ppermute | solution.py:342

commit v7 on v6

--- a/solution.py
+++ b/solution.py
@@ -1,3 +1,5 @@
+import functools
+
 import jax
 import jax.numpy as jnp
 from jax import lax
@@ -133,7 +135,7 @@
 def first_kernel(*refs):
     pieces, ins, outs = refs[: 2 * NEAR], refs[2 * NEAR : 2 * NEAR + 5], refs[2 * NEAR + 5 :]
     plan, limits, left, right, _ = ins
-    theirs, acc, wave, flip, sums, rows, places, sem = outs
+    theirs, (acc, wave, flip, sums, rows, places, sem) = outs[:NEAR], outs[NEAR:]
     span, width = pieces[0].shape[0], pieces[0].shape[2]
     chips = NEAR * span
     copy = pltpu.make_async_copy(plan, places, sem)
@@ -158,13 +160,17 @@
     copy.wait()
     apply_blocks(places, wave, left, right, acc, flip)
 
-    def store(j, ray):
-        a, b = acc[j], acc[chips + j]
-        theirs[at(j, width)] = b.astype(BF16)
-        return ray + eight(wave[j].astype(F32) * a + wave[chips + j].astype(F32) * b)
-
-    ray = fold(each(chips, store, jnp.zeros((8, width), F32)))
-    theirs[chips * width :] = tail_of([ray])
+    def store(i, ray):
+        for k in range(NEAR):
+            j = NEAR * i + k
+            a, b = acc[j], acc[chips + j]
+            theirs[k][at(i, width)] = b.astype(BF16)
+            ray = ray + eight(wave[j].astype(F32) * a + wave[chips + j].astype(F32) * b)
+        return ray
+
+    ray = fold(each(span, store, jnp.zeros((8, width), F32)))
+    for part in theirs:
+        part[span * width :] = tail_of([ray])
     sums[0:1] = fold(halve(rows[...])[0])
     sums[1:2] = ray
 
@@ -172,7 +178,7 @@
 def second_kernel(*refs):
     pieces, ins, outs = refs[: 2 * NEAR], refs[2 * NEAR : 2 * NEAR + 6], refs[2 * NEAR + 6 :]
     plan, wave, left, right, first, keep = ins
-    theirs, acc, sums, sigma, vec, places, sems = outs
+    theirs, (acc, sums, sigma, vec, places, sems) = outs[:NEAR], outs[NEAR:]
     span, width = pieces[0].shape[0], pieces[0].shape[2]
     chips = NEAR * span
     copy = pltpu.make_async_copy(plan, places, sems.at[0])
@@ -193,42 +199,46 @@
     copy.wait()
     apply_blocks(places, vec, left, right, acc)
 
-    def store(j, carry):
+    def store(i, carry):
         cross, square = carry
-        a, b = acc[j], acc[chips + j]
-        theirs[at(j, width)] = b.astype(BF16)
-        cross = cross + eight(wave[j].astype(F32) * a + wave[chips + j].astype(F32) * b)
-        square = square + eight(vec[j].astype(F32) * a + vec[chips + j].astype(F32) * b)
+        for k in range(NEAR):
+            j = NEAR * i + k
+            a, b = acc[j], acc[chips + j]
+            theirs[k][at(i, width)] = b.astype(BF16)
+            cross = cross + eight(wave[j].astype(F32) * a + wave[chips + j].astype(F32) * b)
+            square = square + eight(vec[j].astype(F32) * a + vec[chips + j].astype(F32) * b)
         return cross, square
 
     zero = jnp.zeros((8, width), F32)
-    rows = [fold(x) for x in each(chips, store, (zero, zero))]
+    rows = [fold(x) for x in each(span, store, (zero, zero))]
     rows += [keep[2 + i : 3 + i] for i in range(3)]
-    theirs[chips * width :] = tail_of(rows)
+    for part in theirs:
+        part[span * width :] = tail_of(rows)
     for i, row in enumerate(rows):
         sums[i : i + 1] = row
     result.wait()
 
 
-def chip_kernel(start, count, mine, got, sums, base, *sends):
+def chip_kernel(k, start, count, mine, got, sums, out):
     width = mine.shape[2]
-    chips, span = mine.shape[0] // 2, base.shape[0]
-    rows = rows_of(got[chips * width :], count)
+    span = mine.shape[0] // 2 // NEAR
+    rows = rows_of(got[span * width :], count)
     rows = [sums[start + i : start + i + 1] + rows[i] for i in range(count)]
-    tail = tail_of(rows)
 
     def store(i, carry):
-        base[i, 0:width] = mine[NEAR * i] + got[at(NEAR * i, width)].astype(F32)
-        for k, send in enumerate(sends, 1):
-            rel = NEAR * i + k
-            send[at(i, width)] = (mine[rel] + got[at(rel, width)].astype(F32)).astype(BF16)
+        block = mine[NEAR * i + k] + got[at(i, width)].astype(F32)
+        if k:
+            out[at(i, width)] = block.astype(BF16)
+        else:
+            out[i, 0:width] = block
         return carry
 
     each(span, store, 0)
-    for send in sends:
-        send[span * width :] = tail
-    for i, row in enumerate(rows):
-        base[0, width + i : width + i + 1] = row
+    if k:
+        out[span * width :] = tail_of(rows)
+    else:
+        for i, row in enumerate(rows):
+            out[0, width + i : width + i + 1] = row
 
 
 def near_kernel(count, base, *refs):
@@ -354,12 +364,16 @@
 def scatter(theirs, mine, sums, start, count):
     chips, width = mine.shape[0] // 2, mine.shape[2]
     span, wide = chips // NEAR, width + 8
-    sent = [shape(span * width + TAIL, width, dtype=BF16)] * (NEAR - 1)
-    base, *sends = call(
-        lambda *refs: chip_kernel(start, count, *refs), "chip_sum", [VMEM] * 3,
-        [shape(span, wide, width)] + sent, [], (mine, swap(theirs), sums), mine.size,
-    )
-    gots = [flip_chip(send, k) for k, send in enumerate(sends, 1)]
+    gots = [swap(part) for part in theirs[::-1]][::-1]
+    sent = shape(span * width + TAIL, width, dtype=BF16)
+    sends = [
+        call(
+            functools.partial(chip_kernel, k, start, count), "chip_sum", [VMEM] * 3,
+            [sent if k else shape(span, wide, width)], [], (mine, gots[k], sums), mine.size // 4,
+        )[0]
+        for k in range(NEAR)
+    ]
+    base, *gots = [flip_chip(send, k) if k else send for k, send in enumerate(sends)]
     (part,) = call(
         lambda *refs: near_kernel(count, *refs), "near_sum", [VMEM] * NEAR,
         [shape(span, wide, width)], [], (base, *gots), mine.size,
@@ -378,7 +392,8 @@
     near = [VMEM] * (2 * NEAR)
     block = shape(1, width, width)
     sums_of = shape(8, width)
-    after_h = [shape(chips * width + TAIL, width, dtype=BF16), shape(every, width, width)]
+    theirs_of = shape(chips // NEAR * width + TAIL, width, dtype=BF16)
+    after_h = [theirs_of] * NEAR + [shape(every, width, width)]
     vectors = shape(every, width, width, dtype=BF16)
     places = pltpu.SMEM(source.shape, jnp.int32)
 
@@ -401,7 +416,7 @@
         pieces = gather(pair)
         far = flip_chip(precond, NEAR)
     with jax.named_scope("first_sigma"):
-        theirs, mine, wave, flip, sums = call(
+        *theirs, mine, wave, flip, sums = call(
             first_kernel, "first_sigma", near + [HBM] + [VMEM] * 4,
             after_h + [vectors, shape(*right.shape, dtype=BF16), sums_of],
             [pltpu.VMEM((every, 8, width), F32), places, pltpu.SemaphoreType.DMA],
@@ -423,10 +438,10 @@
     with jax.named_scope("gather_residual"):
         pieces = gather(send)
     with jax.named_scope("second_sigma"):
-        theirs, mine, sums, sigma = call(
+        *theirs, mine, sums, sigma = call(
             second_kernel, "second_sigma", near + [HBM] + [VMEM] * 5, after_h + [sums_of, block],
             [pltpu.VMEM((every, width, width), BF16), places, pltpu.SemaphoreType.DMA((2,))],
-            (*pieces, plan, wave, left, flip, first, keep), flops, [VMEM] * 3 + [HBM],
+            (*pieces, plan, wave, left, flip, first, keep), flops, [VMEM] * (NEAR + 2) + [HBM],
         )
     with jax.named_scope("sum_second"):
         part = scatter(theirs, mine, sums, 0, 5)

time: 63.6 us -> 63.4 us (level)
  waiting for transfers between devices: 22.4 us -> 20.2 us
  starting transfers between devices: 29 us -> 31.1 us
    ppermute x10 -> x16, waiting for transfers between devices: 3.92 us -> 1.76 us  [swap(): return lax.ppermute(x, 'core', [(0, 1), (1, 0)])]
    ppermute x10 -> x16, starting transfers between devices: 1.85 us -> 3.48 us  [swap(): return lax.ppermute(x, 'core', [(0, 1), (1, 0)])]
    pallas_call x13 -> x19, Pallas kernels: 9.69 us -> 9.65 us  [call(): pl.pallas_call(kernel, name=name, in_specs=ins, out_specs=out_specs or [V...]
  transfers between devices with their start and end apart: 26 -> 32, of which waited for: 18 -> 18; matrix products, arithmetic and copies ran while one was open for 0% -> 0% of each run, Pallas kernels for 1% -> 1%
where the time goes in v7:
time: 63.4 us; the launch traced here: 63.2 us
  starting transfers between devices  31.1 us (49%)
  waiting for transfers between devices  20.2 us (32%)
  Pallas kernels  9.65 us (15%)
  local copies, waits for them, and re-layouts  1.47 us (2%)
  between operations  0.8 us (1%)
    ppermute x16, starting transfers between devices, flip_chip(): return lax.ppermute(x, 'chip', [(i, i ^ bits) for i in range(chips)])  27.6 us
    ppermute x16, waiting for transfers between devices, flip_chip(): return lax.ppermute(x, 'chip', [(i, i ^ bits) for i in range(chips)])  18.5 us
    pallas_call x19, Pallas kernels, call(): pl.pallas_call(kernel, name=name, in_specs=ins, out_specs=out_specs or [V...  9.65 us
    ppermute x16, starting transfers between devices, swap(): return lax.ppermute(x, 'core', [(0, 1), (1, 0)])  3.48 us
    ppermute x16, waiting for transfers between devices, swap(): return lax.ppermute(x, 'core', [(0, 1), (1, 0)])  1.76 us
    unnamed x14, local copies, waits for them, and re-layouts  1.47 us
  transfers between devices with their start and end apart: 32, of which 18 were waited for; matrix products, arithmetic and copies ran while one was open for 0% of the time, Pallas kernels for 1%

profile of v7, /device:TPU:0, one launch (start us, length us, event | category | flops | bytes accessed | tf_op | source)
XLA Modules:
  0.0 63.2 jit_solution(16482444402926141600)
XLA Ops:
  0.7 4.1 %collective-permute-start = (bf16[1,128,128]{2,1,0:T(8,128)(2,1)}, bf16[1,128,128]{2,1,0:T(8,128)(2,1)S(1)}, u32[]{:S(2)}, u32[]{:S(2)}) collective-permute-start(bf16[1,128,128]{2,1,0:T(8,128)(2,1)} %block.1), channel_id=1, source_target_pairs={{0,8},{2,10},{4,12},{6,14},{8,0},{10,2},{12,4},{14,6},{1,9},{3,11}... | collective-permute-start | bytes 98312 | tf_op jit(solution)/shard_map/gather_state/ppermute | solution.py:352
  4.8 0.8 %copy-done.5 = bf16[1,128,128]{2,1,0:T(8,128)(2,1)S(1)} copy-done((bf16[1,128,128]{2,1,0:T(8,128)(2,1)S(1)}, bf16[1,128,128]{2,1,0:T(8,128)(2,1)}, u32[]{:S(2)}) %copy-start.5) | copy-done | bytes 32792
  5.6 0.7 %copy-done.6 = s32[16]{0:T(128)S(1)} copy-done((s32[16]{0:T(128)S(1)}, s32[16]{0:T(128)}, u32[]{:S(2)}) %copy-start.6) | copy-done | bytes 88
  6.2 0.6 masks.1
  6.8 0.4 collective-permute-done.far
  7.2 2.5 %collective-permute-start.3 = (bf16[2,128,128]{2,1,0:T(8,128)(2,1)S(1)}, bf16[2,128,128]{2,1,0:T(8,128)(2,1)S(1)}, u32[]{:S(2)}, u32[]{:S(2)}) collective-permute-start(bf16[2,128,128]{2,1,0:T(8,128)(2,1)S(1)} %pair.1.refs_0_), channel_id=1, source_target_pairs={{0,6},{2,4},{4,2},{6,0},{8,14},{10,12},{12,10},{14,8},{1,7},{3,5},... | collective-permute-start | bytes 196616 | tf_op jit(solution)/shard_map/gather_state/ppermute | solution.py:352
  9.7 0.7 %collective-permute-start.2 = (bf16[2,128,128]{2,1,0:T(8,128)(2,1)S(1)}, bf16[2,128,128]{2,1,0:T(8,128)(2,1)S(1)}, u32[]{:S(2)}, u32[]{:S(2)}) collective-permute-start(bf16[2,128,128]{2,1,0:T(8,128)(2,1)S(1)} %pair.1.refs_0_), channel_id=1, source_target_pairs={{0,4},{2,6},{4,0},{6,2},{8,12},{10,14},{12,8},{14,10},{1,5},{3,7},... | collective-permute-start | bytes 196616 | tf_op jit(solution)/shard_map/gather_state/ppermute | solution.py:352
  10.4 0.3 collective-permute-start.1
  10.7 2.6 %collective-permute-start.8 = (f32[1,128,128]{2,1,0:T(8,128)S(1)}, f32[1,128,128]{2,1,0:T(8,128)S(1)}, u32[]{:S(2)}, u32[]{:S(2)}) collective-permute-start(f32[1,128,128]{2,1,0:T(8,128)S(1)} %copy-done.2), channel_id=1, source_target_pairs={{0,8},{2,10},{4,12},{6,14},{8,0},{10,2},{12,4},{14,6},{1,9},{3,11}... | collective-permute-start | bytes 196616 | tf_op jit(solution)/shard_map/gather_state/ppermute | solution.py:352
  13.3 0.0 collective-permute-start.4
  13.3 0.0 collective-permute-done.3.refs_3_
  13.3 0.5 collective-permute-start.7
  13.8 0.6 collective-permute-done.2.refs_2_
  14.4 0.0 collective-permute-start.6
  14.4 0.2 collective-permute-done.1.refs_1_
  14.7 0.3 collective-permute-start.5
  15.0 0.9 %collective-permute-done.8.refs_12_.far = f32[1,128,128]{2,1,0:T(8,128)S(1)} collective-permute-done((f32[1,128,128]{2,1,0:T(8,128)S(1)}, f32[1,128,128]{2,1,0:T(8,128)S(1)}, u32[]{:S(2)}, u32[]{:S(2)}) %collective-permute-start.8) | collective-permute-done | bytes 65568 | tf_op jit(solution)/shard_map/gather_state/ppermute | solution.py:352
  15.9 0.0 collective-permute-done.4.refs_4_
  15.9 0.0 collective-permute-done.7.refs_7_
  15.9 0.0 collective-permute-done.6.refs_6_
  15.9 0.0 collective-permute-done.5.refs_5_
  15.9 3.9 %first_sigma.1 = (bf16[272,128]{1,0:T(8,128)(2,1)S(1)}, bf16[272,128]{1,0:T(8,128)(2,1)S(1)}, bf16[272,128]{1,0:T(8,128)(2,1)S(1)}, bf16[272,128]{1,0:T(8,128)(2...) custom-call(bf16[2,128,128]{2,1,0:T(8,128)(2,1)S(1)} %pair.1.refs_0_, ...), custom_call_target="tpu_custom_call" | custom-call | flops 1207959552 | bytes 10035776 | tf_op jit(solution)/shard_map/first_sigma/first_sigma/pallas_call | solution.py:330
  19.8 0.3 collective-permute-start.10
  20.2 0.2 collective-permute-start.12
  20.4 0.3 collective-permute-start.14
  20.7 0.2 collective-permute-start.9
  20.9 0.2 collective-permute-done.10.got
  21.2 1.8 %collective-permute-start.11 = (bf16[272,128]{1,0:T(8,128)(2,1)S(1)}, bf16[272,128]{1,0:T(8,128)(2,1)S(1)}, u32[]{:S(2)}, u32[]{:S(2)}) collective-permute-start(bf16[272,128]{1,0:T(8,128)(2,1)S(1)} %chip_sum.9), channel_id=1, source_target_pairs={{0,2},{2,0},{4,6},{6,4},{8,10},{10,8},{12,14},{14,12},{1,3},{3,1},... | collective-permute-start | bytes 208904 | tf_op jit(solution)/shard_map/sum_first/ppermute | solution.py:352
  23.0 0.0 collective-permute-done.12.got
  23.0 1.4 %collective-permute-start.13 = (bf16[272,128]{1,0:T(8,128)(2,1)S(1)}, bf16[272,128]{1,0:T(8,128)(2,1)S(1)}, u32[]{:S(2)}, u32[]{:S(2)}) collective-permute-start(bf16[272,128]{1,0:T(8,128)(2,1)S(1)} %chip_sum.10), channel_id=1, source_target_pairs={{0,4},{2,6},{4,0},{6,2},{8,12},{10,14},{12,8},{14,10},{1,5},{3,7},... | collective-permute-start | bytes 208904 | tf_op jit(solution)/shard_map/sum_first/ppermute | solution.py:352
  24.5 0.5 collective-permute-start.15
  25.0 0.6 %collective-permute-done.11.refs_1_ = bf16[272,128]{1,0:T(8,128)(2,1)S(1)} collective-permute-done((bf16[272,128]{1,0:T(8,128)(2,1)S(1)}, bf16[272,128]{1,0:T(8,128)(2,1)S(1)}, u32[]{:S(2)}, u32[]{:S(2)}) %collective-permute-start.11) | collective-permute-done | bytes 69664 | tf_op jit(solution)/shard_map/sum_first/ppermute | solution.py:352
  25.6 2.4 %collective-permute-done.13.refs_2_ = bf16[272,128]{1,0:T(8,128)(2,1)S(1)} collective-permute-done((bf16[272,128]{1,0:T(8,128)(2,1)S(1)}, bf16[272,128]{1,0:T(8,128)(2,1)S(1)}, u32[]{:S(2)}, u32[]{:S(2)}) %collective-permute-start.13) | collective-permute-done | bytes 69664 | tf_op jit(solution)/shard_map/sum_first/ppermute | solution.py:352
  28.0 1.7 %collective-permute-done.15.refs_3_ = bf16[272,128]{1,0:T(8,128)(2,1)S(1)} collective-permute-done((bf16[272,128]{1,0:T(8,128)(2,1)S(1)}, bf16[272,128]{1,0:T(8,128)(2,1)S(1)}, u32[]{:S(2)}, u32[]{:S(2)}) %collective-permute-start.15) | collective-permute-done | bytes 69664 | tf_op jit(solution)/shard_map/sum_first/ppermute | solution.py:352
  29.8 3.3 %collective-permute-start.16 = (bf16[400,128]{1,0:T(8,128)(2,1)S(1)}, bf16[400,128]{1,0:T(8,128)(2,1)S(1)}, u32[]{:S(2)}, u32[]{:S(2)}) collective-permute-start(bf16[400,128]{1,0:T(8,128)(2,1)S(1)} %for_far.2), channel_id=1, source_target_pairs={{0,8},{2,10},{4,12},{6,14},{8,0},{10,2},{12,4},{14,6},{1,9},{3,11}... | collective-permute-start | bytes 307208 | tf_op jit(solution)/shard_map/sum_first/ppermute | solution.py:352
  33.1 3.7 %collective-permute-done.16.got = bf16[400,128]{1,0:T(8,128)(2,1)S(1)} collective-permute-done((bf16[400,128]{1,0:T(8,128)(2,1)S(1)}, bf16[400,128]{1,0:T(8,128)(2,1)S(1)}, u32[]{:S(2)}, u32[]{:S(2)}) %collective-permute-start.16) | collective-permute-done | bytes 102432 | tf_op jit(solution)/shard_map/sum_first/ppermute | solution.py:352
  36.8 0.1 residual.1
  36.9 0.7 %collective-permute-start.19 = (bf16[2,128,128]{2,1,0:T(8,128)(2,1)S(1)}, bf16[2,128,128]{2,1,0:T(8,128)(2,1)S(1)}, u32[]{:S(2)}, u32[]{:S(2)}) collective-permute-start(bf16[2,128,128]{2,1,0:T(8,128)(2,1)S(1)} %get-tuple-element.39.refs_0_), channel_id=1, source_target_pairs={{0,6},{2,4},{4,2},{6,0},{8,14},{10,12},{12,10},{14,8},{1,7},{3,5},... | collective-permute-start | bytes 196616 | tf_op jit(solution)/shard_map/gather_residual/ppermute | solution.py:352
  37.6 1.5 %collective-permute-start.18 = (bf16[2,128,128]{2,1,0:T(8,128)(2,1)S(1)}, bf16[2,128,128]{2,1,0:T(8,128)(2,1)S(1)}, u32[]{:S(2)}, u32[]{:S(2)}) collective-permute-start(bf16[2,128,128]{2,1,0:T(8,128)(2,1)S(1)} %get-tuple-element.39.refs_0_), channel_id=1, source_target_pairs={{0,4},{2,6},{4,0},{6,2},{8,12},{10,14},{12,8},{14,10},{1,5},{3,7},... | collective-permute-start | bytes 196616 | tf_op jit(solution)/shard_map/gather_residual/ppermute | solution.py:352
  39.1 1.4 %collective-permute-start.17 = (bf16[2,128,128]{2,1,0:T(8,128)(2,1)S(1)}, bf16[2,128,128]{2,1,0:T(8,128)(2,1)S(1)}, u32[]{:S(2)}, u32[]{:S(2)}) collective-permute-start(bf16[2,128,128]{2,1,0:T(8,128)(2,1)S(1)} %get-tuple-element.39.refs_0_), channel_id=1, source_target_pairs={{0,2},{2,0},{4,6},{6,4},{8,10},{10,8},{12,14},{14,12},{1,3},{3,1},... | collective-permute-start | bytes 196616 | tf_op jit(solution)/shard_map/gather_residual/ppermute | solution.py:352
  40.4 0.0 collective-permute-start.20
  40.4 1.7 %collective-permute-done.19.refs_3_ = bf16[2,128,128]{2,1,0:T(8,128)(2,1)S(1)} collective-permute-done((bf16[2,128,128]{2,1,0:T(8,128)(2,1)S(1)}, bf16[2,128,128]{2,1,0:T(8,128)(2,1)S(1)}, u32[]{:S(2)}, u32[]{:S(2)}) %collective-permute-start.19) | collective-permute-done | bytes 65568 | tf_op jit(solution)/shard_map/gather_residual/ppermute | solution.py:352
  42.1 0.0 collective-permute-start.23
  42.1 0.0 collective-permute-done.18.refs_2_
  42.1 0.5 collective-permute-start.22
  42.6 0.7 %collective-permute-done.17.refs_1_ = bf16[2,128,128]{2,1,0:T(8,128)(2,1)S(1)} collective-permute-done((bf16[2,128,128]{2,1,0:T(8,128)(2,1)S(1)}, bf16[2,128,128]{2,1,0:T(8,128)(2,1)S(1)}, u32[]{:S(2)}, u32[]{:S(2)}) %collective-permute-start.17) | collective-permute-done | bytes 65568 | tf_op jit(solution)/shard_map/gather_residual/ppermute | solution.py:352
  43.4 0.0 collective-permute-done.23.refs_7_
  43.4 0.2 collective-permute-done.22.refs_6_
  43.5 1.1 %collective-permute-done.21.refs_5_ = bf16[2,128,128]{2,1,0:T(8,128)(2,1)S(1)} collective-permute-done((bf16[2,128,128]{2,1,0:T(8,128)(2,1)S(1)}, bf16[2,128,128]{2,1,0:T(8,128)(2,1)S(1)}, u32[]{:S(2)}, u32[]{:S(2)}) %collective-permute-start.21) | collective-permute-done | bytes 65568 | tf_op jit(solution)/shard_map/gather_residual/ppermute | solution.py:347
  44.6 3.9 %second_sigma.1 = (bf16[272,128]{1,0:T(8,128)(2,1)S(1)}, bf16[272,128]{1,0:T(8,128)(2,1)S(1)}, bf16[272,128]{1,0:T(8,128)(2,1)S(1)}, bf16[272,128]{1,0:T(8,128)(...) custom-call(bf16[2,128,128]{2,1,0:T(8,128)(2,1)S(1)} %get-tuple-element.39.refs_0_, ...), custom_call_target="tpu_custom_call" | custom-call | flops 1207959552 | bytes 10555968 | tf_op jit(solution)/shard_map/second_sigma/second_sigma/pallas_call | solution.py:330
  48.5 0.2 collective-permute-start.25
  48.8 0.4 collective-permute-start.27
  49.1 0.2 collective-permute-start.29
  49.3 0.4 collective-permute-start.24
  49.6 0.2 collective-permute-done.25.got
  49.9 1.4 %collective-permute-start.26 = (bf16[272,128]{1,0:T(8,128)(2,1)S(1)}, bf16[272,128]{1,0:T(8,128)(2,1)S(1)}, u32[]{:S(2)}, u32[]{:S(2)}) collective-permute-start(bf16[272,128]{1,0:T(8,128)(2,1)S(1)} %chip_sum.13), channel_id=1, source_target_pairs={{0,2},{2,0},{4,6},{6,4},{8,10},{10,8},{12,14},{14,12},{1,3},{3,1},... | collective-permute-start | bytes 208904 | tf_op jit(solution)/shard_map/sum_second/ppermute | solution.py:352
  51.4 0.4 collective-permute-start.28
  51.8 1.9 %collective-permute-start.30 = (bf16[272,128]{1,0:T(8,128)(2,1)S(1)}, bf16[272,128]{1,0:T(8,128)(2,1)S(1)}, u32[]{:S(2)}, u32[]{:S(2)}) collective-permute-start(bf16[272,128]{1,0:T(8,128)(2,1)S(1)} %chip_sum.15), channel_id=1, source_target_pairs={{0,6},{2,4},{4,2},{6,0},{8,14},{10,12},{12,10},{14,8},{1,7},{3,5},... | collective-permute-start | bytes 208904 | tf_op jit(solution)/shard_map/sum_second/ppermute | solution.py:352
  53.7 0.6 collective-permute-done.26.refs_1_
  54.3 1.9 %collective-permute-done.28.refs_2_ = bf16[272,128]{1,0:T(8,128)(2,1)S(1)} collective-permute-done((bf16[272,128]{1,0:T(8,128)(2,1)S(1)}, bf16[272,128]{1,0:T(8,128)(2,1)S(1)}, u32[]{:S(2)}, u32[]{:S(2)}) %collective-permute-start.28) | collective-permute-done | bytes 69664 | tf_op jit(solution)/shard_map/sum_second/ppermute | solution.py:352
  56.2 1.1 %collective-permute-done.30.refs_3_ = bf16[272,128]{1,0:T(8,128)(2,1)S(1)} collective-permute-done((bf16[272,128]{1,0:T(8,128)(2,1)S(1)}, bf16[272,128]{1,0:T(8,128)(2,1)S(1)}, u32[]{:S(2)}, u32[]{:S(2)}) %collective-permute-start.30) | collective-permute-done | bytes 69664 | tf_op jit(solution)/shard_map/sum_second/ppermute | solution.py:352
  57.3 3.2 %collective-permute-start.31 = (bf16[144,128]{1,0:T(8,128)(2,1)S(1)}, bf16[144,128]{1,0:T(8,128)(2,1)S(1)}, u32[]{:S(2)}, u32[]{:S(2)}) collective-permute-start(bf16[144,128]{1,0:T(8,128)(2,1)S(1)} %for_far.3), channel_id=1, source_target_pairs={{0,8},{2,10},{4,12},{6,14},{8,0},{10,2},{12,4},{14,6},{1,9},{3,11}... | collective-permute-start | bytes 110600 | tf_op jit(solution)/shard_map/sum_second/ppermute | solution.py:352
  60.5 1.9 %collective-permute-done.31.got = bf16[144,128]{1,0:T(8,128)(2,1)S(1)} collective-permute-done((bf16[144,128]{1,0:T(8,128)(2,1)S(1)}, bf16[144,128]{1,0:T(8,128)(2,1)S(1)}, u32[]{:S(2)}, u32[]{:S(2)}) %collective-permute-start.31) | collective-permute-done | bytes 36896 | tf_op jit(solution)/shard_map/sum_second/ppermute | solution.py:352
  62.5 0.7 %outputs.1 = (bf16[1,128,128]{2,1,0:T(8,128)(2,1)}, f32[1,128,128]{2,1,0:T(8,128)}, f32[4]{0:T(128)}) custom-call(f32[2,136,128]{2,1,0:T(8,128)S(1)} %near_sum.3.refs_0_.part, bf16[144,128]{1,0:T(8,128)(2,1)S(1)} %collective-permute-done.31.got, bf16[16,128,128]{2,1,0:T(8,128)(2,1)S(1)} %get-tuple-element.37.wave.refs_9_, ...), custom_call_target="tpu_custom_call" | custom-call | flops 262144 | bytes 966656 | tf_op jit(solution)/shard_map/outputs/outputs/pallas_call | solution.py:330
  (33 shorter events, 0.4 us)
Async XLA Ops:
  0.6 10.1 %copy-start.2 = (f32[1,128,128]{2,1,0:T(8,128)S(1)}, f32[1,128,128]{2,1,0:T(8,128)}, u32[]{:S(2)}) copy-start(f32[1,128,128]{2,1,0:T(8,128)} %precond.1) | copy-start | bytes 196612
  0.6 14.3 %copy-start.4 = (s32[12,12]{1,0:T(8,128)S(1)}, s32[12,12]{1,0:T(8,128)}, u32[]{:S(2)}) copy-start(s32[12,12]{1,0:T(8,128)} %tgt.1) | copy-start | bytes 1732
  0.7 14.3 %copy-start.3 = (s32[12,12]{1,0:T(8,128)S(1)}, s32[12,12]{1,0:T(8,128)}, u32[]{:S(2)}) copy-start(s32[12,12]{1,0:T(8,128)} %src.1) | copy-start | bytes 1732
  0.7 15.3 %copy-start = (bf16[12,12,128,128]{3,2,1,0:T(8,128)(2,1)S(1)}, bf16[12,12,128,128]{3,2,1,0:T(8,128)(2,1)}, u32[]{:S(2)}) copy-start(bf16[12,12,128,128]{3,2,1,0:T(8,128)(2,1)} %refs_10_.3) | copy-start | bytes 14155780
  0.7 15.3 %copy-start.1 = (bf16[12,12,128,128]{3,2,1,0:T(8,128)(2,1)S(1)}, bf16[12,12,128,128]{3,2,1,0:T(8,128)(2,1)}, u32[]{:S(2)}) copy-start(bf16[12,12,128,128]{3,2,1,0:T(8,128)(2,1)} %refs_11_.1) | copy-start | bytes 14155780
  0.7 6.6 %collective-permute-start = (bf16[1,128,128]{2,1,0:T(8,128)(2,1)}, bf16[1,128,128]{2,1,0:T(8,128)(2,1)S(1)}, u32[]{:S(2)}, u32[]{:S(2)}) collective-permute-start(bf16[1,128,128]{2,1,0:T(8,128)(2,1)} %block.1), channel_id=1, source_target_pairs={{0,8},{2,10},{4,12},{6,14},{8,0},{10,2},{12,4},{14,6},{1,9},{3,11}... | collective-permute-start | bytes 98312 | tf_op jit(solution)/shard_map/gather_state/ppermute | solution.py:352
  4.8 0.8 %copy-start.5 = (bf16[1,128,128]{2,1,0:T(8,128)(2,1)S(1)}, bf16[1,128,128]{2,1,0:T(8,128)(2,1)}, u32[]{:S(2)}) copy-start(bf16[1,128,128]{2,1,0:T(8,128)(2,1)} %block.1) | copy-start | bytes 98308
  5.6 0.7 %copy-start.6 = (s32[16]{0:T(128)S(1)}, s32[16]{0:T(128)}, u32[]{:S(2)}) copy-start(s32[16]{0:T(128)} %sizes.1) | copy-start | bytes 196
  7.2 6.1 %collective-permute-start.3 = (bf16[2,128,128]{2,1,0:T(8,128)(2,1)S(1)}, bf16[2,128,128]{2,1,0:T(8,128)(2,1)S(1)}, u32[]{:S(2)}, u32[]{:S(2)}) collective-permute-start(bf16[2,128,128]{2,1,0:T(8,128)(2,1)S(1)} %pair.1.refs_0_), channel_id=1, source_target_pairs={{0,6},{2,4},{4,2},{6,0},{8,14},{10,12},{12,10},{14,8},{1,7},{3,5},... | collective-permute-start | bytes 196616 | tf_op jit(solution)/shard_map/gather_state/ppermute | solution.py:352
  9.7 4.7 %collective-permute-start.2 = (bf16[2,128,128]{2,1,0:T(8,128)(2,1)S(1)}, bf16[2,128,128]{2,1,0:T(8,128)(2,1)S(1)}, u32[]{:S(2)}, u32[]{:S(2)}) collective-permute-start(bf16[2,128,128]{2,1,0:T(8,128)(2,1)S(1)} %pair.1.refs_0_), channel_id=1, source_target_pairs={{0,4},{2,6},{4,0},{6,2},{8,12},{10,14},{12,8},{14,10},{1,5},{3,7},... | collective-permute-start | bytes 196616 | tf_op jit(solution)/shard_map/gather_state/ppermute | solution.py:352
  10.4 4.3 %collective-permute-start.1 = (bf16[2,128,128]{2,1,0:T(8,128)(2,1)S(1)}, bf16[2,128,128]{2,1,0:T(8,128)(2,1)S(1)}, u32[]{:S(2)}, u32[]{:S(2)}) collective-permute-start(bf16[2,128,128]{2,1,0:T(8,128)(2,1)S(1)} %pair.1.refs_0_), channel_id=1, source_target_pairs={{0,2},{2,0},{4,6},{6,4},{8,10},{10,8},{12,14},{14,12},{1,3},{3,1},... | collective-permute-start | bytes 196616 | tf_op jit(solution)/shard_map/gather_state/ppermute | solution.py:352
  10.7 5.2 %collective-permute-start.8 = (f32[1,128,128]{2,1,0:T(8,128)S(1)}, f32[1,128,128]{2,1,0:T(8,128)S(1)}, u32[]{:S(2)}, u32[]{:S(2)}) collective-permute-start(f32[1,128,128]{2,1,0:T(8,128)S(1)} %copy-done.2), channel_id=1, source_target_pairs={{0,8},{2,10},{4,12},{6,14},{8,0},{10,2},{12,4},{14,6},{1,9},{3,11}... | collective-permute-start | bytes 196616 | tf_op jit(solution)/shard_map/gather_state/ppermute | solution.py:352
  13.3 2.6 %collective-permute-start.4 = (bf16[2,128,128]{2,1,0:T(8,128)(2,1)S(1)}, bf16[2,128,128]{2,1,0:T(8,128)(2,1)S(1)}, u32[]{:S(2)}, u32[]{:S(2)}) collective-permute-start(bf16[2,128,128]{2,1,0:T(8,128)(2,1)S(1)} %pair.1.refs_0_), channel_id=1, source_target_pairs={{0,1},{1,0},{2,3},{3,2},{4,5},{5,4},{6,7},{7,6},{8,9},{9,8},{10,11... | collective-permute-start | bytes 196616 | tf_op jit(solution)/shard_map/gather_state/ppermute | solution.py:347
  13.3 2.6 %collective-permute-start.7 = (bf16[2,128,128]{2,1,0:T(8,128)(2,1)S(1)}, bf16[2,128,128]{2,1,0:T(8,128)(2,1)S(1)}, u32[]{:S(2)}, u32[]{:S(2)}) collective-permute-start(bf16[2,128,128]{2,1,0:T(8,128)(2,1)S(1)} %collective-permute-done.3.refs_3_), channel_id=1, source_target_pairs={{0,1},{1,0},{2,3},{3,2},{4,5},{5,4},{6,7},{7,6},{8,9},{9,8},{10,11... | collective-permute-start | bytes 196616 | tf_op jit(solution)/shard_map/gather_state/ppermute | solution.py:347
  14.4 1.5 %collective-permute-start.6 = (bf16[2,128,128]{2,1,0:T(8,128)(2,1)S(1)}, bf16[2,128,128]{2,1,0:T(8,128)(2,1)S(1)}, u32[]{:S(2)}, u32[]{:S(2)}) collective-permute-start(bf16[2,128,128]{2,1,0:T(8,128)(2,1)S(1)} %collective-permute-done.2.refs_2_), channel_id=1, source_target_pairs={{0,1},{1,0},{2,3},{3,2},{4,5},{5,4},{6,7},{7,6},{8,9},{9,8},{10,11... | collective-permute-start | bytes 196616 | tf_op jit(solution)/shard_map/gather_state/ppermute | solution.py:347
  14.7 1.3 %collective-permute-start.5 = (bf16[2,128,128]{2,1,0:T(8,128)(2,1)S(1)}, bf16[2,128,128]{2,1,0:T(8,128)(2,1)S(1)}, u32[]{:S(2)}, u32[]{:S(2)}) collective-permute-start(bf16[2,128,128]{2,1,0:T(8,128)(2,1)S(1)} %collective-permute-done.1.refs_1_), channel_id=1, source_target_pairs={{0,1},{1,0},{2,3},{3,2},{4,5},{5,4},{6,7},{7,6},{8,9},{9,8},{10,11... | collective-permute-start | bytes 196616 | tf_op jit(solution)/shard_map/gather_state/ppermute | solution.py:347
  19.8 1.3 %collective-permute-start.10 = (bf16[272,128]{1,0:T(8,128)(2,1)S(1)}, bf16[272,128]{1,0:T(8,128)(2,1)S(1)}, u32[]{:S(2)}, u32[]{:S(2)}) collective-permute-start(bf16[272,128]{1,0:T(8,128)(2,1)S(1)} %get-tuple-element.34), channel_id=1, source_target_pairs={{0,1},{1,0},{2,3},{3,2},{4,5},{5,4},{6,7},{7,6},{8,9},{9,8},{10,11... | collective-permute-start | bytes 208904 | tf_op jit(solution)/shard_map/sum_first/ppermute | solution.py:347
  20.2 2.8 %collective-permute-start.12 = (bf16[272,128]{1,0:T(8,128)(2,1)S(1)}, bf16[272,128]{1,0:T(8,128)(2,1)S(1)}, u32[]{:S(2)}, u32[]{:S(2)}) collective-permute-start(bf16[272,128]{1,0:T(8,128)(2,1)S(1)} %get-tuple-element.35), channel_id=1, source_target_pairs={{0,1},{1,0},{2,3},{3,2},{4,5},{5,4},{6,7},{7,6},{8,9},{9,8},{10,11... | collective-permute-start | bytes 208904 | tf_op jit(solution)/shard_map/sum_first/ppermute | solution.py:347
  20.4 4.0 %collective-permute-start.14 = (bf16[272,128]{1,0:T(8,128)(2,1)S(1)}, bf16[272,128]{1,0:T(8,128)(2,1)S(1)}, u32[]{:S(2)}, u32[]{:S(2)}) collective-permute-start(bf16[272,128]{1,0:T(8,128)(2,1)S(1)} %get-tuple-element.36), channel_id=1, source_target_pairs={{0,1},{1,0},{2,3},{3,2},{4,5},{5,4},{6,7},{7,6},{8,9},{9,8},{10,11... | collective-permute-start | bytes 208904 | tf_op jit(solution)/shard_map/sum_first/ppermute | solution.py:347
  20.7 4.3 %collective-permute-start.9 = (bf16[272,128]{1,0:T(8,128)(2,1)S(1)}, bf16[272,128]{1,0:T(8,128)(2,1)S(1)}, u32[]{:S(2)}, u32[]{:S(2)}) collective-permute-start(bf16[272,128]{1,0:T(8,128)(2,1)S(1)} %get-tuple-element.32), channel_id=1, source_target_pairs={{0,1},{1,0},{2,3},{3,2},{4,5},{5,4},{6,7},{7,6},{8,9},{9,8},{10,11... | collective-permute-start | bytes 208904 | tf_op jit(solution)/shard_map/sum_first/ppermute | solution.py:347
  21.2 4.4 %collective-permute-start.11 = (bf16[272,128]{1,0:T(8,128)(2,1)S(1)}, bf16[272,128]{1,0:T(8,128)(2,1)S(1)}, u32[]{:S(2)}, u32[]{:S(2)}) collective-permute-start(bf16[272,128]{1,0:T(8,128)(2,1)S(1)} %chip_sum.9), channel_id=1, source_target_pairs={{0,2},{2,0},{4,6},{6,4},{8,10},{10,8},{12,14},{14,12},{1,3},{3,1},... | collective-permute-start | bytes 208904 | tf_op jit(solution)/shard_map/sum_first/ppermute | solution.py:352
  23.0 5.0 %collective-permute-start.13 = (bf16[272,128]{1,0:T(8,128)(2,1)S(1)}, bf16[272,128]{1,0:T(8,128)(2,1)S(1)}, u32[]{:S(2)}, u32[]{:S(2)}) collective-permute-start(bf16[272,128]{1,0:T(8,128)(2,1)S(1)} %chip_sum.10), channel_id=1, source_target_pairs={{0,4},{2,6},{4,0},{6,2},{8,12},{10,14},{12,8},{14,10},{1,5},{3,7},... | collective-permute-start | bytes 208904 | tf_op jit(solution)/shard_map/sum_first/ppermute | solution.py:352
  24.5 5.3 %collective-permute-start.15 = (bf16[272,128]{1,0:T(8,128)(2,1)S(1)}, bf16[272,128]{1,0:T(8,128)(2,1)S(1)}, u32[]{:S(2)}, u32[]{:S(2)}) collective-permute-start(bf16[272,128]{1,0:T(8,128)(2,1)S(1)} %chip_sum.11), channel_id=1, source_target_pairs={{0,6},{2,4},{4,2},{6,0},{8,14},{10,12},{12,10},{14,8},{1,7},{3,5},... | collective-permute-start | bytes 208904 | tf_op jit(solution)/shard_map/sum_first/ppermute | solution.py:352
  29.8 7.0 %collective-permute-start.16 = (bf16[400,128]{1,0:T(8,128)(2,1)S(1)}, bf16[400,128]{1,0:T(8,128)(2,1)S(1)}, u32[]{:S(2)}, u32[]{:S(2)}) collective-permute-start(bf16[400,128]{1,0:T(8,128)(2,1)S(1)} %for_far.2), channel_id=1, source_target_pairs={{0,8},{2,10},{4,12},{6,14},{8,0},{10,2},{12,4},{14,6},{1,9},{3,11}... | collective-permute-start | bytes 307208 | tf_op jit(solution)/shard_map/sum_first/ppermute | solution.py:352
  36.9 5.2 %collective-permute-start.19 = (bf16[2,128,128]{2,1,0:T(8,128)(2,1)S(1)}, bf16[2,128,128]{2,1,0:T(8,128)(2,1)S(1)}, u32[]{:S(2)}, u32[]{:S(2)}) collective-permute-start(bf16[2,128,128]{2,1,0:T(8,128)(2,1)S(1)} %get-tuple-element.39.refs_0_), channel_id=1, source_target_pairs={{0,6},{2,4},{4,2},{6,0},{8,14},{10,12},{12,10},{14,8},{1,7},{3,5},... | collective-permute-start | bytes 196616 | tf_op jit(solution)/shard_map/gather_residual/ppermute | solution.py:352
  37.6 4.5 %collective-permute-start.18 = (bf16[2,128,128]{2,1,0:T(8,128)(2,1)S(1)}, bf16[2,128,128]{2,1,0:T(8,128)(2,1)S(1)}, u32[]{:S(2)}, u32[]{:S(2)}) collective-permute-start(bf16[2,128,128]{2,1,0:T(8,128)(2,1)S(1)} %get-tuple-element.39.refs_0_), channel_id=1, source_target_pairs={{0,4},{2,6},{4,0},{6,2},{8,12},{10,14},{12,8},{14,10},{1,5},{3,7},... | collective-permute-start | bytes 196616 | tf_op jit(solution)/shard_map/gather_residual/ppermute | solution.py:352
  39.1 4.3 %collective-permute-start.17 = (bf16[2,128,128]{2,1,0:T(8,128)(2,1)S(1)}, bf16[2,128,128]{2,1,0:T(8,128)(2,1)S(1)}, u32[]{:S(2)}, u32[]{:S(2)}) collective-permute-start(bf16[2,128,128]{2,1,0:T(8,128)(2,1)S(1)} %get-tuple-element.39.refs_0_), channel_id=1, source_target_pairs={{0,2},{2,0},{4,6},{6,4},{8,10},{10,8},{12,14},{14,12},{1,3},{3,1},... | collective-permute-start | bytes 196616 | tf_op jit(solution)/shard_map/gather_residual/ppermute | solution.py:352
  40.4 2.9 %collective-permute-start.20 = (bf16[2,128,128]{2,1,0:T(8,128)(2,1)S(1)}, bf16[2,128,128]{2,1,0:T(8,128)(2,1)S(1)}, u32[]{:S(2)}, u32[]{:S(2)}) collective-permute-start(bf16[2,128,128]{2,1,0:T(8,128)(2,1)S(1)} %get-tuple-element.39.refs_0_), channel_id=1, source_target_pairs={{0,1},{1,0},{2,3},{3,2},{4,5},{5,4},{6,7},{7,6},{8,9},{9,8},{10,11... | collective-permute-start | bytes 196616 | tf_op jit(solution)/shard_map/gather_residual/ppermute | solution.py:347
  42.1 1.3 %collective-permute-start.23 = (bf16[2,128,128]{2,1,0:T(8,128)(2,1)S(1)}, bf16[2,128,128]{2,1,0:T(8,128)(2,1)S(1)}, u32[]{:S(2)}, u32[]{:S(2)}) collective-permute-start(bf16[2,128,128]{2,1,0:T(8,128)(2,1)S(1)} %collective-permute-done.19.refs_3_), channel_id=1, source_target_pairs={{0,1},{1,0},{2,3},{3,2},{4,5},{5,4},{6,7},{7,6},{8,9},{9,8},{10,11... | collective-permute-start | bytes 196616 | tf_op jit(solution)/shard_map/gather_residual/ppermute | solution.py:347
  42.1 1.4 %collective-permute-start.22 = (bf16[2,128,128]{2,1,0:T(8,128)(2,1)S(1)}, bf16[2,128,128]{2,1,0:T(8,128)(2,1)S(1)}, u32[]{:S(2)}, u32[]{:S(2)}) collective-permute-start(bf16[2,128,128]{2,1,0:T(8,128)(2,1)S(1)} %collective-permute-done.18.refs_2_), channel_id=1, source_target_pairs={{0,1},{1,0},{2,3},{3,2},{4,5},{5,4},{6,7},{7,6},{8,9},{9,8},{10,11... | collective-permute-start | bytes 196616 | tf_op jit(solution)/shard_map/gather_residual/ppermute | solution.py:347
  43.4 1.3 %collective-permute-start.21 = (bf16[2,128,128]{2,1,0:T(8,128)(2,1)S(1)}, bf16[2,128,128]{2,1,0:T(8,128)(2,1)S(1)}, u32[]{:S(2)}, u32[]{:S(2)}) collective-permute-start(bf16[2,128,128]{2,1,0:T(8,128)(2,1)S(1)} %collective-permute-done.17.refs_1_), channel_id=1, source_target_pairs={{0,1},{1,0},{2,3},{3,2},{4,5},{5,4},{6,7},{7,6},{8,9},{9,8},{10,11... | collective-permute-start | bytes 196616 | tf_op jit(solution)/shard_map/gather_residual/ppermute | solution.py:347
  48.5 1.3 %collective-permute-start.25 = (bf16[272,128]{1,0:T(8,128)(2,1)S(1)}, bf16[272,128]{1,0:T(8,128)(2,1)S(1)}, u32[]{:S(2)}, u32[]{:S(2)}) collective-permute-start(bf16[272,128]{1,0:T(8,128)(2,1)S(1)} %get-tuple-element.47), channel_id=1, source_target_pairs={{0,1},{1,0},{2,3},{3,2},{4,5},{5,4},{6,7},{7,6},{8,9},{9,8},{10,11... | collective-permute-start | bytes 208904 | tf_op jit(solution)/shard_map/sum_second/ppermute | solution.py:347
  48.8 2.6 %collective-permute-start.27 = (bf16[272,128]{1,0:T(8,128)(2,1)S(1)}, bf16[272,128]{1,0:T(8,128)(2,1)S(1)}, u32[]{:S(2)}, u32[]{:S(2)}) collective-permute-start(bf16[272,128]{1,0:T(8,128)(2,1)S(1)} %get-tuple-element.48), channel_id=1, source_target_pairs={{0,1},{1,0},{2,3},{3,2},{4,5},{5,4},{6,7},{7,6},{8,9},{9,8},{10,11... | collective-permute-start | bytes 208904 | tf_op jit(solution)/shard_map/sum_second/ppermute | solution.py:347
  49.1 2.6 %collective-permute-start.29 = (bf16[272,128]{1,0:T(8,128)(2,1)S(1)}, bf16[272,128]{1,0:T(8,128)(2,1)S(1)}, u32[]{:S(2)}, u32[]{:S(2)}) collective-permute-start(bf16[272,128]{1,0:T(8,128)(2,1)S(1)} %get-tuple-element.49), channel_id=1, source_target_pairs={{0,1},{1,0},{2,3},{3,2},{4,5},{5,4},{6,7},{7,6},{8,9},{9,8},{10,11... | collective-permute-start | bytes 208904 | tf_op jit(solution)/shard_map/sum_second/ppermute | solution.py:347
  49.3 4.4 %collective-permute-start.24 = (bf16[272,128]{1,0:T(8,128)(2,1)S(1)}, bf16[272,128]{1,0:T(8,128)(2,1)S(1)}, u32[]{:S(2)}, u32[]{:S(2)}) collective-permute-start(bf16[272,128]{1,0:T(8,128)(2,1)S(1)} %get-tuple-element.45), channel_id=1, source_target_pairs={{0,1},{1,0},{2,3},{3,2},{4,5},{5,4},{6,7},{7,6},{8,9},{9,8},{10,11... | collective-permute-start | bytes 208904 | tf_op jit(solution)/shard_map/sum_second/ppermute | solution.py:347
  49.9 4.4 %collective-permute-start.26 = (bf16[272,128]{1,0:T(8,128)(2,1)S(1)}, bf16[272,128]{1,0:T(8,128)(2,1)S(1)}, u32[]{:S(2)}, u32[]{:S(2)}) collective-permute-start(bf16[272,128]{1,0:T(8,128)(2,1)S(1)} %chip_sum.13), channel_id=1, source_target_pairs={{0,2},{2,0},{4,6},{6,4},{8,10},{10,8},{12,14},{14,12},{1,3},{3,1},... | collective-permute-start | bytes 208904 | tf_op jit(solution)/shard_map/sum_second/ppermute | solution.py:352
  51.4 4.8 %collective-permute-start.28 = (bf16[272,128]{1,0:T(8,128)(2,1)S(1)}, bf16[272,128]{1,0:T(8,128)(2,1)S(1)}, u32[]{:S(2)}, u32[]{:S(2)}) collective-permute-start(bf16[272,128]{1,0:T(8,128)(2,1)S(1)} %chip_sum.14), channel_id=1, source_target_pairs={{0,4},{2,6},{4,0},{6,2},{8,12},{10,14},{12,8},{14,10},{1,5},{3,7},... | collective-permute-start | bytes 208904 | tf_op jit(solution)/shard_map/sum_second/ppermute | solution.py:352
  51.8 5.5 %collective-permute-start.30 = (bf16[272,128]{1,0:T(8,128)(2,1)S(1)}, bf16[272,128]{1,0:T(8,128)(2,1)S(1)}, u32[]{:S(2)}, u32[]{:S(2)}) collective-permute-start(bf16[272,128]{1,0:T(8,128)(2,1)S(1)} %chip_sum.15), channel_id=1, source_target_pairs={{0,6},{2,4},{4,2},{6,0},{8,14},{10,12},{12,10},{14,8},{1,7},{3,5},... | collective-permute-start | bytes 208904 | tf_op jit(solution)/shard_map/sum_second/ppermute | solution.py:352
  57.3 5.2 %collective-permute-start.31 = (bf16[144,128]{1,0:T(8,128)(2,1)S(1)}, bf16[144,128]{1,0:T(8,128)(2,1)S(1)}, u32[]{:S(2)}, u32[]{:S(2)}) collective-permute-start(bf16[144,128]{1,0:T(8,128)(2,1)S(1)} %for_far.3), channel_id=1, source_target_pairs={{0,8},{2,10},{4,12},{6,14},{8,0},{10,2},{12,4},{14,6},{1,9},{3,11}... | collective-permute-start | bytes 110600 | tf_op jit(solution)/shard_map/sum_second/ppermute | solution.py:352

commit v8 on v6

--- a/solution.py
+++ b/solution.py
@@ -11,6 +11,7 @@
 TAIL = 16
 LIMIT = 36 << 20
 LONG = 10**11
+TINY = 1e-30
 NEAR = 4
 
 
@@ -165,8 +166,7 @@
 
     ray = fold(each(chips, store, jnp.zeros((8, width), F32)))
     theirs[chips * width :] = tail_of([ray])
-    sums[0:1] = fold(halve(rows[...])[0])
-    sums[1:2] = ray
+    sums[0:1] = ray
 
 
 def second_kernel(*refs):
@@ -250,14 +250,22 @@
     each(span, store, 0)
 
 
-def both_kernel(count, part, out):
+def norm_kernel(rows, norms):
+    norms[0:1] = total(fold(halve(rows[...])[0]))
+    for i in range(2):
+        norms[1 + i : 2 + i] = 1.0 / jnp.maximum(total(fold(rows[NEAR * i])), TINY)
+
+
+def both_kernel(part, wave, norms, out):
     width = part.shape[2]
-    block = part[1, 0:width]
-    high = block.astype(BF16)
-    out[at(0, width)] = high
-    out[at(1, width)] = (block - high.astype(F32)).astype(BF16)
-    out[at(2, width)] = part[0, 0:width].astype(BF16)
-    out[3 * width :] = tail_of([part[0, width + i : width + i + 1] for i in range(count)])
+    rows = [part[0, width : width + 1]]
+    for i in range(2):
+        own = wave[NEAR * (1 - i)].astype(F32)
+        block = part[1 - i, 0:width]
+        share = total(fold(block * own)) * norms[2 - i : 3 - i]
+        out[at(i, width)] = (block - share * own).astype(BF16)
+        rows.append(share)
+    out[2 * width :] = tail_of(rows)
 
 
 def far_kernel(count, part, out):
@@ -266,24 +274,21 @@
     out[width:] = tail_of([part[0, width + i : width + i + 1] for i in range(count)])
 
 
-def residual_kernel(part, got, wave, inside, precond, far, sums, sigma, resid, send, keep):
+def residual_kernel(part, got, wave, inside, precond, far, norms, sigma, resid, send, keep):
     width = part.shape[2]
-    (ray,) = rows_of(got[3 * width :], 1)
-    norm, ray = total(sums[0:1]), total(part[0, width : width + 1] + ray)
+    ray, *shares = rows_of(got[2 * width :], 3)
+    norm, ray = norms[0:1], total(part[0, width : width + 1] + ray)
     energy = ray / norm
-
-    def piece(i):
-        return got[at(i, width)].astype(F32)
-
-    own = wave[0].astype(F32)
-    first = (part[0, 0:width] + (piece(0) + piece(1))) * inside[0]
+    own, other = wave[0].astype(F32), wave[NEAR].astype(F32)
+    first = part[0, 0:width] + (got[at(0, width)].astype(F32) + shares[0] * own)
+    first = first * inside[0]
     q = precond[0] * (first - energy * own)
     low = q.astype(BF16)
     sigma[0] = first
     resid[0] = q
     send[0] = low
-    there = (part[1, 0:width] + piece(2)) * inside[1]
-    send[1] = (far[0] * (there - energy * wave[NEAR].astype(F32))).astype(BF16)
+    there = part[1, 0:width] + (got[at(1, width)].astype(F32) + shares[1] * other)
+    send[1] = (far[0] * (there * inside[1] - energy * other)).astype(BF16)
     rows = (norm, ray, fold(own * q), fold(low.astype(F32) * first), fold(q * q))
     for i, row in enumerate(rows):
         keep[i : i + 1] = row
@@ -401,24 +406,25 @@
         pieces = gather(pair)
         far = flip_chip(precond, NEAR)
     with jax.named_scope("first_sigma"):
-        theirs, mine, wave, flip, sums = call(
+        theirs, mine, wave, flip, sums, rows = call(
             first_kernel, "first_sigma", near + [HBM] + [VMEM] * 4,
-            after_h + [vectors, shape(*right.shape, dtype=BF16), sums_of],
-            [pltpu.VMEM((every, 8, width), F32), places, pltpu.SemaphoreType.DMA],
+            after_h + [vectors, shape(*right.shape, dtype=BF16), sums_of, shape(every, 8, width)],
+            [places, pltpu.SemaphoreType.DMA],
             (*pieces, plan, limits, left, right, far), flops,
         )
     with jax.named_scope("sum_first"):
-        part = scatter(theirs, mine, sums, 1, 1)
+        (norms,) = call(norm_kernel, "norms", [VMEM], [sums_of], [], (rows,), rows.size)
+        part = scatter(theirs, mine, sums, 0, 1)
         (both,) = call(
-            lambda *refs: both_kernel(1, *refs), "for_far", [VMEM],
-            [shape(3 * width + TAIL, width, dtype=BF16)], [], (part,), part.size,
+            both_kernel, "for_far", [VMEM] * 3, [shape(2 * width + TAIL, width, dtype=BF16)], [],
+            (part, wave, norms), part.size,
         )
         got = flip_chip(both, NEAR)
     with jax.named_scope("residual"):
         first, resid, send, keep = call(
             residual_kernel, "residual", [VMEM] * 7,
             [block, block, shape(2, width, width, dtype=BF16), sums_of],
-            [], (part, got, wave, inside, precond, far, sums), mine.size,
+            [], (part, got, wave, inside, precond, far, norms), mine.size,
         )
     with jax.named_scope("gather_residual"):
         pieces = gather(send)

time: 63.6 us -> 63 us (level)
    pallas_call x13 -> x14, Pallas kernels: 9.69 us -> 10 us  [call(): pl.pallas_call(kernel, name=name, in_specs=ins, out_specs=out_specs or [V...]
where the time goes in v8:
time: 63 us; the launch traced here: 62.8 us
  starting transfers between devices  28.6 us (45%)
  waiting for transfers between devices  21.9 us (35%)
  Pallas kernels  10 us (16%)
  local copies, waits for them, and re-layouts  1.47 us (2%)
  between operations  0.77 us (1%)
    ppermute x16, starting transfers between devices, flip_chip(): return lax.ppermute(x, 'chip', [(i, i ^ bits) for i in range(chips)])  26.7 us
    ppermute x16, waiting for transfers between devices, flip_chip(): return lax.ppermute(x, 'chip', [(i, i ^ bits) for i in range(chips)])  18 us
    pallas_call x14, Pallas kernels, call(): pl.pallas_call(kernel, name=name, in_specs=ins, out_specs=out_specs or [V...  10 us
    ppermute x10, waiting for transfers between devices, swap(): return lax.ppermute(x, 'core', [(0, 1), (1, 0)])  3.92 us
    ppermute x10, starting transfers between devices, swap(): return lax.ppermute(x, 'core', [(0, 1), (1, 0)])  1.87 us
    unnamed x14, local copies, waits for them, and re-layouts  1.47 us
  transfers between devices with their start and end apart: 26, of which 18 were waited for; matrix products, arithmetic and copies ran while one was open for 0% of the time, Pallas kernels for 1%

profile of v8, /device:TPU:0, one launch (start us, length us, event | category | flops | bytes accessed | tf_op | source)
XLA Modules:
  0.0 62.8 jit_solution(16414089881409828598)
XLA Ops:
  0.7 4.1 %collective-permute-start = (bf16[1,128,128]{2,1,0:T(8,128)(2,1)}, bf16[1,128,128]{2,1,0:T(8,128)(2,1)S(1)}, u32[]{:S(2)}, u32[]{:S(2)}) collective-permute-start(bf16[1,128,128]{2,1,0:T(8,128)(2,1)} %block.1), channel_id=1, source_target_pairs={{0,8},{2,10},{4,12},{6,14},{8,0},{10,2},{12,4},{14,6},{1,9},{3,11}... | collective-permute-start | bytes 98312 | tf_op jit(solution)/shard_map/gather_state/ppermute | solution.py:347
  4.8 0.8 %copy-done.5 = bf16[1,128,128]{2,1,0:T(8,128)(2,1)S(1)} copy-done((bf16[1,128,128]{2,1,0:T(8,128)(2,1)S(1)}, bf16[1,128,128]{2,1,0:T(8,128)(2,1)}, u32[]{:S(2)}) %copy-start.5) | copy-done | bytes 32792
  5.6 0.7 %copy-done.6 = s32[16]{0:T(128)S(1)} copy-done((s32[16]{0:T(128)S(1)}, s32[16]{0:T(128)}, u32[]{:S(2)}) %copy-start.6) | copy-done | bytes 88
  6.2 0.6 masks.1
  6.8 0.4 collective-permute-done.far
  7.2 2.5 %collective-permute-start.3 = (bf16[2,128,128]{2,1,0:T(8,128)(2,1)S(1)}, bf16[2,128,128]{2,1,0:T(8,128)(2,1)S(1)}, u32[]{:S(2)}, u32[]{:S(2)}) collective-permute-start(bf16[2,128,128]{2,1,0:T(8,128)(2,1)S(1)} %pair.1.refs_0_), channel_id=1, source_target_pairs={{0,6},{2,4},{4,2},{6,0},{8,14},{10,12},{12,10},{14,8},{1,7},{3,5},... | collective-permute-start | bytes 196616 | tf_op jit(solution)/shard_map/gather_state/ppermute | solution.py:347
  9.7 0.7 %collective-permute-start.2 = (bf16[2,128,128]{2,1,0:T(8,128)(2,1)S(1)}, bf16[2,128,128]{2,1,0:T(8,128)(2,1)S(1)}, u32[]{:S(2)}, u32[]{:S(2)}) collective-permute-start(bf16[2,128,128]{2,1,0:T(8,128)(2,1)S(1)} %pair.1.refs_0_), channel_id=1, source_target_pairs={{0,4},{2,6},{4,0},{6,2},{8,12},{10,14},{12,8},{14,10},{1,5},{3,7},... | collective-permute-start | bytes 196616 | tf_op jit(solution)/shard_map/gather_state/ppermute | solution.py:347
  10.4 0.3 collective-permute-start.1
  10.7 0.0 copy-done.2
  10.7 2.6 %collective-permute-start.8 = (f32[1,128,128]{2,1,0:T(8,128)S(1)}, f32[1,128,128]{2,1,0:T(8,128)S(1)}, u32[]{:S(2)}, u32[]{:S(2)}) collective-permute-start(f32[1,128,128]{2,1,0:T(8,128)S(1)} %copy-done.2), channel_id=1, source_target_pairs={{0,8},{2,10},{4,12},{6,14},{8,0},{10,2},{12,4},{14,6},{1,9},{3,11}... | collective-permute-start | bytes 196616 | tf_op jit(solution)/shard_map/gather_state/ppermute | solution.py:347
  13.3 0.0 collective-permute-start.4
  13.3 0.0 collective-permute-done.3.refs_3_
  13.3 0.5 collective-permute-start.7
  13.8 0.6 collective-permute-done.2.refs_2_
  14.4 0.0 collective-permute-start.6
  14.4 0.2 collective-permute-done.1.refs_1_
  14.7 0.3 collective-permute-start.5
  15.0 0.9 %collective-permute-done.8.refs_12_.far = f32[1,128,128]{2,1,0:T(8,128)S(1)} collective-permute-done((f32[1,128,128]{2,1,0:T(8,128)S(1)}, f32[1,128,128]{2,1,0:T(8,128)S(1)}, u32[]{:S(2)}, u32[]{:S(2)}) %collective-permute-start.8) | collective-permute-done | bytes 65568 | tf_op jit(solution)/shard_map/gather_state/ppermute | solution.py:347
  15.9 0.0 collective-permute-done.4.refs_4_
  15.9 0.0 collective-permute-done.7.refs_7_
  15.9 0.0 collective-permute-done.6.refs_6_
  15.9 0.0 collective-permute-done.5.refs_5_
  15.9 4.1 %first_sigma.1 = (bf16[1040,128]{1,0:T(8,128)(2,1)S(1)}, f32[16,128,128]{2,1,0:T(8,128)S(1)}, bf16[16,128,128]{2,1,0:T(8,128)(2,1)S(1)}, bf16[12,12,128,128]{3,2...) custom-call(bf16[2,128,128]{2,1,0:T(8,128)(2,1)S(1)} %pair.1.refs_0_, ...), custom_call_target="tpu_custom_call" | custom-call | flops 1207959552 | bytes 10035776 | tf_op jit(solution)/shard_map/first_sigma/first_sigma/pallas_call | solution.py:325
  20.0 0.3 collective-permute-start.9
  20.4 1.3 %collective-permute-done.9.refs_1_ = bf16[1040,128]{1,0:T(8,128)(2,1)S(1)} collective-permute-done((bf16[1040,128]{1,0:T(8,128)(2,1)S(1)}, bf16[1040,128]{1,0:T(8,128)(2,1)S(1)}, u32[]{:S(2)}, u32[]{:S(2)}) %collective-permute-start.9) | collective-permute-done | bytes 266272 | tf_op jit(solution)/shard_map/sum_first/ppermute | solution.py:342
  21.7 0.1 chip_sum.2
  21.7 1.8 %collective-permute-start.10 = (bf16[272,128]{1,0:T(8,128)(2,1)S(1)}, bf16[272,128]{1,0:T(8,128)(2,1)S(1)}, u32[]{:S(2)}, u32[]{:S(2)}) collective-permute-start(bf16[272,128]{1,0:T(8,128)(2,1)S(1)} %get-tuple-element.38), channel_id=1, source_target_pairs={{0,2},{2,0},{4,6},{6,4},{8,10},{10,8},{12,14},{14,12},{1,3},{3,1},... | collective-permute-start | bytes 208904 | tf_op jit(solution)/shard_map/sum_first/ppermute | solution.py:347
  23.5 1.3 %collective-permute-start.11 = (bf16[272,128]{1,0:T(8,128)(2,1)S(1)}, bf16[272,128]{1,0:T(8,128)(2,1)S(1)}, u32[]{:S(2)}, u32[]{:S(2)}) collective-permute-start(bf16[272,128]{1,0:T(8,128)(2,1)S(1)} %get-tuple-element.39), channel_id=1, source_target_pairs={{0,4},{2,6},{4,0},{6,2},{8,12},{10,14},{12,8},{14,10},{1,5},{3,7},... | collective-permute-start | bytes 208904 | tf_op jit(solution)/shard_map/sum_first/ppermute | solution.py:347
  24.8 0.4 collective-permute-start.12
  25.3 0.1 norms.1
  25.4 0.8 %collective-permute-done.10.refs_1_ = bf16[272,128]{1,0:T(8,128)(2,1)S(1)} collective-permute-done((bf16[272,128]{1,0:T(8,128)(2,1)S(1)}, bf16[272,128]{1,0:T(8,128)(2,1)S(1)}, u32[]{:S(2)}, u32[]{:S(2)}) %collective-permute-start.10) | collective-permute-done | bytes 69664 | tf_op jit(solution)/shard_map/sum_first/ppermute | solution.py:347
  26.1 2.4 %collective-permute-done.11.refs_2_ = bf16[272,128]{1,0:T(8,128)(2,1)S(1)} collective-permute-done((bf16[272,128]{1,0:T(8,128)(2,1)S(1)}, bf16[272,128]{1,0:T(8,128)(2,1)S(1)}, u32[]{:S(2)}, u32[]{:S(2)}) %collective-permute-start.11) | collective-permute-done | bytes 69664 | tf_op jit(solution)/shard_map/sum_first/ppermute | solution.py:347
  28.5 1.5 %collective-permute-done.12.refs_3_ = bf16[272,128]{1,0:T(8,128)(2,1)S(1)} collective-permute-done((bf16[272,128]{1,0:T(8,128)(2,1)S(1)}, bf16[272,128]{1,0:T(8,128)(2,1)S(1)}, u32[]{:S(2)}, u32[]{:S(2)}) %collective-permute-start.12) | collective-permute-done | bytes 69664 | tf_op jit(solution)/shard_map/sum_first/ppermute | solution.py:347
  30.1 0.1 for_far.2
  30.2 3.3 %collective-permute-start.13 = (bf16[272,128]{1,0:T(8,128)(2,1)S(1)}, bf16[272,128]{1,0:T(8,128)(2,1)S(1)}, u32[]{:S(2)}, u32[]{:S(2)}) collective-permute-start(bf16[272,128]{1,0:T(8,128)(2,1)S(1)} %for_far.2), channel_id=1, source_target_pairs={{0,8},{2,10},{4,12},{6,14},{8,0},{10,2},{12,4},{14,6},{1,9},{3,11}... | collective-permute-start | bytes 208904 | tf_op jit(solution)/shard_map/sum_first/ppermute | solution.py:347
  33.5 2.9 %collective-permute-done.13.got = bf16[272,128]{1,0:T(8,128)(2,1)S(1)} collective-permute-done((bf16[272,128]{1,0:T(8,128)(2,1)S(1)}, bf16[272,128]{1,0:T(8,128)(2,1)S(1)}, u32[]{:S(2)}, u32[]{:S(2)}) %collective-permute-start.13) | collective-permute-done | bytes 69664 | tf_op jit(solution)/shard_map/sum_first/ppermute | solution.py:347
  36.3 0.1 residual.1
  36.5 0.9 %collective-permute-start.16 = (bf16[2,128,128]{2,1,0:T(8,128)(2,1)S(1)}, bf16[2,128,128]{2,1,0:T(8,128)(2,1)S(1)}, u32[]{:S(2)}, u32[]{:S(2)}) collective-permute-start(bf16[2,128,128]{2,1,0:T(8,128)(2,1)S(1)} %get-tuple-element.44.refs_0_), channel_id=1, source_target_pairs={{0,6},{2,4},{4,2},{6,0},{8,14},{10,12},{12,10},{14,8},{1,7},{3,5},... | collective-permute-start | bytes 196616 | tf_op jit(solution)/shard_map/gather_residual/ppermute | solution.py:347
  37.4 1.3 %collective-permute-start.15 = (bf16[2,128,128]{2,1,0:T(8,128)(2,1)S(1)}, bf16[2,128,128]{2,1,0:T(8,128)(2,1)S(1)}, u32[]{:S(2)}, u32[]{:S(2)}) collective-permute-start(bf16[2,128,128]{2,1,0:T(8,128)(2,1)S(1)} %get-tuple-element.44.refs_0_), channel_id=1, source_target_pairs={{0,4},{2,6},{4,0},{6,2},{8,12},{10,14},{12,8},{14,10},{1,5},{3,7},... | collective-permute-start | bytes 196616 | tf_op jit(solution)/shard_map/gather_residual/ppermute | solution.py:347
  38.7 1.3 %collective-permute-start.14 = (bf16[2,128,128]{2,1,0:T(8,128)(2,1)S(1)}, bf16[2,128,128]{2,1,0:T(8,128)(2,1)S(1)}, u32[]{:S(2)}, u32[]{:S(2)}) collective-permute-start(bf16[2,128,128]{2,1,0:T(8,128)(2,1)S(1)} %get-tuple-element.44.refs_0_), channel_id=1, source_target_pairs={{0,2},{2,0},{4,6},{6,4},{8,10},{10,8},{12,14},{14,12},{1,3},{3,1},... | collective-permute-start | bytes 196616 | tf_op jit(solution)/shard_map/gather_residual/ppermute | solution.py:347
  40.0 0.0 collective-permute-start.17
  40.0 1.7 %collective-permute-done.16.refs_3_ = bf16[2,128,128]{2,1,0:T(8,128)(2,1)S(1)} collective-permute-done((bf16[2,128,128]{2,1,0:T(8,128)(2,1)S(1)}, bf16[2,128,128]{2,1,0:T(8,128)(2,1)S(1)}, u32[]{:S(2)}, u32[]{:S(2)}) %collective-permute-start.16) | collective-permute-done | bytes 65568 | tf_op jit(solution)/shard_map/gather_residual/ppermute | solution.py:347
  41.7 0.0 collective-permute-start.20
  41.7 0.0 collective-permute-done.15.refs_2_
  41.7 0.5 collective-permute-start.19
  42.2 0.7 %collective-permute-done.14.refs_1_ = bf16[2,128,128]{2,1,0:T(8,128)(2,1)S(1)} collective-permute-done((bf16[2,128,128]{2,1,0:T(8,128)(2,1)S(1)}, bf16[2,128,128]{2,1,0:T(8,128)(2,1)S(1)}, u32[]{:S(2)}, u32[]{:S(2)}) %collective-permute-start.14) | collective-permute-done | bytes 65568 | tf_op jit(solution)/shard_map/gather_residual/ppermute | solution.py:347
  43.0 0.0 collective-permute-start.18
  43.0 0.0 collective-permute-done.17.refs_4_
  43.0 0.0 collective-permute-done.20.refs_7_
  43.0 0.1 collective-permute-done.19.refs_6_
  43.1 1.1 %collective-permute-done.18.refs_5_ = bf16[2,128,128]{2,1,0:T(8,128)(2,1)S(1)} collective-permute-done((bf16[2,128,128]{2,1,0:T(8,128)(2,1)S(1)}, bf16[2,128,128]{2,1,0:T(8,128)(2,1)S(1)}, u32[]{:S(2)}, u32[]{:S(2)}) %collective-permute-start.18) | collective-permute-done | bytes 65568 | tf_op jit(solution)/shard_map/gather_residual/ppermute | solution.py:342
  44.2 4.0 %second_sigma.1 = (bf16[1040,128]{1,0:T(8,128)(2,1)S(1)}, f32[16,128,128]{2,1,0:T(8,128)S(1)}, f32[8,128]{1,0:T(8,128)S(1)}, f32[1,128,128]{2,1,0:T(8,128)}) custom-call(bf16[2,128,128]{2,1,0:T(8,128)(2,1)S(1)} %get-tuple-element.44.refs_0_, bf16[2,128,128]{2,1,0:T(8,128)(2,1)S(1)} %collective-permute-done.14.refs_1_, ...), custom_call_target="tpu_custom_call" | custom-call | flops 1207959552 | bytes 10555968 | tf_op jit(solution)/shard_map/second_sigma/second_sigma/pallas_call | solution.py:325
  48.3 0.2 collective-permute-start.21
  48.5 1.4 %collective-permute-done.21.refs_1_ = bf16[1040,128]{1,0:T(8,128)(2,1)S(1)} collective-permute-done((bf16[1040,128]{1,0:T(8,128)(2,1)S(1)}, bf16[1040,128]{1,0:T(8,128)(2,1)S(1)}, u32[]{:S(2)}, u32[]{:S(2)}) %collective-permute-start.21) | collective-permute-done | bytes 266272 | tf_op jit(solution)/shard_map/sum_second/ppermute | solution.py:342
  49.9 0.1 chip_sum.3
  50.0 1.4 %collective-permute-start.22 = (bf16[272,128]{1,0:T(8,128)(2,1)S(1)}, bf16[272,128]{1,0:T(8,128)(2,1)S(1)}, u32[]{:S(2)}, u32[]{:S(2)}) collective-permute-start(bf16[272,128]{1,0:T(8,128)(2,1)S(1)} %get-tuple-element.53), channel_id=1, source_target_pairs={{0,2},{2,0},{4,6},{6,4},{8,10},{10,8},{12,14},{14,12},{1,3},{3,1},... | collective-permute-start | bytes 208904 | tf_op jit(solution)/shard_map/sum_second/ppermute | solution.py:347
  51.4 0.2 collective-permute-start.23
  51.5 2.0 %collective-permute-start.24 = (bf16[272,128]{1,0:T(8,128)(2,1)S(1)}, bf16[272,128]{1,0:T(8,128)(2,1)S(1)}, u32[]{:S(2)}, u32[]{:S(2)}) collective-permute-start(bf16[272,128]{1,0:T(8,128)(2,1)S(1)} %get-tuple-element.55), channel_id=1, source_target_pairs={{0,6},{2,4},{4,2},{6,0},{8,14},{10,12},{12,10},{14,8},{1,7},{3,5},... | collective-permute-start | bytes 208904 | tf_op jit(solution)/shard_map/sum_second/ppermute | solution.py:347
  53.5 0.8 %collective-permute-done.22.refs_1_ = bf16[272,128]{1,0:T(8,128)(2,1)S(1)} collective-permute-done((bf16[272,128]{1,0:T(8,128)(2,1)S(1)}, bf16[272,128]{1,0:T(8,128)(2,1)S(1)}, u32[]{:S(2)}, u32[]{:S(2)}) %collective-permute-start.22) | collective-permute-done | bytes 69664 | tf_op jit(solution)/shard_map/sum_second/ppermute | solution.py:347
  54.3 1.7 %collective-permute-done.23.refs_2_ = bf16[272,128]{1,0:T(8,128)(2,1)S(1)} collective-permute-done((bf16[272,128]{1,0:T(8,128)(2,1)S(1)}, bf16[272,128]{1,0:T(8,128)(2,1)S(1)}, u32[]{:S(2)}, u32[]{:S(2)}) %collective-permute-start.23) | collective-permute-done | bytes 69664 | tf_op jit(solution)/shard_map/sum_second/ppermute | solution.py:347
  56.1 1.0 %collective-permute-done.24.refs_3_ = bf16[272,128]{1,0:T(8,128)(2,1)S(1)} collective-permute-done((bf16[272,128]{1,0:T(8,128)(2,1)S(1)}, bf16[272,128]{1,0:T(8,128)(2,1)S(1)}, u32[]{:S(2)}, u32[]{:S(2)}) %collective-permute-start.24) | collective-permute-done | bytes 69664 | tf_op jit(solution)/shard_map/sum_second/ppermute | solution.py:347
  57.1 2.6 %collective-permute-start.25 = (bf16[144,128]{1,0:T(8,128)(2,1)S(1)}, bf16[144,128]{1,0:T(8,128)(2,1)S(1)}, u32[]{:S(2)}, u32[]{:S(2)}) collective-permute-start(bf16[144,128]{1,0:T(8,128)(2,1)S(1)} %for_far.3), channel_id=1, source_target_pairs={{0,8},{2,10},{4,12},{6,14},{8,0},{10,2},{12,4},{14,6},{1,9},{3,11}... | collective-permute-start | bytes 110600 | tf_op jit(solution)/shard_map/sum_second/ppermute | solution.py:347
  59.7 2.3 %collective-permute-done.25.got = bf16[144,128]{1,0:T(8,128)(2,1)S(1)} collective-permute-done((bf16[144,128]{1,0:T(8,128)(2,1)S(1)}, bf16[144,128]{1,0:T(8,128)(2,1)S(1)}, u32[]{:S(2)}, u32[]{:S(2)}) %collective-permute-start.25) | collective-permute-done | bytes 36896 | tf_op jit(solution)/shard_map/sum_second/ppermute | solution.py:347
  62.0 0.7 %outputs.1 = (bf16[1,128,128]{2,1,0:T(8,128)(2,1)}, f32[1,128,128]{2,1,0:T(8,128)}, f32[4]{0:T(128)}) custom-call(f32[2,136,128]{2,1,0:T(8,128)S(1)} %near_sum.3.refs_0_.part, bf16[144,128]{1,0:T(8,128)(2,1)S(1)} %collective-permute-done.25.got, bf16[16,128,128]{2,1,0:T(8,128)(2,1)S(1)} %get-tuple-element.41.wave.refs_9_, ...), custom_call_target="tpu_custom_call" | custom-call | flops 262144 | bytes 966656 | tf_op jit(solution)/shard_map/outputs/outputs/pallas_call | solution.py:325
  (16 shorter events, 0.1 us)
Async XLA Ops:
  0.6 10.1 %copy-start.2 = (f32[1,128,128]{2,1,0:T(8,128)S(1)}, f32[1,128,128]{2,1,0:T(8,128)}, u32[]{:S(2)}) copy-start(f32[1,128,128]{2,1,0:T(8,128)} %precond.1) | copy-start | bytes 196612
  0.6 14.3 %copy-start.4 = (s32[12,12]{1,0:T(8,128)S(1)}, s32[12,12]{1,0:T(8,128)}, u32[]{:S(2)}) copy-start(s32[12,12]{1,0:T(8,128)} %tgt.1) | copy-start | bytes 1732
  0.7 14.3 %copy-start.3 = (s32[12,12]{1,0:T(8,128)S(1)}, s32[12,12]{1,0:T(8,128)}, u32[]{:S(2)}) copy-start(s32[12,12]{1,0:T(8,128)} %src.1) | copy-start | bytes 1732
  0.7 15.3 %copy-start = (bf16[12,12,128,128]{3,2,1,0:T(8,128)(2,1)S(1)}, bf16[12,12,128,128]{3,2,1,0:T(8,128)(2,1)}, u32[]{:S(2)}) copy-start(bf16[12,12,128,128]{3,2,1,0:T(8,128)(2,1)} %refs_10_.3) | copy-start | bytes 14155780
  0.7 15.3 %copy-start.1 = (bf16[12,12,128,128]{3,2,1,0:T(8,128)(2,1)S(1)}, bf16[12,12,128,128]{3,2,1,0:T(8,128)(2,1)}, u32[]{:S(2)}) copy-start(bf16[12,12,128,128]{3,2,1,0:T(8,128)(2,1)} %refs_11_.1) | copy-start | bytes 14155780
  0.7 6.6 %collective-permute-start = (bf16[1,128,128]{2,1,0:T(8,128)(2,1)}, bf16[1,128,128]{2,1,0:T(8,128)(2,1)S(1)}, u32[]{:S(2)}, u32[]{:S(2)}) collective-permute-start(bf16[1,128,128]{2,1,0:T(8,128)(2,1)} %block.1), channel_id=1, source_target_pairs={{0,8},{2,10},{4,12},{6,14},{8,0},{10,2},{12,4},{14,6},{1,9},{3,11}... | collective-permute-start | bytes 98312 | tf_op jit(solution)/shard_map/gather_state/ppermute | solution.py:347
  4.8 0.8 %copy-start.5 = (bf16[1,128,128]{2,1,0:T(8,128)(2,1)S(1)}, bf16[1,128,128]{2,1,0:T(8,128)(2,1)}, u32[]{:S(2)}) copy-start(bf16[1,128,128]{2,1,0:T(8,128)(2,1)} %block.1) | copy-start | bytes 98308
  5.6 0.7 %copy-start.6 = (s32[16]{0:T(128)S(1)}, s32[16]{0:T(128)}, u32[]{:S(2)}) copy-start(s32[16]{0:T(128)} %sizes.1) | copy-start | bytes 196
  7.2 6.1 %collective-permute-start.3 = (bf16[2,128,128]{2,1,0:T(8,128)(2,1)S(1)}, bf16[2,128,128]{2,1,0:T(8,128)(2,1)S(1)}, u32[]{:S(2)}, u32[]{:S(2)}) collective-permute-start(bf16[2,128,128]{2,1,0:T(8,128)(2,1)S(1)} %pair.1.refs_0_), channel_id=1, source_target_pairs={{0,6},{2,4},{4,2},{6,0},{8,14},{10,12},{12,10},{14,8},{1,7},{3,5},... | collective-permute-start | bytes 196616 | tf_op jit(solution)/shard_map/gather_state/ppermute | solution.py:347
  9.7 4.7 %collective-permute-start.2 = (bf16[2,128,128]{2,1,0:T(8,128)(2,1)S(1)}, bf16[2,128,128]{2,1,0:T(8,128)(2,1)S(1)}, u32[]{:S(2)}, u32[]{:S(2)}) collective-permute-start(bf16[2,128,128]{2,1,0:T(8,128)(2,1)S(1)} %pair.1.refs_0_), channel_id=1, source_target_pairs={{0,4},{2,6},{4,0},{6,2},{8,12},{10,14},{12,8},{14,10},{1,5},{3,7},... | collective-permute-start | bytes 196616 | tf_op jit(solution)/shard_map/gather_state/ppermute | solution.py:347
  10.4 4.3 %collective-permute-start.1 = (bf16[2,128,128]{2,1,0:T(8,128)(2,1)S(1)}, bf16[2,128,128]{2,1,0:T(8,128)(2,1)S(1)}, u32[]{:S(2)}, u32[]{:S(2)}) collective-permute-start(bf16[2,128,128]{2,1,0:T(8,128)(2,1)S(1)} %pair.1.refs_0_), channel_id=1, source_target_pairs={{0,2},{2,0},{4,6},{6,4},{8,10},{10,8},{12,14},{14,12},{1,3},{3,1},... | collective-permute-start | bytes 196616 | tf_op jit(solution)/shard_map/gather_state/ppermute | solution.py:347
  10.7 5.2 %collective-permute-start.8 = (f32[1,128,128]{2,1,0:T(8,128)S(1)}, f32[1,128,128]{2,1,0:T(8,128)S(1)}, u32[]{:S(2)}, u32[]{:S(2)}) collective-permute-start(f32[1,128,128]{2,1,0:T(8,128)S(1)} %copy-done.2), channel_id=1, source_target_pairs={{0,8},{2,10},{4,12},{6,14},{8,0},{10,2},{12,4},{14,6},{1,9},{3,11}... | collective-permute-start | bytes 196616 | tf_op jit(solution)/shard_map/gather_state/ppermute | solution.py:347
  13.3 2.6 %collective-permute-start.4 = (bf16[2,128,128]{2,1,0:T(8,128)(2,1)S(1)}, bf16[2,128,128]{2,1,0:T(8,128)(2,1)S(1)}, u32[]{:S(2)}, u32[]{:S(2)}) collective-permute-start(bf16[2,128,128]{2,1,0:T(8,128)(2,1)S(1)} %pair.1.refs_0_), channel_id=1, source_target_pairs={{0,1},{1,0},{2,3},{3,2},{4,5},{5,4},{6,7},{7,6},{8,9},{9,8},{10,11... | collective-permute-start | bytes 196616 | tf_op jit(solution)/shard_map/gather_state/ppermute | solution.py:342
  13.3 2.6 %collective-permute-start.7 = (bf16[2,128,128]{2,1,0:T(8,128)(2,1)S(1)}, bf16[2,128,128]{2,1,0:T(8,128)(2,1)S(1)}, u32[]{:S(2)}, u32[]{:S(2)}) collective-permute-start(bf16[2,128,128]{2,1,0:T(8,128)(2,1)S(1)} %collective-permute-done.3.refs_3_), channel_id=1, source_target_pairs={{0,1},{1,0},{2,3},{3,2},{4,5},{5,4},{6,7},{7,6},{8,9},{9,8},{10,11... | collective-permute-start | bytes 196616 | tf_op jit(solution)/shard_map/gather_state/ppermute | solution.py:342
  14.4 1.5 %collective-permute-start.6 = (bf16[2,128,128]{2,1,0:T(8,128)(2,1)S(1)}, bf16[2,128,128]{2,1,0:T(8,128)(2,1)S(1)}, u32[]{:S(2)}, u32[]{:S(2)}) collective-permute-start(bf16[2,128,128]{2,1,0:T(8,128)(2,1)S(1)} %collective-permute-done.2.refs_2_), channel_id=1, source_target_pairs={{0,1},{1,0},{2,3},{3,2},{4,5},{5,4},{6,7},{7,6},{8,9},{9,8},{10,11... | collective-permute-start | bytes 196616 | tf_op jit(solution)/shard_map/gather_state/ppermute | solution.py:342
  14.7 1.3 %collective-permute-start.5 = (bf16[2,128,128]{2,1,0:T(8,128)(2,1)S(1)}, bf16[2,128,128]{2,1,0:T(8,128)(2,1)S(1)}, u32[]{:S(2)}, u32[]{:S(2)}) collective-permute-start(bf16[2,128,128]{2,1,0:T(8,128)(2,1)S(1)} %collective-permute-done.1.refs_1_), channel_id=1, source_target_pairs={{0,1},{1,0},{2,3},{3,2},{4,5},{5,4},{6,7},{7,6},{8,9},{9,8},{10,11... | collective-permute-start | bytes 196616 | tf_op jit(solution)/shard_map/gather_state/ppermute | solution.py:342
  20.0 1.6 %collective-permute-start.9 = (bf16[1040,128]{1,0:T(8,128)(2,1)S(1)}, bf16[1040,128]{1,0:T(8,128)(2,1)S(1)}, u32[]{:S(2)}, u32[]{:S(2)}) collective-permute-start(bf16[1040,128]{1,0:T(8,128)(2,1)S(1)} %get-tuple-element.35), channel_id=1, source_target_pairs={{0,1},{1,0},{2,3},{3,2},{4,5},{5,4},{6,7},{7,6},{8,9},{9,8},{10,11... | collective-permute-start | bytes 798728 | tf_op jit(solution)/shard_map/sum_first/ppermute | solution.py:342
  21.7 4.4 %collective-permute-start.10 = (bf16[272,128]{1,0:T(8,128)(2,1)S(1)}, bf16[272,128]{1,0:T(8,128)(2,1)S(1)}, u32[]{:S(2)}, u32[]{:S(2)}) collective-permute-start(bf16[272,128]{1,0:T(8,128)(2,1)S(1)} %get-tuple-element.38), channel_id=1, source_target_pairs={{0,2},{2,0},{4,6},{6,4},{8,10},{10,8},{12,14},{14,12},{1,3},{3,1},... | collective-permute-start | bytes 208904 | tf_op jit(solution)/shard_map/sum_first/ppermute | solution.py:347
  23.5 5.0 %collective-permute-start.11 = (bf16[272,128]{1,0:T(8,128)(2,1)S(1)}, bf16[272,128]{1,0:T(8,128)(2,1)S(1)}, u32[]{:S(2)}, u32[]{:S(2)}) collective-permute-start(bf16[272,128]{1,0:T(8,128)(2,1)S(1)} %get-tuple-element.39), channel_id=1, source_target_pairs={{0,4},{2,6},{4,0},{6,2},{8,12},{10,14},{12,8},{14,10},{1,5},{3,7},... | collective-permute-start | bytes 208904 | tf_op jit(solution)/shard_map/sum_first/ppermute | solution.py:347
  24.8 5.2 %collective-permute-start.12 = (bf16[272,128]{1,0:T(8,128)(2,1)S(1)}, bf16[272,128]{1,0:T(8,128)(2,1)S(1)}, u32[]{:S(2)}, u32[]{:S(2)}) collective-permute-start(bf16[272,128]{1,0:T(8,128)(2,1)S(1)} %get-tuple-element.40), channel_id=1, source_target_pairs={{0,6},{2,4},{4,2},{6,0},{8,14},{10,12},{12,10},{14,8},{1,7},{3,5},... | collective-permute-start | bytes 208904 | tf_op jit(solution)/shard_map/sum_first/ppermute | solution.py:347
  30.2 6.1 %collective-permute-start.13 = (bf16[272,128]{1,0:T(8,128)(2,1)S(1)}, bf16[272,128]{1,0:T(8,128)(2,1)S(1)}, u32[]{:S(2)}, u32[]{:S(2)}) collective-permute-start(bf16[272,128]{1,0:T(8,128)(2,1)S(1)} %for_far.2), channel_id=1, source_target_pairs={{0,8},{2,10},{4,12},{6,14},{8,0},{10,2},{12,4},{14,6},{1,9},{3,11}... | collective-permute-start | bytes 208904 | tf_op jit(solution)/shard_map/sum_first/ppermute | solution.py:347
  36.5 5.2 %collective-permute-start.16 = (bf16[2,128,128]{2,1,0:T(8,128)(2,1)S(1)}, bf16[2,128,128]{2,1,0:T(8,128)(2,1)S(1)}, u32[]{:S(2)}, u32[]{:S(2)}) collective-permute-start(bf16[2,128,128]{2,1,0:T(8,128)(2,1)S(1)} %get-tuple-element.44.refs_0_), channel_id=1, source_target_pairs={{0,6},{2,4},{4,2},{6,0},{8,14},{10,12},{12,10},{14,8},{1,7},{3,5},... | collective-permute-start | bytes 196616 | tf_op jit(solution)/shard_map/gather_residual/ppermute | solution.py:347
  37.4 4.3 %collective-permute-start.15 = (bf16[2,128,128]{2,1,0:T(8,128)(2,1)S(1)}, bf16[2,128,128]{2,1,0:T(8,128)(2,1)S(1)}, u32[]{:S(2)}, u32[]{:S(2)}) collective-permute-start(bf16[2,128,128]{2,1,0:T(8,128)(2,1)S(1)} %get-tuple-element.44.refs_0_), channel_id=1, source_target_pairs={{0,4},{2,6},{4,0},{6,2},{8,12},{10,14},{12,8},{14,10},{1,5},{3,7},... | collective-permute-start | bytes 196616 | tf_op jit(solution)/shard_map/gather_residual/ppermute | solution.py:347
  38.7 4.3 %collective-permute-start.14 = (bf16[2,128,128]{2,1,0:T(8,128)(2,1)S(1)}, bf16[2,128,128]{2,1,0:T(8,128)(2,1)S(1)}, u32[]{:S(2)}, u32[]{:S(2)}) collective-permute-start(bf16[2,128,128]{2,1,0:T(8,128)(2,1)S(1)} %get-tuple-element.44.refs_0_), channel_id=1, source_target_pairs={{0,2},{2,0},{4,6},{6,4},{8,10},{10,8},{12,14},{14,12},{1,3},{3,1},... | collective-permute-start | bytes 196616 | tf_op jit(solution)/shard_map/gather_residual/ppermute | solution.py:347
  40.0 2.9 %collective-permute-start.17 = (bf16[2,128,128]{2,1,0:T(8,128)(2,1)S(1)}, bf16[2,128,128]{2,1,0:T(8,128)(2,1)S(1)}, u32[]{:S(2)}, u32[]{:S(2)}) collective-permute-start(bf16[2,128,128]{2,1,0:T(8,128)(2,1)S(1)} %get-tuple-element.44.refs_0_), channel_id=1, source_target_pairs={{0,1},{1,0},{2,3},{3,2},{4,5},{5,4},{6,7},{7,6},{8,9},{9,8},{10,11... | collective-permute-start | bytes 196616 | tf_op jit(solution)/shard_map/gather_residual/ppermute | solution.py:342
  41.7 1.3 %collective-permute-start.20 = (bf16[2,128,128]{2,1,0:T(8,128)(2,1)S(1)}, bf16[2,128,128]{2,1,0:T(8,128)(2,1)S(1)}, u32[]{:S(2)}, u32[]{:S(2)}) collective-permute-start(bf16[2,128,128]{2,1,0:T(8,128)(2,1)S(1)} %collective-permute-done.16.refs_3_), channel_id=1, source_target_pairs={{0,1},{1,0},{2,3},{3,2},{4,5},{5,4},{6,7},{7,6},{8,9},{9,8},{10,11... | collective-permute-start | bytes 196616 | tf_op jit(solution)/shard_map/gather_residual/ppermute | solution.py:342
  41.7 1.4 %collective-permute-start.19 = (bf16[2,128,128]{2,1,0:T(8,128)(2,1)S(1)}, bf16[2,128,128]{2,1,0:T(8,128)(2,1)S(1)}, u32[]{:S(2)}, u32[]{:S(2)}) collective-permute-start(bf16[2,128,128]{2,1,0:T(8,128)(2,1)S(1)} %collective-permute-done.15.refs_2_), channel_id=1, source_target_pairs={{0,1},{1,0},{2,3},{3,2},{4,5},{5,4},{6,7},{7,6},{8,9},{9,8},{10,11... | collective-permute-start | bytes 196616 | tf_op jit(solution)/shard_map/gather_residual/ppermute | solution.py:342
  43.0 1.3 %collective-permute-start.18 = (bf16[2,128,128]{2,1,0:T(8,128)(2,1)S(1)}, bf16[2,128,128]{2,1,0:T(8,128)(2,1)S(1)}, u32[]{:S(2)}, u32[]{:S(2)}) collective-permute-start(bf16[2,128,128]{2,1,0:T(8,128)(2,1)S(1)} %collective-permute-done.14.refs_1_), channel_id=1, source_target_pairs={{0,1},{1,0},{2,3},{3,2},{4,5},{5,4},{6,7},{7,6},{8,9},{9,8},{10,11... | collective-permute-start | bytes 196616 | tf_op jit(solution)/shard_map/gather_residual/ppermute | solution.py:342
  48.3 1.6 %collective-permute-start.21 = (bf16[1040,128]{1,0:T(8,128)(2,1)S(1)}, bf16[1040,128]{1,0:T(8,128)(2,1)S(1)}, u32[]{:S(2)}, u32[]{:S(2)}) collective-permute-start(bf16[1040,128]{1,0:T(8,128)(2,1)S(1)} %get-tuple-element.50), channel_id=1, source_target_pairs={{0,1},{1,0},{2,3},{3,2},{4,5},{5,4},{6,7},{7,6},{8,9},{9,8},{10,11... | collective-permute-start | bytes 798728 | tf_op jit(solution)/shard_map/sum_second/ppermute | solution.py:342
  50.0 4.4 %collective-permute-start.22 = (bf16[272,128]{1,0:T(8,128)(2,1)S(1)}, bf16[272,128]{1,0:T(8,128)(2,1)S(1)}, u32[]{:S(2)}, u32[]{:S(2)}) collective-permute-start(bf16[272,128]{1,0:T(8,128)(2,1)S(1)} %get-tuple-element.53), channel_id=1, source_target_pairs={{0,2},{2,0},{4,6},{6,4},{8,10},{10,8},{12,14},{14,12},{1,3},{3,1},... | collective-permute-start | bytes 208904 | tf_op jit(solution)/shard_map/sum_second/ppermute | solution.py:347
  51.4 4.7 %collective-permute-start.23 = (bf16[272,128]{1,0:T(8,128)(2,1)S(1)}, bf16[272,128]{1,0:T(8,128)(2,1)S(1)}, u32[]{:S(2)}, u32[]{:S(2)}) collective-permute-start(bf16[272,128]{1,0:T(8,128)(2,1)S(1)} %get-tuple-element.54), channel_id=1, source_target_pairs={{0,4},{2,6},{4,0},{6,2},{8,12},{10,14},{12,8},{14,10},{1,5},{3,7},... | collective-permute-start | bytes 208904 | tf_op jit(solution)/shard_map/sum_second/ppermute | solution.py:347
  51.5 5.5 %collective-permute-start.24 = (bf16[272,128]{1,0:T(8,128)(2,1)S(1)}, bf16[272,128]{1,0:T(8,128)(2,1)S(1)}, u32[]{:S(2)}, u32[]{:S(2)}) collective-permute-start(bf16[272,128]{1,0:T(8,128)(2,1)S(1)} %get-tuple-element.55), channel_id=1, source_target_pairs={{0,6},{2,4},{4,2},{6,0},{8,14},{10,12},{12,10},{14,8},{1,7},{3,5},... | collective-permute-start | bytes 208904 | tf_op jit(solution)/shard_map/sum_second/ppermute | solution.py:347
  57.1 4.9 %collective-permute-start.25 = (bf16[144,128]{1,0:T(8,128)(2,1)S(1)}, bf16[144,128]{1,0:T(8,128)(2,1)S(1)}, u32[]{:S(2)}, u32[]{:S(2)}) collective-permute-start(bf16[144,128]{1,0:T(8,128)(2,1)S(1)} %for_far.3), channel_id=1, source_target_pairs={{0,8},{2,10},{4,12},{6,14},{8,0},{10,2},{12,4},{14,6},{1,9},{3,11}... | collective-permute-start | bytes 110600 | tf_op jit(solution)/shard_map/sum_second/ppermute | solution.py:347

commit v9 on v8

--- a/solution.py
+++ b/solution.py
@@ -13,6 +13,8 @@
 LONG = 10**11
 TINY = 1e-30
 NEAR = 4
+GATHER = ((1, 2, 3), (1, 2, 3))
+SUMS = ((3, 1, 2), (2, 1, 3))
 
 
 def each(count, body, carry):
@@ -78,6 +80,13 @@
     return rows
 
 
+def near_of(orders, core, n):
+    if n == 0:
+        return 0
+    first, second = (order[n - 1] for order in orders)
+    return first + (second - first) * core
+
+
 def apply_blocks(plan, vec, left, right, acc, keep=None):
     terms, nnz = left.shape[0], left.shape[1]
     per = 6 if terms % 6 == 0 else 1
@@ -137,6 +146,7 @@
     theirs, acc, wave, flip, sums, rows, places, sem = outs
     span, width = pieces[0].shape[0], pieces[0].shape[2]
     chips = NEAR * span
+    core = lax.axis_index("core")
     copy = pltpu.make_async_copy(plan, places, sem)
     copy.start()
     across = lax.broadcasted_iota(jnp.int32, (width, width), 0)
@@ -148,7 +158,7 @@
             piece = pieces[other * NEAR + k]
 
             def load(i, carry, other=other, k=k, piece=piece):
-                rel = other * chips + NEAR * i + k
+                rel = other * chips + NEAR * i + near_of(GATHER, core ^ other, k)
                 limit = limits[pl.ds(rel, 1)]
                 block = jnp.where((across < limit) & (along < limit), piece[i].astype(F32), 0.0)
                 wave[rel] = block.astype(BF16)
@@ -175,6 +185,7 @@
     theirs, acc, sums, sigma, vec, places, sems = outs
     span, width = pieces[0].shape[0], pieces[0].shape[2]
     chips = NEAR * span
+    core = lax.axis_index("core")
     copy = pltpu.make_async_copy(plan, places, sems.at[0])
     result = pltpu.make_async_copy(first, sigma, sems.at[1])
     copy.start()
@@ -186,7 +197,7 @@
             piece = pieces[other * NEAR + k]
 
             def load(i, carry, other=other, k=k, piece=piece):
-                vec[other * chips + NEAR * i + k] = piece[i]
+                vec[other * chips + NEAR * i + near_of(GATHER, core ^ other, k)] = piece[i]
                 return carry
 
             each(span, load, 0)
@@ -213,14 +224,15 @@
 def chip_kernel(start, count, mine, got, sums, base, *sends):
     width = mine.shape[2]
     chips, span = mine.shape[0] // 2, base.shape[0]
+    core = lax.axis_index("core")
     rows = rows_of(got[chips * width :], count)
     rows = [sums[start + i : start + i + 1] + rows[i] for i in range(count)]
     tail = tail_of(rows)
 
     def store(i, carry):
         base[i, 0:width] = mine[NEAR * i] + got[at(NEAR * i, width)].astype(F32)
-        for k, send in enumerate(sends, 1):
-            rel = NEAR * i + k
+        for n, send in enumerate(sends, 1):
+            rel = NEAR * i + near_of(SUMS, core, n)
             send[at(i, width)] = (mine[rel] + got[at(rel, width)].astype(F32)).astype(BF16)
         return carry
 
@@ -235,7 +247,11 @@
     gots, out = refs[:-1], refs[-1]
     span, width = base.shape[0], base.shape[2]
     parts = [[base[0, width + i : width + i + 1] for i in range(count)]]
-    parts += [rows_of(got[span * width :], count) for got in gots]
+    came = [rows_of(got[span * width :], count) for got in gots]
+    first = lax.axis_index("core") == 0
+    for k in range(1, NEAR):
+        a, b = (came[order.index(k)] for order in SUMS)
+        parts.append([jnp.where(first, x, y) for x, y in zip(a, b)])
     rows = [halve(jnp.concatenate([part[i] for part in parts], axis=0)) for i in range(count)]
 
     def store(i, carry):
@@ -347,12 +363,18 @@
     return lax.ppermute(x, "chip", [(i, i ^ bits) for i in range(chips)])
 
 
+def flip_near(x, orders, n):
+    chips = lax.axis_size("chip")
+    pairs = [(2 * i + c, 2 * (i ^ near_of(orders, c, n)) + c) for i in range(chips) for c in range(2)]
+    return lax.ppermute(x, ("chip", "core"), pairs)
+
+
 def gather(block):
     step = NEAR * block.shape[0]
     while step < lax.axis_size("chip"):
         block = jnp.concatenate([block, flip_chip(block, step)], axis=0)
         step *= 2
-    pieces = [block] + [flip_chip(block, k) for k in range(1, NEAR)]
+    pieces = [block] + [flip_near(block, GATHER, n) for n in range(1, NEAR)]
     return pieces + [swap(piece) for piece in pieces]
 
 
@@ -364,7 +386,7 @@
         lambda *refs: chip_kernel(start, count, *refs), "chip_sum", [VMEM] * 3,
         [shape(span, wide, width)] + sent, [], (mine, swap(theirs), sums), mine.size,
     )
-    gots = [flip_chip(send, k) for k, send in enumerate(sends, 1)]
+    gots = [flip_near(send, SUMS, n) for n, send in enumerate(sends, 1)]
     (part,) = call(
         lambda *refs: near_kernel(count, *refs), "near_sum", [VMEM] * NEAR,
         [shape(span, wide, width)], [], (base, *gots), mine.size,

time: 63 us -> 62.2 us (0.987)
    ppermute x0 -> x12, starting transfers between devices: none -> 14.1 us  [flip_near(): return lax.ppermute(x, ('chip', 'core'), pairs)]
    ppermute x16 -> x4, starting transfers between devices: 26.7 us -> 12.6 us  [flip_chip(): return lax.ppermute(x, 'chip', [(i, i ^ bits) for i in range(chips)])]
    ppermute x16 -> x4, waiting for transfers between devices: 18 us -> 6.69 us  [flip_chip(): return lax.ppermute(x, 'chip', [(i, i ^ bits) for i in range(chips)])]
    ppermute x0 -> x12, waiting for transfers between devices: none -> 10.7 us  [flip_near(): return lax.ppermute(x, ('chip', 'core'), pairs)]
  transfers between devices with their start and end apart: 26 -> 26, of which waited for: 18 -> 16; matrix products, arithmetic and copies ran while one was open for 0% -> 0% of each run, Pallas kernels for 1% -> 1%
where the time goes in v9:
time: 62.2 us; the launch traced here: 62 us
  starting transfers between devices  28.3 us (45%)
  waiting for transfers between devices  21.4 us (34%)
  Pallas kernels  10.1 us (16%)
  local copies, waits for them, and re-layouts  1.47 us (2%)
  between operations  0.78 us (1%)
    ppermute x12, starting transfers between devices, flip_near(): return lax.ppermute(x, ('chip', 'core'), pairs)  14.1 us
    ppermute x4, starting transfers between devices, flip_chip(): return lax.ppermute(x, 'chip', [(i, i ^ bits) for i in range(chips)])  12.6 us
    ppermute x12, waiting for transfers between devices, flip_near(): return lax.ppermute(x, ('chip', 'core'), pairs)  10.7 us
    pallas_call x14, Pallas kernels, call(): pl.pallas_call(kernel, name=name, in_specs=ins, out_specs=out_specs or [V...  10.1 us
    ppermute x4, waiting for transfers between devices, flip_chip(): return lax.ppermute(x, 'chip', [(i, i ^ bits) for i in range(chips)])  6.69 us
    ppermute x10, waiting for transfers between devices, swap(): return lax.ppermute(x, 'core', [(0, 1), (1, 0)])  3.92 us
    ppermute x10, starting transfers between devices, swap(): return lax.ppermute(x, 'core', [(0, 1), (1, 0)])  1.57 us
    unnamed x14, local copies, waits for them, and re-layouts  1.47 us
  transfers between devices with their start and end apart: 26, of which 16 were waited for; matrix products, arithmetic and copies ran while one was open for 0% of the time, Pallas kernels for 1%

profile of v9, /device:TPU:0, one launch (start us, length us, event | category | flops | bytes accessed | tf_op | source)
XLA Modules:
  0.0 62.0 jit_solution(6062048894867470666)
XLA Ops:
  0.7 4.1 %collective-permute-start = (bf16[1,128,128]{2,1,0:T(8,128)(2,1)}, bf16[1,128,128]{2,1,0:T(8,128)(2,1)S(1)}, u32[]{:S(2)}, u32[]{:S(2)}) collective-permute-start(bf16[1,128,128]{2,1,0:T(8,128)(2,1)} %block.1), channel_id=1, source_target_pairs={{0,8},{2,10},{4,12},{6,14},{8,0},{10,2},{12,4},{14,6},{1,9},{3,11}... | collective-permute-start | bytes 98312 | tf_op jit(solution)/shard_map/gather_state/ppermute | solution.py:363
  4.8 0.8 %copy-done.5 = bf16[1,128,128]{2,1,0:T(8,128)(2,1)S(1)} copy-done((bf16[1,128,128]{2,1,0:T(8,128)(2,1)S(1)}, bf16[1,128,128]{2,1,0:T(8,128)(2,1)}, u32[]{:S(2)}) %copy-start.5) | copy-done | bytes 32792
  5.6 0.7 %copy-done.6 = s32[16]{0:T(128)S(1)} copy-done((s32[16]{0:T(128)S(1)}, s32[16]{0:T(128)}, u32[]{:S(2)}) %copy-start.6) | copy-done | bytes 88
  6.2 0.6 masks.1
  6.8 0.4 collective-permute-done.far
  7.2 2.5 %collective-permute-start.3 = (bf16[2,128,128]{2,1,0:T(8,128)(2,1)S(1)}, bf16[2,128,128]{2,1,0:T(8,128)(2,1)S(1)}, u32[]{:S(2)}, u32[]{:S(2)}) collective-permute-start(bf16[2,128,128]{2,1,0:T(8,128)(2,1)S(1)} %pair.1.refs_0_), channel_id=1, source_target_pairs={{0,6},{1,7},{2,4},{3,5},{4,2},{5,3},{6,0},{7,1},{8,14},{9,15},{10,... | collective-permute-start | bytes 196616 | tf_op jit(solution)/shard_map/gather_state/ppermute | solution.py:369
  9.7 0.7 %collective-permute-start.2 = (bf16[2,128,128]{2,1,0:T(8,128)(2,1)S(1)}, bf16[2,128,128]{2,1,0:T(8,128)(2,1)S(1)}, u32[]{:S(2)}, u32[]{:S(2)}) collective-permute-start(bf16[2,128,128]{2,1,0:T(8,128)(2,1)S(1)} %pair.1.refs_0_), channel_id=1, source_target_pairs={{0,4},{1,5},{2,6},{3,7},{4,0},{5,1},{6,2},{7,3},{8,12},{9,13},{10,... | collective-permute-start | bytes 196616 | tf_op jit(solution)/shard_map/gather_state/ppermute | solution.py:369
  10.4 0.3 collective-permute-start.1
  10.7 2.6 %collective-permute-start.8 = (f32[1,128,128]{2,1,0:T(8,128)S(1)}, f32[1,128,128]{2,1,0:T(8,128)S(1)}, u32[]{:S(2)}, u32[]{:S(2)}) collective-permute-start(f32[1,128,128]{2,1,0:T(8,128)S(1)} %copy-done.2), channel_id=1, source_target_pairs={{0,8},{2,10},{4,12},{6,14},{8,0},{10,2},{12,4},{14,6},{1,9},{3,11}... | collective-permute-start | bytes 196616 | tf_op jit(solution)/shard_map/gather_state/ppermute | solution.py:363
  13.3 0.0 collective-permute-start.4
  13.3 0.0 collective-permute-done.3.refs_3_
  13.3 0.5 collective-permute-start.7
  13.8 0.6 collective-permute-done.2.refs_2_
  14.4 0.0 collective-permute-start.6
  14.4 0.2 collective-permute-done.1.refs_1_
  14.7 0.3 collective-permute-start.5
  15.0 0.0 copy-done.3
  15.0 0.9 %collective-permute-done.8.refs_12_.far = f32[1,128,128]{2,1,0:T(8,128)S(1)} collective-permute-done((f32[1,128,128]{2,1,0:T(8,128)S(1)}, f32[1,128,128]{2,1,0:T(8,128)S(1)}, u32[]{:S(2)}, u32[]{:S(2)}) %collective-permute-start.8) | collective-permute-done | bytes 65568 | tf_op jit(solution)/shard_map/gather_state/ppermute | solution.py:363
  15.9 0.0 collective-permute-done.4.refs_4_
  15.9 0.0 collective-permute-done.7.refs_7_
  15.9 0.0 collective-permute-done.6.refs_6_
  15.9 0.0 collective-permute-done.5.refs_5_
  15.9 4.1 %first_sigma.1 = (bf16[1040,128]{1,0:T(8,128)(2,1)S(1)}, f32[16,128,128]{2,1,0:T(8,128)S(1)}, bf16[16,128,128]{2,1,0:T(8,128)(2,1)S(1)}, bf16[12,12,128,128]{3,2...) custom-call(bf16[2,128,128]{2,1,0:T(8,128)(2,1)S(1)} %pair.1.refs_0_, ...), custom_call_target="tpu_custom_call" | custom-call | flops 1207959552 | bytes 10035776 | tf_op jit(solution)/shard_map/first_sigma/first_sigma/pallas_call | solution.py:341
  20.0 0.3 collective-permute-start.9
  20.4 1.3 %collective-permute-done.9.refs_1_ = bf16[1040,128]{1,0:T(8,128)(2,1)S(1)} collective-permute-done((bf16[1040,128]{1,0:T(8,128)(2,1)S(1)}, bf16[1040,128]{1,0:T(8,128)(2,1)S(1)}, u32[]{:S(2)}, u32[]{:S(2)}) %collective-permute-start.9) | collective-permute-done | bytes 266272 | tf_op jit(solution)/shard_map/sum_first/ppermute | solution.py:358
  21.7 0.1 chip_sum.2
  21.7 2.5 %collective-permute-start.10 = (bf16[272,128]{1,0:T(8,128)(2,1)S(1)}, bf16[272,128]{1,0:T(8,128)(2,1)S(1)}, u32[]{:S(2)}, u32[]{:S(2)}) collective-permute-start(bf16[272,128]{1,0:T(8,128)(2,1)S(1)} %get-tuple-element.38), channel_id=1, source_target_pairs={{0,6},{1,5},{2,4},{3,7},{4,2},{5,1},{6,0},{7,3},{8,14},{9,13},{10,... | collective-permute-start | bytes 208904 | tf_op jit(solution)/shard_map/sum_first/ppermute | solution.py:369
  24.3 0.6 collective-permute-start.11
  24.9 0.4 collective-permute-start.12
  25.3 0.1 norms.1
  25.4 1.8 %collective-permute-done.10.refs_1_ = bf16[272,128]{1,0:T(8,128)(2,1)S(1)} collective-permute-done((bf16[272,128]{1,0:T(8,128)(2,1)S(1)}, bf16[272,128]{1,0:T(8,128)(2,1)S(1)}, u32[]{:S(2)}, u32[]{:S(2)}) %collective-permute-start.10) | collective-permute-done | bytes 69664 | tf_op jit(solution)/shard_map/sum_first/ppermute | solution.py:369
  27.2 2.1 %collective-permute-done.11.refs_2_ = bf16[272,128]{1,0:T(8,128)(2,1)S(1)} collective-permute-done((bf16[272,128]{1,0:T(8,128)(2,1)S(1)}, bf16[272,128]{1,0:T(8,128)(2,1)S(1)}, u32[]{:S(2)}, u32[]{:S(2)}) %collective-permute-start.11) | collective-permute-done | bytes 69664 | tf_op jit(solution)/shard_map/sum_first/ppermute | solution.py:369
  29.3 0.0 collective-permute-done.12.refs_3_
  29.4 0.1 for_far.2
  29.5 3.3 %collective-permute-start.13 = (bf16[272,128]{1,0:T(8,128)(2,1)S(1)}, bf16[272,128]{1,0:T(8,128)(2,1)S(1)}, u32[]{:S(2)}, u32[]{:S(2)}) collective-permute-start(bf16[272,128]{1,0:T(8,128)(2,1)S(1)} %for_far.2), channel_id=1, source_target_pairs={{0,8},{2,10},{4,12},{6,14},{8,0},{10,2},{12,4},{14,6},{1,9},{3,11}... | collective-permute-start | bytes 208904 | tf_op jit(solution)/shard_map/sum_first/ppermute | solution.py:363
  32.8 3.1 %collective-permute-done.13.got = bf16[272,128]{1,0:T(8,128)(2,1)S(1)} collective-permute-done((bf16[272,128]{1,0:T(8,128)(2,1)S(1)}, bf16[272,128]{1,0:T(8,128)(2,1)S(1)}, u32[]{:S(2)}, u32[]{:S(2)}) %collective-permute-start.13) | collective-permute-done | bytes 69664 | tf_op jit(solution)/shard_map/sum_first/ppermute | solution.py:363
  35.8 0.1 residual.1
  36.0 0.4 collective-permute-start.16
  36.4 2.1 %collective-permute-start.15 = (bf16[2,128,128]{2,1,0:T(8,128)(2,1)S(1)}, bf16[2,128,128]{2,1,0:T(8,128)(2,1)S(1)}, u32[]{:S(2)}, u32[]{:S(2)}) collective-permute-start(bf16[2,128,128]{2,1,0:T(8,128)(2,1)S(1)} %get-tuple-element.44.refs_0_), channel_id=1, source_target_pairs={{0,4},{1,5},{2,6},{3,7},{4,0},{5,1},{6,2},{7,3},{8,12},{9,13},{10,... | collective-permute-start | bytes 196616 | tf_op jit(solution)/shard_map/gather_residual/ppermute | solution.py:369
  38.6 1.0 %collective-permute-start.14 = (bf16[2,128,128]{2,1,0:T(8,128)(2,1)S(1)}, bf16[2,128,128]{2,1,0:T(8,128)(2,1)S(1)}, u32[]{:S(2)}, u32[]{:S(2)}) collective-permute-start(bf16[2,128,128]{2,1,0:T(8,128)(2,1)S(1)} %get-tuple-element.44.refs_0_), channel_id=1, source_target_pairs={{0,2},{1,3},{2,0},{3,1},{4,6},{5,7},{6,4},{7,5},{8,10},{9,11},{10,... | collective-permute-start | bytes 196616 | tf_op jit(solution)/shard_map/gather_residual/ppermute | solution.py:369
  39.5 0.0 collective-permute-start.17
  39.5 1.7 %collective-permute-done.16.refs_3_ = bf16[2,128,128]{2,1,0:T(8,128)(2,1)S(1)} collective-permute-done((bf16[2,128,128]{2,1,0:T(8,128)(2,1)S(1)}, bf16[2,128,128]{2,1,0:T(8,128)(2,1)S(1)}, u32[]{:S(2)}, u32[]{:S(2)}) %collective-permute-start.16) | collective-permute-done | bytes 65568 | tf_op jit(solution)/shard_map/gather_residual/ppermute | solution.py:369
  41.2 0.0 collective-permute-start.20
  41.2 0.3 collective-permute-done.15.refs_2_
  41.5 0.2 collective-permute-start.19
  41.7 1.1 %collective-permute-done.14.refs_1_ = bf16[2,128,128]{2,1,0:T(8,128)(2,1)S(1)} collective-permute-done((bf16[2,128,128]{2,1,0:T(8,128)(2,1)S(1)}, bf16[2,128,128]{2,1,0:T(8,128)(2,1)S(1)}, u32[]{:S(2)}, u32[]{:S(2)}) %collective-permute-start.14) | collective-permute-done | bytes 65568 | tf_op jit(solution)/shard_map/gather_residual/ppermute | solution.py:369
  42.8 0.0 collective-permute-start.18
  42.8 0.0 collective-permute-done.17.refs_4_
  42.8 0.0 collective-permute-done.20.refs_7_
  42.9 0.0 collective-permute-done.19.refs_6_
  42.9 1.2 %collective-permute-done.18.refs_5_ = bf16[2,128,128]{2,1,0:T(8,128)(2,1)S(1)} collective-permute-done((bf16[2,128,128]{2,1,0:T(8,128)(2,1)S(1)}, bf16[2,128,128]{2,1,0:T(8,128)(2,1)S(1)}, u32[]{:S(2)}, u32[]{:S(2)}) %collective-permute-start.18) | collective-permute-done | bytes 65568 | tf_op jit(solution)/shard_map/gather_residual/ppermute | solution.py:358
  44.1 4.0 %second_sigma.1 = (bf16[1040,128]{1,0:T(8,128)(2,1)S(1)}, f32[16,128,128]{2,1,0:T(8,128)S(1)}, f32[8,128]{1,0:T(8,128)S(1)}, f32[1,128,128]{2,1,0:T(8,128)}) custom-call(bf16[2,128,128]{2,1,0:T(8,128)(2,1)S(1)} %get-tuple-element.44.refs_0_, bf16[2,128,128]{2,1,0:T(8,128)(2,1)S(1)} %collective-permute-done.14.refs_1_, ...), custom_call_target="tpu_custom_call" | custom-call | flops 1207959552 | bytes 10555968 | tf_op jit(solution)/shard_map/second_sigma/second_sigma/pallas_call | solution.py:341
  48.1 0.2 collective-permute-start.21
  48.4 1.4 %collective-permute-done.21.refs_1_ = bf16[1040,128]{1,0:T(8,128)(2,1)S(1)} collective-permute-done((bf16[1040,128]{1,0:T(8,128)(2,1)S(1)}, bf16[1040,128]{1,0:T(8,128)(2,1)S(1)}, u32[]{:S(2)}, u32[]{:S(2)}) %collective-permute-start.21) | collective-permute-done | bytes 266272 | tf_op jit(solution)/shard_map/sum_second/ppermute | solution.py:358
  49.8 0.1 chip_sum.3
  49.8 0.6 %collective-permute-start.22 = (bf16[272,128]{1,0:T(8,128)(2,1)S(1)}, bf16[272,128]{1,0:T(8,128)(2,1)S(1)}, u32[]{:S(2)}, u32[]{:S(2)}) collective-permute-start(bf16[272,128]{1,0:T(8,128)(2,1)S(1)} %get-tuple-element.53), channel_id=1, source_target_pairs={{0,6},{1,5},{2,4},{3,7},{4,2},{5,1},{6,0},{7,3},{8,14},{9,13},{10,... | collective-permute-start | bytes 208904 | tf_op jit(solution)/shard_map/sum_second/ppermute | solution.py:369
  50.5 1.1 %collective-permute-start.23 = (bf16[272,128]{1,0:T(8,128)(2,1)S(1)}, bf16[272,128]{1,0:T(8,128)(2,1)S(1)}, u32[]{:S(2)}, u32[]{:S(2)}) collective-permute-start(bf16[272,128]{1,0:T(8,128)(2,1)S(1)} %get-tuple-element.54), channel_id=1, source_target_pairs={{0,2},{1,3},{2,0},{3,1},{4,6},{5,7},{6,4},{7,5},{8,10},{9,11},{10,... | collective-permute-start | bytes 208904 | tf_op jit(solution)/shard_map/sum_second/ppermute | solution.py:369
  51.5 1.9 %collective-permute-start.24 = (bf16[272,128]{1,0:T(8,128)(2,1)S(1)}, bf16[272,128]{1,0:T(8,128)(2,1)S(1)}, u32[]{:S(2)}, u32[]{:S(2)}) collective-permute-start(bf16[272,128]{1,0:T(8,128)(2,1)S(1)} %get-tuple-element.55), channel_id=1, source_target_pairs={{0,4},{1,7},{2,6},{3,5},{4,0},{5,3},{6,2},{7,1},{8,12},{9,15},{10,... | collective-permute-start | bytes 208904 | tf_op jit(solution)/shard_map/sum_second/ppermute | solution.py:369
  53.4 2.5 %collective-permute-done.22.refs_1_ = bf16[272,128]{1,0:T(8,128)(2,1)S(1)} collective-permute-done((bf16[272,128]{1,0:T(8,128)(2,1)S(1)}, bf16[272,128]{1,0:T(8,128)(2,1)S(1)}, u32[]{:S(2)}, u32[]{:S(2)}) %collective-permute-start.22) | collective-permute-done | bytes 69664 | tf_op jit(solution)/shard_map/sum_second/ppermute | solution.py:369
  55.9 0.4 collective-permute-done.23.refs_2_
  56.3 0.0 collective-permute-done.24.refs_3_
  56.3 2.7 %collective-permute-start.25 = (bf16[144,128]{1,0:T(8,128)(2,1)S(1)}, bf16[144,128]{1,0:T(8,128)(2,1)S(1)}, u32[]{:S(2)}, u32[]{:S(2)}) collective-permute-start(bf16[144,128]{1,0:T(8,128)(2,1)S(1)} %for_far.3), channel_id=1, source_target_pairs={{0,8},{2,10},{4,12},{6,14},{8,0},{10,2},{12,4},{14,6},{1,9},{3,11}... | collective-permute-start | bytes 110600 | tf_op jit(solution)/shard_map/sum_second/ppermute | solution.py:363
  59.0 2.3 %collective-permute-done.25.got = bf16[144,128]{1,0:T(8,128)(2,1)S(1)} collective-permute-done((bf16[144,128]{1,0:T(8,128)(2,1)S(1)}, bf16[144,128]{1,0:T(8,128)(2,1)S(1)}, u32[]{:S(2)}, u32[]{:S(2)}) %collective-permute-start.25) | collective-permute-done | bytes 36896 | tf_op jit(solution)/shard_map/sum_second/ppermute | solution.py:363
  61.3 0.7 %outputs.1 = (bf16[1,128,128]{2,1,0:T(8,128)(2,1)}, f32[1,128,128]{2,1,0:T(8,128)}, f32[4]{0:T(128)}) custom-call(f32[2,136,128]{2,1,0:T(8,128)S(1)} %near_sum.3.refs_0_.part, bf16[144,128]{1,0:T(8,128)(2,1)S(1)} %collective-permute-done.25.got, bf16[16,128,128]{2,1,0:T(8,128)(2,1)S(1)} %get-tuple-element.41.wave.refs_9_, ...), custom_call_target="tpu_custom_call" | custom-call | flops 262144 | bytes 966656 | tf_op jit(solution)/shard_map/outputs/outputs/pallas_call | solution.py:341
  (16 shorter events, 0.1 us)
Async XLA Ops:
  0.6 10.1 %copy-start.2 = (f32[1,128,128]{2,1,0:T(8,128)S(1)}, f32[1,128,128]{2,1,0:T(8,128)}, u32[]{:S(2)}) copy-start(f32[1,128,128]{2,1,0:T(8,128)} %precond.1) | copy-start | bytes 196612
  0.6 14.3 %copy-start.4 = (s32[12,12]{1,0:T(8,128)S(1)}, s32[12,12]{1,0:T(8,128)}, u32[]{:S(2)}) copy-start(s32[12,12]{1,0:T(8,128)} %tgt.1) | copy-start | bytes 1732
  0.7 14.3 %copy-start.3 = (s32[12,12]{1,0:T(8,128)S(1)}, s32[12,12]{1,0:T(8,128)}, u32[]{:S(2)}) copy-start(s32[12,12]{1,0:T(8,128)} %src.1) | copy-start | bytes 1732
  0.7 15.3 %copy-start = (bf16[12,12,128,128]{3,2,1,0:T(8,128)(2,1)S(1)}, bf16[12,12,128,128]{3,2,1,0:T(8,128)(2,1)}, u32[]{:S(2)}) copy-start(bf16[12,12,128,128]{3,2,1,0:T(8,128)(2,1)} %refs_10_.3) | copy-start | bytes 14155780
  0.7 15.3 %copy-start.1 = (bf16[12,12,128,128]{3,2,1,0:T(8,128)(2,1)S(1)}, bf16[12,12,128,128]{3,2,1,0:T(8,128)(2,1)}, u32[]{:S(2)}) copy-start(bf16[12,12,128,128]{3,2,1,0:T(8,128)(2,1)} %refs_11_.1) | copy-start | bytes 14155780
  0.7 6.6 %collective-permute-start = (bf16[1,128,128]{2,1,0:T(8,128)(2,1)}, bf16[1,128,128]{2,1,0:T(8,128)(2,1)S(1)}, u32[]{:S(2)}, u32[]{:S(2)}) collective-permute-start(bf16[1,128,128]{2,1,0:T(8,128)(2,1)} %block.1), channel_id=1, source_target_pairs={{0,8},{2,10},{4,12},{6,14},{8,0},{10,2},{12,4},{14,6},{1,9},{3,11}... | collective-permute-start | bytes 98312 | tf_op jit(solution)/shard_map/gather_state/ppermute | solution.py:363
  4.8 0.8 %copy-start.5 = (bf16[1,128,128]{2,1,0:T(8,128)(2,1)S(1)}, bf16[1,128,128]{2,1,0:T(8,128)(2,1)}, u32[]{:S(2)}) copy-start(bf16[1,128,128]{2,1,0:T(8,128)(2,1)} %block.1) | copy-start | bytes 98308
  5.6 0.7 %copy-start.6 = (s32[16]{0:T(128)S(1)}, s32[16]{0:T(128)}, u32[]{:S(2)}) copy-start(s32[16]{0:T(128)} %sizes.1) | copy-start | bytes 196
  7.2 6.1 %collective-permute-start.3 = (bf16[2,128,128]{2,1,0:T(8,128)(2,1)S(1)}, bf16[2,128,128]{2,1,0:T(8,128)(2,1)S(1)}, u32[]{:S(2)}, u32[]{:S(2)}) collective-permute-start(bf16[2,128,128]{2,1,0:T(8,128)(2,1)S(1)} %pair.1.refs_0_), channel_id=1, source_target_pairs={{0,6},{1,7},{2,4},{3,5},{4,2},{5,3},{6,0},{7,1},{8,14},{9,15},{10,... | collective-permute-start | bytes 196616 | tf_op jit(solution)/shard_map/gather_state/ppermute | solution.py:369
  9.7 4.7 %collective-permute-start.2 = (bf16[2,128,128]{2,1,0:T(8,128)(2,1)S(1)}, bf16[2,128,128]{2,1,0:T(8,128)(2,1)S(1)}, u32[]{:S(2)}, u32[]{:S(2)}) collective-permute-start(bf16[2,128,128]{2,1,0:T(8,128)(2,1)S(1)} %pair.1.refs_0_), channel_id=1, source_target_pairs={{0,4},{1,5},{2,6},{3,7},{4,0},{5,1},{6,2},{7,3},{8,12},{9,13},{10,... | collective-permute-start | bytes 196616 | tf_op jit(solution)/shard_map/gather_state/ppermute | solution.py:369
  10.4 4.3 %collective-permute-start.1 = (bf16[2,128,128]{2,1,0:T(8,128)(2,1)S(1)}, bf16[2,128,128]{2,1,0:T(8,128)(2,1)S(1)}, u32[]{:S(2)}, u32[]{:S(2)}) collective-permute-start(bf16[2,128,128]{2,1,0:T(8,128)(2,1)S(1)} %pair.1.refs_0_), channel_id=1, source_target_pairs={{0,2},{1,3},{2,0},{3,1},{4,6},{5,7},{6,4},{7,5},{8,10},{9,11},{10,... | collective-permute-start | bytes 196616 | tf_op jit(solution)/shard_map/gather_state/ppermute | solution.py:369
  10.7 5.2 %collective-permute-start.8 = (f32[1,128,128]{2,1,0:T(8,128)S(1)}, f32[1,128,128]{2,1,0:T(8,128)S(1)}, u32[]{:S(2)}, u32[]{:S(2)}) collective-permute-start(f32[1,128,128]{2,1,0:T(8,128)S(1)} %copy-done.2), channel_id=1, source_target_pairs={{0,8},{2,10},{4,12},{6,14},{8,0},{10,2},{12,4},{14,6},{1,9},{3,11}... | collective-permute-start | bytes 196616 | tf_op jit(solution)/shard_map/gather_state/ppermute | solution.py:363
  13.3 2.6 %collective-permute-start.4 = (bf16[2,128,128]{2,1,0:T(8,128)(2,1)S(1)}, bf16[2,128,128]{2,1,0:T(8,128)(2,1)S(1)}, u32[]{:S(2)}, u32[]{:S(2)}) collective-permute-start(bf16[2,128,128]{2,1,0:T(8,128)(2,1)S(1)} %pair.1.refs_0_), channel_id=1, source_target_pairs={{0,1},{1,0},{2,3},{3,2},{4,5},{5,4},{6,7},{7,6},{8,9},{9,8},{10,11... | collective-permute-start | bytes 196616 | tf_op jit(solution)/shard_map/gather_state/ppermute | solution.py:358
  13.3 2.6 %collective-permute-start.7 = (bf16[2,128,128]{2,1,0:T(8,128)(2,1)S(1)}, bf16[2,128,128]{2,1,0:T(8,128)(2,1)S(1)}, u32[]{:S(2)}, u32[]{:S(2)}) collective-permute-start(bf16[2,128,128]{2,1,0:T(8,128)(2,1)S(1)} %collective-permute-done.3.refs_3_), channel_id=1, source_target_pairs={{0,1},{1,0},{2,3},{3,2},{4,5},{5,4},{6,7},{7,6},{8,9},{9,8},{10,11... | collective-permute-start | bytes 196616 | tf_op jit(solution)/shard_map/gather_state/ppermute | solution.py:358
  14.4 1.5 %collective-permute-start.6 = (bf16[2,128,128]{2,1,0:T(8,128)(2,1)S(1)}, bf16[2,128,128]{2,1,0:T(8,128)(2,1)S(1)}, u32[]{:S(2)}, u32[]{:S(2)}) collective-permute-start(bf16[2,128,128]{2,1,0:T(8,128)(2,1)S(1)} %collective-permute-done.2.refs_2_), channel_id=1, source_target_pairs={{0,1},{1,0},{2,3},{3,2},{4,5},{5,4},{6,7},{7,6},{8,9},{9,8},{10,11... | collective-permute-start | bytes 196616 | tf_op jit(solution)/shard_map/gather_state/ppermute | solution.py:358
  14.7 1.3 %collective-permute-start.5 = (bf16[2,128,128]{2,1,0:T(8,128)(2,1)S(1)}, bf16[2,128,128]{2,1,0:T(8,128)(2,1)S(1)}, u32[]{:S(2)}, u32[]{:S(2)}) collective-permute-start(bf16[2,128,128]{2,1,0:T(8,128)(2,1)S(1)} %collective-permute-done.1.refs_1_), channel_id=1, source_target_pairs={{0,1},{1,0},{2,3},{3,2},{4,5},{5,4},{6,7},{7,6},{8,9},{9,8},{10,11... | collective-permute-start | bytes 196616 | tf_op jit(solution)/shard_map/gather_state/ppermute | solution.py:358
  20.0 1.6 %collective-permute-start.9 = (bf16[1040,128]{1,0:T(8,128)(2,1)S(1)}, bf16[1040,128]{1,0:T(8,128)(2,1)S(1)}, u32[]{:S(2)}, u32[]{:S(2)}) collective-permute-start(bf16[1040,128]{1,0:T(8,128)(2,1)S(1)} %get-tuple-element.35), channel_id=1, source_target_pairs={{0,1},{1,0},{2,3},{3,2},{4,5},{5,4},{6,7},{7,6},{8,9},{9,8},{10,11... | collective-permute-start | bytes 798728 | tf_op jit(solution)/shard_map/sum_first/ppermute | solution.py:358
  21.7 5.5 %collective-permute-start.10 = (bf16[272,128]{1,0:T(8,128)(2,1)S(1)}, bf16[272,128]{1,0:T(8,128)(2,1)S(1)}, u32[]{:S(2)}, u32[]{:S(2)}) collective-permute-start(bf16[272,128]{1,0:T(8,128)(2,1)S(1)} %get-tuple-element.38), channel_id=1, source_target_pairs={{0,6},{1,5},{2,4},{3,7},{4,2},{5,1},{6,0},{7,3},{8,14},{9,13},{10,... | collective-permute-start | bytes 208904 | tf_op jit(solution)/shard_map/sum_first/ppermute | solution.py:369
  24.3 5.1 %collective-permute-start.11 = (bf16[272,128]{1,0:T(8,128)(2,1)S(1)}, bf16[272,128]{1,0:T(8,128)(2,1)S(1)}, u32[]{:S(2)}, u32[]{:S(2)}) collective-permute-start(bf16[272,128]{1,0:T(8,128)(2,1)S(1)} %get-tuple-element.39), channel_id=1, source_target_pairs={{0,2},{1,3},{2,0},{3,1},{4,6},{5,7},{6,4},{7,5},{8,10},{9,11},{10,... | collective-permute-start | bytes 208904 | tf_op jit(solution)/shard_map/sum_first/ppermute | solution.py:369
  24.9 4.5 %collective-permute-start.12 = (bf16[272,128]{1,0:T(8,128)(2,1)S(1)}, bf16[272,128]{1,0:T(8,128)(2,1)S(1)}, u32[]{:S(2)}, u32[]{:S(2)}) collective-permute-start(bf16[272,128]{1,0:T(8,128)(2,1)S(1)} %get-tuple-element.40), channel_id=1, source_target_pairs={{0,4},{1,7},{2,6},{3,5},{4,0},{5,3},{6,2},{7,1},{8,12},{9,15},{10,... | collective-permute-start | bytes 208904 | tf_op jit(solution)/shard_map/sum_first/ppermute | solution.py:369
  29.5 6.4 %collective-permute-start.13 = (bf16[272,128]{1,0:T(8,128)(2,1)S(1)}, bf16[272,128]{1,0:T(8,128)(2,1)S(1)}, u32[]{:S(2)}, u32[]{:S(2)}) collective-permute-start(bf16[272,128]{1,0:T(8,128)(2,1)S(1)} %for_far.2), channel_id=1, source_target_pairs={{0,8},{2,10},{4,12},{6,14},{8,0},{10,2},{12,4},{14,6},{1,9},{3,11}... | collective-permute-start | bytes 208904 | tf_op jit(solution)/shard_map/sum_first/ppermute | solution.py:363
  36.0 5.2 %collective-permute-start.16 = (bf16[2,128,128]{2,1,0:T(8,128)(2,1)S(1)}, bf16[2,128,128]{2,1,0:T(8,128)(2,1)S(1)}, u32[]{:S(2)}, u32[]{:S(2)}) collective-permute-start(bf16[2,128,128]{2,1,0:T(8,128)(2,1)S(1)} %get-tuple-element.44.refs_0_), channel_id=1, source_target_pairs={{0,6},{1,7},{2,4},{3,5},{4,2},{5,3},{6,0},{7,1},{8,14},{9,15},{10,... | collective-permute-start | bytes 196616 | tf_op jit(solution)/shard_map/gather_residual/ppermute | solution.py:369
  36.4 5.1 %collective-permute-start.15 = (bf16[2,128,128]{2,1,0:T(8,128)(2,1)S(1)}, bf16[2,128,128]{2,1,0:T(8,128)(2,1)S(1)}, u32[]{:S(2)}, u32[]{:S(2)}) collective-permute-start(bf16[2,128,128]{2,1,0:T(8,128)(2,1)S(1)} %get-tuple-element.44.refs_0_), channel_id=1, source_target_pairs={{0,4},{1,5},{2,6},{3,7},{4,0},{5,1},{6,2},{7,3},{8,12},{9,13},{10,... | collective-permute-start | bytes 196616 | tf_op jit(solution)/shard_map/gather_residual/ppermute | solution.py:369
  38.6 4.3 %collective-permute-start.14 = (bf16[2,128,128]{2,1,0:T(8,128)(2,1)S(1)}, bf16[2,128,128]{2,1,0:T(8,128)(2,1)S(1)}, u32[]{:S(2)}, u32[]{:S(2)}) collective-permute-start(bf16[2,128,128]{2,1,0:T(8,128)(2,1)S(1)} %get-tuple-element.44.refs_0_), channel_id=1, source_target_pairs={{0,2},{1,3},{2,0},{3,1},{4,6},{5,7},{6,4},{7,5},{8,10},{9,11},{10,... | collective-permute-start | bytes 196616 | tf_op jit(solution)/shard_map/gather_residual/ppermute | solution.py:369
  39.5 3.3 %collective-permute-start.17 = (bf16[2,128,128]{2,1,0:T(8,128)(2,1)S(1)}, bf16[2,128,128]{2,1,0:T(8,128)(2,1)S(1)}, u32[]{:S(2)}, u32[]{:S(2)}) collective-permute-start(bf16[2,128,128]{2,1,0:T(8,128)(2,1)S(1)} %get-tuple-element.44.refs_0_), channel_id=1, source_target_pairs={{0,1},{1,0},{2,3},{3,2},{4,5},{5,4},{6,7},{7,6},{8,9},{9,8},{10,11... | collective-permute-start | bytes 196616 | tf_op jit(solution)/shard_map/gather_residual/ppermute | solution.py:358
  41.2 1.6 %collective-permute-start.20 = (bf16[2,128,128]{2,1,0:T(8,128)(2,1)S(1)}, bf16[2,128,128]{2,1,0:T(8,128)(2,1)S(1)}, u32[]{:S(2)}, u32[]{:S(2)}) collective-permute-start(bf16[2,128,128]{2,1,0:T(8,128)(2,1)S(1)} %collective-permute-done.16.refs_3_), channel_id=1, source_target_pairs={{0,1},{1,0},{2,3},{3,2},{4,5},{5,4},{6,7},{7,6},{8,9},{9,8},{10,11... | collective-permute-start | bytes 196616 | tf_op jit(solution)/shard_map/gather_residual/ppermute | solution.py:358
  41.5 1.3 %collective-permute-start.19 = (bf16[2,128,128]{2,1,0:T(8,128)(2,1)S(1)}, bf16[2,128,128]{2,1,0:T(8,128)(2,1)S(1)}, u32[]{:S(2)}, u32[]{:S(2)}) collective-permute-start(bf16[2,128,128]{2,1,0:T(8,128)(2,1)S(1)} %collective-permute-done.15.refs_2_), channel_id=1, source_target_pairs={{0,1},{1,0},{2,3},{3,2},{4,5},{5,4},{6,7},{7,6},{8,9},{9,8},{10,11... | collective-permute-start | bytes 196616 | tf_op jit(solution)/shard_map/gather_residual/ppermute | solution.py:358
  42.8 1.3 %collective-permute-start.18 = (bf16[2,128,128]{2,1,0:T(8,128)(2,1)S(1)}, bf16[2,128,128]{2,1,0:T(8,128)(2,1)S(1)}, u32[]{:S(2)}, u32[]{:S(2)}) collective-permute-start(bf16[2,128,128]{2,1,0:T(8,128)(2,1)S(1)} %collective-permute-done.14.refs_1_), channel_id=1, source_target_pairs={{0,1},{1,0},{2,3},{3,2},{4,5},{5,4},{6,7},{7,6},{8,9},{9,8},{10,11... | collective-permute-start | bytes 196616 | tf_op jit(solution)/shard_map/gather_residual/ppermute | solution.py:358
  48.1 1.6 %collective-permute-start.21 = (bf16[1040,128]{1,0:T(8,128)(2,1)S(1)}, bf16[1040,128]{1,0:T(8,128)(2,1)S(1)}, u32[]{:S(2)}, u32[]{:S(2)}) collective-permute-start(bf16[1040,128]{1,0:T(8,128)(2,1)S(1)} %get-tuple-element.50), channel_id=1, source_target_pairs={{0,1},{1,0},{2,3},{3,2},{4,5},{5,4},{6,7},{7,6},{8,9},{9,8},{10,11... | collective-permute-start | bytes 798728 | tf_op jit(solution)/shard_map/sum_second/ppermute | solution.py:358
  49.8 6.1 %collective-permute-start.22 = (bf16[272,128]{1,0:T(8,128)(2,1)S(1)}, bf16[272,128]{1,0:T(8,128)(2,1)S(1)}, u32[]{:S(2)}, u32[]{:S(2)}) collective-permute-start(bf16[272,128]{1,0:T(8,128)(2,1)S(1)} %get-tuple-element.53), channel_id=1, source_target_pairs={{0,6},{1,5},{2,4},{3,7},{4,2},{5,1},{6,0},{7,3},{8,14},{9,13},{10,... | collective-permute-start | bytes 208904 | tf_op jit(solution)/shard_map/sum_second/ppermute | solution.py:369
  50.5 5.8 %collective-permute-start.23 = (bf16[272,128]{1,0:T(8,128)(2,1)S(1)}, bf16[272,128]{1,0:T(8,128)(2,1)S(1)}, u32[]{:S(2)}, u32[]{:S(2)}) collective-permute-start(bf16[272,128]{1,0:T(8,128)(2,1)S(1)} %get-tuple-element.54), channel_id=1, source_target_pairs={{0,2},{1,3},{2,0},{3,1},{4,6},{5,7},{6,4},{7,5},{8,10},{9,11},{10,... | collective-permute-start | bytes 208904 | tf_op jit(solution)/shard_map/sum_second/ppermute | solution.py:369
  51.5 4.7 %collective-permute-start.24 = (bf16[272,128]{1,0:T(8,128)(2,1)S(1)}, bf16[272,128]{1,0:T(8,128)(2,1)S(1)}, u32[]{:S(2)}, u32[]{:S(2)}) collective-permute-start(bf16[272,128]{1,0:T(8,128)(2,1)S(1)} %get-tuple-element.55), channel_id=1, source_target_pairs={{0,4},{1,7},{2,6},{3,5},{4,0},{5,3},{6,2},{7,1},{8,12},{9,15},{10,... | collective-permute-start | bytes 208904 | tf_op jit(solution)/shard_map/sum_second/ppermute | solution.py:369
  56.3 4.9 %collective-permute-start.25 = (bf16[144,128]{1,0:T(8,128)(2,1)S(1)}, bf16[144,128]{1,0:T(8,128)(2,1)S(1)}, u32[]{:S(2)}, u32[]{:S(2)}) collective-permute-start(bf16[144,128]{1,0:T(8,128)(2,1)S(1)} %for_far.3), channel_id=1, source_target_pairs={{0,8},{2,10},{4,12},{6,14},{8,0},{10,2},{12,4},{14,6},{1,9},{3,11}... | collective-permute-start | bytes 110600 | tf_op jit(solution)/shard_map/sum_second/ppermute | solution.py:363

commit v10 on v9

--- a/solution.py
+++ b/solution.py
@@ -266,10 +266,13 @@
     each(span, store, 0)
 
 
-def norm_kernel(rows, norms):
+def norm_kernel(rows, wave, base, norms):
     norms[0:1] = total(fold(halve(rows[...])[0]))
+    width = wave.shape[2]
+    half = wave.shape[0] // 4
     for i in range(2):
-        norms[1 + i : 2 + i] = 1.0 / jnp.maximum(total(fold(rows[NEAR * i])), TINY)
+        dot = total(fold(base[i, 0:width] * wave[NEAR * i].astype(F32)))
+        norms[1 + i : 2 + i] = half * dot / jnp.maximum(total(fold(rows[NEAR * i])), TINY)
 
 
 def both_kernel(part, wave, norms, out):
@@ -278,7 +281,7 @@
     for i in range(2):
         own = wave[NEAR * (1 - i)].astype(F32)
         block = part[1 - i, 0:width]
-        share = total(fold(block * own)) * norms[2 - i : 3 - i]
+        share = norms[2 - i : 3 - i]
         out[at(i, width)] = (block - share * own).astype(BF16)
         rows.append(share)
     out[2 * width :] = tail_of(rows)
@@ -394,7 +397,7 @@
     while span > 2:
         span //= 2
         part = part[:span] + flip_chip(part[span:], NEAR * span)
-    return part
+    return part, base
 
 
 def shards(state, sector_sizes, left, right, source, target, precond):
@@ -435,8 +438,10 @@
             (*pieces, plan, limits, left, right, far), flops,
         )
     with jax.named_scope("sum_first"):
-        (norms,) = call(norm_kernel, "norms", [VMEM], [sums_of], [], (rows,), rows.size)
-        part = scatter(theirs, mine, sums, 0, 1)
+        part, base = scatter(theirs, mine, sums, 0, 1)
+        (norms,) = call(
+            norm_kernel, "norms", [VMEM] * 3, [sums_of], [], (rows, wave, base), rows.size
+        )
         (both,) = call(
             both_kernel, "for_far", [VMEM] * 3, [shape(2 * width + TAIL, width, dtype=BF16)], [],
             (part, wave, norms), part.size,
@@ -457,7 +462,7 @@
             (*pieces, plan, wave, left, flip, first, keep), flops, [VMEM] * 3 + [HBM],
         )
     with jax.named_scope("sum_second"):
-        part = scatter(theirs, mine, sums, 0, 5)
+        part, _ = scatter(theirs, mine, sums, 0, 5)
         (both,) = call(
             lambda *refs: far_kernel(5, *refs), "for_far", [VMEM],
             [shape(width + TAIL, width, dtype=BF16)], [], (part,), part.size,

time: 62.2 us -> 62.1 us (level)
  no operation moved by 1% of the time
where the time goes in v10:
time: 62.1 us; the launch traced here: 61.9 us
  starting transfers between devices  28.3 us (46%)
  waiting for transfers between devices  21.3 us (34%)
  Pallas kernels  9.99 us (16%)
  local copies, waits for them, and re-layouts  1.47 us (2%)
  between operations  0.78 us (1%)
    ppermute x12, starting transfers between devices, flip_near(): return lax.ppermute(x, ('chip', 'core'), pairs)  14.1 us
    ppermute x4, starting transfers between devices, flip_chip(): return lax.ppermute(x, 'chip', [(i, i ^ bits) for i in range(chips)])  12.6 us
    ppermute x12, waiting for transfers between devices, flip_near(): return lax.ppermute(x, ('chip', 'core'), pairs)  10.7 us
    pallas_call x14, Pallas kernels, call(): pl.pallas_call(kernel, name=name, in_specs=ins, out_specs=out_specs or [V...  9.99 us
    ppermute x4, waiting for transfers between devices, flip_chip(): return lax.ppermute(x, 'chip', [(i, i ^ bits) for i in range(chips)])  6.68 us
    ppermute x10, waiting for transfers between devices, swap(): return lax.ppermute(x, 'core', [(0, 1), (1, 0)])  3.93 us
    ppermute x10, starting transfers between devices, swap(): return lax.ppermute(x, 'core', [(0, 1), (1, 0)])  1.56 us
    unnamed x14, local copies, waits for them, and re-layouts  1.47 us
  transfers between devices with their start and end apart: 26, of which 16 were waited for; matrix products, arithmetic and copies ran while one was open for 0% of the time, Pallas kernels for 1%

profile of v10, /device:TPU:0, one launch (start us, length us, event | category | flops | bytes accessed | tf_op | source)
XLA Modules:
  0.0 61.9 jit_solution(9757476501978573880)
XLA Ops:
  0.7 4.1 %collective-permute-start = (bf16[1,128,128]{2,1,0:T(8,128)(2,1)}, bf16[1,128,128]{2,1,0:T(8,128)(2,1)S(1)}, u32[]{:S(2)}, u32[]{:S(2)}) collective-permute-start(bf16[1,128,128]{2,1,0:T(8,128)(2,1)} %block.1), channel_id=1, source_target_pairs={{0,8},{2,10},{4,12},{6,14},{8,0},{10,2},{12,4},{14,6},{1,9},{3,11}... | collective-permute-start | bytes 98312 | tf_op jit(solution)/shard_map/gather_state/ppermute | solution.py:366
  4.8 0.8 %copy-done.5 = bf16[1,128,128]{2,1,0:T(8,128)(2,1)S(1)} copy-done((bf16[1,128,128]{2,1,0:T(8,128)(2,1)S(1)}, bf16[1,128,128]{2,1,0:T(8,128)(2,1)}, u32[]{:S(2)}) %copy-start.5) | copy-done | bytes 32792
  5.6 0.7 %copy-done.6 = s32[16]{0:T(128)S(1)} copy-done((s32[16]{0:T(128)S(1)}, s32[16]{0:T(128)}, u32[]{:S(2)}) %copy-start.6) | copy-done | bytes 88
  6.2 0.6 masks.1
  6.8 0.4 collective-permute-done.far
  7.2 2.5 %collective-permute-start.3 = (bf16[2,128,128]{2,1,0:T(8,128)(2,1)S(1)}, bf16[2,128,128]{2,1,0:T(8,128)(2,1)S(1)}, u32[]{:S(2)}, u32[]{:S(2)}) collective-permute-start(bf16[2,128,128]{2,1,0:T(8,128)(2,1)S(1)} %pair.1.refs_0_), channel_id=1, source_target_pairs={{0,6},{1,7},{2,4},{3,5},{4,2},{5,3},{6,0},{7,1},{8,14},{9,15},{10,... | collective-permute-start | bytes 196616 | tf_op jit(solution)/shard_map/gather_state/ppermute | solution.py:372
  9.7 0.7 %collective-permute-start.2 = (bf16[2,128,128]{2,1,0:T(8,128)(2,1)S(1)}, bf16[2,128,128]{2,1,0:T(8,128)(2,1)S(1)}, u32[]{:S(2)}, u32[]{:S(2)}) collective-permute-start(bf16[2,128,128]{2,1,0:T(8,128)(2,1)S(1)} %pair.1.refs_0_), channel_id=1, source_target_pairs={{0,4},{1,5},{2,6},{3,7},{4,0},{5,1},{6,2},{7,3},{8,12},{9,13},{10,... | collective-permute-start | bytes 196616 | tf_op jit(solution)/shard_map/gather_state/ppermute | solution.py:372
  10.4 0.3 collective-permute-start.1
  10.7 2.6 %collective-permute-start.8 = (f32[1,128,128]{2,1,0:T(8,128)S(1)}, f32[1,128,128]{2,1,0:T(8,128)S(1)}, u32[]{:S(2)}, u32[]{:S(2)}) collective-permute-start(f32[1,128,128]{2,1,0:T(8,128)S(1)} %copy-done.2), channel_id=1, source_target_pairs={{0,8},{2,10},{4,12},{6,14},{8,0},{10,2},{12,4},{14,6},{1,9},{3,11}... | collective-permute-start | bytes 196616 | tf_op jit(solution)/shard_map/gather_state/ppermute | solution.py:366
  13.3 0.0 collective-permute-start.4
  13.3 0.0 collective-permute-done.3.refs_3_
  13.3 0.5 collective-permute-start.7
  13.8 0.6 collective-permute-done.2.refs_2_
  14.4 0.0 collective-permute-start.6
  14.4 0.2 collective-permute-done.1.refs_1_
  14.7 0.3 collective-permute-start.5
  15.0 0.0 copy-done.3
  15.0 0.9 %collective-permute-done.8.refs_12_.far = f32[1,128,128]{2,1,0:T(8,128)S(1)} collective-permute-done((f32[1,128,128]{2,1,0:T(8,128)S(1)}, f32[1,128,128]{2,1,0:T(8,128)S(1)}, u32[]{:S(2)}, u32[]{:S(2)}) %collective-permute-start.8) | collective-permute-done | bytes 65568 | tf_op jit(solution)/shard_map/gather_state/ppermute | solution.py:366
  15.9 0.0 collective-permute-done.4.refs_4_
  15.9 0.0 collective-permute-done.7.refs_7_
  15.9 0.0 collective-permute-done.6.refs_6_
  15.9 0.0 collective-permute-done.5.refs_5_
  15.9 0.0 copy-done
  15.9 4.1 %first_sigma.1 = (bf16[1040,128]{1,0:T(8,128)(2,1)S(1)}, f32[16,128,128]{2,1,0:T(8,128)S(1)}, bf16[16,128,128]{2,1,0:T(8,128)(2,1)S(1)}, bf16[12,12,128,128]{3,2...) custom-call(bf16[2,128,128]{2,1,0:T(8,128)(2,1)S(1)} %pair.1.refs_0_, ...), custom_call_target="tpu_custom_call" | custom-call | flops 1207959552 | bytes 10035776 | tf_op jit(solution)/shard_map/first_sigma/first_sigma/pallas_call | solution.py:344
  20.0 0.3 collective-permute-start.9
  20.4 1.3 %collective-permute-done.9.refs_1_ = bf16[1040,128]{1,0:T(8,128)(2,1)S(1)} collective-permute-done((bf16[1040,128]{1,0:T(8,128)(2,1)S(1)}, bf16[1040,128]{1,0:T(8,128)(2,1)S(1)}, u32[]{:S(2)}, u32[]{:S(2)}) %collective-permute-start.9) | collective-permute-done | bytes 266272 | tf_op jit(solution)/shard_map/sum_first/ppermute | solution.py:361
  21.7 0.1 chip_sum.2
  21.7 2.5 %collective-permute-start.10 = (bf16[272,128]{1,0:T(8,128)(2,1)S(1)}, bf16[272,128]{1,0:T(8,128)(2,1)S(1)}, u32[]{:S(2)}, u32[]{:S(2)}) collective-permute-start(bf16[272,128]{1,0:T(8,128)(2,1)S(1)} %get-tuple-element.38), channel_id=1, source_target_pairs={{0,6},{1,5},{2,4},{3,7},{4,2},{5,1},{6,0},{7,3},{8,14},{9,13},{10,... | collective-permute-start | bytes 208904 | tf_op jit(solution)/shard_map/sum_first/ppermute | solution.py:372
  24.3 0.6 collective-permute-start.11
  24.9 0.4 collective-permute-start.12
  25.3 0.1 norms.1
  25.4 1.8 %collective-permute-done.10.refs_1_ = bf16[272,128]{1,0:T(8,128)(2,1)S(1)} collective-permute-done((bf16[272,128]{1,0:T(8,128)(2,1)S(1)}, bf16[272,128]{1,0:T(8,128)(2,1)S(1)}, u32[]{:S(2)}, u32[]{:S(2)}) %collective-permute-start.10) | collective-permute-done | bytes 69664 | tf_op jit(solution)/shard_map/sum_first/ppermute | solution.py:372
  27.2 2.1 %collective-permute-done.11.refs_2_ = bf16[272,128]{1,0:T(8,128)(2,1)S(1)} collective-permute-done((bf16[272,128]{1,0:T(8,128)(2,1)S(1)}, bf16[272,128]{1,0:T(8,128)(2,1)S(1)}, u32[]{:S(2)}, u32[]{:S(2)}) %collective-permute-start.11) | collective-permute-done | bytes 69664 | tf_op jit(solution)/shard_map/sum_first/ppermute | solution.py:372
  29.3 0.0 collective-permute-done.12.refs_3_
  29.4 3.3 %collective-permute-start.13 = (bf16[272,128]{1,0:T(8,128)(2,1)S(1)}, bf16[272,128]{1,0:T(8,128)(2,1)S(1)}, u32[]{:S(2)}, u32[]{:S(2)}) collective-permute-start(bf16[272,128]{1,0:T(8,128)(2,1)S(1)} %for_far.2), channel_id=1, source_target_pairs={{0,8},{2,10},{4,12},{6,14},{8,0},{10,2},{12,4},{14,6},{1,9},{3,11}... | collective-permute-start | bytes 208904 | tf_op jit(solution)/shard_map/sum_first/ppermute | solution.py:366
  32.7 3.1 %collective-permute-done.13.got = bf16[272,128]{1,0:T(8,128)(2,1)S(1)} collective-permute-done((bf16[272,128]{1,0:T(8,128)(2,1)S(1)}, bf16[272,128]{1,0:T(8,128)(2,1)S(1)}, u32[]{:S(2)}, u32[]{:S(2)}) %collective-permute-start.13) | collective-permute-done | bytes 69664 | tf_op jit(solution)/shard_map/sum_first/ppermute | solution.py:366
  35.8 0.1 residual.1
  35.9 0.4 collective-permute-start.16
  36.3 2.1 %collective-permute-start.15 = (bf16[2,128,128]{2,1,0:T(8,128)(2,1)S(1)}, bf16[2,128,128]{2,1,0:T(8,128)(2,1)S(1)}, u32[]{:S(2)}, u32[]{:S(2)}) collective-permute-start(bf16[2,128,128]{2,1,0:T(8,128)(2,1)S(1)} %get-tuple-element.44.refs_0_), channel_id=1, source_target_pairs={{0,4},{1,5},{2,6},{3,7},{4,0},{5,1},{6,2},{7,3},{8,12},{9,13},{10,... | collective-permute-start | bytes 196616 | tf_op jit(solution)/shard_map/gather_residual/ppermute | solution.py:372
  38.5 1.0 %collective-permute-start.14 = (bf16[2,128,128]{2,1,0:T(8,128)(2,1)S(1)}, bf16[2,128,128]{2,1,0:T(8,128)(2,1)S(1)}, u32[]{:S(2)}, u32[]{:S(2)}) collective-permute-start(bf16[2,128,128]{2,1,0:T(8,128)(2,1)S(1)} %get-tuple-element.44.refs_0_), channel_id=1, source_target_pairs={{0,2},{1,3},{2,0},{3,1},{4,6},{5,7},{6,4},{7,5},{8,10},{9,11},{10,... | collective-permute-start | bytes 196616 | tf_op jit(solution)/shard_map/gather_residual/ppermute | solution.py:372
  39.4 0.0 collective-permute-start.17
  39.4 1.7 %collective-permute-done.16.refs_3_ = bf16[2,128,128]{2,1,0:T(8,128)(2,1)S(1)} collective-permute-done((bf16[2,128,128]{2,1,0:T(8,128)(2,1)S(1)}, bf16[2,128,128]{2,1,0:T(8,128)(2,1)S(1)}, u32[]{:S(2)}, u32[]{:S(2)}) %collective-permute-start.16) | collective-permute-done | bytes 65568 | tf_op jit(solution)/shard_map/gather_residual/ppermute | solution.py:372
  41.1 0.0 collective-permute-start.20
  41.1 0.3 collective-permute-done.15.refs_2_
  41.4 0.2 collective-permute-start.19
  41.6 1.1 %collective-permute-done.14.refs_1_ = bf16[2,128,128]{2,1,0:T(8,128)(2,1)S(1)} collective-permute-done((bf16[2,128,128]{2,1,0:T(8,128)(2,1)S(1)}, bf16[2,128,128]{2,1,0:T(8,128)(2,1)S(1)}, u32[]{:S(2)}, u32[]{:S(2)}) %collective-permute-start.14) | collective-permute-done | bytes 65568 | tf_op jit(solution)/shard_map/gather_residual/ppermute | solution.py:372
  42.8 0.0 collective-permute-start.18
  42.8 0.0 collective-permute-done.17.refs_4_
  42.8 0.0 collective-permute-done.20.refs_7_
  42.8 0.0 collective-permute-done.19.refs_6_
  42.8 1.2 %collective-permute-done.18.refs_5_ = bf16[2,128,128]{2,1,0:T(8,128)(2,1)S(1)} collective-permute-done((bf16[2,128,128]{2,1,0:T(8,128)(2,1)S(1)}, bf16[2,128,128]{2,1,0:T(8,128)(2,1)S(1)}, u32[]{:S(2)}, u32[]{:S(2)}) %collective-permute-start.18) | collective-permute-done | bytes 65568 | tf_op jit(solution)/shard_map/gather_residual/ppermute | solution.py:361
  44.0 4.0 %second_sigma.1 = (bf16[1040,128]{1,0:T(8,128)(2,1)S(1)}, f32[16,128,128]{2,1,0:T(8,128)S(1)}, f32[8,128]{1,0:T(8,128)S(1)}, f32[1,128,128]{2,1,0:T(8,128)}) custom-call(bf16[2,128,128]{2,1,0:T(8,128)(2,1)S(1)} %get-tuple-element.44.refs_0_, bf16[2,128,128]{2,1,0:T(8,128)(2,1)S(1)} %collective-permute-done.14.refs_1_, ...), custom_call_target="tpu_custom_call" | custom-call | flops 1207959552 | bytes 10555968 | tf_op jit(solution)/shard_map/second_sigma/second_sigma/pallas_call | solution.py:344
  48.1 0.2 collective-permute-start.21
  48.3 1.4 %collective-permute-done.21.refs_1_ = bf16[1040,128]{1,0:T(8,128)(2,1)S(1)} collective-permute-done((bf16[1040,128]{1,0:T(8,128)(2,1)S(1)}, bf16[1040,128]{1,0:T(8,128)(2,1)S(1)}, u32[]{:S(2)}, u32[]{:S(2)}) %collective-permute-start.21) | collective-permute-done | bytes 266272 | tf_op jit(solution)/shard_map/sum_second/ppermute | solution.py:361
  49.7 0.1 chip_sum.3
  49.7 0.6 collective-permute-start.22
  50.4 1.1 %collective-permute-start.23 = (bf16[272,128]{1,0:T(8,128)(2,1)S(1)}, bf16[272,128]{1,0:T(8,128)(2,1)S(1)}, u32[]{:S(2)}, u32[]{:S(2)}) collective-permute-start(bf16[272,128]{1,0:T(8,128)(2,1)S(1)} %get-tuple-element.54), channel_id=1, source_target_pairs={{0,2},{1,3},{2,0},{3,1},{4,6},{5,7},{6,4},{7,5},{8,10},{9,11},{10,... | collective-permute-start | bytes 208904 | tf_op jit(solution)/shard_map/sum_second/ppermute | solution.py:372
  51.4 1.9 %collective-permute-start.24 = (bf16[272,128]{1,0:T(8,128)(2,1)S(1)}, bf16[272,128]{1,0:T(8,128)(2,1)S(1)}, u32[]{:S(2)}, u32[]{:S(2)}) collective-permute-start(bf16[272,128]{1,0:T(8,128)(2,1)S(1)} %get-tuple-element.55), channel_id=1, source_target_pairs={{0,4},{1,7},{2,6},{3,5},{4,0},{5,3},{6,2},{7,1},{8,12},{9,15},{10,... | collective-permute-start | bytes 208904 | tf_op jit(solution)/shard_map/sum_second/ppermute | solution.py:372
  53.3 2.5 %collective-permute-done.22.refs_1_ = bf16[272,128]{1,0:T(8,128)(2,1)S(1)} collective-permute-done((bf16[272,128]{1,0:T(8,128)(2,1)S(1)}, bf16[272,128]{1,0:T(8,128)(2,1)S(1)}, u32[]{:S(2)}, u32[]{:S(2)}) %collective-permute-start.22) | collective-permute-done | bytes 69664 | tf_op jit(solution)/shard_map/sum_second/ppermute | solution.py:372
  55.8 0.3 collective-permute-done.23.refs_2_
  56.2 0.0 collective-permute-done.24.refs_3_
  56.2 2.7 %collective-permute-start.25 = (bf16[144,128]{1,0:T(8,128)(2,1)S(1)}, bf16[144,128]{1,0:T(8,128)(2,1)S(1)}, u32[]{:S(2)}, u32[]{:S(2)}) collective-permute-start(bf16[144,128]{1,0:T(8,128)(2,1)S(1)} %for_far.3), channel_id=1, source_target_pairs={{0,8},{2,10},{4,12},{6,14},{8,0},{10,2},{12,4},{14,6},{1,9},{3,11}... | collective-permute-start | bytes 110600 | tf_op jit(solution)/shard_map/sum_second/ppermute | solution.py:366
  58.9 2.2 %collective-permute-done.25.got = bf16[144,128]{1,0:T(8,128)(2,1)S(1)} collective-permute-done((bf16[144,128]{1,0:T(8,128)(2,1)S(1)}, bf16[144,128]{1,0:T(8,128)(2,1)S(1)}, u32[]{:S(2)}, u32[]{:S(2)}) %collective-permute-start.25) | collective-permute-done | bytes 36896 | tf_op jit(solution)/shard_map/sum_second/ppermute | solution.py:366
  61.2 0.7 %outputs.1 = (bf16[1,128,128]{2,1,0:T(8,128)(2,1)}, f32[1,128,128]{2,1,0:T(8,128)}, f32[4]{0:T(128)}) custom-call(f32[2,136,128]{2,1,0:T(8,128)S(1)} %near_sum.3.refs_0_.part, bf16[144,128]{1,0:T(8,128)(2,1)S(1)} %collective-permute-done.25.got, bf16[16,128,128]{2,1,0:T(8,128)(2,1)S(1)} %get-tuple-element.41.wave.refs_9_, ...), custom_call_target="tpu_custom_call" | custom-call | flops 262144 | bytes 966656 | tf_op jit(solution)/shard_map/outputs/outputs/pallas_call | solution.py:344
  (16 shorter events, 0.2 us)
Async XLA Ops:
  0.6 10.1 %copy-start.2 = (f32[1,128,128]{2,1,0:T(8,128)S(1)}, f32[1,128,128]{2,1,0:T(8,128)}, u32[]{:S(2)}) copy-start(f32[1,128,128]{2,1,0:T(8,128)} %precond.1) | copy-start | bytes 196612
  0.6 14.3 %copy-start.4 = (s32[12,12]{1,0:T(8,128)S(1)}, s32[12,12]{1,0:T(8,128)}, u32[]{:S(2)}) copy-start(s32[12,12]{1,0:T(8,128)} %tgt.1) | copy-start | bytes 1732
  0.7 14.3 %copy-start.3 = (s32[12,12]{1,0:T(8,128)S(1)}, s32[12,12]{1,0:T(8,128)}, u32[]{:S(2)}) copy-start(s32[12,12]{1,0:T(8,128)} %src.1) | copy-start | bytes 1732
  0.7 15.3 %copy-start = (bf16[12,12,128,128]{3,2,1,0:T(8,128)(2,1)S(1)}, bf16[12,12,128,128]{3,2,1,0:T(8,128)(2,1)}, u32[]{:S(2)}) copy-start(bf16[12,12,128,128]{3,2,1,0:T(8,128)(2,1)} %refs_10_.3) | copy-start | bytes 14155780
  0.7 15.3 %copy-start.1 = (bf16[12,12,128,128]{3,2,1,0:T(8,128)(2,1)S(1)}, bf16[12,12,128,128]{3,2,1,0:T(8,128)(2,1)}, u32[]{:S(2)}) copy-start(bf16[12,12,128,128]{3,2,1,0:T(8,128)(2,1)} %refs_11_.1) | copy-start | bytes 14155780
  0.7 6.6 %collective-permute-start = (bf16[1,128,128]{2,1,0:T(8,128)(2,1)}, bf16[1,128,128]{2,1,0:T(8,128)(2,1)S(1)}, u32[]{:S(2)}, u32[]{:S(2)}) collective-permute-start(bf16[1,128,128]{2,1,0:T(8,128)(2,1)} %block.1), channel_id=1, source_target_pairs={{0,8},{2,10},{4,12},{6,14},{8,0},{10,2},{12,4},{14,6},{1,9},{3,11}... | collective-permute-start | bytes 98312 | tf_op jit(solution)/shard_map/gather_state/ppermute | solution.py:366
  4.8 0.8 %copy-start.5 = (bf16[1,128,128]{2,1,0:T(8,128)(2,1)S(1)}, bf16[1,128,128]{2,1,0:T(8,128)(2,1)}, u32[]{:S(2)}) copy-start(bf16[1,128,128]{2,1,0:T(8,128)(2,1)} %block.1) | copy-start | bytes 98308
  5.6 0.7 %copy-start.6 = (s32[16]{0:T(128)S(1)}, s32[16]{0:T(128)}, u32[]{:S(2)}) copy-start(s32[16]{0:T(128)} %sizes.1) | copy-start | bytes 196
  7.2 6.1 %collective-permute-start.3 = (bf16[2,128,128]{2,1,0:T(8,128)(2,1)S(1)}, bf16[2,128,128]{2,1,0:T(8,128)(2,1)S(1)}, u32[]{:S(2)}, u32[]{:S(2)}) collective-permute-start(bf16[2,128,128]{2,1,0:T(8,128)(2,1)S(1)} %pair.1.refs_0_), channel_id=1, source_target_pairs={{0,6},{1,7},{2,4},{3,5},{4,2},{5,3},{6,0},{7,1},{8,14},{9,15},{10,... | collective-permute-start | bytes 196616 | tf_op jit(solution)/shard_map/gather_state/ppermute | solution.py:372
  9.7 4.7 %collective-permute-start.2 = (bf16[2,128,128]{2,1,0:T(8,128)(2,1)S(1)}, bf16[2,128,128]{2,1,0:T(8,128)(2,1)S(1)}, u32[]{:S(2)}, u32[]{:S(2)}) collective-permute-start(bf16[2,128,128]{2,1,0:T(8,128)(2,1)S(1)} %pair.1.refs_0_), channel_id=1, source_target_pairs={{0,4},{1,5},{2,6},{3,7},{4,0},{5,1},{6,2},{7,3},{8,12},{9,13},{10,... | collective-permute-start | bytes 196616 | tf_op jit(solution)/shard_map/gather_state/ppermute | solution.py:372
  10.4 4.3 %collective-permute-start.1 = (bf16[2,128,128]{2,1,0:T(8,128)(2,1)S(1)}, bf16[2,128,128]{2,1,0:T(8,128)(2,1)S(1)}, u32[]{:S(2)}, u32[]{:S(2)}) collective-permute-start(bf16[2,128,128]{2,1,0:T(8,128)(2,1)S(1)} %pair.1.refs_0_), channel_id=1, source_target_pairs={{0,2},{1,3},{2,0},{3,1},{4,6},{5,7},{6,4},{7,5},{8,10},{9,11},{10,... | collective-permute-start | bytes 196616 | tf_op jit(solution)/shard_map/gather_state/ppermute | solution.py:372
  10.7 5.2 %collective-permute-start.8 = (f32[1,128,128]{2,1,0:T(8,128)S(1)}, f32[1,128,128]{2,1,0:T(8,128)S(1)}, u32[]{:S(2)}, u32[]{:S(2)}) collective-permute-start(f32[1,128,128]{2,1,0:T(8,128)S(1)} %copy-done.2), channel_id=1, source_target_pairs={{0,8},{2,10},{4,12},{6,14},{8,0},{10,2},{12,4},{14,6},{1,9},{3,11}... | collective-permute-start | bytes 196616 | tf_op jit(solution)/shard_map/gather_state/ppermute | solution.py:366
  13.3 2.6 %collective-permute-start.4 = (bf16[2,128,128]{2,1,0:T(8,128)(2,1)S(1)}, bf16[2,128,128]{2,1,0:T(8,128)(2,1)S(1)}, u32[]{:S(2)}, u32[]{:S(2)}) collective-permute-start(bf16[2,128,128]{2,1,0:T(8,128)(2,1)S(1)} %pair.1.refs_0_), channel_id=1, source_target_pairs={{0,1},{1,0},{2,3},{3,2},{4,5},{5,4},{6,7},{7,6},{8,9},{9,8},{10,11... | collective-permute-start | bytes 196616 | tf_op jit(solution)/shard_map/gather_state/ppermute | solution.py:361
  13.3 2.6 %collective-permute-start.7 = (bf16[2,128,128]{2,1,0:T(8,128)(2,1)S(1)}, bf16[2,128,128]{2,1,0:T(8,128)(2,1)S(1)}, u32[]{:S(2)}, u32[]{:S(2)}) collective-permute-start(bf16[2,128,128]{2,1,0:T(8,128)(2,1)S(1)} %collective-permute-done.3.refs_3_), channel_id=1, source_target_pairs={{0,1},{1,0},{2,3},{3,2},{4,5},{5,4},{6,7},{7,6},{8,9},{9,8},{10,11... | collective-permute-start | bytes 196616 | tf_op jit(solution)/shard_map/gather_state/ppermute | solution.py:361
  14.4 1.5 %collective-permute-start.6 = (bf16[2,128,128]{2,1,0:T(8,128)(2,1)S(1)}, bf16[2,128,128]{2,1,0:T(8,128)(2,1)S(1)}, u32[]{:S(2)}, u32[]{:S(2)}) collective-permute-start(bf16[2,128,128]{2,1,0:T(8,128)(2,1)S(1)} %collective-permute-done.2.refs_2_), channel_id=1, source_target_pairs={{0,1},{1,0},{2,3},{3,2},{4,5},{5,4},{6,7},{7,6},{8,9},{9,8},{10,11... | collective-permute-start | bytes 196616 | tf_op jit(solution)/shard_map/gather_state/ppermute | solution.py:361
  14.7 1.3 %collective-permute-start.5 = (bf16[2,128,128]{2,1,0:T(8,128)(2,1)S(1)}, bf16[2,128,128]{2,1,0:T(8,128)(2,1)S(1)}, u32[]{:S(2)}, u32[]{:S(2)}) collective-permute-start(bf16[2,128,128]{2,1,0:T(8,128)(2,1)S(1)} %collective-permute-done.1.refs_1_), channel_id=1, source_target_pairs={{0,1},{1,0},{2,3},{3,2},{4,5},{5,4},{6,7},{7,6},{8,9},{9,8},{10,11... | collective-permute-start | bytes 196616 | tf_op jit(solution)/shard_map/gather_state/ppermute | solution.py:361
  20.0 1.6 %collective-permute-start.9 = (bf16[1040,128]{1,0:T(8,128)(2,1)S(1)}, bf16[1040,128]{1,0:T(8,128)(2,1)S(1)}, u32[]{:S(2)}, u32[]{:S(2)}) collective-permute-start(bf16[1040,128]{1,0:T(8,128)(2,1)S(1)} %get-tuple-element.35), channel_id=1, source_target_pairs={{0,1},{1,0},{2,3},{3,2},{4,5},{5,4},{6,7},{7,6},{8,9},{9,8},{10,11... | collective-permute-start | bytes 798728 | tf_op jit(solution)/shard_map/sum_first/ppermute | solution.py:361
  21.7 5.5 %collective-permute-start.10 = (bf16[272,128]{1,0:T(8,128)(2,1)S(1)}, bf16[272,128]{1,0:T(8,128)(2,1)S(1)}, u32[]{:S(2)}, u32[]{:S(2)}) collective-permute-start(bf16[272,128]{1,0:T(8,128)(2,1)S(1)} %get-tuple-element.38), channel_id=1, source_target_pairs={{0,6},{1,5},{2,4},{3,7},{4,2},{5,1},{6,0},{7,3},{8,14},{9,13},{10,... | collective-permute-start | bytes 208904 | tf_op jit(solution)/shard_map/sum_first/ppermute | solution.py:372
  24.3 5.1 %collective-permute-start.11 = (bf16[272,128]{1,0:T(8,128)(2,1)S(1)}, bf16[272,128]{1,0:T(8,128)(2,1)S(1)}, u32[]{:S(2)}, u32[]{:S(2)}) collective-permute-start(bf16[272,128]{1,0:T(8,128)(2,1)S(1)} %get-tuple-element.39), channel_id=1, source_target_pairs={{0,2},{1,3},{2,0},{3,1},{4,6},{5,7},{6,4},{7,5},{8,10},{9,11},{10,... | collective-permute-start | bytes 208904 | tf_op jit(solution)/shard_map/sum_first/ppermute | solution.py:372
  24.9 4.5 %collective-permute-start.12 = (bf16[272,128]{1,0:T(8,128)(2,1)S(1)}, bf16[272,128]{1,0:T(8,128)(2,1)S(1)}, u32[]{:S(2)}, u32[]{:S(2)}) collective-permute-start(bf16[272,128]{1,0:T(8,128)(2,1)S(1)} %get-tuple-element.40), channel_id=1, source_target_pairs={{0,4},{1,7},{2,6},{3,5},{4,0},{5,3},{6,2},{7,1},{8,12},{9,15},{10,... | collective-permute-start | bytes 208904 | tf_op jit(solution)/shard_map/sum_first/ppermute | solution.py:372
  29.4 6.3 %collective-permute-start.13 = (bf16[272,128]{1,0:T(8,128)(2,1)S(1)}, bf16[272,128]{1,0:T(8,128)(2,1)S(1)}, u32[]{:S(2)}, u32[]{:S(2)}) collective-permute-start(bf16[272,128]{1,0:T(8,128)(2,1)S(1)} %for_far.2), channel_id=1, source_target_pairs={{0,8},{2,10},{4,12},{6,14},{8,0},{10,2},{12,4},{14,6},{1,9},{3,11}... | collective-permute-start | bytes 208904 | tf_op jit(solution)/shard_map/sum_first/ppermute | solution.py:366
  35.9 5.2 %collective-permute-start.16 = (bf16[2,128,128]{2,1,0:T(8,128)(2,1)S(1)}, bf16[2,128,128]{2,1,0:T(8,128)(2,1)S(1)}, u32[]{:S(2)}, u32[]{:S(2)}) collective-permute-start(bf16[2,128,128]{2,1,0:T(8,128)(2,1)S(1)} %get-tuple-element.44.refs_0_), channel_id=1, source_target_pairs={{0,6},{1,7},{2,4},{3,5},{4,2},{5,3},{6,0},{7,1},{8,14},{9,15},{10,... | collective-permute-start | bytes 196616 | tf_op jit(solution)/shard_map/gather_residual/ppermute | solution.py:372
  36.3 5.1 %collective-permute-start.15 = (bf16[2,128,128]{2,1,0:T(8,128)(2,1)S(1)}, bf16[2,128,128]{2,1,0:T(8,128)(2,1)S(1)}, u32[]{:S(2)}, u32[]{:S(2)}) collective-permute-start(bf16[2,128,128]{2,1,0:T(8,128)(2,1)S(1)} %get-tuple-element.44.refs_0_), channel_id=1, source_target_pairs={{0,4},{1,5},{2,6},{3,7},{4,0},{5,1},{6,2},{7,3},{8,12},{9,13},{10,... | collective-permute-start | bytes 196616 | tf_op jit(solution)/shard_map/gather_residual/ppermute | solution.py:372
  38.5 4.3 %collective-permute-start.14 = (bf16[2,128,128]{2,1,0:T(8,128)(2,1)S(1)}, bf16[2,128,128]{2,1,0:T(8,128)(2,1)S(1)}, u32[]{:S(2)}, u32[]{:S(2)}) collective-permute-start(bf16[2,128,128]{2,1,0:T(8,128)(2,1)S(1)} %get-tuple-element.44.refs_0_), channel_id=1, source_target_pairs={{0,2},{1,3},{2,0},{3,1},{4,6},{5,7},{6,4},{7,5},{8,10},{9,11},{10,... | collective-permute-start | bytes 196616 | tf_op jit(solution)/shard_map/gather_residual/ppermute | solution.py:372
  39.4 3.3 %collective-permute-start.17 = (bf16[2,128,128]{2,1,0:T(8,128)(2,1)S(1)}, bf16[2,128,128]{2,1,0:T(8,128)(2,1)S(1)}, u32[]{:S(2)}, u32[]{:S(2)}) collective-permute-start(bf16[2,128,128]{2,1,0:T(8,128)(2,1)S(1)} %get-tuple-element.44.refs_0_), channel_id=1, source_target_pairs={{0,1},{1,0},{2,3},{3,2},{4,5},{5,4},{6,7},{7,6},{8,9},{9,8},{10,11... | collective-permute-start | bytes 196616 | tf_op jit(solution)/shard_map/gather_residual/ppermute | solution.py:361
  41.1 1.6 %collective-permute-start.20 = (bf16[2,128,128]{2,1,0:T(8,128)(2,1)S(1)}, bf16[2,128,128]{2,1,0:T(8,128)(2,1)S(1)}, u32[]{:S(2)}, u32[]{:S(2)}) collective-permute-start(bf16[2,128,128]{2,1,0:T(8,128)(2,1)S(1)} %collective-permute-done.16.refs_3_), channel_id=1, source_target_pairs={{0,1},{1,0},{2,3},{3,2},{4,5},{5,4},{6,7},{7,6},{8,9},{9,8},{10,11... | collective-permute-start | bytes 196616 | tf_op jit(solution)/shard_map/gather_residual/ppermute | solution.py:361
  41.4 1.3 %collective-permute-start.19 = (bf16[2,128,128]{2,1,0:T(8,128)(2,1)S(1)}, bf16[2,128,128]{2,1,0:T(8,128)(2,1)S(1)}, u32[]{:S(2)}, u32[]{:S(2)}) collective-permute-start(bf16[2,128,128]{2,1,0:T(8,128)(2,1)S(1)} %collective-permute-done.15.refs_2_), channel_id=1, source_target_pairs={{0,1},{1,0},{2,3},{3,2},{4,5},{5,4},{6,7},{7,6},{8,9},{9,8},{10,11... | collective-permute-start | bytes 196616 | tf_op jit(solution)/shard_map/gather_residual/ppermute | solution.py:361
  42.8 1.3 %collective-permute-start.18 = (bf16[2,128,128]{2,1,0:T(8,128)(2,1)S(1)}, bf16[2,128,128]{2,1,0:T(8,128)(2,1)S(1)}, u32[]{:S(2)}, u32[]{:S(2)}) collective-permute-start(bf16[2,128,128]{2,1,0:T(8,128)(2,1)S(1)} %collective-permute-done.14.refs_1_), channel_id=1, source_target_pairs={{0,1},{1,0},{2,3},{3,2},{4,5},{5,4},{6,7},{7,6},{8,9},{9,8},{10,11... | collective-permute-start | bytes 196616 | tf_op jit(solution)/shard_map/gather_residual/ppermute | solution.py:361
  48.1 1.6 %collective-permute-start.21 = (bf16[1040,128]{1,0:T(8,128)(2,1)S(1)}, bf16[1040,128]{1,0:T(8,128)(2,1)S(1)}, u32[]{:S(2)}, u32[]{:S(2)}) collective-permute-start(bf16[1040,128]{1,0:T(8,128)(2,1)S(1)} %get-tuple-element.50), channel_id=1, source_target_pairs={{0,1},{1,0},{2,3},{3,2},{4,5},{5,4},{6,7},{7,6},{8,9},{9,8},{10,11... | collective-permute-start | bytes 798728 | tf_op jit(solution)/shard_map/sum_second/ppermute | solution.py:361
  49.7 6.1 %collective-permute-start.22 = (bf16[272,128]{1,0:T(8,128)(2,1)S(1)}, bf16[272,128]{1,0:T(8,128)(2,1)S(1)}, u32[]{:S(2)}, u32[]{:S(2)}) collective-permute-start(bf16[272,128]{1,0:T(8,128)(2,1)S(1)} %get-tuple-element.53), channel_id=1, source_target_pairs={{0,6},{1,5},{2,4},{3,7},{4,2},{5,1},{6,0},{7,3},{8,14},{9,13},{10,... | collective-permute-start | bytes 208904 | tf_op jit(solution)/shard_map/sum_second/ppermute | solution.py:372
  50.4 5.8 %collective-permute-start.23 = (bf16[272,128]{1,0:T(8,128)(2,1)S(1)}, bf16[272,128]{1,0:T(8,128)(2,1)S(1)}, u32[]{:S(2)}, u32[]{:S(2)}) collective-permute-start(bf16[272,128]{1,0:T(8,128)(2,1)S(1)} %get-tuple-element.54), channel_id=1, source_target_pairs={{0,2},{1,3},{2,0},{3,1},{4,6},{5,7},{6,4},{7,5},{8,10},{9,11},{10,... | collective-permute-start | bytes 208904 | tf_op jit(solution)/shard_map/sum_second/ppermute | solution.py:372
  51.4 4.7 %collective-permute-start.24 = (bf16[272,128]{1,0:T(8,128)(2,1)S(1)}, bf16[272,128]{1,0:T(8,128)(2,1)S(1)}, u32[]{:S(2)}, u32[]{:S(2)}) collective-permute-start(bf16[272,128]{1,0:T(8,128)(2,1)S(1)} %get-tuple-element.55), channel_id=1, source_target_pairs={{0,4},{1,7},{2,6},{3,5},{4,0},{5,3},{6,2},{7,1},{8,12},{9,15},{10,... | collective-permute-start | bytes 208904 | tf_op jit(solution)/shard_map/sum_second/ppermute | solution.py:372
  56.2 4.9 %collective-permute-start.25 = (bf16[144,128]{1,0:T(8,128)(2,1)S(1)}, bf16[144,128]{1,0:T(8,128)(2,1)S(1)}, u32[]{:S(2)}, u32[]{:S(2)}) collective-permute-start(bf16[144,128]{1,0:T(8,128)(2,1)S(1)} %for_far.3), channel_id=1, source_target_pairs={{0,8},{2,10},{4,12},{6,14},{8,0},{10,2},{12,4},{14,6},{1,9},{3,11}... | collective-permute-start | bytes 110600 | tf_op jit(solution)/shard_map/sum_second/ppermute | solution.py:366
